TPU v7x, 32 devices: a whole 2x2x4 slice. The times are simulated.
32 devices in a mesh: dp: 8 (over z, x), mp: 4 (over y, core).
Axes of the slice: x: 2, y: 2, z: 4, core: 2. Of those that a mesh axis runs over, the one named last changes fastest.
Arguments:
- tokens_in: bfloat16 [128, 128, 768], P('dp', 'mp'), may hold values from -6 to 6
- seg: int32 [128, 128], replicated, may hold values from 0 to 3, as said below
- route: int32 [128], replicated, may hold values from 0 to 127, as said below
- w_qkv: bfloat16 [768, 3, 768], P(None, None, 'mp'), may hold values from -0.21875 to 0.21875
- b_qv: float32 [2, 768], P(None, 'mp'), may hold values from -3 to 3
- w_out: bfloat16 [768, 768], P('mp'), may hold values from -0.625 to 0.625
- b_out: float32 [768], replicated, may hold values from -2 to 2
- gain_attn: float32 [768], replicated, may hold values from 0.5 to 1.5
- bias_attn: float32 [768], replicated, may hold values from -2 to 2
- w_in: bfloat16 [768, 3072], P(None, 'mp'), may hold values from -0.21875 to 0.21875
- b_in: float32 [3072], P('mp'), may hold values from -3 to 3
- w_down: bfloat16 [3072, 768], P('mp'), may hold values from -0.109375 to 0.109375
- b_down: float32 [768], replicated, may hold values from -2 to 2
- gain_ffn: float32 [768], replicated, may hold values from 0.5 to 1.5
- bias_ffn: float32 [768], replicated, may hold values from -2 to 2
- out_grad: bfloat16 [128, 128, 768], P('dp'), may hold values from -6 to 6
- pool_grad: float32 [128, 4, 768], P('dp'), may hold values from -24 to 24
Outputs:
- tokens_out: bfloat16 [128, 128, 768], P('dp', 'mp')
- pooled: float32 [128, 4, 768], P('dp')
- grad_x: bfloat16 [128, 128, 768], P('dp', 'mp')
- grad_w_qkv: float32 [768, 3, 768], P(None, None, 'mp')
- grad_b_qv: float32 [2, 768], P(None, 'mp')
- grad_w_out: float32 [768, 768], P('mp')
- grad_b_out: float32 [768], replicated
- grad_gain_attn: float32 [768], replicated
- grad_bias_attn: float32 [768], replicated
- grad_w_in: float32 [768, 3072], P(None, 'mp')
- grad_b_in: float32 [3072], P('mp')
- grad_w_down: float32 [3072, 768], P('mp')
- grad_b_down: float32 [768], replicated
- grad_gain_ffn: float32 [768], replicated
- grad_bias_ffn: float32 [768], replicated
Inputs may be any that keep to these rules, and one draw needn't show every extreme that they name: route is a permutation of the 128 rows; regrouped row q belongs to index q // 16 of dp; the rows of one index of dp go to 8 different indices, exactly 2 to each. `seg`: each row holds 4 segments in order, each of one or more positions; segment numbers never fall along a row; one segment of each row covers three quarters of the row or more.
All inputs are finite; a program needn't handle non-finite values.
Results may differ from a plain program's by a relative error of at most 0.013.
Values may be sent and summed in bfloat16 or wider, within the bound.
No kernel may reach another device: no remote copies, remote signals or barrier semaphores. Data moves between devices by JAX's collectives and lax.ppermute only.
A program may use at most 192 MiB of HBM per device.

v0:
```python
import jax
import jax.numpy as jnp
from jax import lax
from jax.sharding import PartitionSpec as P

HD = 64
SEGS = 4


EPSILON = 1e-12
MASKED = -1e30


def normalize(values):
    centre = values - jnp.mean(values, axis=-1, keepdims=True)
    scale_inv = lax.rsqrt(jnp.mean(centre * centre, axis=-1, keepdims=True) + EPSILON)
    return (centre * scale_inv, scale_inv[..., 0])


def norm_back(grad_hat, normed_hat, inverse):
    mean_grad = jnp.mean(grad_hat, axis=-1, keepdims=True)
    mean_proj = jnp.mean(grad_hat * normed_hat, axis=-1, keepdims=True)
    return inverse[..., None] * (grad_hat - mean_grad - normed_hat * mean_proj)


def pack_rows(values, position, filled):
    picked = jnp.take(values, position, axis=0)
    shape_mask = filled.reshape((-1,) + (1,) * (values.ndim - 1))
    return jnp.where(shape_mask, picked, jnp.zeros_like(picked))


def per_device(
    tokens_in,
    seg,
    route,
    w_qkv,
    b_qv,
    w_out,
    b_out,
    gain_attn,
    bias_attn,
    w_in,
    b_in,
    w_down,
    b_down,
    gain_ffn,
    bias_ffn,
    out_grad,
    pool_grad,
):
    f32 = jnp.float32
    bf16 = jnp.bfloat16
    devices = lax.axis_size("dp")
    row_local = tokens_in.shape[0]
    quarter = tokens_in.shape[1]
    all_rows = route.shape[0]
    capacity = max(1, row_local // devices)
    buffer_len = devices * capacity
    my_index = lax.axis_index("dp")
    target_dev = route // row_local
    dest_grid = target_dev.reshape(devices, row_local)
    before = jnp.arange(row_local)[None, :] < jnp.arange(row_local)[:, None]
    same_dest = dest_grid[:, :, None] == dest_grid[:, None, :]
    earlier_count = (
        jnp.sum(jnp.where(same_dest & before[None], 1, 0), axis=2).reshape(-1).astype(jnp.int32)
    )
    slot_out = target_dev * capacity + earlier_count
    slot_in = jnp.arange(all_rows, dtype=jnp.int32) // row_local * capacity + earlier_count
    own_slots = lax.dynamic_slice_in_dim(slot_out, my_index * row_local, row_local)
    local_rows = jnp.arange(row_local, dtype=jnp.int32)
    send_pos = jnp.zeros(buffer_len, jnp.int32).at[own_slots].set(local_rows)
    send_fill = jnp.zeros(buffer_len, jnp.bool_).at[own_slots].set(True)
    arrive = jnp.where(target_dev == my_index, route - my_index * row_local, row_local)
    recv_pos = jnp.zeros(row_local, jnp.int32).at[arrive].set(slot_in, mode="drop")
    anchor = (
        jnp.zeros(row_local, jnp.int32)
        .at[arrive]
        .set(jnp.arange(all_rows, dtype=jnp.int32), mode="drop")
    )
    back_pos = jnp.zeros(buffer_len, jnp.int32).at[recv_pos].set(local_rows)
    back_fill = jnp.zeros(buffer_len, jnp.bool_).at[recv_pos].set(True)
    arrived = lax.all_to_all(
        pack_rows(tokens_in, send_pos, send_fill), "dp", split_axis=0, concat_axis=0, tiled=True
    )
    rows_x = jnp.take(arrived, recv_pos, axis=0)
    segment = jnp.take(seg, anchor, axis=0)
    full_len = segment.shape[1]
    mp_index = lax.axis_index("mp")

    def own_part(values):
        return lax.dynamic_slice_in_dim(values, mp_index * quarter, quarter, 1)

    gathered = lax.all_gather(rows_x, "mp", axis=1, tiled=True)
    head_width = w_qkv.shape[2]
    local_heads = head_width // HD
    head_shape = (row_local, full_len, local_heads, HD)
    projected = jnp.einsum("rsd,dcf->rscf", gathered, w_qkv, preferred_element_type=f32)
    query_heads = (projected[:, :, 0] + b_qv[0]).astype(bf16).reshape(head_shape)
    key_heads = projected[:, :, 1].astype(bf16).reshape(head_shape)
    value_heads = (projected[:, :, 2] + b_qv[1]).astype(bf16).reshape(head_shape)
    allowed = (segment[:, :, None] == segment[:, None, :])[:, None]
    factor = HD ** (-0.5)

    def scores_of():
        raw_scores = (
            jnp.einsum("rqhe,rkhe->rhqk", query_heads, key_heads, preferred_element_type=f32)
            * factor
        )
        return jnp.where(allowed, raw_scores, MASKED)

    scores = scores_of()
    row_peak = jnp.max(scores, axis=-1, keepdims=True)
    raised = jnp.exp(scores - row_peak)
    weight_total = jnp.sum(raised, axis=-1, keepdims=True)
    log_total = row_peak + jnp.log(weight_total)
    attention = raised / weight_total
    attended = jnp.einsum(
        "rhqk,rkhe->rqhe", attention.astype(bf16), value_heads, preferred_element_type=f32
    )
    attended = attended.astype(bf16).reshape(row_local, full_len, head_width)
    branch = jnp.einsum("rsf,fd->rsd", attended, w_out, preferred_element_type=f32)
    summed_branch = lax.psum_scatter(branch, "mp", scatter_dimension=1, tiled=True)
    hat_attn, inv_attn = normalize(rows_x.astype(f32) + summed_branch + b_out)
    normed_low = (hat_attn * gain_attn + bias_attn).astype(bf16)
    normed_all = lax.all_gather(normed_low, "mp", axis=1, tiled=True)
    hidden = jnp.einsum("rsd,df->rsf", normed_all, w_in, preferred_element_type=f32) + b_in
    active, gelu_back = jax.vjp(lambda values: jax.nn.gelu(values, approximate=False), hidden)
    active_low = active.astype(bf16)
    ffn_part = jnp.einsum("rsf,fd->rsd", active_low, w_down, preferred_element_type=f32)
    ffn_total = lax.psum(ffn_part, "mp")
    hat_ffn, inv_ffn = normalize(normed_all.astype(f32) + ffn_total + b_down)
    block_out = hat_ffn * gain_ffn + bias_ffn
    output_rows = own_part(block_out).astype(bf16)
    member = (segment[:, :, None] == jnp.arange(SEGS)[None, None, :]).astype(f32)
    counts = jnp.sum(member, axis=1)
    pooled_rows = (
        jnp.einsum("rsg,rsd->rgd", member, block_out, precision=lax.Precision.HIGHEST)
        / counts[:, :, None]
    )
    pooled_back = lax.all_to_all(
        pack_rows(pooled_rows, back_pos, back_fill).astype(jnp.bfloat16),
        "dp",
        split_axis=0,
        concat_axis=0,
        tiled=True,
    ).astype(jnp.float32)
    pooled = jnp.take(pooled_back, own_slots, axis=0)
    pool_arrived = lax.all_to_all(
        pack_rows(pool_grad, send_pos, send_fill), "dp", split_axis=0, concat_axis=0, tiled=True
    )
    pool_rows = jnp.take(pool_arrived, recv_pos, axis=0)
    grad_final = out_grad.astype(f32) + jnp.einsum(
        "rsg,rgd->rsd", member, pool_rows / counts[:, :, None], precision=lax.Precision.HIGHEST
    )
    grad_mix = norm_back(grad_final * gain_ffn, hat_ffn, inv_ffn)
    grad_gain_ffn = jnp.sum(grad_final * hat_ffn, axis=(0, 1))
    grad_bias_ffn = jnp.sum(grad_final, axis=(0, 1))
    grad_b_down = jnp.sum(grad_mix, axis=(0, 1))
    mix_low = grad_mix.astype(bf16)
    grad_w_down = jnp.einsum("rsf,rsd->fd", active_low, mix_low, preferred_element_type=f32)
    grad_active = jnp.einsum("rsd,fd->rsf", mix_low, w_down, preferred_element_type=f32)
    grad_hidden = gelu_back(grad_active)[0].astype(bf16)
    grad_w_in = jnp.einsum("rsd,rsf->df", normed_all, grad_hidden, preferred_element_type=f32)
    grad_b_in = jnp.sum(grad_hidden.astype(f32), axis=(0, 1))
    normed_part = jnp.einsum("rsf,df->rsd", grad_hidden, w_in, preferred_element_type=f32)
    grad_normed = lax.psum_scatter(normed_part, "mp", scatter_dimension=1, tiled=True) + own_part(
        grad_mix
    )
    gain_attn_part = jnp.sum(grad_normed * hat_attn, axis=(0, 1))
    bias_attn_part = jnp.sum(grad_normed, axis=(0, 1))
    grad_inner = norm_back(grad_normed * gain_attn, hat_attn, inv_attn)
    stat_terms = jnp.stack([jnp.sum(grad_inner, axis=(0, 1)), gain_attn_part, bias_attn_part])[None]
    inner_all, stats_all = (
        lax.all_gather(grad_inner.astype(jnp.bfloat16), "mp", axis=1, tiled=True).astype(
            grad_inner.dtype
        ),
        lax.all_gather(stat_terms.astype(jnp.bfloat16), "mp", axis=0, tiled=True).astype(
            stat_terms.dtype
        ),
    )
    stat_sums = jnp.sum(stats_all, axis=0)
    inner_low = inner_all.astype(bf16)
    grad_w_out = jnp.einsum("rsf,rsd->fd", attended, inner_low, preferred_element_type=f32)
    grad_attended = (
        jnp.einsum("rsd,fd->rsf", inner_low, w_out, preferred_element_type=f32)
        .astype(bf16)
        .reshape(head_shape)
    )
    again = jnp.exp(scores_of() - log_total)
    grad_prob = jnp.einsum(
        "rqhe,rkhe->rhqk", grad_attended, value_heads, preferred_element_type=f32
    )
    grad_values = jnp.einsum(
        "rhqk,rqhe->rkhe", again.astype(bf16), grad_attended, preferred_element_type=f32
    )
    grad_scores = (again * (grad_prob - jnp.sum(grad_prob * again, axis=-1, keepdims=True))).astype(
        bf16
    )
    grad_query = (
        jnp.einsum("rhqk,rkhe->rqhe", grad_scores, key_heads, preferred_element_type=f32) * factor
    ).astype(bf16)
    grad_keys = (
        jnp.einsum("rhqk,rqhe->rkhe", grad_scores, query_heads, preferred_element_type=f32) * factor
    ).astype(bf16)
    flat_shape = (row_local, full_len, head_width)
    grad_mixed = jnp.stack(
        [
            grad_query.reshape(flat_shape),
            grad_keys.reshape(flat_shape),
            grad_values.astype(bf16).reshape(flat_shape),
        ],
        axis=2,
    )
    grad_w_qkv = jnp.einsum("rsd,rscf->dcf", gathered, grad_mixed, preferred_element_type=f32)
    grad_b_qv = jnp.stack(
        [
            jnp.sum(grad_mixed[:, :, 0].astype(f32), axis=(0, 1)),
            jnp.sum(grad_mixed[:, :, 2].astype(f32), axis=(0, 1)),
        ]
    )
    input_part = jnp.einsum("rscf,dcf->rsd", grad_mixed, w_qkv, preferred_element_type=f32)
    grad_rows = (
        lax.psum_scatter(input_part, "mp", scatter_dimension=1, tiled=True) + grad_inner
    ).astype(bf16)
    grad_home = lax.all_to_all(
        pack_rows(grad_rows, back_pos, back_fill), "dp", split_axis=0, concat_axis=0, tiled=True
    )
    grad_input = jnp.take(grad_home, own_slots, axis=0)
    vector_grads = jnp.stack(
        [stat_sums[0], stat_sums[1], stat_sums[2], grad_b_down, grad_gain_ffn, grad_bias_ffn]
    )
    totals = lax.psum(
        (grad_w_qkv, grad_b_qv, grad_w_out, grad_w_in, grad_b_in, grad_w_down, vector_grads), "dp"
    )
    return (
        output_rows,
        pooled,
        grad_input,
        totals[0],
        totals[1],
        totals[2],
        totals[6][0],
        totals[6][1],
        totals[6][2],
        totals[3],
        totals[4],
        totals[5],
        totals[6][3],
        totals[6][4],
        totals[6][5],
    )


def solution(mesh):
    return jax.shard_map(
        per_device,
        mesh=mesh,
        in_specs=(
            P("dp", "mp", None),
            P(),
            P(),
            P(None, None, "mp"),
            P(None, "mp"),
            P("mp", None),
            P(),
            P(),
            P(),
            P(None, "mp"),
            P("mp"),
            P("mp", None),
            P(),
            P(),
            P(),
            P("dp", None, None),
            P("dp", None, None),
        ),
        out_specs=(
            P("dp", "mp", None),
            P("dp", None, None),
            P("dp", "mp", None),
            P(None, None, "mp"),
            P(None, "mp"),
            P("mp", None),
            P(),
            P(),
            P(),
            P(None, "mp"),
            P("mp"),
            P("mp", None),
            P(),
            P(),
            P(),
        ),
        check_vma=False,
    )
```

profile of v0, /device:TPU:4, one launch (start us, length us, event | category | flops | bytes accessed | tf_op | source)
XLA Modules:
  0.0 795.5 jit_solution(7515726337202355531)
XLA Ops:
  10.4 1.7 gather_fusion.1
  13.2 5.9 all-to-all-start
  20.8 18.6 %all-to-all-done = bf16[16,32,768]{2,1,0:T(8,128)(2,1)S(1)} async-done(((bf16[16,32,768]{2,1,0:T(8,128)(2,1)}), bf16[16,32,768]{2,1,0:T(8,128)(2,1)S(1)}, u32[]{:S(2)}, u32[]{:S(2)}) %all-to-all-start) | async-done | bytes 786464 | tf_op jit(solution)/shard_map/all_to_all | solution.py:82
  43.3 24.2 %all-gather.4.cloned.1.call-done = bf16[16,128,768]{2,1,0:T(8,128)(2,1)} async-done(((bf16[16,32,768]{2,1,0:T(8,128)(2,1)}), bf16[16,128,768]{2,1,0:T(8,128)(2,1)}) %all-gather.4.cloned.1.call-update) | async-done | bytes 3145744 | tf_op jit(solution)/shard_map/all_gather | solution.py:93
  67.5 4.2 fusion.8
  76.2 3.7 fusion.38
  80.0 58.5 %reduce-scatter.4.cloned.1.call-done = f32[16,32,768]{2,1,0:T(8,128)} async-done(((f32[16,128,768]{2,1,0:T(8,128)}), f32[16,32,768]{2,1,0:T(8,128)}) %reduce-scatter.4.cloned.1.call-update) | async-done | bytes 1572880 | tf_op jit(solution)/shard_map/reduce_scatter | solution.py:122
  138.5 1.8 fusion.69
  140.6 1.9 add_convert_fusion.2
  142.8 28.4 %all-gather.6.cloned.1.call-done = bf16[16,128,768]{2,1,0:T(8,128)(2,1)} async-done(((bf16[16,32,768]{2,1,0:T(8,128)(2,1)}), bf16[16,128,768]{2,1,0:T(8,128)(2,1)}) %all-gather.6.cloned.1.call-update) | async-done | bytes 3145744 | tf_op jit(solution)/shard_map/all_gather | solution.py:125
  171.2 6.1 fusion.11
  177.4 15.2 %multiply_convert_fusion = (bf16[16,128,768]{2,1,0:T(8,128)(2,1)S(1)}, f32[16,128,768]{2,1,0:T(8,128)}) fusion(f32[16,128,768]{2,1,0:T(8,128)S(1)} %get-tuple-element.64, f32[768]{0:T(1024)S(1)} %copy-done.50, u16[128,768]{1,0:T(8,128)(2,1)S(1)} %get-tuple-element.21, u16[128,768]{1,0:T(8,128)(2,1)S(1)} %get-tuple-element.20), kind=kLoop, calls=%fused_computation.31 | loop fusion | flops 111673344 | bytes 16124928 | tf_op jit(solution)/shard_map/convert_element_type | solution.py:128
  192.6 1.7 copy-done.9
  194.3 4.5 fusion.28
  201.4 5.7 all-to-all-start.2
  207.8 7.7 all-to-all-done.2
  216.3 102.6 %all-reduce.5.cloned.1.call-done = f32[16,128,768]{2,1,0:T(8,128)} async-done(((f32[16,128,768]{2,1,0:T(8,128)}), f32[16,128,768]{2,1,0:T(8,128)}) %all-reduce.5.cloned.1.call-update) | async-done | bytes 6291472 | tf_op jit(solution)/shard_map/psum | solution.py:130
  318.8 4.6 fusion.67
  325.4 8.0 %multiply_reduce_fusion = (f32[768]{0:T(1024)}, f32[16,128]{1,0:T(8,128)S(1)}, f32[16,128]{1,0:T(8,128)S(1)}, f32[768]{0:T(1024)}, f32[16,128,768]{2,1,0:T(8,128)}) fusion(f32[16,128,768]{2,1,0:T(8,128)S(1)} %get-tuple-element.50, f32[16,128]{1,0:T(8,128)S(1)} %add_rsqrt_fusion, f32[16,128]{1,0:T(8,128)S(1)} %broadcast_multiply_fusion.2, ...), kind=kOutput, calls=%fused_computation.23 | convolution fusion | flops 92899840 | bytes 15975696 | tf_op jit(solution)/shard_map/rsg,rgd->rsd/dot_general | solution.py:152
  333.5 6.9 fusion.66
  340.4 10.6 %convert_reduce_fusion = (f32[768]{0:T(1024)}, bf16[16,128,768]{2,1,0:T(8,128)(2,1)}) fusion(f32[16,128,768]{2,1,0:T(8,128)} %get-tuple-element.52, bf16[768,768]{1,0:T(8,128)(2,1)S(1)} %copy-done.68, f32[16,128,768]{2,1,0:T(8,128)S(1)} %get-tuple-element.45, f32[16,128,768]{2,1,0:T(8,128)S(1)} %bitcast.101, f32[768]{0:T(1024)S(1)} %copy-done.50), kind=kOutput, calls=%fused_computation.22 | convolution fusion | flops 2444229888 | bytes 23205888 | tf_op jit(solution)/shard_map/rsd,fd->rsf/dot_general | solution.py:161
  351.1 7.1 fusion.30
  358.3 58.4 %reduce-scatter.6.cloned.1.call-done = f32[16,32,768]{2,1,0:T(8,128)} async-done(((f32[16,128,768]{2,1,0:T(8,128)}), f32[16,32,768]{2,1,0:T(8,128)}) %reduce-scatter.6.cloned.1.call-update) | async-done | bytes 1572880 | tf_op jit(solution)/shard_map/reduce_scatter | solution.py:166
  416.7 3.4 multiply_reduce_fusion.5
  420.1 1.1 fusion.65
  421.2 1.2 copy-done.7
  423.6 28.4 %all-gather.8.cloned.1.call-done = bf16[16,128,768]{2,1,0:T(8,128)(2,1)} async-done(((bf16[16,32,768]{2,1,0:T(8,128)(2,1)}), bf16[16,128,768]{2,1,0:T(8,128)(2,1)}) %all-gather.8.cloned.1.call-update) | async-done | bytes 3145744 | tf_op jit(solution)/shard_map/all_gather | solution.py:174
  452.1 3.1 convolution_convert_fusion
  455.2 1.3 convert_reduce_fusion.1
  456.6 1.1 multiply_reduce_fusion.4
  459.1 1.2 multiply_convert_fusion.2
  461.9 4.5 convolution_bitcast_fusion
  466.5 7.1 convolution_bitcast_fusion.2
  473.6 7.9 convolution_bitcast_fusion.1
  481.5 1.6 convolution_bitcast_fusion.3
  483.1 3.3 fusion.20
  488.0 6.0 convolution_divide_fusion
  495.5 5.8 all-to-all-start.1
  501.2 23.7 %reduce-scatter.8.cloned.1.call-done = f32[16,32,768]{2,1,0:T(8,128)} async-done(((f32[16,128,768]{2,1,0:T(8,128)}), f32[16,32,768]{2,1,0:T(8,128)}) %reduce-scatter.8.cloned.1.call-update) | async-done | bytes 1572880 | tf_op jit(solution)/shard_map/reduce_scatter | solution.py:223
  524.9 1.6 add_convert_fusion.1
  528.3 5.7 all-to-all-start.3
  534.1 2.4 dynamic-slice_convert_fusion
  538.1 5.2 all_gather.15
  543.5 54.5 %all-reduce = (f32[2,192]{1,0:T(2,128)}, f32[6,768]{1,0:T(8,128)S(1)}, f32[768]{0:T(1024)}) all-reduce(f32[2,192]{1,0:T(2,128)S(1)} %pad_maximum_fusion.5, f32[6,768]{1,0:T(8,128)S(1)} %pad_maximum_fusion.3, f32[768]{0:T(1024)S(1)} %copy-done.51), channel_id=1, replica_groups=mesh['dp'=8,'mp'=4] {'dp'}, use_global_device_ids=true, to_apply=%region_26.29 | all-reduce | flops 5760 | bytes 46080 | tf_op jit(solution)/shard_map/psum | solution.py:232
  600.3 181.5 %all-reduce.7.cloned.1.call-done = (f32[768,3,192]{0,2,1:T(8,128)}, f32[192,768]{1,0:T(8,128)}, f32[768,768]{1,0:T(8,128)}, f32[768,768]{1,0:T(8,128)}) async-done(((f32[768,3,192]{0,2,1:T(8,128)}, f32[192,768]{1,0:T(8,128)}, f32[768,768]{1,0:T(8,128)}, f32[768,768]{1,0:T(8,128)}), (f32[768,3,192]{0,2,1:T(8,128)}, f32[192,768]{1,0:T(8,128)}, f32[768,768]{1,0:T(8,128)}, ...) | async-done | bytes 7077904 | tf_op jit(solution)/shard_map/psum | solution.py:232
  781.8 2.9 copy.72
  785.6 1.4 copy.74
  787.0 1.4 copy.75
  (247 shorter events, 34.4 us)
Async XLA Ops:
  7.2 164.0 %copy-start = (bf16[768,768]{1,0:T(8,128)(2,1)S(1)}, bf16[768,768]{1,0:T(8,128)(2,1)}, u32[]{:S(2)}) copy-start(bf16[768,768]{1,0:T(8,128)(2,1)} %param.30) | copy-start | bytes 3538948
  9.7 9.5 %copy-start.70 = (pred[16]{0:T(512)(128)(4,1)}, pred[16]{0:T(512)(128)(4,1)S(1)}, u32[]{:S(2)}) copy-start(pred[16]{0:T(512)(128)(4,1)S(1)} %broadcast.246) | copy-start | bytes 52
  13.2 28.8 %copy-start.61 = (f32[2,192]{1,0:T(2,128)S(1)}, f32[2,192]{1,0:T(2,128)}, u32[]{:S(2)}) copy-start(f32[2,192]{1,0:T(2,128)} %param.25) | copy-start | bytes 4612
  13.2 29.0 %copy-start.35 = (s32[128,128]{1,0:T(8,128)S(1)}, s32[128,128]{1,0:T(8,128)}, u32[]{:S(2)}) copy-start(s32[128,128]{1,0:T(8,128)} %param.22) | copy-start | bytes 196612
  13.2 26.1 %all-to-all-start = ((bf16[16,32,768]{2,1,0:T(8,128)(2,1)}), bf16[16,32,768]{2,1,0:T(8,128)(2,1)S(1)}, u32[]{:S(2)}, u32[]{:S(2)}) async-start(bf16[16,32,768]{2,1,0:T(8,128)(2,1)} %select_select_fusion.1), calls=%async_computation | async-start | bytes 1572864 | tf_op jit(solution)/shard_map/all_to_all | solution.py:82
  19.2 48.3 %all-gather.4.cloned.1.call-start = ((), (), s32[]{:S(2)}) async-start(), calls=%async_computation.7 | async-start | bytes 3932160 | tf_op jit(solution)/shard_map/all_gather | solution.py:93
  20.7 21.5 %copy-start.46 = (s32[1024]{0:T(1024)}, s32[1024]{0:T(1024)S(1)}, u32[]{:S(2)}) copy-start(s32[1024]{0:T(1024)S(1)} %pad_clamp_fusion.3) | copy-start | bytes 12292
  20.7 21.5 %copy-start.55 = (pred[16]{0:T(512)(128)(4,1)}, pred[16]{0:T(512)(128)(4,1)S(1)}, u32[]{:S(2)}) copy-start(pred[16]{0:T(512)(128)(4,1)S(1)} %compare_and_fusion.2) | copy-start | bytes 52
  41.0 97.5 %reduce-scatter.4.cloned.1.call-start = ((), (), s32[]{:S(2)}) async-start(), calls=%async_computation.8 | async-start | bytes 7864320 | tf_op jit(solution)/shard_map/reduce_scatter | solution.py:122
  42.1 32.3 %copy-start.43 = (f32[3,64]{1,0:T(4,128)}, f32[3,64]{1,0:T(4,128)S(1)}, u32[]{:S(2)}) copy-start(f32[3,64]{1,0:T(4,128)S(1)} %add.171) | copy-start | bytes 2308
  80.0 60.7 %copy-start.36 = (f32[768]{0:T(1024)S(1)}, f32[768]{0:T(1024)}, u32[]{:S(2)}) copy-start(f32[768]{0:T(1024)} %param.28) | copy-start | bytes 9220
  80.0 91.2 %all-gather.6.cloned.1.call-start = ((), (), s32[]{:S(2)}) async-start(), calls=%async_computation.9 | async-start | bytes 3932160 | tf_op jit(solution)/shard_map/all_gather | solution.py:125
  140.3 30.9 %copy-start.50 = (f32[768]{0:T(1024)S(1)}, f32[768]{0:T(1024)}, u32[]{:S(2)}) copy-start(f32[768]{0:T(1024)} %param.31) | copy-start | bytes 9220
  142.5 176.3 %all-reduce.5.cloned.1.call-start = ((), (), s32[]{:S(2)}) async-start(), calls=%async_computation.10 | async-start | bytes 12582912 | tf_op jit(solution)/shard_map/psum | solution.py:130
  177.4 15.2 %copy-start.13 = (f32[16,128,768]{2,1,0:T(8,128)}, f32[16,128,768]{2,1,0:T(8,128)S(1)}, u32[]{:S(2)}) copy-start(f32[16,128,768]{2,1,0:T(8,128)S(1)} %get-tuple-element.64) | copy-start | bytes 18874372
  177.4 16.9 %copy-start.67 = (bf16[768,768]{1,0:T(8,128)(2,1)S(1)}, bf16[768,768]{1,0:T(8,128)(2,1)}, u32[]{:S(2)}) copy-start(bf16[768,768]{1,0:T(8,128)(2,1)} %param.32) | copy-start | bytes 3538948
  198.9 120.0 %copy-start.54 = (f32[768]{0:T(1024)S(1)}, f32[768]{0:T(1024)}, u32[]{:S(2)}) copy-start(f32[768]{0:T(1024)} %param.33) | copy-start | bytes 9220
  201.4 14.1 %all-to-all-start.2 = ((f32[16,4,768]{2,1,0:T(4,128)}), f32[16,4,768]{2,1,0:T(4,128)S(1)}, u32[]{:S(2)}, u32[]{:S(2)}) async-start(f32[16,4,768]{2,1,0:T(4,128)} %select_select_fusion.2), calls=%async_computation.3 | async-start | bytes 393216 | tf_op jit(solution)/shard_map/all_to_all | solution.py:148
  207.1 209.6 %reduce-scatter.6.cloned.1.call-start = ((), (), s32[]{:S(2)}) async-start(), calls=%async_computation.11 | async-start | bytes 7864320 | tf_op jit(solution)/shard_map/reduce_scatter | solution.py:166
  207.7 116.6 %copy-start.37 = (f32[16,4]{1,0:T(8,128)}, f32[16,4]{1,0:T(8,128)S(1)}, u32[]{:S(2)}) copy-start(f32[16,4]{1,0:T(8,128)S(1)} %convert_reduce_fusion.4) | copy-start | bytes 772
  325.4 8.1 %copy-start.49 = (f32[768]{0:T(1024)S(1)}, f32[768]{0:T(1024)}, u32[]{:S(2)}) copy-start(f32[768]{0:T(1024)} %param.35) | copy-start | bytes 9220
  325.4 15.0 %slice-start = ((s8[6291456]{0:T(1024)(128)(4,1)}), s8[4194304]{0:T(1024)(128)(4,1)S(1)}, s32[]{:S(2)}) async-start(s8[6291456]{0:T(1024)(128)(4,1)} %bitcast.100), calls=%async_computation.15 | async-start | bytes 8388608
  333.4 7.0 slice-start.1
  333.4 7.0 copy-start.68
  340.4 10.7 %copy-start.4 = (f32[16,128,768]{2,1,0:T(8,128)}, f32[16,128,768]{2,1,0:T(8,128)S(1)}, u32[]{:S(2)}) copy-start(f32[16,128,768]{2,1,0:T(8,128)S(1)} %get-tuple-element.45) | copy-start | bytes 18874372
  358.2 93.9 %all-gather.8.cloned.1.call-start = ((), (), s32[]{:S(2)}) async-start(), calls=%async_computation.12 | async-start | bytes 3932160 | tf_op jit(solution)/shard_map/all_gather | solution.py:174
  420.1 32.0 %copy-start.31 = (bf16[192,768]{1,0:T(8,128)(2,1)S(1)}, bf16[192,768]{1,0:T(8,128)(2,1)}, u32[]{:S(2)}) copy-start(bf16[192,768]{1,0:T(8,128)(2,1)} %param.26) | copy-start | bytes 884740
  423.3 31.8 %copy-start.3 = (f32[16,3,128,128]{2,3,1,0:T(8,128)S(1)}, f32[16,3,128,128]{2,3,1,0:T(8,128)}, u32[]{:S(2)}) copy-start(f32[16,3,128,128]{2,3,1,0:T(8,128)} %copy-done.2) | copy-start | bytes 9437188
  423.4 101.6 %reduce-scatter.8.cloned.1.call-start = ((), (), s32[]{:S(2)}) async-start(), calls=%async_computation.13 | async-start | bytes 7864320 | tf_op jit(solution)/shard_map/reduce_scatter | solution.py:223
  456.5 4.5 copy-start.25
  466.4 7.1 copy-start.10
  466.4 315.4 %all-reduce.7.cloned.1.call-start = ((), (), s32[]{:S(2)}) async-start(), calls=%async_computation.14 | async-start | bytes 14155776 | tf_op jit(solution)/shard_map/psum | solution.py:232
  473.5 7.9 copy-start.16
  473.6 7.9 copy-start.18
  473.6 9.5 %copy-start.66 = (bf16[16,128,768]{2,1,0:T(8,128)(2,1)S(1)}, bf16[16,128,768]{2,1,0:T(8,128)(2,1)}, u32[]{:S(2)}) copy-start(bf16[16,128,768]{2,1,0:T(8,128)(2,1)} %all-gather.4.cloned.1.call-done) | copy-start | bytes 9437188
  488.0 37.0 %copy-start.8 = (f32[16,32,768]{2,1,0:T(8,128)S(1)}, f32[16,32,768]{2,1,0:T(8,128)}, u32[]{:S(2)}) copy-start(f32[16,32,768]{2,1,0:T(8,128)} %copy-done.7) | copy-start | bytes 4718596
  495.5 32.8 %all-to-all-start.1 = ((bf16[16,4,768]{2,1,0:T(4,128)(2,1)}), bf16[16,4,768]{2,1,0:T(4,128)(2,1)S(1)}, u32[]{:S(2)}, u32[]{:S(2)}) async-start(bf16[16,4,768]{2,1,0:T(4,128)(2,1)} %fusion.42), calls=%async_computation.2 | async-start | bytes 196608 | tf_op jit(solution)/shard_map/all_to_all | solution.py:140
  526.5 7.5 copy-start.63
  526.5 7.5 copy-start.53
  526.5 7.5 copy-start.52
  526.5 7.6 copy-start.39
  526.5 10.7 %copy-start.47 = (pred[16]{0:T(512)(128)(4,1)S(1)}, pred[16]{0:T(512)(128)(4,1)}, u32[]{:S(2)}) copy-start(pred[16]{0:T(512)(128)(4,1)} %get-tuple-element.47) | copy-start | bytes 52
  527.2 10.8 %copy-start.41 = (bf16[768]{0:T(1024)(128)(2,1)S(1)}, bf16[768]{0:T(1024)(128)(2,1)}, u32[]{:S(2)}) copy-start(bf16[768]{0:T(1024)(128)(2,1)} %get-tuple-element.23) | copy-start | bytes 4612
  527.2 10.8 %copy-start.40 = (bf16[768]{0:T(1024)(128)(2,1)S(1)}, bf16[768]{0:T(1024)(128)(2,1)}, u32[]{:S(2)}) copy-start(bf16[768]{0:T(1024)(128)(2,1)} %get-tuple-element.26) | copy-start | bytes 4612
  527.2 10.8 %copy-start.42 = (bf16[768]{0:T(1024)(128)(2,1)S(1)}, bf16[768]{0:T(1024)(128)(2,1)}, u32[]{:S(2)}) copy-start(bf16[768]{0:T(1024)(128)(2,1)} %get-tuple-element.42) | copy-start | bytes 4612
  527.2 16.3 %copy-start.51 = (f32[768]{0:T(1024)S(1)}, f32[768]{0:T(1024)}, u32[]{:S(2)}) copy-start(f32[768]{0:T(1024)} %get-tuple-element.72) | copy-start | bytes 9220
  528.3 70.4 %all-to-all-start.3 = ((bf16[16,32,768]{2,1,0:T(8,128)(2,1)}), bf16[16,32,768]{2,1,0:T(8,128)(2,1)S(1)}, u32[]{:S(2)}, u32[]{:S(2)}) async-start(bf16[16,32,768]{2,1,0:T(8,128)(2,1)} %select_select_fusion), calls=%async_computation.6 | async-start | bytes 1572864 | tf_op jit(solution)/shard_map/all_to_all | solution.py:225
  781.8 3.8 copy-start.20
  (37 other events, 62.8 us)
Sparse Core Ops, SparseCore 0:
  41.1 26.3 all-gather.3
  80.1 58.3 reduce-scatter.3
  142.6 28.5 all-gather.5
  199.0 119.7 all-reduce.4
  358.3 58.3 reduce-scatter.5
  423.5 28.5 all-gather.7
  466.5 58.3 reduce-scatter.7
  531.1 250.6 all-reduce.6
where the time goes:
time: 804 us; the launch traced here: 795 us
  waiting for transfers between devices  532 us (66%)
  matrix products  83.7 us (10%)
  blocking collectives  59.7 us (7%)
  other arithmetic  49.1 us (6%)
  local copies, waits for them, and re-layouts  30.9 us (4%)
  starting transfers between devices  24.4 us (3%)
  between operations  15.4 us (2%)
    psum x1, waiting for transfers between devices, per_device(): lax.psum((grad_w_qkv, grad_b_qv, grad_w_out, grad_w_in, grad_b_in, grad_w...  182 us
    psum x1, waiting for transfers between devices, per_device(): ffn_total = lax.psum(ffn_part, 'mp')  103 us
    reduce_scatter x1, waiting for transfers between devices, per_device(): lax.psum_scatter(branch, 'mp', scatter_dimension=1, tiled=True)  58.5 us
    reduce_scatter x1, waiting for transfers between devices, per_device(): lax.psum_scatter(normed_part, 'mp', scatter_dimension=1, tiled=True)  58.4 us
    psum x1, blocking collectives, per_device(): lax.psum((grad_w_qkv, grad_b_qv, grad_w_out, grad_w_in, grad_b_in, grad_w...  54.5 us
    all_gather x1, waiting for transfers between devices, per_device(): lax.all_gather(grad_inner.astype(jnp.bfloat16), 'mp', axis=1, tiled=True)  28.4 us
    all_gather x1, waiting for transfers between devices, per_device(): normed_all = lax.all_gather(normed_low, 'mp', axis=1, tiled=True)  28.4 us
    all_gather x1, waiting for transfers between devices, per_device(): gathered = lax.all_gather(rows_x, 'mp', axis=1, tiled=True)  24.2 us
  transfers between devices with their start and end apart: 12, of which 10 were waited for; matrix products, arithmetic and copies ran while one was open for 6% of the time, Pallas kernels for 0%

commit v1 on v0

--- a/solution.py
+++ b/solution.py
@@ -1,6 +1,8 @@
 import jax
 import jax.numpy as jnp
 from jax import lax
+from jax.experimental import pallas as pl
+from jax.experimental.pallas import tpu as pltpu
 from jax.sharding import PartitionSpec as P
 
 HD = 64
@@ -9,6 +11,8 @@
 
 EPSILON = 1e-12
 MASKED = -1e30
+f32 = jnp.float32
+bf16 = jnp.bfloat16
 
 
 def normalize(values):
@@ -29,7 +33,7 @@
     return jnp.where(shape_mask, picked, jnp.zeros_like(picked))
 
 
-def per_device(
+def per_device_general(
     tokens_in,
     seg,
     route,
@@ -251,9 +255,1351 @@
     )
 
 
+VM = pl.BlockSpec(memory_space=pltpu.VMEM)
+SM = pl.BlockSpec(memory_space=pltpu.SMEM)
+HB = pl.BlockSpec(memory_space=pl.ANY)
+HM = pl.BlockSpec(memory_space=pltpu.HBM)
+ROOM = 48 * 1024 * 1024
+
+
+def shape_of(shape, dtype=bf16):
+    return jax.ShapeDtypeStruct(shape, dtype)
+
+
+def call(
+    body, outs, out_specs, in_specs, scratch=(), us=2, room=ROOM, name=None, after=()
+):
+    n, extra = len(in_specs), len(after)
+
+    def trimmed(*refs):
+        body(*refs[:n], *refs[n + extra :])
+
+    made = pl.pallas_call(
+        trimmed,
+        out_shape=outs,
+        in_specs=list(in_specs) + [HB] * extra,
+        out_specs=out_specs,
+        scratch_shapes=list(scratch),
+        compiler_params=pltpu.CompilerParams(vmem_limit_bytes=room),
+        cost_estimate=pl.CostEstimate(flops=int(us * 1.15e9), bytes_accessed=0, transcendentals=0),
+        name=name,
+    )
+    return lambda *args: made(*args, *after)
+
+
+def mm(a, b):
+    return lax.dot_general(a, b, (((1,), (0,)), ((), ())), preferred_element_type=f32)
+
+
+def mm_nt(a, b):
+    return lax.dot_general(a, b, (((1,), (1,)), ((), ())), preferred_element_type=f32)
+
+
+def mm_tn(a, b):
+    return lax.dot_general(a, b, (((0,), (0,)), ((), ())), preferred_element_type=f32)
+
+
+def split3(values):
+    high = values.astype(bf16)
+    rest = values - high.astype(f32)
+    middle = rest.astype(bf16)
+    low = (rest - middle.astype(f32)).astype(bf16)
+    return high, middle, low
+
+
+def prep_rows(sent, tokens, b_qv, b_in, dims):
+    devices, count, rows, quarter, full, width = dims
+    here = rows // count
+    head_width = b_qv.shape[1]
+    tile = here * quarter
+
+    def body(sent_ref, tok, bqv_ref, bin_ref, x0, x1, x2, x3, extra, sems):
+        xs = (x0, x1, x2, x3)
+        copies = []
+        for kk in reversed(range(count)):
+            for j in range(here):
+                at = kk * here + j
+                copies.append(
+                    pltpu.make_async_copy(
+                        tok.at[sent_ref[at]], xs[kk].at[pl.ds(j * quarter, quarter)], sems.at[at]
+                    )
+                )
+        for copy in copies:
+            copy.start()
+        extra[...] = jnp.zeros_like(extra)
+        for j, term in enumerate(split3(bqv_ref[...])):
+            extra[j : j + 1, 0:head_width] = term[0:1]
+            extra[j : j + 1, 256 : 256 + head_width] = term[1:2]
+        for j, term in enumerate(split3(bin_ref[...])):
+            extra[3 + j : 4 + j, :] = term
+        tails = [
+            pltpu.make_async_copy(extra, xs[kk].at[pl.ds(tile, 16)], sems.at[rows + kk])
+            for kk in range(count)
+        ]
+        for copy in tails:
+            copy.start()
+        for copy in copies + tails:
+            copy.wait()
+
+    return call(
+        body,
+        [shape_of((tile + 16, width))] * count,
+        [HB] * count,
+        [SM, HM, VM, VM],
+        [pltpu.VMEM((16, width), bf16), pltpu.SemaphoreType.DMA((rows + count,))],
+        us=2,
+        name="prep_rows",
+    )(sent, tokens, b_qv, b_in.reshape(1, -1))
+
+
+def prep_halves(ids, w_q, w_out, w_in, w_down, after):
+    width = w_q.shape[1]
+    halves = [w.shape[0] // 2 for w in (w_q, w_out, w_in, w_down)]
+
+    def body(ids_ref, wq, wo, wi, wd, q, oi, dn, sems):
+        parity = ids_ref[2]
+
+        def copy(src, half, dst, at):
+            return pltpu.make_async_copy(
+                src.at[pl.ds(pl.multiple_of(parity * half, 16), half)], dst, sems.at[at]
+            )
+
+        copies = [
+            copy(wq, halves[0], q, 0),
+            copy(wo, halves[1], oi.at[pl.ds(0, halves[1])], 1),
+            copy(wi, halves[2], oi.at[pl.ds(halves[1], halves[2])], 2),
+            copy(wd, halves[3], dn, 3),
+        ]
+        for c in copies:
+            c.start()
+        for c in copies:
+            c.wait()
+
+    return call(
+        body,
+        [
+            shape_of((halves[0], width)),
+            shape_of((halves[1] + halves[2], width)),
+            shape_of((halves[3], width)),
+        ],
+        [VM] * 3,
+        [SM] + [HM] * 4,
+        [pltpu.SemaphoreType.DMA((4,))],
+        us=2,
+        name="prep_halves",
+        after=after,
+    )(ids, w_q, w_out, w_in, w_down)
+
+
+def prep_cot(asked, out_grad, dims, after):
+    devices, count, rows, quarter, full, width = dims
+    cap, reach = rows // devices, devices // count
+
+    def body(asked_ref, og, *refs):
+        outs, sems = refs[:reach], refs[reach]
+        copies = []
+        for k in range(reach):
+            for c in range(cap):
+                at = k * cap + c
+                copies.append(
+                    pltpu.make_async_copy(og.at[asked_ref[at]], outs[k].at[c], sems.at[at])
+                )
+        for copy in copies:
+            copy.start()
+        for copy in copies:
+            copy.wait()
+
+    return call(
+        body,
+        [shape_of((cap, full, width))] * reach,
+        [HB] * reach,
+        [SM, HM],
+        [pltpu.SemaphoreType.DMA((reach * cap,))],
+        us=2,
+        name="prep_cot",
+        after=after,
+    )(asked, out_grad)
+
+
+def bias_rows(piece, at, count):
+    terms = piece[at : at + 16, :].astype(f32)
+    first = 0 if count == 0 else 3
+    return terms[first : first + 1] + terms[first + 1 : first + 2] + terms[first + 2 : first + 3]
+
+
+def head_masks(head_width):
+    lane = lax.broadcasted_iota(jnp.int32, (1, head_width), 1)
+    return [(lane >= h * HD) & (lane < (h + 1) * HD) for h in range(head_width // HD)]
+
+
+def stack_heads(values, masks):
+    zero = jnp.zeros_like(values)
+    return jnp.concatenate([jnp.where(mask, values, zero) for mask in masks], axis=0)
+
+
+def pick_heads(stacked, masks):
+    size = stacked.shape[0] // len(masks)
+    out = stacked[:size]
+    for h in range(1, len(masks)):
+        out = jnp.where(masks[h], stacked[h * size : (h + 1) * size], out)
+    return out
+
+
+def load_parts(parts, parity, half, dst, offset, sems, at):
+    if len(parts) == 1:
+        return [pltpu.make_async_copy(parts[0], dst.at[pl.ds(offset, 2 * half)], sems.at[at])]
+    first = pl.multiple_of(parity * half, 16)
+    second = pl.multiple_of((1 - parity) * half, 16)
+    return [
+        pltpu.make_async_copy(parts[0], dst.at[pl.ds(offset + first, half)], sems.at[at]),
+        pltpu.make_async_copy(parts[1], dst.at[pl.ds(offset + second, half)], sems.at[at + 1]),
+    ]
+
+
+def attend(ids, segr, pieces, parts, pair, dims, keep_x, after=()):
+    devices, count, rows, quarter, full, width = dims
+    here = rows // count
+    tokens = here * full
+    tile = here * quarter
+    inner = sum(ref.shape[0] for ref in parts[0])
+    head_width = inner // 3
+    n_heads = head_width // HD
+    n_parts = [len(p) for p in parts]
+    flat = [ref for p in parts for ref in p]
+
+    def body(ids_ref, segr_ref, *refs):
+        piece_refs = refs[:count]
+        w_refs = refs[count : count + len(flat)]
+        out = list(refs[count + len(flat) :])
+        if keep_x:
+            x_out = out.pop(0)
+        ol_out, qkv_out, p_out, x_ref, w_ref, sems = out
+        copies = []
+        at = 0
+        for b, n in enumerate(n_parts):
+            copies += load_parts(
+                w_refs[at : at + n], ids_ref[2], inner // 2, w_ref.at[b], 0, sems, at
+            )
+            at += n
+        for copy in copies:
+            copy.start()
+        for r in range(here):
+            for kk in range(count):
+                x_ref[r * full + kk * quarter : r * full + (kk + 1) * quarter, :] = piece_refs[kk][
+                    r * quarter : (r + 1) * quarter, :
+                ]
+        if keep_x:
+            x_out[...] = x_ref[...]
+        masks = head_masks(head_width)
+        for copy in copies:
+            copy.wait()
+        for b in range(2):
+            bias = bias_rows(piece_refs[pair[b]], tile, 0)
+            bias_q, bias_v = bias[:, 0:head_width], bias[:, 256 : 256 + head_width]
+
+            @pl.loop(0, here)
+            def _(r):
+                start = pl.multiple_of(r * full, full)
+                projected = mm_nt(x_ref[pl.ds(start, full), :], w_ref[b])
+                query = (projected[:, 0:head_width] + bias_q).astype(bf16)
+                key = projected[:, head_width : 2 * head_width].astype(bf16)
+                value = (projected[:, 2 * head_width :] + bias_v).astype(bf16)
+                line = segr_ref[pl.ds(r, 1), :].astype(f32)
+                wide = jnp.broadcast_to(line, (full, full))
+                allowed = wide == wide.T
+                stacked = stack_heads(query, masks)
+                raw = mm_nt(stacked, key) * (HD ** -0.5)
+                allowed3 = jnp.concatenate([allowed] * n_heads, axis=0)
+                scores = jnp.where(allowed3, raw, MASKED)
+                raised = jnp.exp(scores - jnp.max(scores, axis=1, keepdims=True))
+                prob = raised / jnp.sum(raised, axis=1, keepdims=True)
+                low = prob.astype(bf16)
+                attended = pick_heads(mm(low, value), masks).astype(bf16)
+                ol_out[b, pl.ds(start, full), :] = attended
+                qkv_out[b, 0, pl.ds(start, full), :] = query
+                qkv_out[b, 1, pl.ds(start, full), :] = key
+                qkv_out[b, 2, pl.ds(start, full), :] = value
+                p_out[b, r] = low
+
+    outs = [
+        shape_of((2, tokens, head_width)),
+        shape_of((2, 3, tokens, head_width)),
+        shape_of((2, here, n_heads * full, full)),
+    ]
+    if keep_x:
+        outs = [shape_of((tokens, width))] + outs
+    return call(
+        body,
+        outs,
+        [VM] * len(outs),
+        [SM, VM] + [VM] * count + [HB] * len(flat),
+        [
+            pltpu.VMEM((tokens, width), bf16),
+            pltpu.VMEM((2, inner, width), bf16),
+            pltpu.SemaphoreType.DMA((len(flat),)),
+        ],
+        us=10,
+        name="attend",
+        after=after,
+    )(ids, segr, *pieces, *flat)
+
+
+def gelu_pair(u):
+    z = jnp.abs(u) * (0.5 ** 0.5)
+    t = 1.0 / (1.0 + 0.3275911 * z)
+    poly = t * (
+        0.254829592
+        + t * (-0.284496736 + t * (1.421413741 + t * (-1.453152027 + t * 1.061405429)))
+    )
+    bell = jnp.exp(-0.5 * u * u)
+    tail = 0.5 * poly * bell
+    cdf = jnp.where(u >= 0, 1.0 - tail, tail)
+    return u * cdf, cdf + u * bell * 0.3989422804014327
+
+
+def norm_rows(values):
+    centre = values - jnp.mean(values, axis=1, keepdims=True)
+    inverse = lax.rsqrt(jnp.mean(centre * centre, axis=1, keepdims=True) + EPSILON)
+    return centre * inverse, inverse
+
+
+def ffn(ids, sent, segr, x, ols, pieces, vecs, ogs, pool_grad, out_in_parts, down_parts, dims):
+    devices, count, rows, quarter, full, width = dims
+    here, cap, reach = rows // count, rows // devices, devices // count
+    tokens = here * full
+    tile = here * quarter
+    head_width = ols[0].shape[2]
+    hidden = width
+    flat_oi = [ref for p in out_in_parts for ref in p]
+    flat_dn = [ref for p in down_parts for ref in p]
+    n_oi, n_dn = len(flat_oi), len(flat_dn)
+    half_out, half_in = head_width // 2, width // 2
+
+    def body(ids_ref, sent_ref, segr_ref, x_ref, ol_a, ol_b, *refs):
+        refs = list(refs)
+        piece_refs = [refs.pop(0) for _ in range(count)]
+        vec_ref = refs.pop(0)
+        og_refs = [refs.pop(0) for _ in range(reach)]
+        pool_ref = refs.pop(0)
+        oi_refs = [refs.pop(0) for _ in range(n_oi)]
+        dn_refs = [refs.pop(0) for _ in range(n_dn)]
+        (
+            al_out, hat_out, inv_out, hl_out, gp_out, tk0, tk1, pooled_out, dz_out, low_out,
+            sums_out, down_out,
+            wo, wi, wd, og_buf, acc, hl, gp, sems, out_sems,
+        ) = refs
+        mi, parity = ids_ref[1], ids_ref[2]
+        first, later, last = [], [], []
+        at = 0
+        for kk in range(count):
+            own = out_in_parts[kk]
+            if len(own) == 2 and own[0].shape[0] == 2 * half_out:
+                first.append(
+                    pltpu.make_async_copy(oi_refs[at], wo.at[kk], sems.at[2 * at])
+                )
+                later.append(
+                    pltpu.make_async_copy(oi_refs[at + 1], wi.at[kk], sems.at[2 * at + 2])
+                )
+            else:
+                for j in range(2):
+                    place = parity if j == 0 else 1 - parity
+                    src = oi_refs[at + j]
+                    first.append(
+                        pltpu.make_async_copy(
+                            src.at[pl.ds(0, half_out)],
+                            wo.at[kk, pl.ds(pl.multiple_of(place * half_out, 16), half_out)],
+                            sems.at[2 * (at + j)],
+                        )
+                    )
+                    later.append(
+                        pltpu.make_async_copy(
+                            src.at[pl.ds(half_out, half_in)],
+                            wi.at[kk, pl.ds(pl.multiple_of(place * half_in, 16), half_in)],
+                            sems.at[2 * (at + j) + 1],
+                        )
+                    )
+            at += 2
+        base = 2 * n_oi
+        at = 0
+        for kk in range(count):
+            n = len(down_parts[kk])
+            last += load_parts(dn_refs[at : at + n], parity, width // 2, wd.at[kk], 0, sems, base + at)
+            at += n
+        base += n_dn
+        pool_at = base
+        cots = []
+        for k in range(reach):
+            for c in range(cap):
+                r = k * cap + c
+                for kk in range(count):
+                    cots.append(
+                        pltpu.make_async_copy(
+                            og_refs[k].at[c, pl.ds(pl.multiple_of((mi ^ kk) * quarter, quarter), quarter)],
+                            og_buf.at[pl.ds(r * full + kk * quarter, quarter)],
+                            sems.at[pool_at + r * count + kk],
+                        )
+                    )
+        for copy in first + later + last + cots:
+            copy.start()
+        b_out, gain_a, bias_a = vec_ref[0:1], vec_ref[1:2], vec_ref[2:3]
+        b_down, gain_f, bias_f = vec_ref[3:4], vec_ref[4:5], vec_ref[5:6]
+        for copy in first:
+            copy.wait()
+
+        @pl.loop(0, here)
+        def _(r):
+            span = pl.ds(pl.multiple_of(r * full, full), full)
+            total = x_ref[span, :].astype(f32) + b_out
+            for kk in range(count):
+                ol = (ol_a, ol_b)[kk // 2]
+                total = total + mm(ol[kk % 2, span, :], wo[kk])
+            hat, inverse = norm_rows(total)
+            hat_out[span, :] = hat
+            inv_out[span, :] = jnp.broadcast_to(inverse, (full, 128))
+            al_out[span, :] = (hat * gain_a + bias_a).astype(bf16)
+
+        for copy in later + last:
+            copy.wait()
+        half = tokens // 2
+        outs = []
+        for kk in range(count):
+            bias = bias_rows(piece_refs[kk], tile, 3)
+            for m in range(2):
+                span = slice(m * half, (m + 1) * half)
+                u = mm(al_out[span, :], wi[kk]) + bias
+                active, slope = gelu_pair(u)
+                active = active.astype(bf16)
+                hl[kk, span, :] = active
+                gp[kk, span, :] = slope.astype(bf16)
+                part = mm(active, wd[kk])
+                if kk == 0:
+                    acc[span, :] = part
+                else:
+                    acc[span, :] += part
+            for j, (src, dst) in enumerate(((hl, hl_out), (gp, gp_out))):
+                copy = pltpu.make_async_copy(src.at[kk], dst.at[kk], out_sems.at[2 * kk + j])
+                copy.start()
+                outs.append(copy)
+        for copy in cots:
+            copy.wait()
+        sums_out[...] = jnp.zeros_like(sums_out)
+        for r in range(here):
+            span = slice(r * full, (r + 1) * full)
+            hat, inverse = norm_rows(al_out[span, :].astype(f32) + acc[span, :] + b_down)
+            final = hat * gain_f + bias_f
+            (tk0, tk1)[r // cap][r % cap] = final.astype(bf16)
+            line = jnp.broadcast_to(segr_ref[r : r + 1, :].astype(f32), (full, full)).T[:, 0:1]
+            cot = og_buf[span, :].astype(f32)
+            row = sent_ref[r]
+            for g in range(SEGS):
+                inside = line == float(g)
+                number = jnp.sum(jnp.where(inside, 1.0, 0.0), axis=0, keepdims=True)
+                share = 1.0 / number
+                pooled_out[r * SEGS + g : r * SEGS + g + 1, :] = (
+                    jnp.sum(jnp.where(inside, final, 0.0), axis=0, keepdims=True) * share
+                )
+                cot = cot + jnp.where(inside, pool_ref[row, g : g + 1, :] * share, 0.0)
+            e = cot * gain_f
+            mean_e = jnp.mean(e, axis=1, keepdims=True)
+            mean_p = jnp.mean(e * hat, axis=1, keepdims=True)
+            dz = inverse * (e - mean_e - hat * mean_p)
+            dz_out[span, :] = dz
+            low_out[span, :] = dz.astype(bf16)
+            sums_out[0:1, :] += jnp.sum(dz, axis=0, keepdims=True)
+            sums_out[1:2, :] += jnp.sum(cot * hat, axis=0, keepdims=True)
+            sums_out[2:3, :] += jnp.sum(cot, axis=0, keepdims=True)
+        for b, kk in enumerate((1, 3)):
+            for c in range(3):
+                cols = slice(c * 256, (c + 1) * 256)
+                down_out[b, cols, :] = mm_tn(hl[kk, :, cols], low_out[...]).astype(bf16)
+        for copy in outs:
+            copy.wait()
+
+    wide = (tokens, width)
+    return call(
+        body,
+        [
+            shape_of(wide), shape_of(wide, f32), shape_of((tokens, 128), f32),
+            shape_of((count,) + wide), shape_of((count,) + wide),
+            shape_of((cap, full, width)), shape_of((cap, full, width)),
+            shape_of((here * SEGS, width), f32), shape_of(wide, f32), shape_of(wide),
+            shape_of((8, width), f32), shape_of((2, hidden, width)),
+        ],
+        [VM, VM, VM, HB, HB] + [VM] * 7,
+        [SM, SM, VM, VM, VM, VM] + [VM] * count + [VM] + [HB] * reach + [VM] + [HB] * (n_oi + n_dn),
+        [
+            pltpu.VMEM((count, head_width, width), bf16),
+            pltpu.VMEM((count, width, hidden), bf16),
+            pltpu.VMEM((count, hidden, width), bf16),
+            pltpu.VMEM(wide, bf16),
+            pltpu.VMEM(wide, f32),
+            pltpu.VMEM((count,) + wide, bf16),
+            pltpu.VMEM((count,) + wide, bf16),
+            pltpu.SemaphoreType.DMA((2 * n_oi + n_dn + here * count,)),
+            pltpu.SemaphoreType.DMA((2 * count,)),
+        ],
+        us=20,
+        name="ffn",
+    )(ids, sent, segr, x, ols[0], ols[1], *pieces, vecs, *ogs, pool_grad, *flat_oi, *flat_dn)
+
+
+def ffn_back(ids, low, gp, al, down_parts, dims):
+    devices, count, rows, quarter, full, width = dims
+    tokens = low.shape[0]
+    hidden = width
+    flat = [ref for p in down_parts for ref in p]
+    n = len(flat)
+
+    def body(ids_ref, low_ref, gp_ref, al_ref, *refs):
+        dn_refs = refs[:n]
+        du_out, in_out, bin_out, wd, gpb, du, sems, out_sems = refs[n:]
+        copies = []
+        at = 0
+        for kk in range(count):
+            m = len(down_parts[kk])
+            copies.append(
+                load_parts(dn_refs[at : at + m], ids_ref[2], width // 2, wd.at[kk], 0, sems, at)
+                + [pltpu.make_async_copy(gp_ref.at[kk], gpb.at[kk], sems.at[n + kk])]
+            )
+            at += m
+        outs = []
+        turn = (1, 3, 2, 0)
+        for kk in turn:
+            for copy in copies[kk]:
+                copy.start()
+        half = tokens // 2
+        for kk in turn:
+            for copy in copies[kk]:
+                copy.wait()
+            total = jnp.zeros((1, hidden), f32)
+            for m in range(2):
+                span = slice(m * half, (m + 1) * half)
+                part = (mm_nt(low_ref[span, :], wd[kk]) * gpb[kk, span, :].astype(f32)).astype(bf16)
+                du[kk, span, :] = part
+                total = total + jnp.sum(part.astype(f32), axis=0, keepdims=True)
+            bin_out[kk : kk + 1, :] = total
+            copy = pltpu.make_async_copy(du.at[kk], du_out.at[kk], out_sems.at[kk])
+            copy.start()
+            outs.append(copy)
+        for b, kk in enumerate((1, 3)):
+            for c in range(3):
+                cols = slice(c * 256, (c + 1) * 256)
+                in_out[b, cols, :] = mm_tn(al_ref[:, cols], du[kk]).astype(bf16)
+        for copy in outs:
+            copy.wait()
+
+    return call(
+        body,
+        [
+            shape_of((count, tokens, hidden)),
+            shape_of((2, width, hidden)),
+            shape_of((count, hidden), f32),
+        ],
+        [HB, VM, VM],
+        [SM, VM, HB, VM] + [HB] * n,
+        [
+            pltpu.VMEM((count, hidden, width), bf16),
+            pltpu.VMEM((count, tokens, hidden), bf16),
+            pltpu.VMEM((count, tokens, hidden), bf16),
+            pltpu.SemaphoreType.DMA((n + count,)),
+            pltpu.SemaphoreType.DMA((count,)),
+        ],
+        us=9,
+        name="ffn_back",
+    )(ids, low, gp, al, *flat)
+
+
+def norm_back_attn(ids, du, al, dz, hat, inv, vecs, out_in_parts, dims, half_out, after=()):
+    devices, count, rows, quarter, full, width = dims
+    tokens = al.shape[0]
+    hidden = width
+    flat = [ref for p in out_in_parts for ref in p]
+    n = len(flat)
+    half_in = width // 2
+
+    def body(ids_ref, du_ref, dz_ref, hat_ref, inv_ref, vec_ref, *refs):
+        oi_refs = refs[:n]
+        dz1_out, low_out, sums_out, wi, dub, acc, sems = refs[n:]
+        parity = ids_ref[2]
+        copies = []
+        at = 0
+        for kk in range(count):
+            own = out_in_parts[kk]
+            group = [pltpu.make_async_copy(du_ref.at[kk], dub.at[kk], sems.at[2 * n + kk])]
+            if len(own) == 1:
+                group.append(pltpu.make_async_copy(oi_refs[at], wi.at[kk], sems.at[2 * at]))
+            else:
+                for j in range(2):
+                    place = parity if j == 0 else 1 - parity
+                    group.append(
+                        pltpu.make_async_copy(
+                            oi_refs[at + j].at[pl.ds(half_out, half_in)],
+                            wi.at[kk, pl.ds(pl.multiple_of(place * half_in, 16), half_in)],
+                            sems.at[2 * (at + j)],
+                        )
+                    )
+            at += len(own)
+            copies.append(group)
+        for group in copies:
+            for copy in group:
+                copy.start()
+        half = tokens // 2
+        for kk in range(count):
+            for copy in copies[kk]:
+                copy.wait()
+            for m in range(2):
+                span = slice(m * half, (m + 1) * half)
+                part = mm_nt(dub[kk, span, :], wi[kk])
+                if kk == 0:
+                    acc[span, :] = part + dz_ref[span, :]
+                else:
+                    acc[span, :] += part
+        gain_a = vec_ref[1:2]
+        sums_out[...] = jnp.zeros_like(sums_out)
+
+        @pl.loop(0, tokens // full)
+        def _(r):
+            span = pl.ds(pl.multiple_of(r * full, full), full)
+            da = acc[span, :]
+            hat_r = hat_ref[span, :]
+            e = da * gain_a
+            mean_e = jnp.mean(e, axis=1, keepdims=True)
+            mean_p = jnp.mean(e * hat_r, axis=1, keepdims=True)
+            dz1 = inv_ref[span, 0:1] * (e - mean_e - hat_r * mean_p)
+            dz1_out[span, :] = dz1
+            low_out[span, :] = dz1.astype(bf16)
+            sums_out[0:1, :] += jnp.sum(dz1, axis=0, keepdims=True)
+            sums_out[1:2, :] += jnp.sum(da * hat_r, axis=0, keepdims=True)
+            sums_out[2:3, :] += jnp.sum(da, axis=0, keepdims=True)
+
+    wide = (tokens, width)
+    return call(
+        body,
+        [shape_of(wide, f32), shape_of(wide), shape_of((8, width), f32)],
+        [VM] * 3,
+        [SM, HB, VM, VM, VM, VM] + [HB] * n,
+        [
+            pltpu.VMEM((count, width, hidden), bf16),
+            pltpu.VMEM((count, tokens, hidden), bf16),
+            pltpu.VMEM(wide, f32),
+            pltpu.SemaphoreType.DMA((2 * n + count,)),
+        ],
+        us=8,
+        name="norm_back",
+        after=after,
+    )(ids, du, dz, hat, inv, vecs, *flat)
+
+
+def attend_back(ids, low, x, blocks, extras, dims, after=()):
+    devices, count, rows, quarter, full, width = dims
+    here = rows // count
+    tokens = x.shape[0]
+    head_width = blocks[0][2].shape[2]
+    inner = 3 * head_width
+    flat = [ref for b in blocks for ref in b[5]]
+    n = len(flat)
+    half_out = head_width // 2
+    nb = len(blocks)
+
+    def body(ids_ref, low_ref, x_ref, bin_ref, ffn_ref, norm_ref, *refs):
+        data = refs[: 3 * nb]
+        w_refs = refs[3 * nb : 3 * nb + n]
+        mix_out, grad_out, wo, sums, sems = refs[3 * nb + n :]
+        parity = ids_ref[2]
+        copies = []
+        at = 0
+        for b in range(nb):
+            own = blocks[b][5]
+            if len(own) == 1:
+                copies.append(pltpu.make_async_copy(w_refs[at], wo.at[b], sems.at[at]))
+            else:
+                for j in range(2):
+                    place = parity if j == 0 else 1 - parity
+                    copies.append(
+                        pltpu.make_async_copy(
+                            w_refs[at + j].at[pl.ds(0, half_out)],
+                            wo.at[b, pl.ds(pl.multiple_of(place * half_out, 16), half_out)],
+                            sems.at[at + j],
+                        )
+                    )
+            at += len(own)
+        for copy in copies:
+            copy.start()
+        for copy in copies:
+            copy.wait()
+        masks = head_masks(head_width)
+        sums[...] = jnp.zeros_like(sums)
+        for b in range(nb):
+            kk, place = blocks[b][:2]
+            ol_ref, qkv_ref, p_ref = data[3 * b : 3 * b + 3]
+
+            @pl.loop(0, here)
+            def _(r):
+                span = pl.ds(pl.multiple_of(r * full, full), full)
+                dol = mm_nt(low_ref[span, :], wo[b]).astype(bf16)
+                query, key, value = (qkv_ref[place, i, span, :] for i in range(3))
+                low_p = p_ref[place, r]
+                prob = low_p.astype(f32)
+                dos = stack_heads(dol, masks)
+                dp = mm_nt(dos, value)
+                ds = (prob * (dp - jnp.sum(dp * prob, axis=1, keepdims=True))).astype(bf16)
+                dv = mm_tn(low_p, dos).astype(bf16)
+                dq = (pick_heads(mm(ds, key), masks) * (HD ** -0.5)).astype(bf16)
+                dk = (mm_tn(ds, stack_heads(query, masks)) * (HD ** -0.5)).astype(bf16)
+                mix_out[b, span, 0:head_width] = dq
+                mix_out[b, span, head_width : 2 * head_width] = dk
+                mix_out[b, span, 2 * head_width :] = dv
+                sums[b : b + 1, 0:head_width] += jnp.sum(dq.astype(f32), axis=0, keepdims=True)
+                sums[b : b + 1, 256 : 256 + head_width] += jnp.sum(
+                    dv.astype(f32), axis=0, keepdims=True
+                )
+
+            for c in range(3):
+                part = slice(c * head_width, (c + 1) * head_width)
+                grad_out[b, part, :] = mm_tn(mix_out[b, :, part], x_ref[...]).astype(bf16)
+            grad_out[b, inner:width, :] = mm_tn(ol_ref[place], low_ref[...]).astype(bf16)
+            lines = jnp.concatenate(
+                [sums[b : b + 1], bin_ref[kk : kk + 1], norm_ref[0:3], ffn_ref[0:3]], axis=0
+            )
+            grad_out[b, width : width + 16, :] = two_terms(lines)
+
+    return call(
+        body,
+        [shape_of((nb, tokens, inner)), shape_of((nb, width + 16, width))],
+        [VM] * 2,
+        [SM] + [VM] * (5 + 3 * nb) + [HB] * n,
+        [
+            pltpu.VMEM((nb, head_width, width), bf16),
+            pltpu.VMEM((8, width), f32),
+            pltpu.SemaphoreType.DMA((n,)),
+        ],
+        us=13,
+        name="attend_back",
+        after=after,
+    )(ids, low, x, *extras, *[v for b in blocks for v in b[2:5]], *flat)
+
+
+def two_terms(lines):
+    high = lines.astype(bf16)
+    return jnp.concatenate([high, (lines - high.astype(f32)).astype(bf16)], axis=0)
+
+
+def one_term(lines):
+    return lines[0:8].astype(f32) + lines[8:16].astype(f32)
+
+
+def peer_grad(lhs, rhs, got, after=()):
+    tokens, width = rhs.shape
+    hidden = lhs.shape[-1]
+
+    def body(lhs_ref, rhs_ref, got_ref, out, a_buf, g_buf, sems):
+        copies = [
+            pltpu.make_async_copy(lhs_ref.at[2], a_buf, sems.at[0]),
+            pltpu.make_async_copy(got_ref.at[1], g_buf, sems.at[1]),
+        ]
+        for copy in copies:
+            copy.start()
+        for copy in copies:
+            copy.wait()
+        for c in range(hidden // 256):
+            cols = slice(c * 256, (c + 1) * 256)
+            out[cols, :] = (mm_tn(a_buf[:, cols], rhs_ref[...]) + g_buf[cols, :].astype(f32)).astype(
+                bf16
+            )
+
+    return call(
+        body,
+        shape_of((hidden, width)),
+        VM,
+        [HB, VM, HB],
+        [
+            pltpu.VMEM((tokens, hidden), bf16),
+            pltpu.VMEM((hidden, width), bf16),
+            pltpu.SemaphoreType.DMA((2,)),
+        ],
+        us=3,
+        name="peer_grad",
+        after=after,
+    )(lhs, rhs, got)
+
+
+def shards(acc, ids_ref, devices, bits, size, send, keep):
+    for p in range(devices):
+        mirror = sum(((p >> j) & 1) << (bits - 1 - j) for j in range(bits))
+        rows = acc[pl.ds(pl.multiple_of((ids_ref[0] ^ mirror) * size, 16), size), :]
+        if p < devices // 2:
+            keep[p * size : (p + 1) * size, :] = rows
+        else:
+            q = p - devices // 2
+            send[q * size : (q + 1) * size, :] = rows.astype(bf16)
+
+
+def own_grad(ids, lhs, rhs, got, crossed, devices, lhs_own, after=()):
+    tokens = rhs.shape[-2]
+    width = rhs.shape[-1]
+    hidden = lhs.shape[-1]
+    bits = devices.bit_length() - 1
+    size = hidden // devices
+
+    def body(ids_ref, lhs_ref, rhs_ref, got_ref, cross_ref, send, keep, a_buf, b_buf, g_buf, acc, sems):
+        copies = [
+            pltpu.make_async_copy(lhs_ref.at[0] if lhs_own else lhs_ref, a_buf, sems.at[0]),
+            pltpu.make_async_copy(rhs_ref if lhs_own else rhs_ref.at[0], b_buf, sems.at[1]),
+            pltpu.make_async_copy(got_ref.at[0], g_buf, sems.at[2]),
+        ]
+        for copy in copies:
+            copy.start()
+        for copy in copies:
+            copy.wait()
+        for c in range(hidden // 256):
+            cols = slice(c * 256, (c + 1) * 256)
+            acc[cols, :] = (
+                mm_tn(a_buf[:, cols], b_buf[...])
+                + g_buf[cols, :].astype(f32)
+                + cross_ref[cols, :].astype(f32)
+            )
+        shards(acc, ids_ref, devices, bits, size, send, keep)
+
+    return call(
+        body,
+        [shape_of((hidden // 2, width)), shape_of((hidden // 2, width), f32)],
+        [VM, VM],
+        [SM, HB, HB, HB, VM],
+        [
+            pltpu.VMEM((tokens, hidden), bf16),
+            pltpu.VMEM((tokens, width), bf16),
+            pltpu.VMEM((hidden, width), bf16),
+            pltpu.VMEM((hidden, width), f32),
+            pltpu.SemaphoreType.DMA((3,)),
+        ],
+        us=3,
+        name="own_grad",
+        after=after,
+    )(ids, lhs, rhs, got, crossed)
+
+
+def peer_grad_in(al, du, got, after=()):
+    tokens, width = al.shape
+    hidden = du.shape[-1]
+
+    def body(al_ref, du_ref, got_ref, out, b_buf, g_buf, sems):
+        copies = [
+            pltpu.make_async_copy(du_ref.at[2], b_buf, sems.at[0]),
+            pltpu.make_async_copy(got_ref.at[1], g_buf, sems.at[1]),
+        ]
+        for copy in copies:
+            copy.start()
+        for copy in copies:
+            copy.wait()
+        for c in range(width // 256):
+            cols = slice(c * 256, (c + 1) * 256)
+            out[cols, :] = (mm_tn(al_ref[:, cols], b_buf[...]) + g_buf[cols, :].astype(f32)).astype(
+                bf16
+            )
+
+    return call(
+        body,
+        shape_of((width, hidden)),
+        VM,
+        [VM, HB, HB],
+        [
+            pltpu.VMEM((tokens, hidden), bf16),
+            pltpu.VMEM((width, hidden), bf16),
+            pltpu.SemaphoreType.DMA((2,)),
+        ],
+        us=3,
+        name="peer_grad_in",
+        after=after,
+    )(al, du, got)
+
+
+def peer_last(grads, got, at, after=()):
+    _, high, width = grads.shape
+
+    def body(a_ref, g_ref, out):
+        out[0 : high - 16, :] = (
+            a_ref[at, 0 : high - 16, :].astype(f32) + g_ref[1, 0 : high - 16, :].astype(f32)
+        ).astype(bf16)
+        out[high - 16 :, :] = two_terms(
+            one_term(a_ref[at, high - 16 :, :]) + one_term(g_ref[1, high - 16 :, :])
+        )
+
+    return call(
+        body, shape_of((high, width)), VM, [VM, VM], us=2, name="peer_last", after=after
+    )(grads, got)
+
+
+def own_last(ids, grads, got, crossed, at, devices, after=()):
+    _, high, width = grads.shape
+    body_rows = high - 16
+    bits = devices.bit_length() - 1
+    size = body_rows // devices
+
+    def body(ids_ref, a_ref, g_ref, c_ref, send, keep, vec, acc):
+        acc[...] = (
+            a_ref[at, 0:body_rows, :].astype(f32)
+            + g_ref[0, 0:body_rows, :].astype(f32)
+            + c_ref[0:body_rows, :].astype(f32)
+        )
+        shards(acc, ids_ref, devices, bits, size, send, keep)
+        lines = (
+            one_term(a_ref[at, body_rows:, :])
+            + one_term(g_ref[0, body_rows:, :])
+            + one_term(c_ref[body_rows:, :])
+        )
+        send[body_rows // 2 :, :] = two_terms(lines)
+        vec[...] = lines
+
+    return call(
+        body,
+        [
+            shape_of((body_rows // 2 + 16, width)),
+            shape_of((body_rows // 2, width), f32),
+            shape_of((8, width), f32),
+        ],
+        [VM] * 3,
+        [SM, VM, VM, VM],
+        [pltpu.VMEM((body_rows, width), f32)],
+        us=3,
+        name="own_last",
+        after=after,
+    )(ids, grads, got, crossed)
+
+
+def halve(keep, got, vec=None):
+    high, width = keep.shape
+    last = vec is not None
+    tail = 16 if last else 0
+    return_send = True
+
+    def body(*refs):
+        keep_ref, got_ref = refs[:2]
+        rest = refs[2:]
+        if last:
+            vec_ref, rest = rest[0], rest[1:]
+        send, kept = rest[:2]
+        half = high // 2
+        kept[...] = keep_ref[0:half, :] + got_ref[0:half, :].astype(f32)
+        send[0:half, :] = (keep_ref[half:, :] + got_ref[half:high, :].astype(f32)).astype(bf16)
+        if last:
+            lines = vec_ref[...] + one_term(got_ref[high:, :])
+            send[half:, :] = two_terms(lines)
+            rest[2][...] = lines
+
+    outs = [shape_of((high // 2 + tail, width)), shape_of((high // 2, width), f32)]
+    args = [keep, got]
+    if last:
+        outs.append(shape_of((8, width), f32))
+        args.append(vec)
+    return call(
+        body, outs, [VM] * len(outs), [VM] * len(args), us=1, name="halve"
+    )(*args)
+
+
+def end_halving(keep, got, vec=None):
+    high, width = keep.shape
+    last = vec is not None
+
+    def body(*refs):
+        keep_ref, got_ref = refs[:2]
+        rest = refs[2:]
+        if last:
+            vec_ref, rest = rest[0], rest[1:]
+        rest[0][...] = (keep_ref[...] + got_ref[0:high, :].astype(f32)).astype(bf16)
+        if last:
+            rest[1][...] = vec_ref[...] + one_term(got_ref[high:, :])
+
+    outs = [shape_of((high, width))]
+    args = [keep, got]
+    if last:
+        outs.append(shape_of((8, width), f32))
+        args.append(vec)
+    return call(
+        body, outs, [VM] * len(outs), [VM] * len(args), us=1, name="end_halving"
+    )(*args)
+
+
+def reduce_dp(send, keep, vec, devices):
+    bits = devices.bit_length() - 1
+    for j in range(bits - 1):
+        got = swap(send, "dp", 1 << j)
+        out = halve(keep, got, vec)
+        send, keep = out[:2]
+        vec = out[2] if vec is not None else None
+    got = swap(send, "dp", 1 << (bits - 1))
+    out = end_halving(keep, got, vec)
+    pieces = [out[0]]
+    for j in reversed(range(bits)):
+        whole = pieces[0] if len(pieces) == 1 else jnp.concatenate(pieces, axis=0)
+        pieces.append(swap(whole, "dp", 1 << j))
+    return pieces, (out[1] if vec is not None else None)
+
+
+def place_shards(ids_ref, pieces, devices, size, put):
+    bits = devices.bit_length() - 1
+    p = 0
+    for piece in pieces:
+        for q in range(piece.shape[0] // size):
+            mirror = sum(((p >> j) & 1) << (bits - 1 - j) for j in range(bits))
+            at = pl.multiple_of((ids_ref[0] ^ mirror) * size, 8)
+            put(at, piece[q * size : (q + 1) * size, :].astype(f32))
+            p += 1
+
+
+def whole_grad(ids, pieces, devices):
+    size, width = pieces[0].shape
+    n = len(pieces)
+
+    def body(ids_ref, *refs):
+        out = refs[n]
+
+        def put(at, rows):
+            out[pl.ds(at, size), :] = rows
+
+        place_shards(ids_ref, refs[:n], devices, size, put)
+
+    return call(
+        body,
+        shape_of((size * devices, width), f32),
+        VM,
+        [SM] + [VM] * n,
+        us=2,
+        name="whole_grad",
+    )(ids, *pieces)
+
+
+def grad_input_rows(ids, dz1, mixes, parts, pooled, dims, after=()):
+    devices, count, rows, quarter, full, width = dims
+    here = rows // count
+    tokens = here * full
+    tile = here * quarter
+    inner = mixes[0].shape[2]
+    flat = [ref for p in parts for ref in p]
+    n = len(flat)
+    turn = (1, 3, 2, 0)
+
+    def body(ids_ref, dz_ref, m_a, m_b, pool_ref, *refs):
+        w_refs = refs[:n]
+        outs = refs[n : n + count]
+        wq, acc, sems = refs[n + count :]
+        copies = []
+        at = 0
+        for kk in range(count):
+            m = len(parts[kk])
+            copies.append(
+                load_parts(w_refs[at : at + m], ids_ref[2], inner // 2, wq.at[kk], 0, sems, at)
+            )
+            at += m
+        for kk in turn:
+            for copy in copies[kk]:
+                copy.start()
+        half = tokens // 2
+        for i, kk in enumerate(turn):
+            for copy in copies[kk]:
+                copy.wait()
+            mix = (m_a, m_b)[i // 2]
+            for m in range(2):
+                span = slice(m * half, (m + 1) * half)
+                part = mm(mix[i % 2, span, :], wq[kk])
+                if i == 0:
+                    acc[span, :] = part + dz_ref[span, :]
+                else:
+                    acc[span, :] += part
+        for kk in range(count):
+            for r in range(here):
+                outs[kk][r * quarter : (r + 1) * quarter, :] = acc[
+                    r * full + kk * quarter : r * full + (kk + 1) * quarter, :
+                ].astype(bf16)
+            outs[kk][tile:, :] = pool_ref[...].astype(bf16)
+
+    return call(
+        body,
+        [shape_of((tile + here * SEGS, width))] * count,
+        [VM] * count,
+        [SM] + [VM] * 4 + [HB] * n,
+        [
+            pltpu.VMEM((count, inner, width), bf16),
+            pltpu.VMEM((tokens, width), f32),
+            pltpu.SemaphoreType.DMA((n,)),
+        ],
+        us=6,
+        name="grad_input_rows",
+        after=after,
+    )(ids, dz1, *mixes, pooled, *flat)
+
+
+def land_grad(sent, pieces, dims):
+    devices, count, rows, quarter, full, width = dims
+    here = rows // count
+    tile = here * quarter
+
+    def body(sent_ref, *refs):
+        piece_refs = refs[:count]
+        out, pooled, sems = refs[count:]
+        copies = []
+        for kk in range(count):
+            for j in range(here):
+                at = kk * here + j
+                copy = pltpu.make_async_copy(
+                    piece_refs[kk].at[pl.ds(j * quarter, quarter)], out.at[sent_ref[at]], sems.at[at]
+                )
+                copy.start()
+                copies.append(copy)
+                pooled[sent_ref[at]] = piece_refs[kk][
+                    tile : tile + here * SEGS, :
+                ].astype(f32)[j * SEGS : (j + 1) * SEGS]
+        for copy in copies:
+            copy.wait()
+
+    return call(
+        body,
+        [shape_of((rows, quarter, width)), shape_of((rows, SEGS, width), f32)],
+        [HB, VM],
+        [SM] + [VM] * count,
+        [pltpu.SemaphoreType.DMA((rows,))],
+        us=2,
+        name="land_grad",
+    )(sent, *pieces)
+
+
+def turn_output(ids, hops, dims, after=()):
+    devices, count, rows, quarter, full, width = dims
+    here, cap, reach = rows // count, rows // devices, devices // count
+
+    def body(ids_ref, *refs):
+        hop_refs = refs[:reach]
+        outs = refs[reach : reach + count]
+        sems = refs[reach + count]
+        handler = lax.div(ids_ref[0], reach)
+        copies = []
+        for kk in range(count):
+            block = ids_ref[1] ^ kk ^ handler
+            for k in range(reach):
+                for c in range(cap):
+                    j = k * cap + c
+                    copy = pltpu.make_async_copy(
+                        hop_refs[k].at[c, pl.ds(pl.multiple_of(block * quarter, quarter), quarter)],
+                        outs[kk].at[pl.ds(j * quarter, quarter)],
+                        sems.at[kk * here + j],
+                    )
+                    copy.start()
+                    copies.append(copy)
+        for copy in copies:
+            copy.wait()
+
+    return call(
+        body,
+        [shape_of((here * quarter, width))] * count,
+        [HB] * count,
+        [SM] + [HB] * reach,
+        [pltpu.SemaphoreType.DMA((rows,))],
+        us=2,
+        name="turn_output",
+        after=after,
+    )(ids, *hops)
+
+
+def land_output(spots, pieces, dims):
+    devices, count, rows, quarter, full, width = dims
+    here = rows // count
+
+    def body(spots_ref, *refs):
+        piece_refs = refs[:count]
+        out, sems = refs[count:]
+        copies = []
+        for kk in range(count):
+            for j in range(here):
+                at = kk * here + j
+                copy = pltpu.make_async_copy(
+                    piece_refs[kk].at[pl.ds(j * quarter, quarter)], out.at[spots_ref[at]], sems.at[at]
+                )
+                copy.start()
+                copies.append(copy)
+        for copy in copies:
+            copy.wait()
+
+    return call(
+        body,
+        shape_of((rows, quarter, width)),
+        HB,
+        [SM] + [HB] * count,
+        [pltpu.SemaphoreType.DMA((rows,))],
+        us=2,
+        name="land_output",
+    )(spots, *pieces)
+
+
+def swap(values, axis, bit):
+    return lax.ppermute(values, axis, [(i, i ^ bit) for i in range(lax.axis_size(axis))])
+
+
+def per_device(
+    tokens_in, seg, route, w_qkv, b_qv, w_out, b_out, gain_attn, bias_attn, w_in, b_in, w_down,
+    b_down, gain_ffn, bias_ffn, out_grad, pool_grad,
+):
+    devices, count = lax.axis_size("dp"), lax.axis_size("mp")
+    rows, quarter, width = tokens_in.shape
+    full = seg.shape[1]
+    dims = (devices, count, rows, quarter, full, width)
+    here, cap, reach = rows // count, rows // devices, devices // count
+    my, mi = lax.axis_index("dp"), lax.axis_index("mp")
+    parity = lax.rem(my, 2)
+    ints = jnp.int32
+    ids = jnp.stack([my, mi, parity]).astype(ints)
+    head_width = w_qkv.shape[2]
+    inner = 3 * head_width
+
+    places = jnp.arange(rows, dtype=ints)
+    routes = route.reshape(devices, rows)
+    key = routes // rows * rows + places[None]
+    rank = jnp.sum((key[:, None, :] < key[:, :, None]).astype(ints), axis=2)
+    placed = rank[:, :, None] == places[None, None, :]
+    table = jnp.sum(jnp.where(placed, routes[:, :, None], 0), axis=1)
+    own_rank = lax.dynamic_index_in_dim(rank, my, 0, keepdims=False)
+    steps = jnp.arange(reach, dtype=ints)
+    copies = jnp.arange(cap, dtype=ints)
+    blocks = jnp.arange(count, dtype=ints)
+    near = lax.rem(my // count - steps + reach, reach)
+    slots = (
+        ((mi ^ blocks)[:, None, None] * reach + near[None, :, None]) * cap + copies[None, None, :]
+    ).reshape(rows)
+    sent = jnp.sum(jnp.where(own_rank[None, :] == slots[:, None], places[None, :], 0), axis=1)
+    pair = lax.dynamic_slice_in_dim(table, my * cap, cap, 1) - my * rows
+    sources = (mi ^ blocks)[:, None] + count * lax.rem(my + steps, reach)[None, :]
+    spots = jnp.sum(
+        jnp.where(
+            sources[:, :, None, None] == jnp.arange(devices, dtype=ints)[None, None, :, None],
+            pair[None, None],
+            0,
+        ),
+        axis=2,
+    ).reshape(rows)
+    asked = spots[: reach * cap]
+    mine = my * rows + sent[:here]
+    lines = jnp.sum(
+        jnp.where(
+            mine[:, None, None] == jnp.arange(devices * rows, dtype=ints)[None, :, None], seg[None], 0
+        ),
+        axis=1,
+    ).reshape(here, count, quarter)
+    lines = jnp.sum(
+        jnp.where((mi ^ blocks)[:, None, None, None] == blocks[None, None, :, None], lines[None], 0),
+        axis=2,
+    )
+    segr = jnp.pad(lines.transpose(1, 0, 2).reshape(here, full), ((0, 8 - here), (0, 0)))
+
+    def to_place(k):
+        return [
+            (s * count + f, (reach * f + (s // count - k) % reach) * count + s % count)
+            for s in range(devices)
+            for f in range(count)
+        ]
+
+    def from_place(k):
+        return [(b, a) for a, b in to_place(k)]
+
+    sends = prep_rows(sent, tokens_in, b_qv, b_in, dims)
+    pieces = [sends[0]] + [swap(sends[k], "mp", k) for k in range(1, count)]
+    wq = w_qkv.transpose(1, 2, 0).reshape(inner, width)
+    half_q, half_oi, half_dn = prep_halves(ids, wq, w_out, w_in, w_down, (sends[0],))
+
+    def cross(half, after=None):
+        direct = swap(half, "mp", 2)
+        if after is not None:
+            direct, _ = lax.optimization_barrier((direct, after))
+        return direct, swap(direct, "dp", 1)
+
+    def sibling(values):
+        return tuple(swap(v, "mp", 1) for v in values)
+
+    far_q = cross(half_q)
+    q_parts = [(wq,), sibling((wq,)), far_q, sibling(far_q)]
+    vecs = jnp.stack(
+        [b_out, gain_attn, bias_attn, b_down, gain_ffn, bias_ffn, gain_ffn, bias_ffn]
+    )
+    x, ol_a, qkv_a, p_a = attend(
+        ids, segr, pieces, q_parts[:2], (0, 1), dims, True, (far_q[0],)
+    )
+    far_oi = cross(half_oi, ol_a)
+    oi_parts = [(w_out, w_in), sibling((w_out, w_in)), far_oi, sibling(far_oi)]
+    far_dn = cross(half_dn)
+    dn_parts = [(w_down,), sibling((w_down,)), far_dn, sibling(far_dn)]
+    in_parts = [p[1:] if k < 2 else p for k, p in enumerate(oi_parts)]
+    wo_parts = [p[:1] if k < 2 else p for k, p in enumerate(oi_parts)]
+
+    og_sends = prep_cot(asked, out_grad, dims, (ol_a,))
+    ogs = [lax.ppermute(og_sends[k], ("dp", "mp"), from_place(k)) for k in range(reach)]
+    ol_b, qkv_b, p_b = attend(
+        ids, segr, pieces, q_parts[2:], (2, 3), dims, False, (og_sends[0],)
+    )
+    (
+        al, hat, inv, hl, gp, tk0, tk1, pooled, dz, low, ffn_sums, down_pair,
+    ) = ffn(
+        ids, sent, segr, x, (ol_a, ol_b), pieces, vecs, ogs, pool_grad, oi_parts, dn_parts, dims
+    )
+    got_down = swap(down_pair, "mp", 1)
+    hops = [lax.ppermute(t, ("dp", "mp"), to_place(k)) for k, t in enumerate((tk0, tk1))]
+    du, in_pair, bin_sums = ffn_back(ids, low, gp, al, dn_parts, dims)
+    got_in = swap(in_pair, "mp", 1)
+    down_far = peer_grad(hl, low, got_down, (bin_sums,))
+    crossed_down = swap(down_far, "mp", 2)
+    dz1, low1, norm_sums = norm_back_attn(
+        ids, du, al, dz, hat, inv, vecs, in_parts, dims, head_width // 2, (down_far,)
+    )
+    in_far = peer_grad_in(al, du, got_in, (norm_sums,))
+    crossed_in = swap(in_far, "mp", 2)
+    extras = (bin_sums, ffn_sums, norm_sums)
+    mix_a, grads_a = attend_back(
+        ids, low1, x,
+        [(1, 1, ol_a, qkv_a, p_a, wo_parts[1]), (3, 1, ol_b, qkv_b, p_b, wo_parts[3])],
+        extras, dims, (in_far,),
+    )
+    got_last = swap(grads_a, "mp", 1)
+    send_down, keep_down = own_grad(
+        ids, hl, low, got_down, crossed_down, devices, True, (grads_a,)
+    )
+    mix_b, grads_b = attend_back(
+        ids, low1, x,
+        [(2, 0, ol_b, qkv_b, p_b, wo_parts[2]), (0, 0, ol_a, qkv_a, p_a, wo_parts[0])],
+        extras, dims, (send_down,),
+    )
+    last_far = peer_last(grads_b, got_last, 0)
+    crossed_last = swap(last_far, "mp", 2)
+    gx = grad_input_rows(ids, dz1, (mix_a, mix_b), q_parts, pooled, dims, (last_far,))
+    gx_got = [gx[0]] + [swap(gx[k], "mp", k) for k in range(1, count)]
+    grad_input, pooled_out = land_grad(sent, gx_got, dims)
+
+    turned = turn_output(ids, hops, dims, (gx[0],))
+    landed = [turned[0]] + [swap(turned[k], "mp", k) for k in range(1, count)]
+    tokens_out = land_output(spots, landed, dims)
+
+    down_shards, _ = reduce_dp(send_down, keep_down, None, devices)
+    g_down = whole_grad(ids, down_shards, devices)
+    send, keep = own_grad(ids, al, du, got_in, crossed_in, devices, False, (gx[0],))
+    in_shards, _ = reduce_dp(send, keep, None, devices)
+    g_in = whole_grad(ids, in_shards, devices)
+    send, keep, vec = own_last(ids, grads_b, got_last, crossed_last, 1, devices)
+    last_shards, vec = reduce_dp(send, keep, vec, devices)
+    g_last = whole_grad(ids, last_shards, devices)
+    g_qkv = g_last[:inner].reshape(3, head_width, width).transpose(2, 0, 1)
+    g_bqv = jnp.stack([vec[0, :head_width], vec[0, 256 : 256 + head_width]])
+    return (
+        tokens_out, pooled_out, grad_input, g_qkv, g_bqv, g_last[inner:],
+        vec[2], vec[3], vec[4], g_in, vec[1], g_down, vec[5], vec[6], vec[7],
+    )
+
+
 def solution(mesh):
+    devices, count = mesh.shape["dp"], mesh.shape["mp"]
+
+    def body(*args):
+        rows = args[0].shape[0]
+        even = rows % devices == 0 and devices % count == 0 and count == 4
+        even = even and devices & (devices - 1) == 0 and rows // count == 2 * (rows // devices)
+        return (per_device if even else per_device_general)(*args)
+
     return jax.shard_map(
-        per_device,
+        body,
         mesh=mesh,
         in_specs=(
             P("dp", "mp", None),

time: 804 us -> 381 us (0.47)
  waiting for transfers between devices: 532 us -> 121 us
  Pallas kernels: 0 us -> 128 us
  matrix products: 83.7 us -> 0 us
  blocking collectives: 59.7 us -> 0 us
  starting transfers between devices: 24.4 us -> 83.3 us
  other arithmetic: 49.1 us -> 2.36 us
  between operations: 15.4 us -> 2.04 us
    psum x2 -> x0, waiting for transfers between devices: 284 us -> none  [the longest x1 182 us: per_device(): lax.psum((grad_w_qkv, grad_b_qv, grad_w_out, grad_w_in, grad_b_in, grad_w...]
    reduce_scatter x3 -> x0, waiting for transfers between devices: 141 us -> none  [the longest x1 58.5 us: per_device(): lax.psum_scatter(branch, 'mp', scatter_dimension=1, tiled=True)]
    pallas_call x0 -> x32, Pallas kernels: none -> 128 us  [call(): return lambda *args: made(*args, *after)]
    ppermute x0 -> x53, waiting for transfers between devices: none -> 121 us  [the longest x49 102 us: swap(): lax.ppermute(values, axis, [(i, i ^ bit) for i in range(lax.axis_size(axi...]
    dot_general x20 -> x0, matrix products: 83.7 us -> none  [the longest x1 10.6 us: per_device(): jnp.einsum('rsd,fd->rsf', mix_low, w_down, preferred_element_type=f32)]
    ppermute x0 -> x53, starting transfers between devices: none -> 83.3 us  [the longest x49 70.3 us: swap(): lax.ppermute(values, axis, [(i, i ^ bit) for i in range(lax.axis_size(axi...]
    all_gather x3 -> x0, waiting for transfers between devices: 81.1 us -> none  [the longest x1 28.4 us: per_device(): lax.all_gather(grad_inner.astype(jnp.bfloat16), 'mp', axis=1, tiled=True)]
    psum x1 -> x0, blocking collectives: 54.5 us -> none  [per_device(): lax.psum((grad_w_qkv, grad_b_qv, grad_w_out, grad_w_in, grad_b_in, grad_w...]
  transfers between devices with their start and end apart: 12 -> 53, of which waited for: 10 -> 14; matrix products, arithmetic and copies ran while one was open for 6% -> 1% of each run, Pallas kernels for 0% -> 28%
where the time goes in v1:
time: 381 us; the launch traced here: 374 us
  Pallas kernels  128 us (34%)
  waiting for transfers between devices  121 us (32%)
  starting transfers between devices  83.3 us (22%)
  local copies, waits for them, and re-layouts  37.5 us (10%)
    pallas_call x32, Pallas kernels, call(): return lambda *args: made(*args, *after)  128 us
    ppermute x49, waiting for transfers between devices, swap(): lax.ppermute(values, axis, [(i, i ^ bit) for i in range(lax.axis_size(axi...  102 us
    ppermute x49, starting transfers between devices, swap(): lax.ppermute(values, axis, [(i, i ^ bit) for i in range(lax.axis_size(axi...  70.3 us
    unnamed x156, local copies, waits for them, and re-layouts  32.4 us
    ppermute x2, waiting for transfers between devices, per_device(): lax.ppermute(t, ('dp', 'mp'), to_place(k))  11.4 us
    ppermute x2, starting transfers between devices, per_device(): lax.ppermute(og_sends[k], ('dp', 'mp'), from_place(k))  8.25 us
  transfers between devices with their start and end apart: 53, of which 14 were waited for; matrix products, arithmetic and copies ran while one was open for 1% of the time, Pallas kernels for 28%

profile of v1, /device:TPU:4, one launch (start us, length us, event | category | flops | bytes accessed | tf_op | source)
XLA Modules:
  0.0 374.0 jit_solution(163992085842995248)
XLA Ops:
  4.7 2.0 prep_rows.1
  7.4 2.9 prep_halves.1
  11.1 1.8 collective-permute-start.4
  17.1 27.1 %collective-permute-done.2.refs_5_.refs_9_ = bf16[144,768]{1,0:T(8,128)(2,1)S(1)} collective-permute-done((bf16[144,768]{1,0:T(8,128)(2,1)S(1)}, bf16[144,768]{1,0:T(8,128)(2,1)S(1)}, u32[]{:S(2)}, u32[]{:S(2)}) %collective-permute-start.2) | collective-permute-done | bytes 221216 | tf_op jit(solution)/shard_map/ppermute | solution.py:1433
  52.8 11.5 %attend.2 = (bf16[512,768]{1,0:T(8,128)(2,1)S(1)}, bf16[2,512,192]{2,1,0:T(8,128)(2,1)S(1)}, bf16[2,3,512,192]{3,2,1,0:T(8,128)(2,1)}, bf16[2,4,384,128]{3,2,1,0:T(8,128)(2,1)S(1)}) custom-call(s32[3]{0:T(128)S(1)} %pad_add_fusion.refs_0_, s32[8,128]{1,0:T(8,128)S(1)} %pad.4.refs_1_.refs_2_, bf16[144,768]{1,0:T(8,128)(2,1)S(1)} %copy-done.53, ...), custom_call_target="tpu_custom_call" | custom-call | flops 11500000256 | tf_op jit(solution)/shard_map/attend/pallas_call | solution.py:287
  74.6 4.1 %collective-permute-start.9 = (bf16[2,128,768]{2,1,0:T(8,128)(2,1)S(1)}, bf16[2,128,768]{2,1,0:T(8,128)(2,1)S(1)}, u32[]{:S(2)}, u32[]{:S(2)}) collective-permute-start(bf16[2,128,768]{2,1,0:T(8,128)(2,1)S(1)} %get-tuple-element.96), channel_id=1, source_target_pairs={{4,0},{12,1},{20,2},{28,3},{5,4},{13,5},{21,6},{29,7},{6,8},{14,9}... | collective-permute-start | bytes 1179656 | tf_op jit(solution)/shard_map/ppermute | solution.py:1531
  78.6 20.3 %collective-permute-done.18.refs_25_.refs_7_ = bf16[384,768]{1,0:T(8,128)(2,1)} collective-permute-done((bf16[384,768]{1,0:T(8,128)(2,1)}, bf16[384,768]{1,0:T(8,128)(2,1)}, u32[]{:S(2)}, u32[]{:S(2)}) %collective-permute-start.18) | collective-permute-done | bytes 589856 | tf_op jit(solution)/shard_map/ppermute | solution.py:1433
  98.9 4.2 %collective-permute-start.8 = (bf16[2,128,768]{2,1,0:T(8,128)(2,1)S(1)}, bf16[2,128,768]{2,1,0:T(8,128)(2,1)S(1)}, u32[]{:S(2)}, u32[]{:S(2)}) collective-permute-start(bf16[2,128,768]{2,1,0:T(8,128)(2,1)S(1)} %get-tuple-element.94.refs_10_), channel_id=1, source_target_pairs={{0,0},{8,1},{16,2},{24,3},{1,4},{9,5},{17,6},{25,7},{2,8},{10,9},{... | collective-permute-start | bytes 1179656 | tf_op jit(solution)/shard_map/ppermute | solution.py:1531
  103.7 10.5 %attend.3 = (bf16[2,512,192]{2,1,0:T(8,128)(2,1)S(1)}, bf16[2,3,512,192]{3,2,1,0:T(8,128)(2,1)S(1)}, bf16[2,4,384,128]{3,2,1,0:T(8,128)(2,1)S(1)}) custom-call(s32[3]{0:T(128)S(1)} %pad_add_fusion.refs_0_, s32[8,128]{1,0:T(8,128)S(1)} %pad.4.refs_1_.refs_2_, bf16[144,768]{1,0:T(8,128)(2,1)S(1)} %copy-done.54, bf16[144,768]{1,0:T(8,128)(2,1)S(1)} %copy-done.29, ...), custom_call_target="tpu_custom_call" | custom-call | flops 11500000256 | tf_op jit(solution)/shard_map/attend/pallas_call | solution.py:287
  116.3 7.2 %collective-permute-done.8.refs_11_ = bf16[2,128,768]{2,1,0:T(8,128)(2,1)S(1)} collective-permute-done((bf16[2,128,768]{2,1,0:T(8,128)(2,1)S(1)}, bf16[2,128,768]{2,1,0:T(8,128)(2,1)S(1)}, u32[]{:S(2)}, u32[]{:S(2)}) %collective-permute-start.8) | collective-permute-done | bytes 393248 | tf_op jit(solution)/shard_map/ppermute | solution.py:1531
  124.9 22.0 %ffn.1 = (bf16[512,768]{1,0:T(8,128)(2,1)}, f32[512,768]{1,0:T(8,128)}, f32[512,128]{1,0:T(8,128)S(1)}, bf16[4,512,768]{2,1,0:T(8,128)(2,1)}, bf16[4,512,768]{2,...) custom-call(s32[3]{0:T(128)S(1)} %pad_add_fusion.refs_0_, ...), custom_call_target="tpu_custom_call" | custom-call | flops 23000000512 | tf_op jit(solution)/shard_map/ffn/pallas_call | solution.py:287
  151.0 8.8 %ffn_back.1 = (bf16[4,512,768]{2,1,0:T(8,128)(2,1)}, bf16[2,768,768]{2,1,0:T(8,128)(2,1)}, f32[4,768]{1,0:T(4,128)S(1)}) custom-call(s32[3]{0:T(128)S(1)} %pad_add_fusion.refs_0_, bf16[512,768]{1,0:T(8,128)(2,1)S(1)} %copy-done.44, bf16[4,512,768]{2,1,0:T(8,128)(2,1)} %get-tuple-element.103.refs_2_, bf16[512,768]{1,0:T(8,128)(2,1)S(1)} %copy-done.46, ...), custom_call_target="tpu_custom_call" | custom-call | flops 10350000128 | tf_op jit(solution)/shard_map/ffn_back/pallas_call | solution.py:287
  160.4 3.2 peer_grad.1.refs_12_
  163.6 8.3 %collective-permute-start.25 = (bf16[768,768]{1,0:T(8,128)(2,1)}, bf16[768,768]{1,0:T(8,128)(2,1)}, u32[]{:S(2)}, u32[]{:S(2)}) collective-permute-start(bf16[768,768]{1,0:T(8,128)(2,1)} %peer_grad.1.refs_12_), channel_id=1, source_target_pairs={{0,2},{1,3},{2,0},{3,1},{4,6},{5,7},{6,4},{7,5},{8,10},{9,11},{10,... | collective-permute-start | bytes 3538952 | tf_op jit(solution)/shard_map/ppermute | solution.py:1433
  171.9 8.8 %norm_back.1 = (f32[512,768]{1,0:T(8,128)}, bf16[512,768]{1,0:T(8,128)(2,1)S(1)}, f32[8,768]{1,0:T(8,128)S(1)}) custom-call(s32[3]{0:T(128)S(1)} %pad_add_fusion.refs_0_, bf16[4,512,768]{2,1,0:T(8,128)(2,1)} %get-tuple-element.105.refs_1_.refs_2_, f32[512,768]{1,0:T(8,128)} %get-tuple-element.106.refs_2_, f32[512,768]{1,0:T(8,128)} %get-tuple-element.107.refs_3_, ...), custom_call_target="tpu_custom_call" | custom-call | flops 9200000000 | tf_op jit(solution)/shard_map/norm_back/pallas_call | solution.py:287
  180.8 2.7 peer_grad_in.1.refs_15_
  185.7 12.8 %attend_back.2 = (bf16[2,512,576]{2,1,0:T(8,128)(2,1)}, bf16[2,784,768]{2,1,0:T(8,128)(2,1)}) custom-call(s32[3]{0:T(128)S(1)} %pad_add_fusion.refs_0_, bf16[512,768]{1,0:T(8,128)(2,1)S(1)} %get-tuple-element.113.refs_1_, bf16[512,768]{1,0:T(8,128)(2,1)S(1)} %copy-done.61, f32[4,768]{1,0:T(4,128)S(1)} %get-tuple-element.111.refs_3_, ...), custom_call_target="tpu_custom_call" | custom-call | flops 14949999616 | tf_op jit(solution)/shard_map/attend_back/pallas_call | solution.py:287
  199.1 3.4 own_grad.2
  207.3 13.4 %attend_back.3 = (bf16[2,512,576]{2,1,0:T(8,128)(2,1)}, bf16[2,784,768]{2,1,0:T(8,128)(2,1)}) custom-call(s32[3]{0:T(128)S(1)} %pad_add_fusion.refs_0_, bf16[512,768]{1,0:T(8,128)(2,1)S(1)} %copy-done.58, bf16[512,768]{1,0:T(8,128)(2,1)S(1)} %copy-done.62, f32[4,768]{1,0:T(4,128)S(1)} %get-tuple-element.111.refs_3_, ...), custom_call_target="tpu_custom_call" | custom-call | flops 14949999616 | tf_op jit(solution)/shard_map/attend_back/pallas_call | solution.py:287
  220.9 3.7 collective-permute-start.48
  226.0 6.3 %grad_input_rows.1 = (bf16[144,768]{1,0:T(8,128)(2,1)S(1)}, bf16[144,768]{1,0:T(8,128)(2,1)S(1)}, bf16[144,768]{1,0:T(8,128)(2,1)S(1)}, bf16[144,768]{1,0:T(8,128)(2,1)S(1)}) custom-call(s32[3]{0:T(128)S(1)} %pad_add_fusion.refs_0_, f32[512,768]{1,0:T(8,128)} %get-tuple-element.112.refs_1_, bf16[2,512,576]{2,1,0:T(8,128)(2,1)} %get-tuple-element.121.refs_2_, ...), custom_call_target="tpu_custom_call" | custom-call | flops 6899999744 | tf_op jit(solution)/shard_map/grad_input_rows/pallas_call | solution.py:287
  232.5 3.1 own_grad.3
  237.4 2.0 collective-permute-start.49
  239.3 14.7 %collective-permute-done.33.refs_3_ = bf16[784,768]{1,0:T(8,128)(2,1)S(1)} collective-permute-done((bf16[784,768]{1,0:T(8,128)(2,1)S(1)}, bf16[784,768]{1,0:T(8,128)(2,1)S(1)}, u32[]{:S(2)}, u32[]{:S(2)}) %collective-permute-start.33) | collective-permute-done | bytes 1204256 | tf_op jit(solution)/shard_map/ppermute | solution.py:1433
  254.0 2.6 own_last.1
  258.9 1.7 collective-permute-start.42
  260.7 1.8 collective-permute-start.50
  262.5 4.3 %collective-permute-start.21 = (bf16[2,128,768]{2,1,0:T(8,128)(2,1)S(1)}, bf16[2,128,768]{2,1,0:T(8,128)(2,1)S(1)}, u32[]{:S(2)}, u32[]{:S(2)}) collective-permute-start(bf16[2,128,768]{2,1,0:T(8,128)(2,1)S(1)} %get-tuple-element.100), channel_id=1, source_target_pairs={{0,0},{1,8},{2,16},{3,24},{4,1},{5,9},{6,17},{7,25},{8,2},{9,10},{... | collective-permute-start | bytes 1179656 | tf_op jit(solution)/shard_map/ppermute | solution.py:1541
  267.5 4.1 %collective-permute-done.50.refs_2_ = bf16[96,768]{1,0:T(8,128)(2,1)S(1)} collective-permute-done((bf16[96,768]{1,0:T(8,128)(2,1)S(1)}, bf16[96,768]{1,0:T(8,128)(2,1)S(1)}, u32[]{:S(2)}, u32[]{:S(2)}) %collective-permute-start.50) | collective-permute-done | bytes 147488 | tf_op jit(solution)/shard_map/ppermute | solution.py:1433
  272.9 4.2 %collective-permute-start.43 = (bf16[96,768]{1,0:T(8,128)(2,1)S(1)}, bf16[96,768]{1,0:T(8,128)(2,1)S(1)}, u32[]{:S(2)}, u32[]{:S(2)}) collective-permute-start(bf16[96,768]{1,0:T(8,128)(2,1)S(1)} %get-tuple-element.153), channel_id=1, source_target_pairs={{0,16},{4,20},{8,24},{12,28},{16,0},{20,4},{24,8},{28,12},{1,17},{... | collective-permute-start | bytes 442376 | tf_op jit(solution)/shard_map/ppermute | solution.py:1433
  277.2 2.9 collective-permute-start.35
  280.1 5.8 %collective-permute-done.21.refs_1_ = bf16[2,128,768]{2,1,0:T(8,128)(2,1)S(1)} collective-permute-done((bf16[2,128,768]{2,1,0:T(8,128)(2,1)S(1)}, bf16[2,128,768]{2,1,0:T(8,128)(2,1)S(1)}, u32[]{:S(2)}, u32[]{:S(2)}) %collective-permute-start.21) | collective-permute-done | bytes 393248 | tf_op jit(solution)/shard_map/ppermute | solution.py:1541
  285.9 5.6 %collective-permute-done.22.refs_2_ = bf16[2,128,768]{2,1,0:T(8,128)(2,1)S(1)} collective-permute-done((bf16[2,128,768]{2,1,0:T(8,128)(2,1)S(1)}, bf16[2,128,768]{2,1,0:T(8,128)(2,1)S(1)}, u32[]{:S(2)}, u32[]{:S(2)}) %collective-permute-start.22) | collective-permute-done | bytes 393248 | tf_op jit(solution)/shard_map/ppermute | solution.py:1541
  291.5 1.8 turn_output.1
  293.6 18.2 %collective-permute-start.28 = (bf16[128,768]{1,0:T(8,128)(2,1)S(1)}, bf16[128,768]{1,0:T(8,128)(2,1)S(1)}, u32[]{:S(2)}, u32[]{:S(2)}) collective-permute-start(bf16[128,768]{1,0:T(8,128)(2,1)S(1)} %get-tuple-element.130), channel_id=1, source_target_pairs={{0,2},{1,3},{2,0},{3,1},{4,6},{5,7},{6,4},{7,5},{8,10},{9,11},{10,... | collective-permute-start | bytes 589832 | tf_op jit(solution)/shard_map/ppermute | solution.py:1433
  312.1 3.0 collective-permute-start.36
  315.1 9.7 %collective-permute-done.44.refs_2_ = bf16[96,768]{1,0:T(8,128)(2,1)S(1)} collective-permute-done((bf16[96,768]{1,0:T(8,128)(2,1)S(1)}, bf16[96,768]{1,0:T(8,128)(2,1)S(1)}, u32[]{:S(2)}, u32[]{:S(2)}) %collective-permute-start.44) | collective-permute-done | bytes 147488 | tf_op jit(solution)/shard_map/ppermute | solution.py:1433
  324.8 3.0 collective-permute-done.36.refs_1_
  330.5 3.1 collective-permute-start.37
  335.2 4.2 %collective-permute-done.45.refs_3_ = bf16[192,768]{1,0:T(8,128)(2,1)S(1)} collective-permute-done((bf16[192,768]{1,0:T(8,128)(2,1)S(1)}, bf16[192,768]{1,0:T(8,128)(2,1)S(1)}, u32[]{:S(2)}, u32[]{:S(2)}) %collective-permute-start.45) | collective-permute-done | bytes 294944 | tf_op jit(solution)/shard_map/ppermute | solution.py:1433
  340.6 1.9 collective-permute-start.38
  342.5 3.9 %collective-permute-done.32.refs_4_ = bf16[144,768]{1,0:T(8,128)(2,1)S(1)} collective-permute-done((bf16[144,768]{1,0:T(8,128)(2,1)S(1)}, bf16[144,768]{1,0:T(8,128)(2,1)S(1)}, u32[]{:S(2)}, u32[]{:S(2)}) %collective-permute-start.32) | collective-permute-done | bytes 221216 | tf_op jit(solution)/shard_map/ppermute | solution.py:1433
  346.3 2.2 land_grad.1
  348.6 2.1 whole_grad.5
  350.7 1.8 collective-permute-start.39
  352.6 6.4 %collective-permute-done.46.refs_4_ = bf16[384,768]{1,0:T(8,128)(2,1)S(1)} collective-permute-done((bf16[384,768]{1,0:T(8,128)(2,1)S(1)}, bf16[384,768]{1,0:T(8,128)(2,1)S(1)}, u32[]{:S(2)}, u32[]{:S(2)}) %collective-permute-start.46) | collective-permute-done | bytes 589856 | tf_op jit(solution)/shard_map/ppermute | solution.py:1433
  359.0 2.1 whole_grad.4
  362.4 8.4 %collective-permute-done.39.refs_4_ = bf16[384,768]{1,0:T(8,128)(2,1)S(1)} collective-permute-done((bf16[384,768]{1,0:T(8,128)(2,1)S(1)}, bf16[384,768]{1,0:T(8,128)(2,1)S(1)}, u32[]{:S(2)}, u32[]{:S(2)}) %collective-permute-start.39) | collective-permute-done | bytes 589856 | tf_op jit(solution)/shard_map/ppermute | solution.py:1433
  (295 shorter events, 62.6 us)
Async XLA Ops:
  6.9 40.5 %collective-permute-start.3 = (bf16[576,768]{1,0:T(8,128)(2,1)}, bf16[576,768]{1,0:T(8,128)(2,1)}, u32[]{:S(2)}, u32[]{:S(2)}) collective-permute-start(bf16[576,768]{1,0:T(8,128)(2,1)} %bitcast.6.refs_1_.refs_6_.refs_5_), channel_id=1, source_target_pairs={{0,1},{1,0},{2,3},{3,2},{4,5},{5,4},{6,7},{7,6},{8,9},{9,8},{10,11... | collective-permute-start | bytes 2654216 | tf_op jit(solution)/shard_map/ppermute | solution.py:1433
  11.1 34.3 %collective-permute-start.4 = (bf16[288,768]{1,0:T(8,128)(2,1)S(1)}, bf16[288,768]{1,0:T(8,128)(2,1)S(1)}, u32[]{:S(2)}, u32[]{:S(2)}) collective-permute-start(bf16[288,768]{1,0:T(8,128)(2,1)S(1)} %get-tuple-element.91), channel_id=1, source_target_pairs={{0,2},{1,3},{2,0},{3,1},{4,6},{5,7},{6,4},{7,5},{8,10},{9,11},{10,... | collective-permute-start | bytes 1327112 | tf_op jit(solution)/shard_map/ppermute | solution.py:1433
  12.9 34.4 %collective-permute-start.12 = (bf16[480,768]{1,0:T(8,128)(2,1)}, bf16[480,768]{1,0:T(8,128)(2,1)}, u32[]{:S(2)}, u32[]{:S(2)}) collective-permute-start(bf16[480,768]{1,0:T(8,128)(2,1)} %get-tuple-element.97), channel_id=1, source_target_pairs={{0,2},{1,3},{2,0},{3,1},{4,6},{5,7},{6,4},{7,5},{8,10},{9,11},{10,... | collective-permute-start | bytes 2211848 | tf_op jit(solution)/shard_map/ppermute | solution.py:1433
  14.2 30.2 %collective-permute-start.10 = (bf16[192,768]{1,0:T(8,128)(2,1)S(1)}, bf16[192,768]{1,0:T(8,128)(2,1)S(1)}, u32[]{:S(2)}, u32[]{:S(2)}) collective-permute-start(bf16[192,768]{1,0:T(8,128)(2,1)S(1)} %copy-done.18), channel_id=1, source_target_pairs={{0,1},{1,0},{2,3},{3,2},{4,5},{5,4},{6,7},{7,6},{8,9},{9,8},{10,11... | collective-permute-start | bytes 884744 | tf_op jit(solution)/shard_map/ppermute | solution.py:1433
  15.8 28.4 %collective-permute-start.2 = (bf16[144,768]{1,0:T(8,128)(2,1)S(1)}, bf16[144,768]{1,0:T(8,128)(2,1)S(1)}, u32[]{:S(2)}, u32[]{:S(2)}) collective-permute-start(bf16[144,768]{1,0:T(8,128)(2,1)S(1)} %get-tuple-element.90), channel_id=1, source_target_pairs={{0,3},{1,2},{2,1},{3,0},{4,7},{5,6},{6,5},{7,4},{8,11},{9,10},{10,... | collective-permute-start | bytes 663560 | tf_op jit(solution)/shard_map/ppermute | solution.py:1433
  44.2 26.3 %collective-permute-start.11 = (bf16[768,768]{1,0:T(8,128)(2,1)}, bf16[768,768]{1,0:T(8,128)(2,1)}, u32[]{:S(2)}, u32[]{:S(2)}) collective-permute-start(bf16[768,768]{1,0:T(8,128)(2,1)} %refs_6_.1), channel_id=1, source_target_pairs={{0,1},{1,0},{2,3},{3,2},{4,5},{5,4},{6,7},{7,6},{8,9},{9,8},{10,11... | collective-permute-start | bytes 3538952 | tf_op jit(solution)/shard_map/ppermute | solution.py:1433
  45.2 29.0 %collective-permute-start.16 = (bf16[768,768]{1,0:T(8,128)(2,1)}, bf16[768,768]{1,0:T(8,128)(2,1)}, u32[]{:S(2)}, u32[]{:S(2)}) collective-permute-start(bf16[768,768]{1,0:T(8,128)(2,1)} %refs_4_.3), channel_id=1, source_target_pairs={{0,1},{1,0},{2,3},{3,2},{4,5},{5,4},{6,7},{7,6},{8,9},{9,8},{10,11... | collective-permute-start | bytes 3538952 | tf_op jit(solution)/shard_map/ppermute | solution.py:1433
  46.2 21.3 %collective-permute-start.17 = (bf16[384,768]{1,0:T(8,128)(2,1)}, bf16[384,768]{1,0:T(8,128)(2,1)}, u32[]{:S(2)}, u32[]{:S(2)}) collective-permute-start(bf16[384,768]{1,0:T(8,128)(2,1)} %copy-done.10), channel_id=1, source_target_pairs={{0,2},{1,3},{2,0},{3,1},{4,6},{5,7},{6,4},{7,5},{8,10},{9,11},{10,... | collective-permute-start | bytes 1769480 | tf_op jit(solution)/shard_map/ppermute | solution.py:1433
  47.2 20.9 %collective-permute-start.6 = (bf16[288,768]{1,0:T(8,128)(2,1)}, bf16[288,768]{1,0:T(8,128)(2,1)S(1)}, u32[]{:S(2)}, u32[]{:S(2)}) collective-permute-start(bf16[288,768]{1,0:T(8,128)(2,1)} %copy-done.13), channel_id=1, source_target_pairs={{0,1},{1,0},{2,3},{3,2},{4,5},{5,4},{6,7},{7,6},{8,9},{9,8},{10,11... | collective-permute-start | bytes 1327112 | tf_op jit(solution)/shard_map/ppermute | solution.py:1433
  47.4 21.5 %collective-permute-start.5 = (bf16[288,768]{1,0:T(8,128)(2,1)}, bf16[288,768]{1,0:T(8,128)(2,1)}, u32[]{:S(2)}, u32[]{:S(2)}) collective-permute-start(bf16[288,768]{1,0:T(8,128)(2,1)} %copy-done.13), channel_id=1, source_target_pairs={{0,4},{4,0},{8,12},{12,8},{16,20},{20,16},{24,28},{28,24},{1,5},{5... | collective-permute-start | bytes 1327112 | tf_op jit(solution)/shard_map/ppermute | solution.py:1433
  67.5 35.8 %collective-permute-start.13 = (bf16[480,768]{1,0:T(8,128)(2,1)}, bf16[480,768]{1,0:T(8,128)(2,1)}, u32[]{:S(2)}, u32[]{:S(2)}) collective-permute-start(bf16[480,768]{1,0:T(8,128)(2,1)} %collective-permute-done.12.refs_18_.refs_8_.refs_12_), channel_id=1, source_target_pairs={{0,4},{4,0},{8,12},{12,8},{16,20},{20,16},{24,28},{28,24},{1,5},{5... | collective-permute-start | bytes 2211848 | tf_op jit(solution)/shard_map/ppermute | solution.py:1433
  68.9 30.0 %collective-permute-start.18 = (bf16[384,768]{1,0:T(8,128)(2,1)}, bf16[384,768]{1,0:T(8,128)(2,1)}, u32[]{:S(2)}, u32[]{:S(2)}) collective-permute-start(bf16[384,768]{1,0:T(8,128)(2,1)} %collective-permute-done.17.refs_24_.refs_6_), channel_id=1, source_target_pairs={{0,4},{4,0},{8,12},{12,8},{16,20},{20,16},{24,28},{28,24},{1,5},{5... | collective-permute-start | bytes 1769480 | tf_op jit(solution)/shard_map/ppermute | solution.py:1433
  70.5 32.6 %collective-permute-start.7 = (bf16[288,768]{1,0:T(8,128)(2,1)}, bf16[288,768]{1,0:T(8,128)(2,1)}, u32[]{:S(2)}, u32[]{:S(2)}) collective-permute-start(bf16[288,768]{1,0:T(8,128)(2,1)} %collective-permute-done.5.refs_7_.refs_8_), channel_id=1, source_target_pairs={{0,1},{1,0},{2,3},{3,2},{4,5},{5,4},{6,7},{7,6},{8,9},{9,8},{10,11... | collective-permute-start | bytes 1327112 | tf_op jit(solution)/shard_map/ppermute | solution.py:1433
  74.2 49.3 %collective-permute-start.14 = (bf16[480,768]{1,0:T(8,128)(2,1)}, bf16[480,768]{1,0:T(8,128)(2,1)S(1)}, u32[]{:S(2)}, u32[]{:S(2)}) collective-permute-start(bf16[480,768]{1,0:T(8,128)(2,1)} %collective-permute-done.12.refs_18_.refs_8_.refs_12_), channel_id=1, source_target_pairs={{0,1},{1,0},{2,3},{3,2},{4,5},{5,4},{6,7},{7,6},{8,9},{9,8},{10,11... | collective-permute-start | bytes 2211848 | tf_op jit(solution)/shard_map/ppermute | solution.py:1433
  74.6 41.7 %collective-permute-start.9 = (bf16[2,128,768]{2,1,0:T(8,128)(2,1)S(1)}, bf16[2,128,768]{2,1,0:T(8,128)(2,1)S(1)}, u32[]{:S(2)}, u32[]{:S(2)}) collective-permute-start(bf16[2,128,768]{2,1,0:T(8,128)(2,1)S(1)} %get-tuple-element.96), channel_id=1, source_target_pairs={{4,0},{12,1},{20,2},{28,3},{5,4},{13,5},{21,6},{29,7},{6,8},{14,9}... | collective-permute-start | bytes 1179656 | tf_op jit(solution)/shard_map/ppermute | solution.py:1531
  98.9 24.6 %collective-permute-start.8 = (bf16[2,128,768]{2,1,0:T(8,128)(2,1)S(1)}, bf16[2,128,768]{2,1,0:T(8,128)(2,1)S(1)}, u32[]{:S(2)}, u32[]{:S(2)}) collective-permute-start(bf16[2,128,768]{2,1,0:T(8,128)(2,1)S(1)} %get-tuple-element.94.refs_10_), channel_id=1, source_target_pairs={{0,0},{8,1},{16,2},{24,3},{1,4},{9,5},{17,6},{25,7},{2,8},{10,9},{... | collective-permute-start | bytes 1179656 | tf_op jit(solution)/shard_map/ppermute | solution.py:1531
  103.1 20.4 %collective-permute-start.20 = (bf16[384,768]{1,0:T(8,128)(2,1)}, bf16[384,768]{1,0:T(8,128)(2,1)S(1)}, u32[]{:S(2)}, u32[]{:S(2)}) collective-permute-start(bf16[384,768]{1,0:T(8,128)(2,1)} %collective-permute-done.18.refs_25_.refs_7_), channel_id=1, source_target_pairs={{0,1},{1,0},{2,3},{3,2},{4,5},{5,4},{6,7},{7,6},{8,9},{9,8},{10,11... | collective-permute-start | bytes 1769480 | tf_op jit(solution)/shard_map/ppermute | solution.py:1433
  103.3 20.3 %collective-permute-start.15 = (bf16[480,768]{1,0:T(8,128)(2,1)}, bf16[480,768]{1,0:T(8,128)(2,1)S(1)}, u32[]{:S(2)}, u32[]{:S(2)}) collective-permute-start(bf16[480,768]{1,0:T(8,128)(2,1)} %collective-permute-done.13.refs_19_.refs_9_.refs_13_), channel_id=1, source_target_pairs={{0,1},{1,0},{2,3},{3,2},{4,5},{5,4},{6,7},{7,6},{8,9},{9,8},{10,11... | collective-permute-start | bytes 2211848 | tf_op jit(solution)/shard_map/ppermute | solution.py:1433
  147.7 12.7 %collective-permute-start.23 = (bf16[2,768,768]{2,1,0:T(8,128)(2,1)}, bf16[2,768,768]{2,1,0:T(8,128)(2,1)S(1)}, u32[]{:S(2)}, u32[]{:S(2)}) collective-permute-start(bf16[2,768,768]{2,1,0:T(8,128)(2,1)} %get-tuple-element.110), channel_id=1, source_target_pairs={{0,1},{1,0},{2,3},{3,2},{4,5},{5,4},{6,7},{7,6},{8,9},{9,8},{10,11... | collective-permute-start | bytes 7077896 | tf_op jit(solution)/shard_map/ppermute | solution.py:1433
  159.8 21.0 %collective-permute-start.24 = (bf16[2,768,768]{2,1,0:T(8,128)(2,1)}, bf16[2,768,768]{2,1,0:T(8,128)(2,1)S(1)}, u32[]{:S(2)}, u32[]{:S(2)}) collective-permute-start(bf16[2,768,768]{2,1,0:T(8,128)(2,1)} %get-tuple-element.120), channel_id=1, source_target_pairs={{0,1},{1,0},{2,3},{3,2},{4,5},{5,4},{6,7},{7,6},{8,9},{9,8},{10,11... | collective-permute-start | bytes 7077896 | tf_op jit(solution)/shard_map/ppermute | solution.py:1433
  163.6 35.5 %collective-permute-start.25 = (bf16[768,768]{1,0:T(8,128)(2,1)}, bf16[768,768]{1,0:T(8,128)(2,1)}, u32[]{:S(2)}, u32[]{:S(2)}) collective-permute-start(bf16[768,768]{1,0:T(8,128)(2,1)} %peer_grad.1.refs_12_), channel_id=1, source_target_pairs={{0,2},{1,3},{2,0},{3,1},{4,6},{5,7},{6,4},{7,5},{8,10},{9,11},{10,... | collective-permute-start | bytes 3538952 | tf_op jit(solution)/shard_map/ppermute | solution.py:1433
  198.5 26.1 %collective-permute-start.26 = (bf16[2,784,768]{2,1,0:T(8,128)(2,1)}, bf16[2,784,768]{2,1,0:T(8,128)(2,1)S(1)}, u32[]{:S(2)}, u32[]{:S(2)}) collective-permute-start(bf16[2,784,768]{2,1,0:T(8,128)(2,1)} %get-tuple-element.122.refs_5_), channel_id=1, source_target_pairs={{0,1},{1,0},{2,3},{3,2},{4,5},{5,4},{6,7},{7,6},{8,9},{9,8},{10,11... | collective-permute-start | bytes 7225352 | tf_op jit(solution)/shard_map/ppermute | solution.py:1433
  198.8 33.7 %collective-permute-start.40 = (bf16[768,768]{1,0:T(8,128)(2,1)S(1)}, bf16[768,768]{1,0:T(8,128)(2,1)S(1)}, u32[]{:S(2)}, u32[]{:S(2)}) collective-permute-start(bf16[768,768]{1,0:T(8,128)(2,1)S(1)} %copy-done.4), channel_id=1, source_target_pairs={{0,2},{1,3},{2,0},{3,1},{4,6},{5,7},{6,4},{7,5},{8,10},{9,11},{10,... | collective-permute-start | bytes 3538952 | tf_op jit(solution)/shard_map/ppermute | solution.py:1433
  202.5 18.3 %collective-permute-start.47 = (bf16[384,768]{1,0:T(8,128)(2,1)S(1)}, bf16[384,768]{1,0:T(8,128)(2,1)S(1)}, u32[]{:S(2)}, u32[]{:S(2)}) collective-permute-start(bf16[384,768]{1,0:T(8,128)(2,1)S(1)} %get-tuple-element.123.refs_15_), channel_id=1, source_target_pairs={{0,4},{4,0},{8,12},{12,8},{16,20},{20,16},{24,28},{28,24},{1,5},{5... | collective-permute-start | bytes 1769480 | tf_op jit(solution)/shard_map/ppermute | solution.py:1433
  220.9 16.4 %collective-permute-start.48 = (bf16[192,768]{1,0:T(8,128)(2,1)S(1)}, bf16[192,768]{1,0:T(8,128)(2,1)S(1)}, u32[]{:S(2)}, u32[]{:S(2)}) collective-permute-start(bf16[192,768]{1,0:T(8,128)(2,1)S(1)} %get-tuple-element.156), channel_id=1, source_target_pairs={{0,8},{4,12},{8,0},{12,4},{16,24},{20,28},{24,16},{28,20},{1,9},{5... | collective-permute-start | bytes 884744 | tf_op jit(solution)/shard_map/ppermute | solution.py:1433
  226.0 28.0 %collective-permute-start.33 = (bf16[784,768]{1,0:T(8,128)(2,1)S(1)}, bf16[784,768]{1,0:T(8,128)(2,1)S(1)}, u32[]{:S(2)}, u32[]{:S(2)}) collective-permute-start(bf16[784,768]{1,0:T(8,128)(2,1)S(1)} %peer_last.1.refs_11_), channel_id=1, source_target_pairs={{0,2},{1,3},{2,0},{3,1},{4,6},{5,7},{6,4},{7,5},{8,10},{9,11},{10,... | collective-permute-start | bytes 3612680 | tf_op jit(solution)/shard_map/ppermute | solution.py:1433
  236.6 20.7 %collective-permute-start.41 = (bf16[384,768]{1,0:T(8,128)(2,1)S(1)}, bf16[384,768]{1,0:T(8,128)(2,1)S(1)}, u32[]{:S(2)}, u32[]{:S(2)}) collective-permute-start(bf16[384,768]{1,0:T(8,128)(2,1)S(1)} %get-tuple-element.149), channel_id=1, source_target_pairs={{0,4},{4,0},{8,12},{12,8},{16,20},{20,16},{24,28},{28,24},{1,5},{5... | collective-permute-start | bytes 1769480 | tf_op jit(solution)/shard_map/ppermute | solution.py:1433
  237.4 23.3 %collective-permute-start.49 = (bf16[96,768]{1,0:T(8,128)(2,1)S(1)}, bf16[96,768]{1,0:T(8,128)(2,1)S(1)}, u32[]{:S(2)}, u32[]{:S(2)}) collective-permute-start(bf16[96,768]{1,0:T(8,128)(2,1)S(1)} %get-tuple-element.158), channel_id=1, source_target_pairs={{0,16},{4,20},{8,24},{12,28},{16,0},{20,4},{24,8},{28,12},{1,17},{... | collective-permute-start | bytes 442376 | tf_op jit(solution)/shard_map/ppermute | solution.py:1433
  256.6 20.5 %collective-permute-start.34 = (bf16[400,768]{1,0:T(8,128)(2,1)S(1)}, bf16[400,768]{1,0:T(8,128)(2,1)S(1)}, u32[]{:S(2)}, u32[]{:S(2)}) collective-permute-start(bf16[400,768]{1,0:T(8,128)(2,1)S(1)} %get-tuple-element.138), channel_id=1, source_target_pairs={{0,4},{4,0},{8,12},{12,8},{16,20},{20,16},{24,28},{28,24},{1,5},{5... | collective-permute-start | bytes 1843208 | tf_op jit(solution)/shard_map/ppermute | solution.py:1433
  258.9 12.8 %collective-permute-start.42 = (bf16[192,768]{1,0:T(8,128)(2,1)}, bf16[192,768]{1,0:T(8,128)(2,1)S(1)}, u32[]{:S(2)}, u32[]{:S(2)}) collective-permute-start(bf16[192,768]{1,0:T(8,128)(2,1)} %get-tuple-element.151), channel_id=1, source_target_pairs={{0,8},{4,12},{8,0},{12,4},{16,24},{20,28},{24,16},{28,20},{1,9},{5... | collective-permute-start | bytes 884744 | tf_op jit(solution)/shard_map/ppermute | solution.py:1433
  260.7 10.8 %collective-permute-start.50 = (bf16[96,768]{1,0:T(8,128)(2,1)S(1)}, bf16[96,768]{1,0:T(8,128)(2,1)S(1)}, u32[]{:S(2)}, u32[]{:S(2)}) collective-permute-start(bf16[96,768]{1,0:T(8,128)(2,1)S(1)} %end_halving.5.refs_1_), channel_id=1, source_target_pairs={{0,16},{4,20},{8,24},{12,28},{16,0},{20,4},{24,8},{28,12},{1,17},{... | collective-permute-start | bytes 442376 | tf_op jit(solution)/shard_map/ppermute | solution.py:1433
  262.5 23.4 %collective-permute-start.21 = (bf16[2,128,768]{2,1,0:T(8,128)(2,1)S(1)}, bf16[2,128,768]{2,1,0:T(8,128)(2,1)S(1)}, u32[]{:S(2)}, u32[]{:S(2)}) collective-permute-start(bf16[2,128,768]{2,1,0:T(8,128)(2,1)S(1)} %get-tuple-element.100), channel_id=1, source_target_pairs={{0,0},{1,8},{2,16},{3,24},{4,1},{5,9},{6,17},{7,25},{8,2},{9,10},{... | collective-permute-start | bytes 1179656 | tf_op jit(solution)/shard_map/ppermute | solution.py:1541
  266.8 24.7 %collective-permute-start.22 = (bf16[2,128,768]{2,1,0:T(8,128)(2,1)S(1)}, bf16[2,128,768]{2,1,0:T(8,128)(2,1)S(1)}, u32[]{:S(2)}, u32[]{:S(2)}) collective-permute-start(bf16[2,128,768]{2,1,0:T(8,128)(2,1)S(1)} %get-tuple-element.101), channel_id=1, source_target_pairs={{0,4},{1,12},{2,20},{3,28},{4,5},{5,13},{6,21},{7,29},{8,6},{9,14}... | collective-permute-start | bytes 1179656 | tf_op jit(solution)/shard_map/ppermute | solution.py:1541
  271.6 40.5 %collective-permute-start.51 = (bf16[192,768]{1,0:T(8,128)(2,1)S(1)}, bf16[192,768]{1,0:T(8,128)(2,1)S(1)}, u32[]{:S(2)}, u32[]{:S(2)}) collective-permute-start(bf16[192,768]{1,0:T(8,128)(2,1)S(1)} %pad_maximum_fusion.5), channel_id=1, source_target_pairs={{0,8},{4,12},{8,0},{12,4},{16,24},{20,28},{24,16},{28,20},{1,9},{5... | collective-permute-start | bytes 884744 | tf_op jit(solution)/shard_map/ppermute | solution.py:1433
  272.9 38.9 %collective-permute-start.43 = (bf16[96,768]{1,0:T(8,128)(2,1)S(1)}, bf16[96,768]{1,0:T(8,128)(2,1)S(1)}, u32[]{:S(2)}, u32[]{:S(2)}) collective-permute-start(bf16[96,768]{1,0:T(8,128)(2,1)S(1)} %get-tuple-element.153), channel_id=1, source_target_pairs={{0,16},{4,20},{8,24},{12,28},{16,0},{20,4},{24,8},{28,12},{1,17},{... | collective-permute-start | bytes 442376 | tf_op jit(solution)/shard_map/ppermute | solution.py:1433
  277.2 34.7 %collective-permute-start.35 = (bf16[208,768]{1,0:T(8,128)(2,1)S(1)}, bf16[208,768]{1,0:T(8,128)(2,1)S(1)}, u32[]{:S(2)}, u32[]{:S(2)}) collective-permute-start(bf16[208,768]{1,0:T(8,128)(2,1)S(1)} %get-tuple-element.141), channel_id=1, source_target_pairs={{0,8},{4,12},{8,0},{12,4},{16,24},{20,28},{24,16},{28,20},{1,9},{5... | collective-permute-start | bytes 958472 | tf_op jit(solution)/shard_map/ppermute | solution.py:1433
  293.3 34.6 %collective-permute-start.27 = (bf16[128,768]{1,0:T(8,128)(2,1)S(1)}, bf16[128,768]{1,0:T(8,128)(2,1)S(1)}, u32[]{:S(2)}, u32[]{:S(2)}) collective-permute-start(bf16[128,768]{1,0:T(8,128)(2,1)S(1)} %get-tuple-element.129), channel_id=1, source_target_pairs={{0,1},{1,0},{2,3},{3,2},{4,5},{5,4},{6,7},{7,6},{8,9},{9,8},{10,11... | collective-permute-start | bytes 589832 | tf_op jit(solution)/shard_map/ppermute | solution.py:1433
  293.6 36.9 %collective-permute-start.28 = (bf16[128,768]{1,0:T(8,128)(2,1)S(1)}, bf16[128,768]{1,0:T(8,128)(2,1)S(1)}, u32[]{:S(2)}, u32[]{:S(2)}) collective-permute-start(bf16[128,768]{1,0:T(8,128)(2,1)S(1)} %get-tuple-element.130), channel_id=1, source_target_pairs={{0,2},{1,3},{2,0},{3,1},{4,6},{5,7},{6,4},{7,5},{8,10},{9,11},{10,... | collective-permute-start | bytes 589832 | tf_op jit(solution)/shard_map/ppermute | solution.py:1433
  311.7 18.7 %collective-permute-start.29 = (bf16[128,768]{1,0:T(8,128)(2,1)S(1)}, bf16[128,768]{1,0:T(8,128)(2,1)S(1)}, u32[]{:S(2)}, u32[]{:S(2)}) collective-permute-start(bf16[128,768]{1,0:T(8,128)(2,1)S(1)} %get-tuple-element.131), channel_id=1, source_target_pairs={{0,3},{1,2},{2,1},{3,0},{4,7},{5,6},{6,5},{7,4},{8,11},{9,10},{10,... | collective-permute-start | bytes 589832 | tf_op jit(solution)/shard_map/ppermute | solution.py:1433
  311.9 12.9 %collective-permute-start.44 = (bf16[96,768]{1,0:T(8,128)(2,1)S(1)}, bf16[96,768]{1,0:T(8,128)(2,1)S(1)}, u32[]{:S(2)}, u32[]{:S(2)}) collective-permute-start(bf16[96,768]{1,0:T(8,128)(2,1)S(1)} %end_halving.4.refs_1_), channel_id=1, source_target_pairs={{0,16},{4,20},{8,24},{12,28},{16,0},{20,4},{24,8},{28,12},{1,17},{... | collective-permute-start | bytes 442376 | tf_op jit(solution)/shard_map/ppermute | solution.py:1433
  312.1 15.8 %collective-permute-start.36 = (bf16[112,768]{1,0:T(8,128)(2,1)S(1)}, bf16[112,768]{1,0:T(8,128)(2,1)S(1)}, u32[]{:S(2)}, u32[]{:S(2)}) collective-permute-start(bf16[112,768]{1,0:T(8,128)(2,1)S(1)} %get-tuple-element.144), channel_id=1, source_target_pairs={{0,16},{4,20},{8,24},{12,28},{16,0},{20,4},{24,8},{28,12},{1,17},{... | collective-permute-start | bytes 516104 | tf_op jit(solution)/shard_map/ppermute | solution.py:1433
  324.8 15.8 %collective-permute-start.30 = (bf16[144,768]{1,0:T(8,128)(2,1)S(1)}, bf16[144,768]{1,0:T(8,128)(2,1)S(1)}, u32[]{:S(2)}, u32[]{:S(2)}) collective-permute-start(bf16[144,768]{1,0:T(8,128)(2,1)S(1)} %copy-done.26), channel_id=1, source_target_pairs={{0,1},{1,0},{2,3},{3,2},{4,5},{5,4},{6,7},{7,6},{8,9},{9,8},{10,11... | collective-permute-start | bytes 663560 | tf_op jit(solution)/shard_map/ppermute | solution.py:1433
  327.8 11.5 %collective-permute-start.45 = (bf16[192,768]{1,0:T(8,128)(2,1)S(1)}, bf16[192,768]{1,0:T(8,128)(2,1)S(1)}, u32[]{:S(2)}, u32[]{:S(2)}) collective-permute-start(bf16[192,768]{1,0:T(8,128)(2,1)S(1)} %pad_maximum_fusion.4), channel_id=1, source_target_pairs={{0,8},{4,12},{8,0},{12,4},{16,24},{20,28},{24,16},{28,20},{1,9},{5... | collective-permute-start | bytes 884744 | tf_op jit(solution)/shard_map/ppermute | solution.py:1433
  328.8 13.7 %collective-permute-start.31 = (bf16[144,768]{1,0:T(8,128)(2,1)S(1)}, bf16[144,768]{1,0:T(8,128)(2,1)S(1)}, u32[]{:S(2)}, u32[]{:S(2)}) collective-permute-start(bf16[144,768]{1,0:T(8,128)(2,1)S(1)} %copy-done.24), channel_id=1, source_target_pairs={{0,2},{1,3},{2,0},{3,1},{4,6},{5,7},{6,4},{7,5},{8,10},{9,11},{10,... | collective-permute-start | bytes 663560 | tf_op jit(solution)/shard_map/ppermute | solution.py:1433
  330.5 18.1 %collective-permute-start.52 = (bf16[384,768]{1,0:T(8,128)(2,1)S(1)}, bf16[384,768]{1,0:T(8,128)(2,1)S(1)}, u32[]{:S(2)}, u32[]{:S(2)}) collective-permute-start(bf16[384,768]{1,0:T(8,128)(2,1)S(1)} %pad_maximum_fusion.2), channel_id=1, source_target_pairs={{0,4},{4,0},{8,12},{12,8},{16,20},{20,16},{24,28},{28,24},{1,5},{5... | collective-permute-start | bytes 1769480 | tf_op jit(solution)/shard_map/ppermute | solution.py:1433
  340.5 18.5 %collective-permute-start.46 = (bf16[384,768]{1,0:T(8,128)(2,1)S(1)}, bf16[384,768]{1,0:T(8,128)(2,1)S(1)}, u32[]{:S(2)}, u32[]{:S(2)}) collective-permute-start(bf16[384,768]{1,0:T(8,128)(2,1)S(1)} %pad_maximum_fusion.1), channel_id=1, source_target_pairs={{0,4},{4,0},{8,12},{12,8},{16,20},{20,16},{24,28},{28,24},{1,5},{5... | collective-permute-start | bytes 1769480 | tf_op jit(solution)/shard_map/ppermute | solution.py:1433
  340.6 10.1 %collective-permute-start.38 = (bf16[192,768]{1,0:T(8,128)(2,1)S(1)}, bf16[192,768]{1,0:T(8,128)(2,1)S(1)}, u32[]{:S(2)}, u32[]{:S(2)}) collective-permute-start(bf16[192,768]{1,0:T(8,128)(2,1)S(1)} %pad_maximum_fusion.3), channel_id=1, source_target_pairs={{0,8},{4,12},{8,0},{12,4},{16,24},{20,28},{24,16},{28,20},{1,9},{5... | collective-permute-start | bytes 884744 | tf_op jit(solution)/shard_map/ppermute | solution.py:1433
  350.7 20.0 %collective-permute-start.39 = (bf16[384,768]{1,0:T(8,128)(2,1)S(1)}, bf16[384,768]{1,0:T(8,128)(2,1)S(1)}, u32[]{:S(2)}, u32[]{:S(2)}) collective-permute-start(bf16[384,768]{1,0:T(8,128)(2,1)S(1)} %pad_maximum_fusion), channel_id=1, source_target_pairs={{0,4},{4,0},{8,12},{12,8},{16,20},{20,16},{24,28},{28,24},{1,5},{5... | collective-permute-start | bytes 1769480 | tf_op jit(solution)/shard_map/ppermute | solution.py:1433
  (83 other events, 642.8 us)

commit v2 on v1

--- a/solution.py
+++ b/solution.py
@@ -259,7 +259,8 @@
 SM = pl.BlockSpec(memory_space=pltpu.SMEM)
 HB = pl.BlockSpec(memory_space=pl.ANY)
 HM = pl.BlockSpec(memory_space=pltpu.HBM)
-ROOM = 48 * 1024 * 1024
+MIB = 1024 * 1024
+PACE = 2e9
 
 
 def shape_of(shape, dtype=bf16):
@@ -267,7 +268,7 @@
 
 
 def call(
-    body, outs, out_specs, in_specs, scratch=(), us=2, room=ROOM, name=None, after=()
+    body, outs, out_specs, in_specs, scratch=(), us=2, room=16, name=None, after=()
 ):
     n, extra = len(in_specs), len(after)
 
@@ -280,8 +281,8 @@
         in_specs=list(in_specs) + [HB] * extra,
         out_specs=out_specs,
         scratch_shapes=list(scratch),
-        compiler_params=pltpu.CompilerParams(vmem_limit_bytes=room),
-        cost_estimate=pl.CostEstimate(flops=int(us * 1.15e9), bytes_accessed=0, transcendentals=0),
+        compiler_params=pltpu.CompilerParams(vmem_limit_bytes=room * MIB),
+        cost_estimate=pl.CostEstimate(flops=int(us * PACE), bytes_accessed=0, transcendentals=0),
         name=name,
     )
     return lambda *args: made(*args, *after)
@@ -307,88 +308,172 @@
     return high, middle, low
 
 
-def prep_rows(sent, tokens, b_qv, b_in, dims):
+def piece_places(refs, size):
+    return [(refs[0], 0), (refs[1], 0), (refs[2], 0), (refs[3], size)]
+
+
+def exchange(own, near, far):
+    crossed = swap(far, "mp", 2)
+    return [own, swap(near, "mp", 1), crossed, swap(crossed, "mp", 1)]
+
+
+def prep_rows(route, seg, tokens, b_qv, b_in, weights, dims):
     devices, count, rows, quarter, full, width = dims
-    here = rows // count
+    here, cap = rows // count, rows // devices
     head_width = b_qv.shape[1]
     tile = here * quarter
-
-    def body(sent_ref, tok, bqv_ref, bin_ref, x0, x1, x2, x3, extra, sems):
-        xs = (x0, x1, x2, x3)
+    total = devices * rows
+    halves = [w.shape[0] // 2 for w in weights]
+
+    def body(
+        route_ref, seg_ref, tok, bqv_ref, bin_ref, wq, wo, x0, x1, far, segr, sent_ref, spots_ref,
+        ids_ref, lists, sems,
+    ):
+        my, mi = lax.axis_index("dp"), lax.axis_index("mp")
+        crossing = []
+        base = 2 * (tile + 16)
+        for n, (src, half) in enumerate(zip((wq, wo), halves)):
+            crossing.append(
+                pltpu.make_async_copy(
+                    src.at[pl.ds(pl.multiple_of(lax.rem(my, 2) * half, 16), half)],
+                    far.at[pl.ds(base, half)],
+                    sems.at[rows + 2 + n],
+                )
+            )
+            crossing[n].start()
+            base += half
+        ids_ref[0] = my
+        ids_ref[1] = mi
+        ids_ref[2] = lax.rem(my, 2)
+        places = piece_places((x0, x1, far, far), tile + 16)
+        across = jnp.broadcast_to(route_ref[...].reshape(1, total), (total, total)).astype(f32)
+        down = across.T.astype(jnp.int32)
+        across = across.astype(jnp.int32)
+        r = lax.broadcasted_iota(jnp.int32, (total, total), 0)
+        c = lax.broadcasted_iota(jnp.int32, (total, total), 1)
+        key_down = lax.div(down, rows) * total + r
+        key_across = lax.div(across, rows) * total + c
+        before = (lax.div(r, rows) == lax.div(c, rows)) & (key_across < key_down)
+        rank = jnp.sum(jnp.where(before, 1.0, 0.0), axis=1, keepdims=True).astype(jnp.int32)
+        at = lax.rem(c, rows)
+        partner = my ^ ((mi ^ lax.div(at, here)) + count * lax.rem(lax.div(at, cap), here // cap))
+        copy_at = lax.rem(at, cap)
+        source = lax.div(r, rows)
+        going = (source == my) & (rank == partner * cap + copy_at)
+        coming = (source == partner) & (rank == my * cap + copy_at)
+        lists[0:1, :] = jnp.sum(
+            jnp.where(going, lax.rem(r, rows), 0).astype(f32), axis=0, keepdims=True
+        ).astype(jnp.int32)
+        lists[1:2, :] = jnp.sum(
+            jnp.where(coming, down - my * rows, 0).astype(f32), axis=0, keepdims=True
+        ).astype(jnp.int32)
+        moves = [
+            pltpu.make_async_copy(lists.at[0], sent_ref, sems.at[rows]),
+            pltpu.make_async_copy(lists.at[1], spots_ref, sems.at[rows + 1]),
+        ]
+        for move in moves:
+            move.start()
+        zero = jnp.zeros((16, width), bf16)
+        tail = x0.at[pl.ds(tile, 16)]
+        tail[...] = zero
+        for n, term in enumerate(split3(bqv_ref[...])):
+            tail[n : n + 1, 0:head_width] = term[0:1]
+            tail[n : n + 1, 256 : 256 + head_width] = term[1:2]
+        for n, term in enumerate(split3(bin_ref[...].reshape(1, width))):
+            tail[3 + n : 4 + n, :] = term
+        for ref, base in places[1:]:
+            ref[base + tile : base + tile + 16, :] = tail[...]
+        for move in moves:
+            move.wait()
         copies = []
         for kk in reversed(range(count)):
-            for j in range(here):
-                at = kk * here + j
+            for n in range(here):
+                k = kk * here + n
                 copies.append(
                     pltpu.make_async_copy(
-                        tok.at[sent_ref[at]], xs[kk].at[pl.ds(j * quarter, quarter)], sems.at[at]
+                        tok.at[sent_ref[k]],
+                        places[kk][0].at[pl.ds(places[kk][1] + n * quarter, quarter)],
+                        sems.at[k],
                     )
                 )
         for copy in copies:
             copy.start()
-        extra[...] = jnp.zeros_like(extra)
-        for j, term in enumerate(split3(bqv_ref[...])):
-            extra[j : j + 1, 0:head_width] = term[0:1]
-            extra[j : j + 1, 256 : 256 + head_width] = term[1:2]
-        for j, term in enumerate(split3(bin_ref[...])):
-            extra[3 + j : 4 + j, :] = term
-        tails = [
-            pltpu.make_async_copy(extra, xs[kk].at[pl.ds(tile, 16)], sems.at[rows + kk])
-            for kk in range(count)
+        for n in range(here):
+            segr[n : n + 1, :] = seg_ref[pl.ds(my * rows + sent_ref[n], 1), :]
+        segr[here:8, :] = jnp.zeros((8 - here, full), jnp.int32)
+        lane = lax.broadcasted_iota(jnp.int32, (8, full), 1)
+        lines = segr[...]
+        bit = 1
+        while bit < count:
+            step = bit * quarter
+            swapped = jnp.where(
+                lax.rem(lax.div(lane, step), 2) == 0,
+                pltpu.roll(lines, full - step, 1),
+                pltpu.roll(lines, step, 1),
+            )
+            lines = jnp.where(lax.rem(lax.div(mi, bit), 2) == 1, swapped, lines)
+            bit *= 2
+        segr[...] = lines
+        for copy in copies + crossing:
+            copy.wait()
+
+    return call(
+        body,
+        [
+            shape_of((tile + 16, width)),
+            shape_of((tile + 16, width)),
+            shape_of((2 * (tile + 16) + sum(halves), width)),
         ]
-        for copy in tails:
+        + [
+            shape_of((8, full), jnp.int32),
+            shape_of((total,), jnp.int32),
+            shape_of((total,), jnp.int32),
+            shape_of((3,), jnp.int32),
+        ],
+        [VM] * 4 + [SM] * 3,
+        [VM, VM, HM, VM, VM, HM, HM],
+        [pltpu.VMEM((8, total), jnp.int32), pltpu.SemaphoreType.DMA((rows + 4,))],
+        us=3,
+        name="prep_rows",
+        room=60,
+    )(route, seg, tokens, b_qv, b_in, *weights)
+
+
+def prep_halves(weights, bit, after=()):
+    width = weights[0].shape[1]
+    halves = [w.shape[0] // 2 for w in weights]
+    n = len(weights)
+
+    def body(*refs):
+        out, sems = refs[n:]
+        parity = lax.rem(lax.div(lax.axis_index("dp"), bit), 2)
+        copies = []
+        base = 0
+        for at, half in enumerate(halves):
+            copies.append(
+                pltpu.make_async_copy(
+                    refs[at].at[pl.ds(pl.multiple_of(parity * half, 16), half)],
+                    out.at[pl.ds(base, half)],
+                    sems.at[at],
+                )
+            )
+            base += half
+        for copy in copies:
             copy.start()
-        for copy in copies + tails:
+        for copy in copies:
             copy.wait()
 
     return call(
         body,
-        [shape_of((tile + 16, width))] * count,
-        [HB] * count,
-        [SM, HM, VM, VM],
-        [pltpu.VMEM((16, width), bf16), pltpu.SemaphoreType.DMA((rows + count,))],
-        us=2,
-        name="prep_rows",
-    )(sent, tokens, b_qv, b_in.reshape(1, -1))
-
-
-def prep_halves(ids, w_q, w_out, w_in, w_down, after):
-    width = w_q.shape[1]
-    halves = [w.shape[0] // 2 for w in (w_q, w_out, w_in, w_down)]
-
-    def body(ids_ref, wq, wo, wi, wd, q, oi, dn, sems):
-        parity = ids_ref[2]
-
-        def copy(src, half, dst, at):
-            return pltpu.make_async_copy(
-                src.at[pl.ds(pl.multiple_of(parity * half, 16), half)], dst, sems.at[at]
-            )
-
-        copies = [
-            copy(wq, halves[0], q, 0),
-            copy(wo, halves[1], oi.at[pl.ds(0, halves[1])], 1),
-            copy(wi, halves[2], oi.at[pl.ds(halves[1], halves[2])], 2),
-            copy(wd, halves[3], dn, 3),
-        ]
-        for c in copies:
-            c.start()
-        for c in copies:
-            c.wait()
-
-    return call(
-        body,
-        [
-            shape_of((halves[0], width)),
-            shape_of((halves[1] + halves[2], width)),
-            shape_of((halves[3], width)),
-        ],
-        [VM] * 3,
-        [SM] + [HM] * 4,
-        [pltpu.SemaphoreType.DMA((4,))],
-        us=2,
+        shape_of((sum(halves), width)),
+        VM,
+        [HM] * n,
+        [pltpu.SemaphoreType.DMA((n,))],
+        us=1,
         name="prep_halves",
+        room=4,
         after=after,
-    )(ids, w_q, w_out, w_in, w_down)
+    )(*weights)
 
 
 def prep_cot(asked, out_grad, dims, after):
@@ -412,11 +497,12 @@
     return call(
         body,
         [shape_of((cap, full, width))] * reach,
-        [HB] * reach,
+        [VM] * reach,
         [SM, HM],
         [pltpu.SemaphoreType.DMA((reach * cap,))],
         us=2,
         name="prep_cot",
+        room=6,
         after=after,
     )(asked, out_grad)
 
@@ -445,30 +531,41 @@
     return out
 
 
-def load_parts(parts, parity, half, dst, offset, sems, at):
-    if len(parts) == 1:
-        return [pltpu.make_async_copy(parts[0], dst.at[pl.ds(offset, 2 * half)], sems.at[at])]
-    first = pl.multiple_of(parity * half, 16)
-    second = pl.multiple_of((1 - parity) * half, 16)
-    return [
-        pltpu.make_async_copy(parts[0], dst.at[pl.ds(offset + first, half)], sems.at[at]),
-        pltpu.make_async_copy(parts[1], dst.at[pl.ds(offset + second, half)], sems.at[at + 1]),
-    ]
-
-
-def attend(ids, segr, pieces, parts, pair, dims, keep_x, after=()):
+def parity_of(ids_ref, bit):
+    return lax.rem(lax.div(ids_ref[0], bit), 2)
+
+
+def load_parts(refs, bases, parity, half, dst, sems, at, row=0):
+    if len(refs) == 1:
+        return [pltpu.make_async_copy(refs[0], dst, sems.at[at])]
+    copies = []
+    for j, place in enumerate((parity, 1 - parity)):
+        copies.append(
+            pltpu.make_async_copy(
+                refs[j].at[pl.ds(bases[j] + row, half)],
+                dst.at[pl.ds(pl.multiple_of(place * half, 16), half)],
+                sems.at[at + j],
+            )
+        )
+    return copies
+
+
+def bases_of(part):
+    return [base for _, base in part]
+
+
+def attend(ids, segr, pieces, parts, pair, inner, dims, keep_x, after=()):
     devices, count, rows, quarter, full, width = dims
     here = rows // count
     tokens = here * full
     tile = here * quarter
-    inner = sum(ref.shape[0] for ref in parts[0])
     head_width = inner // 3
     n_heads = head_width // HD
     n_parts = [len(p) for p in parts]
-    flat = [ref for p in parts for ref in p]
+    flat = [ref for p in parts for ref, _ in p]
 
     def body(ids_ref, segr_ref, *refs):
-        piece_refs = refs[:count]
+        places = piece_places(refs[:count], tile + 16)
         w_refs = refs[count : count + len(flat)]
         out = list(refs[count + len(flat) :])
         if keep_x:
@@ -478,15 +575,16 @@
         at = 0
         for b, n in enumerate(n_parts):
             copies += load_parts(
-                w_refs[at : at + n], ids_ref[2], inner // 2, w_ref.at[b], 0, sems, at
+                w_refs[at : at + n], bases_of(parts[b]), ids_ref[2], inner // 2, w_ref.at[b], sems, at
             )
             at += n
         for copy in copies:
             copy.start()
         for r in range(here):
             for kk in range(count):
-                x_ref[r * full + kk * quarter : r * full + (kk + 1) * quarter, :] = piece_refs[kk][
-                    r * quarter : (r + 1) * quarter, :
+                ref, base = places[kk]
+                x_ref[r * full + kk * quarter : r * full + (kk + 1) * quarter, :] = ref[
+                    base + r * quarter : base + (r + 1) * quarter, :
                 ]
         if keep_x:
             x_out[...] = x_ref[...]
@@ -494,7 +592,8 @@
         for copy in copies:
             copy.wait()
         for b in range(2):
-            bias = bias_rows(piece_refs[pair[b]], tile, 0)
+            ref, base = places[pair[b]]
+            bias = bias_rows(ref, base + tile, 0)
             bias_q, bias_v = bias[:, 0:head_width], bias[:, 256 : 256 + head_width]
 
             @pl.loop(0, here)
@@ -540,6 +639,7 @@
         ],
         us=10,
         name="attend",
+        room=18,
         after=after,
     )(ids, segr, *pieces, *flat)
 
@@ -563,70 +663,174 @@
     return centre * inverse, inverse
 
 
-def ffn(ids, sent, segr, x, ols, pieces, vecs, ogs, pool_grad, out_in_parts, down_parts, dims):
+def ffn_near(ids, x, ols, pieces, vecs, out_parts, near_in, near_down, inner, dims, after=()):
     devices, count, rows, quarter, full, width = dims
-    here, cap, reach = rows // count, rows // devices, devices // count
+    here = rows // count
     tokens = here * full
     tile = here * quarter
     head_width = ols[0].shape[2]
     hidden = width
-    flat_oi = [ref for p in out_in_parts for ref in p]
-    flat_dn = [ref for p in down_parts for ref in p]
-    n_oi, n_dn = len(flat_oi), len(flat_dn)
-    half_out, half_in = head_width // 2, width // 2
-
-    def body(ids_ref, sent_ref, segr_ref, x_ref, ol_a, ol_b, *refs):
+    flat = [ref for p in out_parts for ref, _ in p]
+    n = len(flat)
+
+    def body(ids_ref, x_ref, ol_a, ol_b, *refs):
         refs = list(refs)
-        piece_refs = [refs.pop(0) for _ in range(count)]
-        vec_ref = refs.pop(0)
+        places = piece_places([refs.pop(0) for _ in range(count)], tile + 16)
+        vec_refs = [refs.pop(0) for _ in range(3)]
+        wo_refs = [refs.pop(0) for _ in range(n)]
+        wi_refs = [refs.pop(0) for _ in range(2)]
+        wd_refs = [refs.pop(0) for _ in range(2)]
+        al_out, hat_out, inv_out, acc_out, hl_out, gp_out, wo, wi, wd, sems = refs
+        first, later = [], []
+        at = 0
+        for kk in range(count):
+            m = len(out_parts[kk])
+            first += load_parts(
+                wo_refs[at : at + m], bases_of(out_parts[kk]), ids_ref[2], head_width // 2, wo.at[kk],
+                sems, at, inner // 2,
+            )
+            at += m
+        for b in range(2):
+            later.append(
+                [
+                    pltpu.make_async_copy(wi_refs[b], wi.at[b], sems.at[n + 2 * b]),
+                    pltpu.make_async_copy(wd_refs[b], wd.at[b], sems.at[n + 2 * b + 1]),
+                ]
+            )
+        for copy in first + later[0] + later[1]:
+            copy.start()
+        b_out, gain_a, bias_a = (v[...].reshape(1, width) for v in vec_refs)
+        for copy in first:
+            copy.wait()
+        for r in range(here):
+            span = slice(r * full, (r + 1) * full)
+            total = x_ref[span, :].astype(f32) + b_out
+            for kk in range(count):
+                ol = (ol_a, ol_b)[kk // 2]
+                total = total + mm(ol[kk % 2, span, :], wo[kk])
+            hat, inverse = norm_rows(total)
+            hat_out[span, :] = hat
+            inv_out[span, :] = jnp.broadcast_to(inverse, (full, 128))
+            al_out[span, :] = (hat * gain_a + bias_a).astype(bf16)
+        half = tokens // 2
+        for b in range(2):
+            for copy in later[b]:
+                copy.wait()
+            ref, base = places[b]
+            bias = bias_rows(ref, base + tile, 3)
+            for m in range(2):
+                span = slice(m * half, (m + 1) * half)
+                u = mm(al_out[span, :], wi[b]) + bias
+                active, slope = gelu_pair(u)
+                active = active.astype(bf16)
+                hl_out[b, span, :] = active
+                gp_out[b, span, :] = slope.astype(bf16)
+                part = mm(active, wd[b])
+                if b == 0:
+                    acc_out[span, :] = part
+                else:
+                    acc_out[span, :] += part
+
+    wide = (tokens, width)
+    return call(
+        body,
+        [
+            shape_of(wide), shape_of(wide, f32), shape_of((tokens, 128), f32), shape_of(wide, f32),
+            shape_of((2,) + wide), shape_of((2,) + wide),
+        ],
+        [VM] * 6,
+        [SM, VM, VM, VM] + [VM] * (count + 3) + [HB] * (n + 4),
+        [
+            pltpu.VMEM((count, head_width, width), bf16),
+            pltpu.VMEM((2, width, hidden), bf16),
+            pltpu.VMEM((2, hidden, width), bf16),
+            pltpu.SemaphoreType.DMA((n + 4,)),
+        ],
+        us=11,
+        name="ffn_near",
+        room=26,
+        after=after,
+    )(ids, x, ols[0], ols[1], *pieces, *vecs, *flat, *near_in, *near_down)
+
+
+def ffn_far(ids, al, pieces, parts, dims, after=()):
+    devices, count, rows, quarter, full, width = dims
+    here = rows // count
+    tokens = here * full
+    tile = here * quarter
+    hidden = width
+    flat = [ref for p in parts for ref, _ in p]
+    n = len(flat)
+
+    def body(ids_ref, al_ref, *refs):
+        places = piece_places(refs[:count], tile + 16)
+        w_refs = refs[count : count + n]
+        hl_out, gp_out, wi, sems = refs[count + n :]
+        copies = []
+        at = 0
+        for b in range(2):
+            m = len(parts[b])
+            copies.append(
+                load_parts(
+                    w_refs[at : at + m], bases_of(parts[b]), ids_ref[2], width // 2, wi.at[b], sems, at
+                )
+            )
+            at += m
+        for copy in copies[0] + copies[1]:
+            copy.start()
+        half = tokens // 2
+        for b in range(2):
+            for copy in copies[b]:
+                copy.wait()
+            ref, base = places[2 + b]
+            bias = bias_rows(ref, base + tile, 3)
+            for m in range(2):
+                span = slice(m * half, (m + 1) * half)
+                active, slope = gelu_pair(mm(al_ref[span, :], wi[b]) + bias)
+                hl_out[b, span, :] = active.astype(bf16)
+                gp_out[b, span, :] = slope.astype(bf16)
+
+    wide = (tokens, width)
+    return call(
+        body,
+        [shape_of((2,) + wide), shape_of((2,) + wide)],
+        [VM] * 2,
+        [SM, VM] + [VM] * count + [HB] * n,
+        [pltpu.VMEM((2, width, hidden), bf16), pltpu.SemaphoreType.DMA((n,))],
+        us=6,
+        name="ffn_far",
+        room=14,
+        after=after,
+    )(ids, al, *pieces, *flat)
+
+
+def ffn_down(ids, sent, segr, al, acc, hls, vecs, ogs, pool_grad, parts, dims):
+    devices, count, rows, quarter, full, width = dims
+    here, cap, reach = rows // count, rows // devices, devices // count
+    tokens = here * full
+    hidden = width
+    flat = [ref for p in parts for ref, _ in p]
+    n = len(flat)
+
+    def body(ids_ref, sent_ref, segr_ref, al_ref, near_ref, hl_near, hl_far, *refs):
+        refs = list(refs)
+        vec_refs = [refs.pop(0) for _ in range(3)]
         og_refs = [refs.pop(0) for _ in range(reach)]
         pool_ref = refs.pop(0)
-        oi_refs = [refs.pop(0) for _ in range(n_oi)]
-        dn_refs = [refs.pop(0) for _ in range(n_dn)]
-        (
-            al_out, hat_out, inv_out, hl_out, gp_out, tk0, tk1, pooled_out, dz_out, low_out,
-            sums_out, down_out,
-            wo, wi, wd, og_buf, acc, hl, gp, sems, out_sems,
-        ) = refs
-        mi, parity = ids_ref[1], ids_ref[2]
-        first, later, last = [], [], []
+        w_refs = [refs.pop(0) for _ in range(n)]
+        tk0, tk1, pooled_out, dz_out, low_out, sums_out, down_out, wd, near, og_buf, acc_ref, sems = refs
+        mi, parity = ids_ref[1], parity_of(ids_ref, 2)
+        groups = []
         at = 0
-        for kk in range(count):
-            own = out_in_parts[kk]
-            if len(own) == 2 and own[0].shape[0] == 2 * half_out:
-                first.append(
-                    pltpu.make_async_copy(oi_refs[at], wo.at[kk], sems.at[2 * at])
+        for b in range(2):
+            m = len(parts[b])
+            groups.append(
+                load_parts(
+                    w_refs[at : at + m], bases_of(parts[b]), parity, width // 2, wd.at[b], sems, at
                 )
-                later.append(
-                    pltpu.make_async_copy(oi_refs[at + 1], wi.at[kk], sems.at[2 * at + 2])
-                )
-            else:
-                for j in range(2):
-                    place = parity if j == 0 else 1 - parity
-                    src = oi_refs[at + j]
-                    first.append(
-                        pltpu.make_async_copy(
-                            src.at[pl.ds(0, half_out)],
-                            wo.at[kk, pl.ds(pl.multiple_of(place * half_out, 16), half_out)],
-                            sems.at[2 * (at + j)],
-                        )
-                    )
-                    later.append(
-                        pltpu.make_async_copy(
-                            src.at[pl.ds(half_out, half_in)],
-                            wi.at[kk, pl.ds(pl.multiple_of(place * half_in, 16), half_in)],
-                            sems.at[2 * (at + j) + 1],
-                        )
-                    )
-            at += 2
-        base = 2 * n_oi
-        at = 0
-        for kk in range(count):
-            n = len(down_parts[kk])
-            last += load_parts(dn_refs[at : at + n], parity, width // 2, wd.at[kk], 0, sems, base + at)
-            at += n
-        base += n_dn
-        pool_at = base
+            )
+            at += m
+        sibling_hl = pltpu.make_async_copy(hl_near.at[1], near, sems.at[n])
         cots = []
         for k in range(reach):
             for c in range(cap):
@@ -636,58 +840,35 @@
                         pltpu.make_async_copy(
                             og_refs[k].at[c, pl.ds(pl.multiple_of((mi ^ kk) * quarter, quarter), quarter)],
                             og_buf.at[pl.ds(r * full + kk * quarter, quarter)],
-                            sems.at[pool_at + r * count + kk],
+                            sems.at[n + 1 + r * count + kk],
                         )
                     )
-        for copy in first + later + last + cots:
+        for copy in groups[0] + groups[1] + cots + [sibling_hl]:
             copy.start()
-        b_out, gain_a, bias_a = vec_ref[0:1], vec_ref[1:2], vec_ref[2:3]
-        b_down, gain_f, bias_f = vec_ref[3:4], vec_ref[4:5], vec_ref[5:6]
-        for copy in first:
-            copy.wait()
-
-        @pl.loop(0, here)
-        def _(r):
-            span = pl.ds(pl.multiple_of(r * full, full), full)
-            total = x_ref[span, :].astype(f32) + b_out
-            for kk in range(count):
-                ol = (ol_a, ol_b)[kk // 2]
-                total = total + mm(ol[kk % 2, span, :], wo[kk])
-            hat, inverse = norm_rows(total)
-            hat_out[span, :] = hat
-            inv_out[span, :] = jnp.broadcast_to(inverse, (full, 128))
-            al_out[span, :] = (hat * gain_a + bias_a).astype(bf16)
-
-        for copy in later + last:
-            copy.wait()
+        b_down, gain_f, bias_f = (v[...].reshape(1, width) for v in vec_refs)
         half = tokens // 2
-        outs = []
-        for kk in range(count):
-            bias = bias_rows(piece_refs[kk], tile, 3)
+        for b in range(2):
+            for copy in groups[b]:
+                copy.wait()
             for m in range(2):
                 span = slice(m * half, (m + 1) * half)
-                u = mm(al_out[span, :], wi[kk]) + bias
-                active, slope = gelu_pair(u)
-                active = active.astype(bf16)
-                hl[kk, span, :] = active
-                gp[kk, span, :] = slope.astype(bf16)
-                part = mm(active, wd[kk])
-                if kk == 0:
-                    acc[span, :] = part
+                part = mm(hl_far[b, span, :], wd[b])
+                if b == 0:
+                    acc_ref[span, :] = part + near_ref[span, :]
                 else:
-                    acc[span, :] += part
-            for j, (src, dst) in enumerate(((hl, hl_out), (gp, gp_out))):
-                copy = pltpu.make_async_copy(src.at[kk], dst.at[kk], out_sems.at[2 * kk + j])
-                copy.start()
-                outs.append(copy)
+                    acc_ref[span, :] += part
         for copy in cots:
             copy.wait()
         sums_out[...] = jnp.zeros_like(sums_out)
         for r in range(here):
             span = slice(r * full, (r + 1) * full)
-            hat, inverse = norm_rows(al_out[span, :].astype(f32) + acc[span, :] + b_down)
+            hat, inverse = norm_rows(al_ref[span, :].astype(f32) + acc_ref[span, :] + b_down)
             final = hat * gain_f + bias_f
-            (tk0, tk1)[r // cap][r % cap] = final.astype(bf16)
+            final_low = final.astype(bf16)
+            for kk in range(count):
+                (tk0, tk1)[r // cap][
+                    kk, (r % cap) * quarter : (r % cap + 1) * quarter, :
+                ] = final_low[kk * quarter : (kk + 1) * quarter, :]
             line = jnp.broadcast_to(segr_ref[r : r + 1, :].astype(f32), (full, full)).T[:, 0:1]
             cot = og_buf[span, :].astype(f32)
             row = sent_ref[r]
@@ -708,58 +889,60 @@
             sums_out[0:1, :] += jnp.sum(dz, axis=0, keepdims=True)
             sums_out[1:2, :] += jnp.sum(cot * hat, axis=0, keepdims=True)
             sums_out[2:3, :] += jnp.sum(cot, axis=0, keepdims=True)
-        for b, kk in enumerate((1, 3)):
-            for c in range(3):
+        sibling_hl.wait()
+        for b in range(2):
+            for c in range(hidden // 256):
                 cols = slice(c * 256, (c + 1) * 256)
-                down_out[b, cols, :] = mm_tn(hl[kk, :, cols], low_out[...]).astype(bf16)
-        for copy in outs:
-            copy.wait()
+                left = near[:, cols] if b == 0 else hl_far[1, :, cols]
+                down_out[b, cols, :] = mm_tn(left, low_out[...]).astype(bf16)
 
     wide = (tokens, width)
     return call(
         body,
         [
-            shape_of(wide), shape_of(wide, f32), shape_of((tokens, 128), f32),
-            shape_of((count,) + wide), shape_of((count,) + wide),
-            shape_of((cap, full, width)), shape_of((cap, full, width)),
+            shape_of((count, cap * quarter, width)), shape_of((count, cap * quarter, width)),
             shape_of((here * SEGS, width), f32), shape_of(wide, f32), shape_of(wide),
             shape_of((8, width), f32), shape_of((2, hidden, width)),
         ],
-        [VM, VM, VM, HB, HB] + [VM] * 7,
-        [SM, SM, VM, VM, VM, VM] + [VM] * count + [VM] + [HB] * reach + [VM] + [HB] * (n_oi + n_dn),
+        [VM] * 7,
+        [SM, SM, VM, VM, VM, HB, VM] + [VM] * 3 + [HB] * reach + [VM] + [HB] * n,
         [
-            pltpu.VMEM((count, head_width, width), bf16),
-            pltpu.VMEM((count, width, hidden), bf16),
-            pltpu.VMEM((count, hidden, width), bf16),
+            pltpu.VMEM((2, hidden, width), bf16),
+            pltpu.VMEM(wide, bf16),
             pltpu.VMEM(wide, bf16),
             pltpu.VMEM(wide, f32),
-            pltpu.VMEM((count,) + wide, bf16),
-            pltpu.VMEM((count,) + wide, bf16),
-            pltpu.SemaphoreType.DMA((2 * n_oi + n_dn + here * count,)),
-            pltpu.SemaphoreType.DMA((2 * count,)),
+            pltpu.SemaphoreType.DMA((n + 1 + here * count,)),
         ],
-        us=20,
-        name="ffn",
-    )(ids, sent, segr, x, ols[0], ols[1], *pieces, vecs, *ogs, pool_grad, *flat_oi, *flat_dn)
-
-
-def ffn_back(ids, low, gp, al, down_parts, dims):
+        us=9,
+        name="ffn_down",
+        room=26,
+    )(ids, sent, segr, al, acc, *hls, *vecs, *ogs, pool_grad, *flat)
+
+
+def ffn_back(ids, low, gps, parts, dims):
     devices, count, rows, quarter, full, width = dims
     tokens = low.shape[0]
     hidden = width
-    flat = [ref for p in down_parts for ref in p]
+    flat = [ref for p in parts for ref, _ in p]
     n = len(flat)
 
-    def body(ids_ref, low_ref, gp_ref, al_ref, *refs):
+    def body(ids_ref, low_ref, gp_near, gp_far, *refs):
         dn_refs = refs[:n]
-        du_out, in_out, bin_out, wd, gpb, du, sems, out_sems = refs[n:]
+        du_out, bin_out, wd, gpb, du, sems, out_sems = refs[n:]
+        parity = parity_of(ids_ref, 2)
         copies = []
         at = 0
         for kk in range(count):
-            m = len(down_parts[kk])
+            m = len(parts[kk])
             copies.append(
-                load_parts(dn_refs[at : at + m], ids_ref[2], width // 2, wd.at[kk], 0, sems, at)
-                + [pltpu.make_async_copy(gp_ref.at[kk], gpb.at[kk], sems.at[n + kk])]
+                load_parts(
+                    dn_refs[at : at + m], bases_of(parts[kk]), parity, width // 2, wd.at[kk], sems, at
+                )
+                + [
+                    pltpu.make_async_copy(
+                        (gp_near, gp_far)[kk // 2].at[kk % 2], gpb.at[kk], sems.at[n + kk]
+                    )
+                ]
             )
             at += m
         outs = []
@@ -781,22 +964,14 @@
             copy = pltpu.make_async_copy(du.at[kk], du_out.at[kk], out_sems.at[kk])
             copy.start()
             outs.append(copy)
-        for b, kk in enumerate((1, 3)):
-            for c in range(3):
-                cols = slice(c * 256, (c + 1) * 256)
-                in_out[b, cols, :] = mm_tn(al_ref[:, cols], du[kk]).astype(bf16)
         for copy in outs:
             copy.wait()
 
     return call(
         body,
-        [
-            shape_of((count, tokens, hidden)),
-            shape_of((2, width, hidden)),
-            shape_of((count, hidden), f32),
-        ],
-        [HB, VM, VM],
-        [SM, VM, HB, VM] + [HB] * n,
+        [shape_of((count, tokens, hidden)), shape_of((count, hidden), f32)],
+        [HB, VM],
+        [SM, VM, HB, HB] + [HB] * n,
         [
             pltpu.VMEM((count, hidden, width), bf16),
             pltpu.VMEM((count, tokens, hidden), bf16),
@@ -804,42 +979,33 @@
             pltpu.SemaphoreType.DMA((n + count,)),
             pltpu.SemaphoreType.DMA((count,)),
         ],
-        us=9,
+        us=5,
         name="ffn_back",
-    )(ids, low, gp, al, *flat)
-
-
-def norm_back_attn(ids, du, al, dz, hat, inv, vecs, out_in_parts, dims, half_out, after=()):
+        room=22,
+    )(ids, low, *gps, *flat)
+
+
+def norm_back_attn(ids, du, al, dz, hat, inv, gain, parts, dims, after=()):
     devices, count, rows, quarter, full, width = dims
     tokens = al.shape[0]
     hidden = width
-    flat = [ref for p in out_in_parts for ref in p]
+    flat = [ref for p in parts for ref, _ in p]
     n = len(flat)
-    half_in = width // 2
-
-    def body(ids_ref, du_ref, dz_ref, hat_ref, inv_ref, vec_ref, *refs):
+
+    def body(ids_ref, du_ref, al_ref, dz_ref, hat_ref, inv_ref, vec_ref, *refs):
         oi_refs = refs[:n]
-        dz1_out, low_out, sums_out, wi, dub, acc, sems = refs[n:]
-        parity = ids_ref[2]
+        dz1_out, low_out, sums_out, in_out, wi, dub, acc, sems = refs[n:]
         copies = []
         at = 0
         for kk in range(count):
-            own = out_in_parts[kk]
-            group = [pltpu.make_async_copy(du_ref.at[kk], dub.at[kk], sems.at[2 * n + kk])]
-            if len(own) == 1:
-                group.append(pltpu.make_async_copy(oi_refs[at], wi.at[kk], sems.at[2 * at]))
-            else:
-                for j in range(2):
-                    place = parity if j == 0 else 1 - parity
-                    group.append(
-                        pltpu.make_async_copy(
-                            oi_refs[at + j].at[pl.ds(half_out, half_in)],
-                            wi.at[kk, pl.ds(pl.multiple_of(place * half_in, 16), half_in)],
-                            sems.at[2 * (at + j)],
-                        )
-                    )
-            at += len(own)
-            copies.append(group)
+            m = len(parts[kk])
+            copies.append(
+                [pltpu.make_async_copy(du_ref.at[kk], dub.at[kk], sems.at[n + kk])]
+                + load_parts(
+                    oi_refs[at : at + m], bases_of(parts[kk]), ids_ref[2], width // 2, wi.at[kk], sems, at
+                )
+            )
+            at += m
         for group in copies:
             for copy in group:
                 copy.start()
@@ -854,7 +1020,7 @@
                     acc[span, :] = part + dz_ref[span, :]
                 else:
                     acc[span, :] += part
-        gain_a = vec_ref[1:2]
+        gain_a = vec_ref[...].reshape(1, width)
         sums_out[...] = jnp.zeros_like(sums_out)
 
         @pl.loop(0, tokens // full)
@@ -872,22 +1038,31 @@
             sums_out[1:2, :] += jnp.sum(da * hat_r, axis=0, keepdims=True)
             sums_out[2:3, :] += jnp.sum(da, axis=0, keepdims=True)
 
+        for b, kk in enumerate((1, 3)):
+            for c in range(width // 256):
+                cols = slice(c * 256, (c + 1) * 256)
+                in_out[b, cols, :] = mm_tn(al_ref[:, cols], dub[kk]).astype(bf16)
+
     wide = (tokens, width)
     return call(
         body,
-        [shape_of(wide, f32), shape_of(wide), shape_of((8, width), f32)],
-        [VM] * 3,
-        [SM, HB, VM, VM, VM, VM] + [HB] * n,
+        [
+            shape_of(wide, f32), shape_of(wide), shape_of((8, width), f32),
+            shape_of((2, width, hidden)),
+        ],
+        [VM] * 4,
+        [SM, HB, VM, VM, VM, VM, VM] + [HB] * n,
         [
             pltpu.VMEM((count, width, hidden), bf16),
             pltpu.VMEM((count, tokens, hidden), bf16),
             pltpu.VMEM(wide, f32),
-            pltpu.SemaphoreType.DMA((2 * n + count,)),
+            pltpu.SemaphoreType.DMA((n + count,)),
         ],
         us=8,
         name="norm_back",
+        room=26,
         after=after,
-    )(ids, du, dz, hat, inv, vecs, *flat)
+    )(ids, du, al, dz, hat, inv, gain, *flat)
 
 
 def attend_back(ids, low, x, blocks, extras, dims, after=()):
@@ -896,7 +1071,7 @@
     tokens = x.shape[0]
     head_width = blocks[0][2].shape[2]
     inner = 3 * head_width
-    flat = [ref for b in blocks for ref in b[5]]
+    flat = [ref for b in blocks for ref, _ in b[5]]
     n = len(flat)
     half_out = head_width // 2
     nb = len(blocks)
@@ -905,24 +1080,15 @@
         data = refs[: 3 * nb]
         w_refs = refs[3 * nb : 3 * nb + n]
         mix_out, grad_out, wo, sums, sems = refs[3 * nb + n :]
-        parity = ids_ref[2]
         copies = []
         at = 0
         for b in range(nb):
-            own = blocks[b][5]
-            if len(own) == 1:
-                copies.append(pltpu.make_async_copy(w_refs[at], wo.at[b], sems.at[at]))
-            else:
-                for j in range(2):
-                    place = parity if j == 0 else 1 - parity
-                    copies.append(
-                        pltpu.make_async_copy(
-                            w_refs[at + j].at[pl.ds(0, half_out)],
-                            wo.at[b, pl.ds(pl.multiple_of(place * half_out, 16), half_out)],
-                            sems.at[at + j],
-                        )
-                    )
-            at += len(own)
+            m = len(blocks[b][5])
+            copies += load_parts(
+                w_refs[at : at + m], bases_of(blocks[b][5]), ids_ref[2], half_out, wo.at[b], sems, at,
+                inner // 2,
+            )
+            at += m
         for copy in copies:
             copy.start()
         for copy in copies:
@@ -975,6 +1141,7 @@
         ],
         us=13,
         name="attend_back",
+        room=26,
         after=after,
     )(ids, low, x, *extras, *[v for b in blocks for v in b[2:5]], *flat)
 
@@ -988,13 +1155,13 @@
     return lines[0:8].astype(f32) + lines[8:16].astype(f32)
 
 
-def peer_grad(lhs, rhs, got, after=()):
+def peer_grad(lhs, rhs, got, at, after=()):
     tokens, width = rhs.shape
     hidden = lhs.shape[-1]
 
     def body(lhs_ref, rhs_ref, got_ref, out, a_buf, g_buf, sems):
         copies = [
-            pltpu.make_async_copy(lhs_ref.at[2], a_buf, sems.at[0]),
+            pltpu.make_async_copy(lhs_ref.at[at], a_buf, sems.at[0]),
             pltpu.make_async_copy(got_ref.at[1], g_buf, sems.at[1]),
         ]
         for copy in copies:
@@ -1019,6 +1186,7 @@
         ],
         us=3,
         name="peer_grad",
+        room=10,
         after=after,
     )(lhs, rhs, got)
 
@@ -1074,6 +1242,7 @@
         ],
         us=3,
         name="own_grad",
+        room=14,
         after=after,
     )(ids, lhs, rhs, got, crossed)
 
@@ -1109,6 +1278,7 @@
         ],
         us=3,
         name="peer_grad_in",
+        room=10,
         after=after,
     )(al, du, got)
 
@@ -1125,7 +1295,9 @@
         )
 
     return call(
-        body, shape_of((high, width)), VM, [VM, VM], us=2, name="peer_last", after=after
+        body, shape_of((high, width)), VM, [VM, VM], us=2, name="peer_last",
+        room=12,
+        after=after,
     )(grads, got)
 
 
@@ -1162,77 +1334,86 @@
         [pltpu.VMEM((body_rows, width), f32)],
         us=3,
         name="own_last",
+        room=16,
         after=after,
     )(ids, grads, got, crossed)
 
 
-def halve(keep, got, vec=None):
+def cut(keep, got, vec, after=()):
     high, width = keep.shape
     last = vec is not None
     tail = 16 if last else 0
-    return_send = True
+    size = high // 4
 
     def body(*refs):
         keep_ref, got_ref = refs[:2]
         rest = refs[2:]
         if last:
             vec_ref, rest = rest[0], rest[1:]
-        send, kept = rest[:2]
-        half = high // 2
-        kept[...] = keep_ref[0:half, :] + got_ref[0:half, :].astype(f32)
-        send[0:half, :] = (keep_ref[half:, :] + got_ref[half:high, :].astype(f32)).astype(bf16)
-        if last:
             lines = vec_ref[...] + one_term(got_ref[high:, :])
-            send[half:, :] = two_terms(lines)
-            rest[2][...] = lines
-
-    outs = [shape_of((high // 2 + tail, width)), shape_of((high // 2, width), f32)]
+            rest[4][...] = lines
+        for p in range(4):
+            span = slice(p * size, (p + 1) * size)
+            total = keep_ref[span, :] + got_ref[span, :].astype(f32)
+            if p == 0:
+                rest[3][...] = total
+            else:
+                rest[p - 1][0:size, :] = total.astype(bf16)
+                if last:
+                    rest[p - 1][size:, :] = two_terms(lines)
+
+    outs = [shape_of((size + tail, width))] * 3 + [shape_of((size, width), f32)]
     args = [keep, got]
     if last:
         outs.append(shape_of((8, width), f32))
         args.append(vec)
     return call(
-        body, outs, [VM] * len(outs), [VM] * len(args), us=1, name="halve"
+        body, outs, [VM] * len(outs), [VM] * len(args), us=1, name="cut", room=8, after=after
     )(*args)
 
 
-def end_halving(keep, got, vec=None):
+def gather_sum(keep, gots, vec, after=()):
     high, width = keep.shape
     last = vec is not None
+    n = len(gots)
 
     def body(*refs):
-        keep_ref, got_ref = refs[:2]
-        rest = refs[2:]
+        keep_ref, got_refs, rest = refs[0], refs[1 : 1 + n], refs[1 + n :]
         if last:
             vec_ref, rest = rest[0], rest[1:]
-        rest[0][...] = (keep_ref[...] + got_ref[0:high, :].astype(f32)).astype(bf16)
-        if last:
-            rest[1][...] = vec_ref[...] + one_term(got_ref[high:, :])
+            lines = vec_ref[...]
+            for got in got_refs:
+                lines = lines + one_term(got[high:, :])
+            rest[1][...] = lines
+        total = keep_ref[...]
+        for got in got_refs:
+            total = total + got[0:high, :].astype(f32)
+        rest[0][...] = total.astype(bf16)
 
     outs = [shape_of((high, width))]
-    args = [keep, got]
+    args = [keep, *gots]
     if last:
         outs.append(shape_of((8, width), f32))
         args.append(vec)
     return call(
-        body, outs, [VM] * len(outs), [VM] * len(args), us=1, name="end_halving"
+        body, outs, [VM] * len(outs), [VM] * len(args), us=1, name="gather_sum", room=8, after=after
     )(*args)
 
 
-def reduce_dp(send, keep, vec, devices):
-    bits = devices.bit_length() - 1
-    for j in range(bits - 1):
-        got = swap(send, "dp", 1 << j)
-        out = halve(keep, got, vec)
-        send, keep = out[:2]
-        vec = out[2] if vec is not None else None
-    got = swap(send, "dp", 1 << (bits - 1))
-    out = end_halving(keep, got, vec)
-    pieces = [out[0]]
-    for j in reversed(range(bits)):
-        whole = pieces[0] if len(pieces) == 1 else jnp.concatenate(pieces, axis=0)
-        pieces.append(swap(whole, "dp", 1 << j))
-    return pieces, (out[1] if vec is not None else None)
+def join(pieces, after=()):
+    size, width = pieces[0].shape
+    n = len(pieces)
+
+    def body(*refs):
+        for p in range(n):
+            refs[n][p * size : (p + 1) * size, :] = refs[p][...]
+
+    return call(
+        body, shape_of((n * size, width)), VM, [VM] * n, us=1, name="join", room=4, after=after
+    )(*pieces)
+
+
+MASKS = (4, 2, 6)
 
 
 def place_shards(ids_ref, pieces, devices, size, put):
@@ -1246,25 +1427,34 @@
             p += 1
 
 
-def whole_grad(ids, pieces, devices):
+def whole_grad(ids, pieces, devices, cuts, after=()):
     size, width = pieces[0].shape
     n = len(pieces)
 
     def body(ids_ref, *refs):
-        out = refs[n]
+        outs = refs[n : n + len(cuts)]
+        acc = refs[n + len(cuts)] if len(cuts) > 1 else outs[0]
 
         def put(at, rows):
-            out[pl.ds(at, size), :] = rows
+            acc[pl.ds(at, size), :] = rows
 
         place_shards(ids_ref, refs[:n], devices, size, put)
-
-    return call(
-        body,
-        shape_of((size * devices, width), f32),
-        VM,
+        if len(cuts) > 1:
+            base = 0
+            for out, rows in zip(outs, cuts):
+                out[...] = acc[base : base + rows, :]
+                base += rows
+
+    return call(
+        body,
+        [shape_of((rows, width), f32) for rows in cuts],
+        [VM] * len(cuts),
         [SM] + [VM] * n,
+        [pltpu.VMEM((size * devices, width), f32)] if len(cuts) > 1 else [],
         us=2,
         name="whole_grad",
+        room=12,
+        after=after,
     )(ids, *pieces)
 
 
@@ -1274,20 +1464,20 @@
     tokens = here * full
     tile = here * quarter
     inner = mixes[0].shape[2]
-    flat = [ref for p in parts for ref in p]
+    flat = [ref for p in parts for ref, _ in p]
     n = len(flat)
     turn = (1, 3, 2, 0)
 
     def body(ids_ref, dz_ref, m_a, m_b, pool_ref, *refs):
         w_refs = refs[:n]
-        outs = refs[n : n + count]
-        wq, acc, sems = refs[n + count :]
+        own, near, far = refs[n : n + 3]
+        wq, acc, sems = refs[n + 3 :]
         copies = []
         at = 0
         for kk in range(count):
             m = len(parts[kk])
             copies.append(
-                load_parts(w_refs[at : at + m], ids_ref[2], inner // 2, wq.at[kk], 0, sems, at)
+                load_parts(w_refs[at : at + m], bases_of(parts[kk]), ids_ref[2], inner // 2, wq.at[kk], sems, at)
             )
             at += m
         for kk in turn:
@@ -1305,17 +1495,18 @@
                     acc[span, :] = part + dz_ref[span, :]
                 else:
                     acc[span, :] += part
-        for kk in range(count):
+        size = tile + here * SEGS
+        for kk, (ref, base) in enumerate(piece_places((own, near, far, far), size)):
             for r in range(here):
-                outs[kk][r * quarter : (r + 1) * quarter, :] = acc[
+                ref[base + r * quarter : base + (r + 1) * quarter, :] = acc[
                     r * full + kk * quarter : r * full + (kk + 1) * quarter, :
                 ].astype(bf16)
-            outs[kk][tile:, :] = pool_ref[...].astype(bf16)
-
-    return call(
-        body,
-        [shape_of((tile + here * SEGS, width))] * count,
-        [VM] * count,
+            ref[base + tile : base + size, :] = pool_ref[...].astype(bf16)
+
+    return call(
+        body,
+        [shape_of((m * (tile + here * SEGS), width)) for m in (1, 1, 2)],
+        [VM] * 3,
         [SM] + [VM] * 4 + [HB] * n,
         [
             pltpu.VMEM((count, inner, width), bf16),
@@ -1324,30 +1515,33 @@
         ],
         us=6,
         name="grad_input_rows",
+        room=22,
         after=after,
     )(ids, dz1, *mixes, pooled, *flat)
 
 
-def land_grad(sent, pieces, dims):
+def land_grad(sent, pieces, dims, after=()):
     devices, count, rows, quarter, full, width = dims
     here = rows // count
     tile = here * quarter
+    size = tile + here * SEGS
 
     def body(sent_ref, *refs):
-        piece_refs = refs[:count]
+        places = piece_places(refs[:count], size)
         out, pooled, sems = refs[count:]
         copies = []
-        for kk in range(count):
+        for kk, (ref, base) in enumerate(places):
             for j in range(here):
                 at = kk * here + j
                 copy = pltpu.make_async_copy(
-                    piece_refs[kk].at[pl.ds(j * quarter, quarter)], out.at[sent_ref[at]], sems.at[at]
+                    ref.at[pl.ds(base + j * quarter, quarter)], out.at[sent_ref[at]], sems.at[at]
                 )
                 copy.start()
                 copies.append(copy)
-                pooled[sent_ref[at]] = piece_refs[kk][
-                    tile : tile + here * SEGS, :
-                ].astype(f32)[j * SEGS : (j + 1) * SEGS]
+        for kk, (ref, base) in enumerate(places):
+            lines = ref[base + tile : base + size, :].astype(f32)
+            for j in range(here):
+                pooled[sent_ref[kk * here + j]] = lines[j * SEGS : (j + 1) * SEGS]
         for copy in copies:
             copy.wait()
 
@@ -1359,62 +1553,69 @@
         [pltpu.SemaphoreType.DMA((rows,))],
         us=2,
         name="land_grad",
+        room=8,
+        after=after,
     )(sent, *pieces)
 
 
-def turn_output(ids, hops, dims, after=()):
+def turn_output(hops, dims, after=()):
+    devices, count, rows, quarter, full, width = dims
+    cap, reach = rows // devices, devices // count
+    part = cap * quarter
+    tile = reach * part
+
+    def body(*refs):
+        hop_refs = refs[:reach]
+        near, far, sems = refs[reach:]
+        copies = []
+        for kk, (ref, base) in enumerate(((near, 0), (far, 0), (far, tile))):
+            for k in range(reach):
+                copies.append(
+                    pltpu.make_async_copy(
+                        hop_refs[k].at[kk + 1],
+                        ref.at[pl.ds(base + k * part, part)],
+                        sems.at[kk * reach + k],
+                    )
+                )
+        for copy in copies:
+            copy.start()
+        for copy in copies:
+            copy.wait()
+
+    return call(
+        body,
+        [shape_of((tile, width)), shape_of((2 * tile, width))],
+        [VM, VM],
+        [HB] * reach,
+        [pltpu.SemaphoreType.DMA((3 * reach,))],
+        us=2,
+        name="turn_output",
+        room=8,
+        after=after,
+    )(*hops)
+
+
+def land_output(spots, hops, pieces, dims, after=()):
     devices, count, rows, quarter, full, width = dims
     here, cap, reach = rows // count, rows // devices, devices // count
-
-    def body(ids_ref, *refs):
+    tile = here * quarter
+
+    def body(spots_ref, *refs):
         hop_refs = refs[:reach]
-        outs = refs[reach : reach + count]
-        sems = refs[reach + count]
-        handler = lax.div(ids_ref[0], reach)
-        copies = []
-        for kk in range(count):
-            block = ids_ref[1] ^ kk ^ handler
-            for k in range(reach):
-                for c in range(cap):
-                    j = k * cap + c
-                    copy = pltpu.make_async_copy(
-                        hop_refs[k].at[c, pl.ds(pl.multiple_of(block * quarter, quarter), quarter)],
-                        outs[kk].at[pl.ds(j * quarter, quarter)],
-                        sems.at[kk * here + j],
-                    )
-                    copy.start()
-                    copies.append(copy)
-        for copy in copies:
-            copy.wait()
-
-    return call(
-        body,
-        [shape_of((here * quarter, width))] * count,
-        [HB] * count,
-        [SM] + [HB] * reach,
-        [pltpu.SemaphoreType.DMA((rows,))],
-        us=2,
-        name="turn_output",
-        after=after,
-    )(ids, *hops)
-
-
-def land_output(spots, pieces, dims):
-    devices, count, rows, quarter, full, width = dims
-    here = rows // count
-
-    def body(spots_ref, *refs):
-        piece_refs = refs[:count]
-        out, sems = refs[count:]
+        places = piece_places((None,) + refs[reach : reach + count - 1], tile)
+        out, sems = refs[reach + count - 1 :]
         copies = []
         for kk in range(count):
             for j in range(here):
                 at = kk * here + j
-                copy = pltpu.make_async_copy(
-                    piece_refs[kk].at[pl.ds(j * quarter, quarter)], out.at[spots_ref[at]], sems.at[at]
-                )
-                copy.start()
-                copies.append(copy)
+                if kk == 0:
+                    src = hop_refs[j // cap].at[0, pl.ds((j % cap) * quarter, quarter)]
+                else:
+                    ref, base = places[kk]
+                    src = ref.at[pl.ds(base + j * quarter, quarter)]
+                copies.append(pltpu.make_async_copy(src, out.at[spots_ref[at]], sems.at[at]))
+        for copy in copies:
+            copy.start()
         for copy in copies:
             copy.wait()
 
@@ -1422,11 +1623,13 @@
         body,
         shape_of((rows, quarter, width)),
         HB,
-        [SM] + [HB] * count,
+        [SM] + [VM] * (reach + count - 1),
         [pltpu.SemaphoreType.DMA((rows,))],
         us=2,
         name="land_output",
-    )(spots, *pieces)
+        room=8,
+        after=after,
+    )(spots, *hops, *pieces)
 
 
 def swap(values, axis, bit):
@@ -1441,122 +1644,95 @@
     rows, quarter, width = tokens_in.shape
     full = seg.shape[1]
     dims = (devices, count, rows, quarter, full, width)
-    here, cap, reach = rows // count, rows // devices, devices // count
-    my, mi = lax.axis_index("dp"), lax.axis_index("mp")
-    parity = lax.rem(my, 2)
-    ints = jnp.int32
-    ids = jnp.stack([my, mi, parity]).astype(ints)
+    reach = devices // count
     head_width = w_qkv.shape[2]
     inner = 3 * head_width
 
-    places = jnp.arange(rows, dtype=ints)
-    routes = route.reshape(devices, rows)
-    key = routes // rows * rows + places[None]
-    rank = jnp.sum((key[:, None, :] < key[:, :, None]).astype(ints), axis=2)
-    placed = rank[:, :, None] == places[None, None, :]
-    table = jnp.sum(jnp.where(placed, routes[:, :, None], 0), axis=1)
-    own_rank = lax.dynamic_index_in_dim(rank, my, 0, keepdims=False)
-    steps = jnp.arange(reach, dtype=ints)
-    copies = jnp.arange(cap, dtype=ints)
-    blocks = jnp.arange(count, dtype=ints)
-    near = lax.rem(my // count - steps + reach, reach)
-    slots = (
-        ((mi ^ blocks)[:, None, None] * reach + near[None, :, None]) * cap + copies[None, None, :]
-    ).reshape(rows)
-    sent = jnp.sum(jnp.where(own_rank[None, :] == slots[:, None], places[None, :], 0), axis=1)
-    pair = lax.dynamic_slice_in_dim(table, my * cap, cap, 1) - my * rows
-    sources = (mi ^ blocks)[:, None] + count * lax.rem(my + steps, reach)[None, :]
-    spots = jnp.sum(
-        jnp.where(
-            sources[:, :, None, None] == jnp.arange(devices, dtype=ints)[None, None, :, None],
-            pair[None, None],
-            0,
-        ),
-        axis=2,
-    ).reshape(rows)
-    asked = spots[: reach * cap]
-    mine = my * rows + sent[:here]
-    lines = jnp.sum(
-        jnp.where(
-            mine[:, None, None] == jnp.arange(devices * rows, dtype=ints)[None, :, None], seg[None], 0
-        ),
-        axis=1,
-    ).reshape(here, count, quarter)
-    lines = jnp.sum(
-        jnp.where((mi ^ blocks)[:, None, None, None] == blocks[None, None, :, None], lines[None], 0),
-        axis=2,
-    )
-    segr = jnp.pad(lines.transpose(1, 0, 2).reshape(here, full), ((0, 8 - here), (0, 0)))
-
-    def to_place(k):
-        return [
-            (s * count + f, (reach * f + (s // count - k) % reach) * count + s % count)
-            for s in range(devices)
-            for f in range(count)
-        ]
-
-    def from_place(k):
-        return [(b, a) for a, b in to_place(k)]
-
-    sends = prep_rows(sent, tokens_in, b_qv, b_in, dims)
-    pieces = [sends[0]] + [swap(sends[k], "mp", k) for k in range(1, count)]
+    def hop(values, k):
+        return lax.ppermute(
+            values,
+            ("dp", "mp"),
+            [
+                (s * count + f, (s ^ (f + count * k)) * count + f)
+                for s in range(devices)
+                for f in range(count)
+            ],
+        )
+
     wq = w_qkv.transpose(1, 2, 0).reshape(inner, width)
-    half_q, half_oi, half_dn = prep_halves(ids, wq, w_out, w_in, w_down, (sends[0],))
-
-    def cross(half, after=None):
-        direct = swap(half, "mp", 2)
-        if after is not None:
-            direct, _ = lax.optimization_barrier((direct, after))
-        return direct, swap(direct, "dp", 1)
+    half_rows = (inner + head_width) // 2
+    *sends, segr, sent, spots, ids = prep_rows(
+        route, seg, tokens_in, b_qv, b_in, (wq, w_out), dims
+    )
+    pieces = exchange(*sends)
 
     def sibling(values):
         return tuple(swap(v, "mp", 1) for v in values)
 
-    far_q = cross(half_q)
-    q_parts = [(wq,), sibling((wq,)), far_q, sibling(far_q)]
-    vecs = jnp.stack(
-        [b_out, gain_attn, bias_attn, b_down, gain_ffn, bias_ffn, gain_ffn, bias_ffn]
-    )
+    def later(values, after):
+        return lax.optimization_barrier((values, after))[0]
+
+    def crossed(half, bit, first, second):
+        direct = later(swap(half, "mp", 2), first)
+        relayed = swap(direct, "dp", bit)
+        far = (direct, relayed)
+        return [
+            [(v, 0) for v in far],
+            [(swap(direct, "mp", 1), 0), (swap(later(relayed, second), "mp", 1), 0)],
+        ]
+
+    below = sends[2].shape[0] - half_rows
+    relay_q = swap(pieces[2][below:], "dp", 1)
+    near_q, near_o = sibling((wq, w_out))
+    near_i, near_d = sibling((w_in, w_down))
+    half_in = prep_halves((w_in,), 1, (pieces[2],))
     x, ol_a, qkv_a, p_a = attend(
-        ids, segr, pieces, q_parts[:2], (0, 1), dims, True, (far_q[0],)
-    )
-    far_oi = cross(half_oi, ol_a)
-    oi_parts = [(w_out, w_in), sibling((w_out, w_in)), far_oi, sibling(far_oi)]
-    far_dn = cross(half_dn)
-    dn_parts = [(w_down,), sibling((w_down,)), far_dn, sibling(far_dn)]
-    in_parts = [p[1:] if k < 2 else p for k, p in enumerate(oi_parts)]
-    wo_parts = [p[:1] if k < 2 else p for k, p in enumerate(oi_parts)]
-
-    og_sends = prep_cot(asked, out_grad, dims, (ol_a,))
-    ogs = [lax.ppermute(og_sends[k], ("dp", "mp"), from_place(k)) for k in range(reach)]
+        ids, segr, pieces, [[(wq, 0)], [(near_q, 0)]], (0, 1), inner, dims, True,
+        (near_o, near_i, near_d, half_in),
+    )
+    relay_q3 = swap(later(relay_q, x), "mp", 1)
+    far_q = [(pieces[2], below), (relay_q, 0)]
+    far_q3 = [(pieces[3], below), (relay_q3, 0)]
+    half_dn = prep_halves((w_down,), 2, (x,))
+    og_sends = prep_cot(spots, out_grad, dims, (half_dn,))
+    ogs = [hop(og_sends[k], k) for k in range(reach)]
     ol_b, qkv_b, p_b = attend(
-        ids, segr, pieces, q_parts[2:], (2, 3), dims, False, (og_sends[0],)
-    )
-    (
-        al, hat, inv, hl, gp, tk0, tk1, pooled, dz, low, ffn_sums, down_pair,
-    ) = ffn(
-        ids, sent, segr, x, (ol_a, ol_b), pieces, vecs, ogs, pool_grad, oi_parts, dn_parts, dims
+        ids, segr, pieces, [far_q, far_q3], (2, 3), inner, dims, False, (og_sends[0],)
+    )
+    q_parts = [[(wq, 0)], [(near_q, 0)], far_q, far_q3]
+    wo_parts = [[(w_out, 0)], [(near_o, 0)], far_q, far_q3]
+    al, hat, inv, acc, hl, gp = ffn_near(
+        ids, x, (ol_a, ol_b), pieces, (b_out, gain_attn, bias_attn), wo_parts, (w_in, near_i),
+        (w_down, near_d), inner, dims,
+    )
+    in_parts = [[(w_in, 0)], [(near_i, 0)], *crossed(half_in, 1, x, ol_b)]
+    dn_parts = [[(w_down, 0)], [(near_d, 0)], *crossed(half_dn, 2, ol_b, al)]
+    hl_far, gp_far = ffn_far(ids, al, pieces, in_parts[2:], dims)
+    tk0, tk1, pooled, dz, low, ffn_sums, down_pair = ffn_down(
+        ids, sent, segr, al, acc, (hl, hl_far), (b_down, gain_ffn, bias_ffn), ogs, pool_grad,
+        dn_parts[2:], dims,
     )
     got_down = swap(down_pair, "mp", 1)
-    hops = [lax.ppermute(t, ("dp", "mp"), to_place(k)) for k, t in enumerate((tk0, tk1))]
-    du, in_pair, bin_sums = ffn_back(ids, low, gp, al, dn_parts, dims)
+    du, bin_sums = ffn_back(ids, low, (gp, gp_far), dn_parts, dims)
+    down_far = peer_grad(hl_far, low, got_down, 0, (bin_sums,))
+    hops = [hop(t, k) for k, t in enumerate(lax.optimization_barrier((tk0, tk1, down_far))[:2])]
+    crossed_down = swap(down_far, "mp", 2)
+    dz1, low1, norm_sums, in_pair = norm_back_attn(
+        ids, du, al, dz, hat, inv, gain_attn, in_parts, dims, (down_far,)
+    )
     got_in = swap(in_pair, "mp", 1)
-    down_far = peer_grad(hl, low, got_down, (bin_sums,))
-    crossed_down = swap(down_far, "mp", 2)
-    dz1, low1, norm_sums = norm_back_attn(
-        ids, du, al, dz, hat, inv, vecs, in_parts, dims, head_width // 2, (down_far,)
-    )
-    in_far = peer_grad_in(al, du, got_in, (norm_sums,))
-    crossed_in = swap(in_far, "mp", 2)
     extras = (bin_sums, ffn_sums, norm_sums)
     mix_a, grads_a = attend_back(
         ids, low1, x,
         [(1, 1, ol_a, qkv_a, p_a, wo_parts[1]), (3, 1, ol_b, qkv_b, p_b, wo_parts[3])],
-        extras, dims, (in_far,),
+        extras, dims,
     )
     got_last = swap(grads_a, "mp", 1)
+    in_far = peer_grad_in(al, du, got_in, (grads_a,))
+    crossed_in = swap(in_far, "mp", 2)
+    turned = turn_output(hops, dims, (in_far,))
     send_down, keep_down = own_grad(
-        ids, hl, low, got_down, crossed_down, devices, True, (grads_a,)
+        ids, hl, low, got_down, crossed_down, devices, True, (turned[0],)
     )
     mix_b, grads_b = attend_back(
         ids, low1, x,
@@ -1565,26 +1741,49 @@
     )
     last_far = peer_last(grads_b, got_last, 0)
     crossed_last = swap(last_far, "mp", 2)
-    gx = grad_input_rows(ids, dz1, (mix_a, mix_b), q_parts, pooled, dims, (last_far,))
-    gx_got = [gx[0]] + [swap(gx[k], "mp", k) for k in range(1, count)]
-    grad_input, pooled_out = land_grad(sent, gx_got, dims)
-
-    turned = turn_output(ids, hops, dims, (gx[0],))
-    landed = [turned[0]] + [swap(turned[k], "mp", k) for k in range(1, count)]
-    tokens_out = land_output(spots, landed, dims)
-
-    down_shards, _ = reduce_dp(send_down, keep_down, None, devices)
-    g_down = whole_grad(ids, down_shards, devices)
-    send, keep = own_grad(ids, al, du, got_in, crossed_in, devices, False, (gx[0],))
-    in_shards, _ = reduce_dp(send, keep, None, devices)
-    g_in = whole_grad(ids, in_shards, devices)
-    send, keep, vec = own_last(ids, grads_b, got_last, crossed_last, 1, devices)
-    last_shards, vec = reduce_dp(send, keep, vec, devices)
-    g_last = whole_grad(ids, last_shards, devices)
-    g_qkv = g_last[:inner].reshape(3, head_width, width).transpose(2, 0, 1)
+
+    def places_of(parts):
+        return [swap(part, "dp", mask) for part, mask in zip(parts, MASKS)]
+
+    cut_down = cut(keep_down, swap(send_down, "dp", 1), None, (last_far,))
+    down_places = places_of(cut_down[:3])
+    gx = grad_input_rows(ids, dz1, (mix_a, mix_b), q_parts, pooled, dims, (cut_down[0],))
+    (shard_down,) = gather_sum(cut_down[3], down_places, None, (gx[0],))
+    down_spread = [shard_down] + places_of([shard_down] * 3)
+    send_in, keep_in = own_grad(
+        ids, al, du, got_in, crossed_in, devices, False, (shard_down,)
+    )
+    in_half = swap(send_in, "dp", 1)
+    half_down = join(down_spread, (send_in,))
+    down_spread.append(swap(half_down, "dp", 1))
+    cut_in = cut(keep_in, in_half, None, (half_down,))
+    in_places = places_of(cut_in[:3])
+    send, keep, vec = own_last(
+        ids, grads_b, got_last, crossed_last, 1, devices, (cut_in[0],)
+    )
+    last_half = swap(send, "dp", 1)
+    (shard_in,) = gather_sum(cut_in[3], in_places, None, (send,))
+    in_spread = [shard_in] + places_of([shard_in] * 3)
+    cut_last = cut(keep, last_half, vec, (shard_in,))
+    last_places = places_of(cut_last[:3])
+    *gx, turned_near, turned_far, _ = lax.optimization_barrier((*gx, *turned, cut_last[0]))
+    landed = exchange(None, turned_near, turned_far)[1:]
+    gx_landed = exchange(*gx)
+    half_in = join(in_spread, (cut_last[0],))
+    in_spread.append(swap(half_in, "dp", 1))
+    shard_last, vec = gather_sum(cut_last[3], last_places, cut_last[4], (half_in,))
+    last_spread = [shard_last] + places_of([shard_last] * 3)
+    tokens_out = land_output(spots, hops, landed, dims, (shard_last,))
+    grad_input, pooled_out = land_grad(sent, gx_landed, dims, (shard_last,))
+    (g_down,) = whole_grad(ids, down_spread, devices, (width,), (shard_last,))
+    half_last = join(last_spread, (g_down,))
+    last_spread.append(swap(half_last, "dp", 1))
+    (g_in,) = whole_grad(ids, in_spread, devices, (width,), (half_last,))
+    g_qkv, g_out = whole_grad(ids, last_spread, devices, (inner, head_width))
+    g_qkv = g_qkv.reshape(3, head_width, width).transpose(2, 0, 1)
     g_bqv = jnp.stack([vec[0, :head_width], vec[0, 256 : 256 + head_width]])
     return (
-        tokens_out, pooled_out, grad_input, g_qkv, g_bqv, g_last[inner:],
+        tokens_out, pooled_out, grad_input, g_qkv, g_bqv, g_out,
         vec[2], vec[3], vec[4], g_in, vec[1], g_down, vec[5], vec[6], vec[7],
     )
 

time: 381 us -> 282 us (0.74)
  local copies, waits for them, and re-layouts: 37.5 us -> 9.99 us
  Pallas kernels: 128 us -> 104 us
  waiting for transfers between devices: 121 us -> 97.9 us
  starting transfers between devices: 83.3 us -> 61.8 us
    pallas_call x32 -> x35, Pallas kernels: 128 us -> 104 us  [call(): return lambda *args: made(*args, *after)]
    unnamed x156 -> x102, local copies, waits for them, and re-layouts: 32.4 us -> 9.29 us
    ppermute x49 -> x53, starting transfers between devices: 70.3 us -> 49.3 us  [swap(): lax.ppermute(values, axis, [(i, i ^ bit) for i in range(lax.axis_size(axi...]
    ppermute x4, waiting for transfers between devices: 18.6 us -> 0.01 us  [hop(): lax.ppermute(values, ('dp', 'mp'), [(s * count + f, (s ^ f + count * k) *...]
    ppermute x49 -> x53, waiting for transfers between devices: 102 us -> 97.9 us  [swap(): lax.ppermute(values, axis, [(i, i ^ bit) for i in range(lax.axis_size(axi...]
  transfers between devices with their start and end apart: 53 -> 57, of which waited for: 14 -> 26; matrix products, arithmetic and copies ran while one was open for 1% -> 0% of each run, Pallas kernels for 28% -> 31%
where the time goes in v2:
time: 282 us; the launch traced here: 276 us
  Pallas kernels  104 us (37%)
  waiting for transfers between devices  97.9 us (35%)
  starting transfers between devices  61.8 us (22%)
  local copies, waits for them, and re-layouts  9.99 us (4%)
    pallas_call x35, Pallas kernels, call(): return lambda *args: made(*args, *after)  104 us
    ppermute x53, waiting for transfers between devices, swap(): lax.ppermute(values, axis, [(i, i ^ bit) for i in range(lax.axis_size(axi...  97.9 us
    ppermute x53, starting transfers between devices, swap(): lax.ppermute(values, axis, [(i, i ^ bit) for i in range(lax.axis_size(axi...  49.3 us
    ppermute x4, starting transfers between devices, hop(): lax.ppermute(values, ('dp', 'mp'), [(s * count + f, (s ^ f + count * k) *...  12.5 us
    unnamed x102, local copies, waits for them, and re-layouts  9.29 us
  transfers between devices with their start and end apart: 57, of which 26 were waited for; matrix products, arithmetic and copies ran while one was open for 0% of the time, Pallas kernels for 31%

profile of v2, /device:TPU:4, one launch (start us, length us, event | category | flops | bytes accessed | tf_op | source)
XLA Modules:
  0.0 276.5 jit_solution(3142717817427845011)
XLA Ops:
  0.7 4.1 %prep_rows.1 = (bf16[144,768]{1,0:T(8,128)(2,1)}, bf16[144,768]{1,0:T(8,128)(2,1)}, bf16[672,768]{1,0:T(8,128)(2,1)}, s32[8,128]{1,0:T(8,128)}, s32[128]{0:T(128)}, /*index=5*/s32[128]{0:T(128)}, s32[3]{0:T(128)}) custom-call(s32[128]{0:T(128)} %refs_0_.3, s32[128,128]{1,0:T(8,128)} %refs_1_.2, bf16[16,32,768]{2,1,0:T(8,128)(2,1)} %refs_2_.1, ...), custom_call_target="tpu_custom_call" | custom-call | flops 6000000000 | tf_op jit(solution)/shard_map/prep_rows/pallas_call | solution.py:288
  5.5 24.2 %collective-permute-done.1.refs_1_.refs_4_.refs_6_.refs_13_.refs_12_.refs_7_ = bf16[672,768]{1,0:T(8,128)(2,1)S(1)} collective-permute-done((bf16[672,768]{1,0:T(8,128)(2,1)}, bf16[672,768]{1,0:T(8,128)(2,1)S(1)}, u32[]{:S(2)}, u32[]{:S(2)}) %collective-permute-start.1) | collective-permute-done | bytes 1032224 | tf_op jit(solution)/shard_map/ppermute | solution.py:1636
  30.2 3.0 %collective-permute-done.refs_3_.refs_5_ = bf16[144,768]{1,0:T(8,128)(2,1)S(1)} collective-permute-done((bf16[144,768]{1,0:T(8,128)(2,1)}, bf16[144,768]{1,0:T(8,128)(2,1)S(1)}, u32[]{:S(2)}, u32[]{:S(2)}) %collective-permute-start) | collective-permute-done | bytes 221216 | tf_op jit(solution)/shard_map/ppermute | solution.py:1636
  36.8 9.5 %attend.2 = (bf16[512,768]{1,0:T(8,128)(2,1)S(1)}, bf16[2,512,192]{2,1,0:T(8,128)(2,1)S(1)}, bf16[2,3,512,192]{3,2,1,0:T(8,128)(2,1)S(1)}, bf16[2,4,384,128]{3,2,1,0:T(8,128)(2,1)S(1)}) custom-call(s32[3]{0:T(128)S(1)} %copy-done.46, s32[8,128]{1,0:T(8,128)S(1)} %copy-done.45, bf16[144,768]{1,0:T(8,128)(2,1)S(1)} %copy-done.30, ...), custom_call_target="tpu_custom_call" | custom-call | flops 20000000000 | tf_op jit(solution)/shard_map/attend/pallas_call | solution.py:288
  46.3 3.8 %collective-permute-done.7.refs_7_.refs_14_.refs_13_.refs_8_ = bf16[384,768]{1,0:T(8,128)(2,1)S(1)} collective-permute-done((bf16[384,768]{1,0:T(8,128)(2,1)S(1)}, bf16[384,768]{1,0:T(8,128)(2,1)S(1)}, u32[]{:S(2)}, u32[]{:S(2)}) %collective-permute-start.7) | collective-permute-done | bytes 589856 | tf_op jit(solution)/shard_map/ppermute | solution.py:1636
  54.4 3.7 %collective-permute-start.14 = (bf16[2,128,768]{2,1,0:T(8,128)(2,1)S(1)}, bf16[2,128,768]{2,1,0:T(8,128)(2,1)S(1)}, u32[]{:S(2)}, u32[]{:S(2)}) collective-permute-start(bf16[2,128,768]{2,1,0:T(8,128)(2,1)S(1)} %get-tuple-element.117), channel_id=1, source_target_pairs={{0,16},{1,21},{2,26},{3,31},{4,20},{5,17},{6,30},{7,27},{8,24},{9,... | collective-permute-start | bytes 1179656 | tf_op jit(solution)/shard_map/ppermute | solution.py:1652
  58.1 2.2 collective-permute-start.13
  60.4 10.1 %attend.3 = (bf16[2,512,192]{2,1,0:T(8,128)(2,1)S(1)}, bf16[2,3,512,192]{3,2,1,0:T(8,128)(2,1)S(1)}, bf16[2,4,384,128]{3,2,1,0:T(8,128)(2,1)S(1)}) custom-call(s32[3]{0:T(128)S(1)} %copy-done.46, s32[8,128]{1,0:T(8,128)S(1)} %copy-done.45, bf16[144,768]{1,0:T(8,128)(2,1)S(1)} %copy-done.30, bf16[144,768]{1,0:T(8,128)(2,1)S(1)} %collective-permute-done.refs_3_.refs_5_, ...), custom_call_target="tpu_custom_call" | custom-call | flops 20000000000 | tf_op jit(solution)/shard_map/attend/pallas_call | solution.py:288
  71.6 2.8 %collective-permute-done.10.refs_7_.refs_10_ = bf16[384,768]{1,0:T(8,128)(2,1)S(1)} collective-permute-done((bf16[384,768]{1,0:T(8,128)(2,1)S(1)}, bf16[384,768]{1,0:T(8,128)(2,1)S(1)}, u32[]{:S(2)}, u32[]{:S(2)}) %collective-permute-start.10) | collective-permute-done | bytes 589856 | tf_op jit(solution)/shard_map/ppermute | solution.py:1636
  74.5 2.4 collective-permute-start.16
  76.9 8.8 %ffn_near.1 = (bf16[512,768]{1,0:T(8,128)(2,1)S(1)}, f32[512,768]{1,0:T(8,128)S(1)}, f32[512,128]{1,0:T(8,128)S(1)}, f32[512,768]{1,0:T(8,128)S(1)}, bf16[2,512,...) custom-call(s32[3]{0:T(128)S(1)} %copy-done.46, bf16[512,768]{1,0:T(8,128)(2,1)S(1)} %get-tuple-element.106.refs_1_.refs_2_, ...), custom_call_target="tpu_custom_call" | custom-call | flops 22000001024 | tf_op jit(solution)/shard_map/ffn_near/pallas_call | solution.py:288
  85.8 5.1 %collective-permute-done.16.refs_14_.refs_7_ = bf16[384,768]{1,0:T(8,128)(2,1)S(1)} collective-permute-done((bf16[384,768]{1,0:T(8,128)(2,1)S(1)}, bf16[384,768]{1,0:T(8,128)(2,1)S(1)}, u32[]{:S(2)}, u32[]{:S(2)}) %collective-permute-start.16) | collective-permute-done | bytes 589856 | tf_op jit(solution)/shard_map/ppermute | solution.py:1636
  91.5 5.0 %ffn_far.1 = (bf16[2,512,768]{2,1,0:T(8,128)(2,1)S(1)}, bf16[2,512,768]{2,1,0:T(8,128)(2,1)S(1)}) custom-call(s32[3]{0:T(128)S(1)} %copy-done.46, bf16[512,768]{1,0:T(8,128)(2,1)S(1)} %get-tuple-element.111.refs_1_.refs_3_.refs_2_.refs_0_, bf16[144,768]{1,0:T(8,128)(2,1)S(1)} %copy-done.30, bf16[144,768]{1,0:T(8,128)(2,1)S(1)} %collective-permute-done.refs_3_.refs_5_, ...), custom_call_target="tpu_custom_call" | custom-call | flops 12000000000 | tf_op jit(solution)/shard_map/ffn_far/pallas_call | solution.py:288
  96.6 8.5 %ffn_down.1 = (bf16[4,64,768]{2,1,0:T(8,128)(2,1)S(1)}, bf16[4,64,768]{2,1,0:T(8,128)(2,1)S(1)}, f32[16,768]{1,0:T(8,128)S(1)}, f32[512,768]{1,0:T(8,128)S(1)}, ...) custom-call(s32[3]{0:T(128)S(1)} %copy-done.46, s32[128]{0:T(128)S(1)} %copy-done.49, ...), custom_call_target="tpu_custom_call" | custom-call | flops 17999998976 | tf_op jit(solution)/shard_map/ffn_down/pallas_call | solution.py:288
  106.3 5.4 %ffn_back.1 = (bf16[4,512,768]{2,1,0:T(8,128)(2,1)S(1)}, f32[4,768]{1,0:T(4,128)S(1)}) custom-call(s32[3]{0:T(128)S(1)} %copy-done.46, bf16[512,768]{1,0:T(8,128)(2,1)S(1)} %get-tuple-element.122.refs_1_.refs_2_, bf16[2,512,768]{2,1,0:T(8,128)(2,1)S(1)} %get-tuple-element.124.refs_2_, bf16[2,512,768]{2,1,0:T(8,128)(2,1)S(1)} %get-tuple-element.125.refs_3_, ...), custom_call_target="tpu_custom_call" | custom-call | flops 10000000000 | tf_op jit(solution)/shard_map/ffn_back/pallas_call | solution.py:288
  113.0 3.9 %collective-permute-start.20 = (bf16[4,64,768]{2,1,0:T(8,128)(2,1)S(1)}, bf16[4,64,768]{2,1,0:T(8,128)(2,1)S(1)}, u32[]{:S(2)}, u32[]{:S(2)}) collective-permute-start(bf16[4,64,768]{2,1,0:T(8,128)(2,1)S(1)} %get-tuple-element.127), channel_id=1, source_target_pairs={{0,0},{1,5},{2,10},{3,15},{4,4},{5,1},{6,14},{7,11},{8,8},{9,13},{... | collective-permute-start | bytes 1179656 | tf_op jit(solution)/shard_map/ppermute | solution.py:1652
  116.9 2.7 collective-permute-start.21
  119.7 7.6 %norm_back.1 = (f32[512,768]{1,0:T(8,128)S(1)}, bf16[512,768]{1,0:T(8,128)(2,1)S(1)}, f32[8,768]{1,0:T(8,128)S(1)}, bf16[2,768,768]{2,1,0:T(8,128)(2,1)S(1)}) custom-call(s32[3]{0:T(128)S(1)} %copy-done.46, bf16[4,512,768]{2,1,0:T(8,128)(2,1)S(1)} %get-tuple-element.129.refs_1_.refs_2_, ...), custom_call_target="tpu_custom_call" | custom-call | flops 16000000000 | tf_op jit(solution)/shard_map/norm_back/pallas_call | solution.py:288
  129.6 9.6 %attend_back.2 = (bf16[2,512,576]{2,1,0:T(8,128)(2,1)S(1)}, bf16[2,784,768]{2,1,0:T(8,128)(2,1)S(1)}) custom-call(s32[3]{0:T(128)S(1)} %copy-done.46, bf16[512,768]{1,0:T(8,128)(2,1)S(1)} %get-tuple-element.134.refs_1_, bf16[512,768]{1,0:T(8,128)(2,1)S(1)} %copy-done.16, f32[4,768]{1,0:T(4,128)S(1)} %get-tuple-element.126.refs_3_, ...), custom_call_target="tpu_custom_call" | custom-call | flops 25999998976 | tf_op jit(solution)/shard_map/attend_back/pallas_call | solution.py:288
  139.8 1.9 copy-done.18
  144.3 1.9 own_grad.2
  146.8 9.6 %attend_back.3 = (bf16[2,512,576]{2,1,0:T(8,128)(2,1)S(1)}, bf16[2,784,768]{2,1,0:T(8,128)(2,1)S(1)}) custom-call(s32[3]{0:T(128)S(1)} %copy-done.46, bf16[512,768]{1,0:T(8,128)(2,1)S(1)} %get-tuple-element.134.refs_1_, bf16[512,768]{1,0:T(8,128)(2,1)S(1)} %copy-done.16, f32[4,768]{1,0:T(4,128)S(1)} %get-tuple-element.126.refs_3_, ...), custom_call_target="tpu_custom_call" | custom-call | flops 25999998976 | tf_op jit(solution)/shard_map/attend_back/pallas_call | solution.py:288
  158.3 3.2 %collective-permute-done.24.refs_1_ = bf16[384,768]{1,0:T(8,128)(2,1)S(1)} collective-permute-done((bf16[384,768]{1,0:T(8,128)(2,1)S(1)}, bf16[384,768]{1,0:T(8,128)(2,1)S(1)}, u32[]{:S(2)}, u32[]{:S(2)}) %collective-permute-start.24) | collective-permute-done | bytes 589856 | tf_op jit(solution)/shard_map/ppermute | solution.py:1636
  163.0 2.2 collective-permute-start.28
  165.2 5.0 %grad_input_rows.1 = (bf16[144,768]{1,0:T(8,128)(2,1)S(1)}, bf16[144,768]{1,0:T(8,128)(2,1)S(1)}, bf16[288,768]{1,0:T(8,128)(2,1)S(1)}) custom-call(s32[3]{0:T(128)S(1)} %copy-done.46, f32[512,768]{1,0:T(8,128)S(1)} %copy-done.25, bf16[2,512,576]{2,1,0:T(8,128)(2,1)S(1)} %get-tuple-element.141.refs_2_, bf16[2,512,576]{2,1,0:T(8,128)(2,1)S(1)} %get-tuple-element.146.refs_3_, ...), custom_call_target="tpu_custom_call" | custom-call | flops 12000000000 | tf_op jit(solution)/shard_map/grad_input_rows/pallas_call | solution.py:288
  170.8 6.4 %collective-permute-done.28.refs_1_ = bf16[96,768]{1,0:T(8,128)(2,1)S(1)} collective-permute-done((bf16[96,768]{1,0:T(8,128)(2,1)S(1)}, bf16[96,768]{1,0:T(8,128)(2,1)S(1)}, u32[]{:S(2)}, u32[]{:S(2)}) %collective-permute-start.28) | collective-permute-done | bytes 147488 | tf_op jit(solution)/shard_map/ppermute | solution.py:1636
  179.0 1.9 own_grad.3
  182.7 3.2 %collective-permute-start.32 = (bf16[96,768]{1,0:T(8,128)(2,1)S(1)}, bf16[96,768]{1,0:T(8,128)(2,1)S(1)}, u32[]{:S(2)}, u32[]{:S(2)}) collective-permute-start(bf16[96,768]{1,0:T(8,128)(2,1)S(1)} %gather_sum.3.refs_5_.refs_0_.refs_1_), channel_id=1, source_target_pairs={{0,16},{4,20},{8,24},{12,28},{16,0},{20,4},{24,8},{28,12},{1,17},{... | collective-permute-start | bytes 442376 | tf_op jit(solution)/shard_map/ppermute | solution.py:1636
  185.9 4.3 %collective-permute-done.34.refs_3_.refs_4_ = bf16[96,768]{1,0:T(8,128)(2,1)S(1)} collective-permute-done((bf16[96,768]{1,0:T(8,128)(2,1)S(1)}, bf16[96,768]{1,0:T(8,128)(2,1)S(1)}, u32[]{:S(2)}, u32[]{:S(2)}) %collective-permute-start.34) | collective-permute-done | bytes 147488 | tf_op jit(solution)/shard_map/ppermute | solution.py:1636
  191.2 3.3 %collective-permute-done.32.refs_1_.refs_2_ = bf16[96,768]{1,0:T(8,128)(2,1)S(1)} collective-permute-done((bf16[96,768]{1,0:T(8,128)(2,1)S(1)}, bf16[96,768]{1,0:T(8,128)(2,1)S(1)}, u32[]{:S(2)}, u32[]{:S(2)}) %collective-permute-start.32) | collective-permute-done | bytes 147488 | tf_op jit(solution)/shard_map/ppermute | solution.py:1636
  199.7 2.4 collective-permute-start.36
  203.6 2.7 collective-permute-done.37.refs_2_
  207.3 7.5 %collective-permute-done.36.refs_1_ = bf16[96,768]{1,0:T(8,128)(2,1)S(1)} collective-permute-done((bf16[96,768]{1,0:T(8,128)(2,1)S(1)}, bf16[96,768]{1,0:T(8,128)(2,1)S(1)}, u32[]{:S(2)}, u32[]{:S(2)}) %collective-permute-start.36) | collective-permute-done | bytes 147488 | tf_op jit(solution)/shard_map/ppermute | solution.py:1636
  215.3 4.0 %collective-permute-start.45 = (bf16[96,768]{1,0:T(8,128)(2,1)S(1)}, bf16[96,768]{1,0:T(8,128)(2,1)S(1)}, u32[]{:S(2)}, u32[]{:S(2)}) collective-permute-start(bf16[96,768]{1,0:T(8,128)(2,1)S(1)} %gather_sum.4.refs_3_.refs_0_.refs_1_), channel_id=1, source_target_pairs={{0,16},{4,20},{8,24},{12,28},{16,0},{20,4},{24,8},{28,12},{1,17},{... | collective-permute-start | bytes 442376 | tf_op jit(solution)/shard_map/ppermute | solution.py:1636
  219.5 4.1 %collective-permute-done.47.refs_3_.refs_4_ = bf16[96,768]{1,0:T(8,128)(2,1)S(1)} collective-permute-done((bf16[96,768]{1,0:T(8,128)(2,1)S(1)}, bf16[96,768]{1,0:T(8,128)(2,1)S(1)}, u32[]{:S(2)}, u32[]{:S(2)}) %collective-permute-start.47) | collective-permute-done | bytes 147488 | tf_op jit(solution)/shard_map/ppermute | solution.py:1636
  224.4 2.9 %collective-permute-start.44 = (bf16[112,768]{1,0:T(8,128)(2,1)S(1)}, bf16[112,768]{1,0:T(8,128)(2,1)S(1)}, u32[]{:S(2)}, u32[]{:S(2)}) collective-permute-start(bf16[112,768]{1,0:T(8,128)(2,1)S(1)} %get-tuple-element.172), channel_id=1, source_target_pairs={{0,24},{4,28},{8,16},{12,20},{16,8},{20,12},{24,0},{28,4},{1,25},{... | collective-permute-start | bytes 516104 | tf_op jit(solution)/shard_map/ppermute | solution.py:1636
  227.3 3.2 %collective-permute-done.45.refs_1_.refs_2_ = bf16[96,768]{1,0:T(8,128)(2,1)S(1)} collective-permute-done((bf16[96,768]{1,0:T(8,128)(2,1)S(1)}, bf16[96,768]{1,0:T(8,128)(2,1)S(1)}, u32[]{:S(2)}, u32[]{:S(2)}) %collective-permute-start.45) | collective-permute-done | bytes 147488 | tf_op jit(solution)/shard_map/ppermute | solution.py:1636
  233.3 4.5 %collective-permute-done.44.refs_3_ = bf16[112,768]{1,0:T(8,128)(2,1)S(1)} collective-permute-done((bf16[112,768]{1,0:T(8,128)(2,1)S(1)}, bf16[112,768]{1,0:T(8,128)(2,1)S(1)}, u32[]{:S(2)}, u32[]{:S(2)}) %collective-permute-start.44) | collective-permute-done | bytes 172064 | tf_op jit(solution)/shard_map/ppermute | solution.py:1636
  239.5 1.8 collective-permute-start.53
  241.3 5.1 %collective-permute-start.52 = (bf16[96,768]{1,0:T(8,128)(2,1)S(1)}, bf16[96,768]{1,0:T(8,128)(2,1)S(1)}, u32[]{:S(2)}, u32[]{:S(2)}) collective-permute-start(bf16[96,768]{1,0:T(8,128)(2,1)S(1)} %get-tuple-element.174.refs_6_.refs_5_.refs_0_.refs_1_), channel_id=1, source_target_pairs={{0,8},{4,12},{8,0},{12,4},{16,24},{20,28},{24,16},{28,20},{1,9},{5... | collective-permute-start | bytes 442376 | tf_op jit(solution)/shard_map/ppermute | solution.py:1636
  246.4 2.1 whole_grad.3.refs_4_
  248.5 2.5 collective-permute-start.51
  252.2 2.7 collective-permute-done.51.refs_1_.refs_2_
  257.2 3.4 %collective-permute-start.55 = (bf16[384,768]{1,0:T(8,128)(2,1)S(1)}, bf16[384,768]{1,0:T(8,128)(2,1)S(1)}, u32[]{:S(2)}, u32[]{:S(2)}) collective-permute-start(bf16[384,768]{1,0:T(8,128)(2,1)S(1)} %join.5.refs_6_), channel_id=1, source_target_pairs={{0,4},{4,0},{8,12},{12,8},{16,20},{20,16},{24,28},{28,24},{1,5},{5... | collective-permute-start | bytes 1769480 | tf_op jit(solution)/shard_map/ppermute | solution.py:1636
  260.6 2.1 whole_grad.5
  264.3 2.2 land_grad.1
  266.5 7.6 %collective-permute-done.55.refs_5_ = bf16[384,768]{1,0:T(8,128)(2,1)S(1)} collective-permute-done((bf16[384,768]{1,0:T(8,128)(2,1)S(1)}, bf16[384,768]{1,0:T(8,128)(2,1)S(1)}, u32[]{:S(2)}, u32[]{:S(2)}) %collective-permute-start.55) | collective-permute-done | bytes 589856 | tf_op jit(solution)/shard_map/ppermute | solution.py:1636
  274.1 2.2 whole_grad.4
  (207 shorter events, 46.5 us)
Async XLA Ops:
  4.8 24.8 %collective-permute-start.1 = (bf16[672,768]{1,0:T(8,128)(2,1)}, bf16[672,768]{1,0:T(8,128)(2,1)S(1)}, u32[]{:S(2)}, u32[]{:S(2)}) collective-permute-start(bf16[672,768]{1,0:T(8,128)(2,1)} %get-tuple-element.105), channel_id=1, source_target_pairs={{0,2},{1,3},{2,0},{3,1},{4,6},{5,7},{6,4},{7,5},{8,10},{9,11},{10,... | collective-permute-start | bytes 3096584 | tf_op jit(solution)/shard_map/ppermute | solution.py:1636
  4.9 31.8 %collective-permute-start.5 = (bf16[768,768]{1,0:T(8,128)(2,1)S(1)}, bf16[768,768]{1,0:T(8,128)(2,1)S(1)}, u32[]{:S(2)}, u32[]{:S(2)}) collective-permute-start(bf16[768,768]{1,0:T(8,128)(2,1)S(1)} %copy-done.2), channel_id=1, source_target_pairs={{0,1},{1,0},{2,3},{3,2},{4,5},{5,4},{6,7},{7,6},{8,9},{9,8},{10,11... | collective-permute-start | bytes 3538952 | tf_op jit(solution)/shard_map/ppermute | solution.py:1636
  5.0 31.7 %collective-permute-start.6 = (bf16[768,768]{1,0:T(8,128)(2,1)S(1)}, bf16[768,768]{1,0:T(8,128)(2,1)S(1)}, u32[]{:S(2)}, u32[]{:S(2)}) collective-permute-start(bf16[768,768]{1,0:T(8,128)(2,1)S(1)} %copy-done.1), channel_id=1, source_target_pairs={{0,1},{1,0},{2,3},{3,2},{4,5},{5,4},{6,7},{7,6},{8,9},{9,8},{10,11... | collective-permute-start | bytes 3538952 | tf_op jit(solution)/shard_map/ppermute | solution.py:1636
  34.7 15.4 %collective-permute-start.7 = (bf16[384,768]{1,0:T(8,128)(2,1)S(1)}, bf16[384,768]{1,0:T(8,128)(2,1)S(1)}, u32[]{:S(2)}, u32[]{:S(2)}) collective-permute-start(bf16[384,768]{1,0:T(8,128)(2,1)S(1)} %slice.40), channel_id=1, source_target_pairs={{0,4},{4,0},{8,12},{12,8},{16,20},{20,16},{24,28},{28,24},{1,5},{5... | collective-permute-start | bytes 1769480 | tf_op jit(solution)/shard_map/ppermute | solution.py:1636
  36.2 15.1 %collective-permute-start.9 = (bf16[384,768]{1,0:T(8,128)(2,1)S(1)}, bf16[384,768]{1,0:T(8,128)(2,1)S(1)}, u32[]{:S(2)}, u32[]{:S(2)}) collective-permute-start(bf16[384,768]{1,0:T(8,128)(2,1)S(1)} %prep_halves.2.refs_11_), channel_id=1, source_target_pairs={{0,2},{1,3},{2,0},{3,1},{4,6},{5,7},{6,4},{7,5},{8,10},{9,11},{10,... | collective-permute-start | bytes 1769480 | tf_op jit(solution)/shard_map/ppermute | solution.py:1636
  50.1 8.0 %collective-permute-start.8 = (bf16[384,768]{1,0:T(8,128)(2,1)S(1)}, bf16[384,768]{1,0:T(8,128)(2,1)S(1)}, u32[]{:S(2)}, u32[]{:S(2)}) collective-permute-start(bf16[384,768]{1,0:T(8,128)(2,1)S(1)} %collective-permute-done.7.refs_7_.refs_14_.refs_13_.refs_8_), channel_id=1, source_target_pairs={{0,1},{1,0},{2,3},{3,2},{4,5},{5,4},{6,7},{7,6},{8,9},{9,8},{10,11... | collective-permute-start | bytes 1769480 | tf_op jit(solution)/shard_map/ppermute | solution.py:1636
  51.3 39.6 %collective-permute-start.11 = (bf16[384,768]{1,0:T(8,128)(2,1)S(1)}, bf16[384,768]{1,0:T(8,128)(2,1)S(1)}, u32[]{:S(2)}, u32[]{:S(2)}) collective-permute-start(bf16[384,768]{1,0:T(8,128)(2,1)S(1)} %collective-permute-done.9.refs_6_.refs_9_), channel_id=1, source_target_pairs={{0,1},{1,0},{2,3},{3,2},{4,5},{5,4},{6,7},{7,6},{8,9},{9,8},{10,11... | collective-permute-start | bytes 1769480 | tf_op jit(solution)/shard_map/ppermute | solution.py:1636
  51.3 23.1 %collective-permute-start.10 = (bf16[384,768]{1,0:T(8,128)(2,1)S(1)}, bf16[384,768]{1,0:T(8,128)(2,1)S(1)}, u32[]{:S(2)}, u32[]{:S(2)}) collective-permute-start(bf16[384,768]{1,0:T(8,128)(2,1)S(1)} %collective-permute-done.9.refs_6_.refs_9_), channel_id=1, source_target_pairs={{0,4},{4,0},{8,12},{12,8},{16,20},{20,16},{24,28},{28,24},{1,5},{5... | collective-permute-start | bytes 1769480 | tf_op jit(solution)/shard_map/ppermute | solution.py:1636
  52.3 19.4 %collective-permute-start.15 = (bf16[384,768]{1,0:T(8,128)(2,1)S(1)}, bf16[384,768]{1,0:T(8,128)(2,1)S(1)}, u32[]{:S(2)}, u32[]{:S(2)}) collective-permute-start(bf16[384,768]{1,0:T(8,128)(2,1)S(1)} %prep_halves.3.refs_2_), channel_id=1, source_target_pairs={{0,2},{1,3},{2,0},{3,1},{4,6},{5,7},{6,4},{7,5},{8,10},{9,11},{10,... | collective-permute-start | bytes 1769480 | tf_op jit(solution)/shard_map/ppermute | solution.py:1636
  54.4 42.1 %collective-permute-start.14 = (bf16[2,128,768]{2,1,0:T(8,128)(2,1)S(1)}, bf16[2,128,768]{2,1,0:T(8,128)(2,1)S(1)}, u32[]{:S(2)}, u32[]{:S(2)}) collective-permute-start(bf16[2,128,768]{2,1,0:T(8,128)(2,1)S(1)} %get-tuple-element.117), channel_id=1, source_target_pairs={{0,16},{1,21},{2,26},{3,31},{4,20},{5,17},{6,30},{7,27},{8,24},{9,... | collective-permute-start | bytes 1179656 | tf_op jit(solution)/shard_map/ppermute | solution.py:1652
  58.1 38.4 %collective-permute-start.13 = (bf16[2,128,768]{2,1,0:T(8,128)(2,1)S(1)}, bf16[2,128,768]{2,1,0:T(8,128)(2,1)S(1)}, u32[]{:S(2)}, u32[]{:S(2)}) collective-permute-start(bf16[2,128,768]{2,1,0:T(8,128)(2,1)S(1)} %get-tuple-element.109.refs_10_), channel_id=1, source_target_pairs={{0,0},{1,5},{2,10},{3,15},{4,4},{5,1},{6,14},{7,11},{8,8},{9,13},{... | collective-permute-start | bytes 1179656 | tf_op jit(solution)/shard_map/ppermute | solution.py:1652
  74.5 17.0 %collective-permute-start.12 = (bf16[384,768]{1,0:T(8,128)(2,1)S(1)}, bf16[384,768]{1,0:T(8,128)(2,1)S(1)}, u32[]{:S(2)}, u32[]{:S(2)}) collective-permute-start(bf16[384,768]{1,0:T(8,128)(2,1)S(1)} %collective-permute-done.10.refs_7_.refs_10_), channel_id=1, source_target_pairs={{0,1},{1,0},{2,3},{3,2},{4,5},{5,4},{6,7},{7,6},{8,9},{9,8},{10,11... | collective-permute-start | bytes 1769480 | tf_op jit(solution)/shard_map/ppermute | solution.py:1636
  74.5 16.4 %collective-permute-start.16 = (bf16[384,768]{1,0:T(8,128)(2,1)S(1)}, bf16[384,768]{1,0:T(8,128)(2,1)S(1)}, u32[]{:S(2)}, u32[]{:S(2)}) collective-permute-start(bf16[384,768]{1,0:T(8,128)(2,1)S(1)} %collective-permute-done.15.refs_13_.refs_6_), channel_id=1, source_target_pairs={{0,8},{4,12},{8,0},{12,4},{16,24},{20,28},{24,16},{28,20},{1,9},{5... | collective-permute-start | bytes 1769480 | tf_op jit(solution)/shard_map/ppermute | solution.py:1636
  112.9 31.4 %collective-permute-start.22 = (bf16[768,768]{1,0:T(8,128)(2,1)S(1)}, bf16[768,768]{1,0:T(8,128)(2,1)S(1)}, u32[]{:S(2)}, u32[]{:S(2)}) collective-permute-start(bf16[768,768]{1,0:T(8,128)(2,1)S(1)} %peer_grad.1.refs_13_), channel_id=1, source_target_pairs={{0,2},{1,3},{2,0},{3,1},{4,6},{5,7},{6,4},{7,5},{8,10},{9,11},{10,... | collective-permute-start | bytes 3538952 | tf_op jit(solution)/shard_map/ppermute | solution.py:1636
  113.0 30.5 %collective-permute-start.20 = (bf16[4,64,768]{2,1,0:T(8,128)(2,1)S(1)}, bf16[4,64,768]{2,1,0:T(8,128)(2,1)S(1)}, u32[]{:S(2)}, u32[]{:S(2)}) collective-permute-start(bf16[4,64,768]{2,1,0:T(8,128)(2,1)S(1)} %get-tuple-element.127), channel_id=1, source_target_pairs={{0,0},{1,5},{2,10},{3,15},{4,4},{5,1},{6,14},{7,11},{8,8},{9,13},{... | collective-permute-start | bytes 1179656 | tf_op jit(solution)/shard_map/ppermute | solution.py:1652
  116.9 26.5 %collective-permute-start.21 = (bf16[4,64,768]{2,1,0:T(8,128)(2,1)S(1)}, bf16[4,64,768]{2,1,0:T(8,128)(2,1)S(1)}, u32[]{:S(2)}, u32[]{:S(2)}) collective-permute-start(bf16[4,64,768]{2,1,0:T(8,128)(2,1)S(1)} %get-tuple-element.128), channel_id=1, source_target_pairs={{0,16},{1,21},{2,26},{3,31},{4,20},{5,17},{6,30},{7,27},{8,24},{9,... | collective-permute-start | bytes 1179656 | tf_op jit(solution)/shard_map/ppermute | solution.py:1652
  127.3 12.4 %collective-permute-start.23 = (bf16[2,768,768]{2,1,0:T(8,128)(2,1)S(1)}, bf16[2,768,768]{2,1,0:T(8,128)(2,1)S(1)}, u32[]{:S(2)}, u32[]{:S(2)}) collective-permute-start(bf16[2,768,768]{2,1,0:T(8,128)(2,1)S(1)} %get-tuple-element.142), channel_id=1, source_target_pairs={{0,1},{1,0},{2,3},{3,2},{4,5},{5,4},{6,7},{7,6},{8,9},{9,8},{10,11... | collective-permute-start | bytes 7077896 | tf_op jit(solution)/shard_map/ppermute | solution.py:1636
  139.2 17.2 %collective-permute-start.25 = (bf16[2,784,768]{2,1,0:T(8,128)(2,1)S(1)}, bf16[2,784,768]{2,1,0:T(8,128)(2,1)S(1)}, u32[]{:S(2)}, u32[]{:S(2)}) collective-permute-start(bf16[2,784,768]{2,1,0:T(8,128)(2,1)S(1)} %get-tuple-element.143.refs_3_), channel_id=1, source_target_pairs={{0,1},{1,0},{2,3},{3,2},{4,5},{5,4},{6,7},{7,6},{8,9},{9,8},{10,11... | collective-permute-start | bytes 7225352 | tf_op jit(solution)/shard_map/ppermute | solution.py:1636
  142.8 34.4 %collective-permute-start.27 = (bf16[768,768]{1,0:T(8,128)(2,1)S(1)}, bf16[768,768]{1,0:T(8,128)(2,1)S(1)}, u32[]{:S(2)}, u32[]{:S(2)}) collective-permute-start(bf16[768,768]{1,0:T(8,128)(2,1)S(1)} %peer_grad_in.1.refs_2_), channel_id=1, source_target_pairs={{0,2},{1,3},{2,0},{3,1},{4,6},{5,7},{6,4},{7,5},{8,10},{9,11},{10,... | collective-permute-start | bytes 3538952 | tf_op jit(solution)/shard_map/ppermute | solution.py:1636
  146.2 15.2 %collective-permute-start.24 = (bf16[384,768]{1,0:T(8,128)(2,1)S(1)}, bf16[384,768]{1,0:T(8,128)(2,1)S(1)}, u32[]{:S(2)}, u32[]{:S(2)}) collective-permute-start(bf16[384,768]{1,0:T(8,128)(2,1)S(1)} %get-tuple-element.145.refs_15_), channel_id=1, source_target_pairs={{0,4},{4,0},{8,12},{12,8},{16,20},{20,16},{24,28},{28,24},{1,5},{5... | collective-permute-start | bytes 1769480 | tf_op jit(solution)/shard_map/ppermute | solution.py:1636
  156.7 39.9 %collective-permute-start.26 = (bf16[784,768]{1,0:T(8,128)(2,1)S(1)}, bf16[784,768]{1,0:T(8,128)(2,1)S(1)}, u32[]{:S(2)}, u32[]{:S(2)}) collective-permute-start(bf16[784,768]{1,0:T(8,128)(2,1)S(1)} %peer_last.1.refs_2_), channel_id=1, source_target_pairs={{0,2},{1,3},{2,0},{3,1},{4,6},{5,7},{6,4},{7,5},{8,10},{9,11},{10,... | collective-permute-start | bytes 3612680 | tf_op jit(solution)/shard_map/ppermute | solution.py:1636
  161.6 8.6 %collective-permute-start.29 = (bf16[96,768]{1,0:T(8,128)(2,1)S(1)}, bf16[96,768]{1,0:T(8,128)(2,1)S(1)}, u32[]{:S(2)}, u32[]{:S(2)}) collective-permute-start(bf16[96,768]{1,0:T(8,128)(2,1)S(1)} %get-tuple-element.156), channel_id=1, source_target_pairs={{0,8},{4,12},{8,0},{12,4},{16,24},{20,28},{24,16},{28,20},{1,9},{5... | collective-permute-start | bytes 442376 | tf_op jit(solution)/shard_map/ppermute | solution.py:1636
  162.1 8.6 %collective-permute-start.30 = (bf16[96,768]{1,0:T(8,128)(2,1)S(1)}, bf16[96,768]{1,0:T(8,128)(2,1)S(1)}, u32[]{:S(2)}, u32[]{:S(2)}) collective-permute-start(bf16[96,768]{1,0:T(8,128)(2,1)S(1)} %get-tuple-element.157), channel_id=1, source_target_pairs={{0,24},{4,28},{8,16},{12,20},{16,8},{20,12},{24,0},{28,4},{1,25},{... | collective-permute-start | bytes 442376 | tf_op jit(solution)/shard_map/ppermute | solution.py:1636
  163.0 14.2 %collective-permute-start.28 = (bf16[96,768]{1,0:T(8,128)(2,1)S(1)}, bf16[96,768]{1,0:T(8,128)(2,1)S(1)}, u32[]{:S(2)}, u32[]{:S(2)}) collective-permute-start(bf16[96,768]{1,0:T(8,128)(2,1)S(1)} %get-tuple-element.150.refs_11_), channel_id=1, source_target_pairs={{0,16},{4,20},{8,24},{12,28},{16,0},{20,4},{24,8},{28,12},{1,17},{... | collective-permute-start | bytes 442376 | tf_op jit(solution)/shard_map/ppermute | solution.py:1636
  180.9 13.9 %collective-permute-start.31 = (bf16[384,768]{1,0:T(8,128)(2,1)S(1)}, bf16[384,768]{1,0:T(8,128)(2,1)S(1)}, u32[]{:S(2)}, u32[]{:S(2)}) collective-permute-start(bf16[384,768]{1,0:T(8,128)(2,1)S(1)} %get-tuple-element.159.refs_4_), channel_id=1, source_target_pairs={{0,4},{4,0},{8,12},{12,8},{16,20},{20,16},{24,28},{28,24},{1,5},{5... | collective-permute-start | bytes 1769480 | tf_op jit(solution)/shard_map/ppermute | solution.py:1636
  181.5 8.7 %collective-permute-start.34 = (bf16[96,768]{1,0:T(8,128)(2,1)S(1)}, bf16[96,768]{1,0:T(8,128)(2,1)S(1)}, u32[]{:S(2)}, u32[]{:S(2)}) collective-permute-start(bf16[96,768]{1,0:T(8,128)(2,1)S(1)} %gather_sum.3.refs_5_.refs_0_.refs_1_), channel_id=1, source_target_pairs={{0,24},{4,28},{8,16},{12,20},{16,8},{20,12},{24,0},{28,4},{1,25},{... | collective-permute-start | bytes 442376 | tf_op jit(solution)/shard_map/ppermute | solution.py:1636
  182.7 8.5 %collective-permute-start.33 = (bf16[96,768]{1,0:T(8,128)(2,1)S(1)}, bf16[96,768]{1,0:T(8,128)(2,1)S(1)}, u32[]{:S(2)}, u32[]{:S(2)}) collective-permute-start(bf16[96,768]{1,0:T(8,128)(2,1)S(1)} %gather_sum.3.refs_5_.refs_0_.refs_1_), channel_id=1, source_target_pairs={{0,8},{4,12},{8,0},{12,4},{16,24},{20,28},{24,16},{28,20},{1,9},{5... | collective-permute-start | bytes 442376 | tf_op jit(solution)/shard_map/ppermute | solution.py:1636
  182.7 11.7 %collective-permute-start.32 = (bf16[96,768]{1,0:T(8,128)(2,1)S(1)}, bf16[96,768]{1,0:T(8,128)(2,1)S(1)}, u32[]{:S(2)}, u32[]{:S(2)}) collective-permute-start(bf16[96,768]{1,0:T(8,128)(2,1)S(1)} %gather_sum.3.refs_5_.refs_0_.refs_1_), channel_id=1, source_target_pairs={{0,16},{4,20},{8,24},{12,28},{16,0},{20,4},{24,8},{28,12},{1,17},{... | collective-permute-start | bytes 442376 | tf_op jit(solution)/shard_map/ppermute | solution.py:1636
  198.0 21.3 %collective-permute-start.35 = (bf16[400,768]{1,0:T(8,128)(2,1)S(1)}, bf16[400,768]{1,0:T(8,128)(2,1)S(1)}, u32[]{:S(2)}, u32[]{:S(2)}) collective-permute-start(bf16[400,768]{1,0:T(8,128)(2,1)S(1)} %get-tuple-element.162.refs_4_), channel_id=1, source_target_pairs={{0,4},{4,0},{8,12},{12,8},{16,20},{20,16},{24,28},{28,24},{1,5},{5... | collective-permute-start | bytes 1843208 | tf_op jit(solution)/shard_map/ppermute | solution.py:1636
  198.6 7.7 %collective-permute-start.37 = (bf16[96,768]{1,0:T(8,128)(2,1)S(1)}, bf16[96,768]{1,0:T(8,128)(2,1)S(1)}, u32[]{:S(2)}, u32[]{:S(2)}) collective-permute-start(bf16[96,768]{1,0:T(8,128)(2,1)S(1)} %get-tuple-element.165), channel_id=1, source_target_pairs={{0,8},{4,12},{8,0},{12,4},{16,24},{20,28},{24,16},{28,20},{1,9},{5... | collective-permute-start | bytes 442376 | tf_op jit(solution)/shard_map/ppermute | solution.py:1636
  198.6 8.6 %collective-permute-start.38 = (bf16[96,768]{1,0:T(8,128)(2,1)S(1)}, bf16[96,768]{1,0:T(8,128)(2,1)S(1)}, u32[]{:S(2)}, u32[]{:S(2)}) collective-permute-start(bf16[96,768]{1,0:T(8,128)(2,1)S(1)} %get-tuple-element.166), channel_id=1, source_target_pairs={{0,24},{4,28},{8,16},{12,20},{16,8},{20,12},{24,0},{28,4},{1,25},{... | collective-permute-start | bytes 442376 | tf_op jit(solution)/shard_map/ppermute | solution.py:1636
  199.7 15.1 %collective-permute-start.36 = (bf16[96,768]{1,0:T(8,128)(2,1)S(1)}, bf16[96,768]{1,0:T(8,128)(2,1)S(1)}, u32[]{:S(2)}, u32[]{:S(2)}) collective-permute-start(bf16[96,768]{1,0:T(8,128)(2,1)S(1)} %get-tuple-element.160.refs_4_), channel_id=1, source_target_pairs={{0,16},{4,20},{8,24},{12,28},{16,0},{20,4},{24,8},{28,12},{1,17},{... | collective-permute-start | bytes 442376 | tf_op jit(solution)/shard_map/ppermute | solution.py:1636
  202.1 39.2 %collective-permute-start.54 = (bf16[384,768]{1,0:T(8,128)(2,1)S(1)}, bf16[384,768]{1,0:T(8,128)(2,1)S(1)}, u32[]{:S(2)}, u32[]{:S(2)}) collective-permute-start(bf16[384,768]{1,0:T(8,128)(2,1)S(1)} %join.3.refs_2_), channel_id=1, source_target_pairs={{0,4},{4,0},{8,12},{12,8},{16,20},{20,16},{24,28},{28,24},{1,5},{5... | collective-permute-start | bytes 1769480 | tf_op jit(solution)/shard_map/ppermute | solution.py:1636
  214.8 8.8 %collective-permute-start.47 = (bf16[96,768]{1,0:T(8,128)(2,1)S(1)}, bf16[96,768]{1,0:T(8,128)(2,1)S(1)}, u32[]{:S(2)}, u32[]{:S(2)}) collective-permute-start(bf16[96,768]{1,0:T(8,128)(2,1)S(1)} %gather_sum.4.refs_3_.refs_0_.refs_1_), channel_id=1, source_target_pairs={{0,24},{4,28},{8,16},{12,20},{16,8},{20,12},{24,0},{28,4},{1,25},{... | collective-permute-start | bytes 442376 | tf_op jit(solution)/shard_map/ppermute | solution.py:1636
  215.3 9.1 %collective-permute-start.46 = (bf16[96,768]{1,0:T(8,128)(2,1)S(1)}, bf16[96,768]{1,0:T(8,128)(2,1)S(1)}, u32[]{:S(2)}, u32[]{:S(2)}) collective-permute-start(bf16[96,768]{1,0:T(8,128)(2,1)S(1)} %gather_sum.4.refs_3_.refs_0_.refs_1_), channel_id=1, source_target_pairs={{0,8},{4,12},{8,0},{12,4},{16,24},{20,28},{24,16},{28,20},{1,9},{5... | collective-permute-start | bytes 442376 | tf_op jit(solution)/shard_map/ppermute | solution.py:1636
  215.3 15.2 %collective-permute-start.45 = (bf16[96,768]{1,0:T(8,128)(2,1)S(1)}, bf16[96,768]{1,0:T(8,128)(2,1)S(1)}, u32[]{:S(2)}, u32[]{:S(2)}) collective-permute-start(bf16[96,768]{1,0:T(8,128)(2,1)S(1)} %gather_sum.4.refs_3_.refs_0_.refs_1_), channel_id=1, source_target_pairs={{0,16},{4,20},{8,24},{12,28},{16,0},{20,4},{24,8},{28,12},{1,17},{... | collective-permute-start | bytes 442376 | tf_op jit(solution)/shard_map/ppermute | solution.py:1636
  219.4 20.0 %collective-permute-start.42 = (bf16[112,768]{1,0:T(8,128)(2,1)S(1)}, bf16[112,768]{1,0:T(8,128)(2,1)S(1)}, u32[]{:S(2)}, u32[]{:S(2)}) collective-permute-start(bf16[112,768]{1,0:T(8,128)(2,1)S(1)} %get-tuple-element.167.refs_4_), channel_id=1, source_target_pairs={{0,16},{4,20},{8,24},{12,28},{16,0},{20,4},{24,8},{28,12},{1,17},{... | collective-permute-start | bytes 516104 | tf_op jit(solution)/shard_map/ppermute | solution.py:1636
  223.6 8.7 %collective-permute-start.43 = (bf16[112,768]{1,0:T(8,128)(2,1)S(1)}, bf16[112,768]{1,0:T(8,128)(2,1)S(1)}, u32[]{:S(2)}, u32[]{:S(2)}) collective-permute-start(bf16[112,768]{1,0:T(8,128)(2,1)S(1)} %get-tuple-element.171), channel_id=1, source_target_pairs={{0,8},{4,12},{8,0},{12,4},{16,24},{20,28},{24,16},{28,20},{1,9},{5... | collective-permute-start | bytes 516104 | tf_op jit(solution)/shard_map/ppermute | solution.py:1636
  224.4 13.4 %collective-permute-start.44 = (bf16[112,768]{1,0:T(8,128)(2,1)S(1)}, bf16[112,768]{1,0:T(8,128)(2,1)S(1)}, u32[]{:S(2)}, u32[]{:S(2)}) collective-permute-start(bf16[112,768]{1,0:T(8,128)(2,1)S(1)} %get-tuple-element.172), channel_id=1, source_target_pairs={{0,24},{4,28},{8,16},{12,20},{16,8},{20,12},{24,0},{28,4},{1,25},{... | collective-permute-start | bytes 516104 | tf_op jit(solution)/shard_map/ppermute | solution.py:1636
  230.5 24.4 %collective-permute-start.40 = (bf16[256,768]{1,0:T(8,128)(2,1)S(1)}, bf16[256,768]{1,0:T(8,128)(2,1)S(1)}, u32[]{:S(2)}, u32[]{:S(2)}) collective-permute-start(bf16[256,768]{1,0:T(8,128)(2,1)S(1)} %get-tuple-element.169), channel_id=1, source_target_pairs={{0,2},{1,3},{2,0},{3,1},{4,6},{5,7},{6,4},{7,5},{8,10},{9,11},{10,... | collective-permute-start | bytes 1179656 | tf_op jit(solution)/shard_map/ppermute | solution.py:1636
  232.3 24.9 %collective-permute-start.49 = (bf16[288,768]{1,0:T(8,128)(2,1)S(1)}, bf16[288,768]{1,0:T(8,128)(2,1)S(1)}, u32[]{:S(2)}, u32[]{:S(2)}) collective-permute-start(bf16[288,768]{1,0:T(8,128)(2,1)S(1)} %get-tuple-element.177), channel_id=1, source_target_pairs={{0,2},{1,3},{2,0},{3,1},{4,6},{5,7},{6,4},{7,5},{8,10},{9,11},{10,... | collective-permute-start | bytes 1327112 | tf_op jit(solution)/shard_map/ppermute | solution.py:1636
  237.8 22.8 %collective-permute-start.56 = (bf16[384,768]{1,0:T(8,128)(2,1)S(1)}, bf16[384,768]{1,0:T(8,128)(2,1)S(1)}, u32[]{:S(2)}, u32[]{:S(2)}) collective-permute-start(bf16[384,768]{1,0:T(8,128)(2,1)S(1)} %join.4.refs_5_), channel_id=1, source_target_pairs={{0,4},{4,0},{8,12},{12,8},{16,20},{20,16},{24,28},{28,24},{1,5},{5... | collective-permute-start | bytes 1769480 | tf_op jit(solution)/shard_map/ppermute | solution.py:1636
  239.5 9.0 %collective-permute-start.53 = (bf16[96,768]{1,0:T(8,128)(2,1)S(1)}, bf16[96,768]{1,0:T(8,128)(2,1)S(1)}, u32[]{:S(2)}, u32[]{:S(2)}) collective-permute-start(bf16[96,768]{1,0:T(8,128)(2,1)S(1)} %get-tuple-element.174.refs_6_.refs_5_.refs_0_.refs_1_), channel_id=1, source_target_pairs={{0,24},{4,28},{8,16},{12,20},{16,8},{20,12},{24,0},{28,4},{1,25},{... | collective-permute-start | bytes 442376 | tf_op jit(solution)/shard_map/ppermute | solution.py:1636
  241.3 10.9 %collective-permute-start.52 = (bf16[96,768]{1,0:T(8,128)(2,1)S(1)}, bf16[96,768]{1,0:T(8,128)(2,1)S(1)}, u32[]{:S(2)}, u32[]{:S(2)}) collective-permute-start(bf16[96,768]{1,0:T(8,128)(2,1)S(1)} %get-tuple-element.174.refs_6_.refs_5_.refs_0_.refs_1_), channel_id=1, source_target_pairs={{0,8},{4,12},{8,0},{12,4},{16,24},{20,28},{24,16},{28,20},{1,9},{5... | collective-permute-start | bytes 442376 | tf_op jit(solution)/shard_map/ppermute | solution.py:1636
  252.2 10.4 %collective-permute-start.39 = (bf16[128,768]{1,0:T(8,128)(2,1)S(1)}, bf16[128,768]{1,0:T(8,128)(2,1)S(1)}, u32[]{:S(2)}, u32[]{:S(2)}) collective-permute-start(bf16[128,768]{1,0:T(8,128)(2,1)S(1)} %get-tuple-element.168.refs_5_), channel_id=1, source_target_pairs={{0,1},{1,0},{2,3},{3,2},{4,5},{5,4},{6,7},{7,6},{8,9},{9,8},{10,11... | collective-permute-start | bytes 589832 | tf_op jit(solution)/shard_map/ppermute | solution.py:1636
  254.9 9.3 %collective-permute-start.48 = (bf16[144,768]{1,0:T(8,128)(2,1)S(1)}, bf16[144,768]{1,0:T(8,128)(2,1)S(1)}, u32[]{:S(2)}, u32[]{:S(2)}) collective-permute-start(bf16[144,768]{1,0:T(8,128)(2,1)S(1)} %get-tuple-element.176), channel_id=1, source_target_pairs={{0,1},{1,0},{2,3},{3,2},{4,5},{5,4},{6,7},{7,6},{8,9},{9,8},{10,11... | collective-permute-start | bytes 663560 | tf_op jit(solution)/shard_map/ppermute | solution.py:1636
  254.9 7.8 %collective-permute-start.41 = (bf16[256,768]{1,0:T(8,128)(2,1)S(1)}, bf16[256,768]{1,0:T(8,128)(2,1)S(1)}, u32[]{:S(2)}, u32[]{:S(2)}) collective-permute-start(bf16[256,768]{1,0:T(8,128)(2,1)S(1)} %collective-permute-done.40.refs_4_), channel_id=1, source_target_pairs={{0,1},{1,0},{2,3},{3,2},{4,5},{5,4},{6,7},{7,6},{8,9},{9,8},{10,11... | collective-permute-start | bytes 1179656 | tf_op jit(solution)/shard_map/ppermute | solution.py:1636
  257.2 16.9 %collective-permute-start.55 = (bf16[384,768]{1,0:T(8,128)(2,1)S(1)}, bf16[384,768]{1,0:T(8,128)(2,1)S(1)}, u32[]{:S(2)}, u32[]{:S(2)}) collective-permute-start(bf16[384,768]{1,0:T(8,128)(2,1)S(1)} %join.5.refs_6_), channel_id=1, source_target_pairs={{0,4},{4,0},{8,12},{12,8},{16,20},{20,16},{24,28},{28,24},{1,5},{5... | collective-permute-start | bytes 1769480 | tf_op jit(solution)/shard_map/ppermute | solution.py:1636
  (60 other events, 628.1 us)

commit v3 on v2

--- a/solution.py
+++ b/solution.py
@@ -270,22 +270,25 @@
 def call(
     body, outs, out_specs, in_specs, scratch=(), us=2, room=16, name=None, after=()
 ):
-    n, extra = len(in_specs), len(after)
-
-    def trimmed(*refs):
-        body(*refs[:n], *refs[n + extra :])
-
     made = pl.pallas_call(
-        trimmed,
+        body,
         out_shape=outs,
-        in_specs=list(in_specs) + [HB] * extra,
+        in_specs=in_specs,
         out_specs=out_specs,
         scratch_shapes=list(scratch),
         compiler_params=pltpu.CompilerParams(vmem_limit_bytes=room * MIB),
         cost_estimate=pl.CostEstimate(flops=int(us * PACE), bytes_accessed=0, transcendentals=0),
         name=name,
     )
-    return lambda *args: made(*args, *after)
+
+    def run(*args):
+        if after:
+            args = list(args)
+            at = min(range(len(args)), key=lambda n: args[n].size)
+            args[at] = lax.optimization_barrier((args[at], *after))[0]
+        return made(*args)
+
+    return run
 
 
 def mm(a, b):
@@ -312,9 +315,12 @@
     return [(refs[0], 0), (refs[1], 0), (refs[2], 0), (refs[3], size)]
 
 
-def exchange(own, near, far):
+def exchange(own, near, far, before=()):
+    near = swap(near, "mp", 1)
     crossed = swap(far, "mp", 2)
-    return [own, swap(near, "mp", 1), crossed, swap(crossed, "mp", 1)]
+    if before:
+        crossed = lax.optimization_barrier((crossed, near, *before))[0]
+    return [own, near, crossed, swap(crossed, "mp", 1)]
 
 
 def prep_rows(route, seg, tokens, b_qv, b_in, weights, dims):
@@ -433,7 +439,7 @@
         [VM] * 4 + [SM] * 3,
         [VM, VM, HM, VM, VM, HM, HM],
         [pltpu.VMEM((8, total), jnp.int32), pltpu.SemaphoreType.DMA((rows + 4,))],
-        us=3,
+        us=2,
         name="prep_rows",
         room=60,
     )(route, seg, tokens, b_qv, b_in, *weights)
@@ -469,7 +475,7 @@
         VM,
         [HM] * n,
         [pltpu.SemaphoreType.DMA((n,))],
-        us=1,
+        us=0.1,
         name="prep_halves",
         room=4,
         after=after,
@@ -500,7 +506,7 @@
         [VM] * reach,
         [SM, HM],
         [pltpu.SemaphoreType.DMA((reach * cap,))],
-        us=2,
+        us=0.1,
         name="prep_cot",
         room=6,
         after=after,
@@ -535,19 +541,14 @@
     return lax.rem(lax.div(ids_ref[0], bit), 2)
 
 
-def load_parts(refs, bases, parity, half, dst, sems, at, row=0):
+def whole_block(refs, bases, parity, half, dst, row=0):
     if len(refs) == 1:
-        return [pltpu.make_async_copy(refs[0], dst, sems.at[at])]
-    copies = []
-    for j, place in enumerate((parity, 1 - parity)):
-        copies.append(
-            pltpu.make_async_copy(
-                refs[j].at[pl.ds(bases[j] + row, half)],
-                dst.at[pl.ds(pl.multiple_of(place * half, 16), half)],
-                sems.at[at + j],
-            )
-        )
-    return copies
+        return refs[0]
+    for ref, base, place in zip(refs, bases, (parity, 1 - parity)):
+        dst[pl.ds(pl.multiple_of(place * half, 16), half), :] = ref[
+            base + row : base + row + half, :
+        ]
+    return dst
 
 
 def bases_of(part):
@@ -570,16 +571,14 @@
         out = list(refs[count + len(flat) :])
         if keep_x:
             x_out = out.pop(0)
-        ol_out, qkv_out, p_out, x_ref, w_ref, sems = out
-        copies = []
+        ol_out, qkv_out, p_out, x_ref, w_ref = out
+        blocks = []
         at = 0
         for b, n in enumerate(n_parts):
-            copies += load_parts(
-                w_refs[at : at + n], bases_of(parts[b]), ids_ref[2], inner // 2, w_ref.at[b], sems, at
+            blocks.append(
+                whole_block(w_refs[at : at + n], bases_of(parts[b]), ids_ref[2], inner // 2, w_ref.at[b])
             )
             at += n
-        for copy in copies:
-            copy.start()
         for r in range(here):
             for kk in range(count):
                 ref, base = places[kk]
@@ -589,8 +588,6 @@
         if keep_x:
             x_out[...] = x_ref[...]
         masks = head_masks(head_width)
-        for copy in copies:
-            copy.wait()
         for b in range(2):
             ref, base = places[pair[b]]
             bias = bias_rows(ref, base + tile, 0)
@@ -599,7 +596,7 @@
             @pl.loop(0, here)
             def _(r):
                 start = pl.multiple_of(r * full, full)
-                projected = mm_nt(x_ref[pl.ds(start, full), :], w_ref[b])
+                projected = mm_nt(x_ref[pl.ds(start, full), :], blocks[b][...])
                 query = (projected[:, 0:head_width] + bias_q).astype(bf16)
                 key = projected[:, head_width : 2 * head_width].astype(bf16)
                 value = (projected[:, 2 * head_width :] + bias_v).astype(bf16)
@@ -631,11 +628,10 @@
         body,
         outs,
         [VM] * len(outs),
-        [SM, VM] + [VM] * count + [HB] * len(flat),
+        [SM, VM] + [VM] * (count + len(flat)),
         [
             pltpu.VMEM((tokens, width), bf16),
             pltpu.VMEM((2, inner, width), bf16),
-            pltpu.SemaphoreType.DMA((len(flat),)),
         ],
         us=10,
         name="attend",
@@ -680,52 +676,42 @@
         wo_refs = [refs.pop(0) for _ in range(n)]
         wi_refs = [refs.pop(0) for _ in range(2)]
         wd_refs = [refs.pop(0) for _ in range(2)]
-        al_out, hat_out, inv_out, acc_out, hl_out, gp_out, wo, wi, wd, sems = refs
-        first, later = [], []
+        al_out, hat_out, inv_out, acc_out, hl0, hl1, gp0, gp1, wo = refs
+        hl_out, gp_out = (hl0, hl1), (gp0, gp1)
+        w_out = []
         at = 0
         for kk in range(count):
             m = len(out_parts[kk])
-            first += load_parts(
-                wo_refs[at : at + m], bases_of(out_parts[kk]), ids_ref[2], head_width // 2, wo.at[kk],
-                sems, at, inner // 2,
+            w_out.append(
+                whole_block(
+                    wo_refs[at : at + m], bases_of(out_parts[kk]), ids_ref[2], head_width // 2,
+                    wo.at[kk], inner // 2,
+                )
             )
             at += m
-        for b in range(2):
-            later.append(
-                [
-                    pltpu.make_async_copy(wi_refs[b], wi.at[b], sems.at[n + 2 * b]),
-                    pltpu.make_async_copy(wd_refs[b], wd.at[b], sems.at[n + 2 * b + 1]),
-                ]
-            )
-        for copy in first + later[0] + later[1]:
-            copy.start()
         b_out, gain_a, bias_a = (v[...].reshape(1, width) for v in vec_refs)
-        for copy in first:
-            copy.wait()
         for r in range(here):
             span = slice(r * full, (r + 1) * full)
             total = x_ref[span, :].astype(f32) + b_out
             for kk in range(count):
                 ol = (ol_a, ol_b)[kk // 2]
-                total = total + mm(ol[kk % 2, span, :], wo[kk])
+                total = total + mm(ol[kk % 2, span, :], w_out[kk][...])
             hat, inverse = norm_rows(total)
             hat_out[span, :] = hat
             inv_out[span, :] = jnp.broadcast_to(inverse, (full, 128))
             al_out[span, :] = (hat * gain_a + bias_a).astype(bf16)
         half = tokens // 2
         for b in range(2):
-            for copy in later[b]:
-                copy.wait()
             ref, base = places[b]
             bias = bias_rows(ref, base + tile, 3)
             for m in range(2):
                 span = slice(m * half, (m + 1) * half)
-                u = mm(al_out[span, :], wi[b]) + bias
+                u = mm(al_out[span, :], wi_refs[b][...]) + bias
                 active, slope = gelu_pair(u)
                 active = active.astype(bf16)
-                hl_out[b, span, :] = active
-                gp_out[b, span, :] = slope.astype(bf16)
-                part = mm(active, wd[b])
+                hl_out[b][span, :] = active
+                gp_out[b][span, :] = slope.astype(bf16)
+                part = mm(active, wd_refs[b][...])
                 if b == 0:
                     acc_out[span, :] = part
                 else:
@@ -736,15 +722,12 @@
         body,
         [
             shape_of(wide), shape_of(wide, f32), shape_of((tokens, 128), f32), shape_of(wide, f32),
-            shape_of((2,) + wide), shape_of((2,) + wide),
+            *[shape_of(wide)] * 4,
         ],
-        [VM] * 6,
-        [SM, VM, VM, VM] + [VM] * (count + 3) + [HB] * (n + 4),
+        [VM] * 8,
+        [SM, VM, VM, VM] + [VM] * (count + n + 7),
         [
             pltpu.VMEM((count, head_width, width), bf16),
-            pltpu.VMEM((2, width, hidden), bf16),
-            pltpu.VMEM((2, hidden, width), bf16),
-            pltpu.SemaphoreType.DMA((n + 4,)),
         ],
         us=11,
         name="ffn_near",
@@ -765,38 +748,33 @@
     def body(ids_ref, al_ref, *refs):
         places = piece_places(refs[:count], tile + 16)
         w_refs = refs[count : count + n]
-        hl_out, gp_out, wi, sems = refs[count + n :]
-        copies = []
+        hl2, hl3, gp2, gp3, wi = refs[count + n :]
+        hl_out, gp_out = (hl2, hl3), (gp2, gp3)
+        blocks = []
         at = 0
         for b in range(2):
             m = len(parts[b])
-            copies.append(
-                load_parts(
-                    w_refs[at : at + m], bases_of(parts[b]), ids_ref[2], width // 2, wi.at[b], sems, at
-                )
+            blocks.append(
+                whole_block(w_refs[at : at + m], bases_of(parts[b]), ids_ref[2], width // 2, wi.at[b])
             )
             at += m
-        for copy in copies[0] + copies[1]:
-            copy.start()
         half = tokens // 2
         for b in range(2):
-            for copy in copies[b]:
-                copy.wait()
             ref, base = places[2 + b]
             bias = bias_rows(ref, base + tile, 3)
             for m in range(2):
                 span = slice(m * half, (m + 1) * half)
-                active, slope = gelu_pair(mm(al_ref[span, :], wi[b]) + bias)
-                hl_out[b, span, :] = active.astype(bf16)
-                gp_out[b, span, :] = slope.astype(bf16)
+                active, slope = gelu_pair(mm(al_ref[span, :], blocks[b][...]) + bias)
+                hl_out[b][span, :] = active.astype(bf16)
+                gp_out[b][span, :] = slope.astype(bf16)
 
     wide = (tokens, width)
     return call(
         body,
-        [shape_of((2,) + wide), shape_of((2,) + wide)],
-        [VM] * 2,
-        [SM, VM] + [VM] * count + [HB] * n,
-        [pltpu.VMEM((2, width, hidden), bf16), pltpu.SemaphoreType.DMA((n,))],
+        [shape_of(wide)] * 4,
+        [VM] * 4,
+        [SM, VM] + [VM] * (count + n),
+        [pltpu.VMEM((2, width, hidden), bf16)],
         us=6,
         name="ffn_far",
         room=14,
@@ -812,25 +790,23 @@
     flat = [ref for p in parts for ref, _ in p]
     n = len(flat)
 
-    def body(ids_ref, sent_ref, segr_ref, al_ref, near_ref, hl_near, hl_far, *refs):
+    def body(ids_ref, sent_ref, segr_ref, al_ref, near_ref, hl1, hl2, hl3, *refs):
+        hl_far = (hl2, hl3)
         refs = list(refs)
         vec_refs = [refs.pop(0) for _ in range(3)]
         og_refs = [refs.pop(0) for _ in range(reach)]
         pool_ref = refs.pop(0)
         w_refs = [refs.pop(0) for _ in range(n)]
-        tk0, tk1, pooled_out, dz_out, low_out, sums_out, down_out, wd, near, og_buf, acc_ref, sems = refs
+        tk0, tk1, pooled_out, dz_out, low_out, sums_out, down_out, wd, og_buf, acc_ref, sems = refs
         mi, parity = ids_ref[1], parity_of(ids_ref, 2)
-        groups = []
+        blocks = []
         at = 0
         for b in range(2):
             m = len(parts[b])
-            groups.append(
-                load_parts(
-                    w_refs[at : at + m], bases_of(parts[b]), parity, width // 2, wd.at[b], sems, at
-                )
+            blocks.append(
+                whole_block(w_refs[at : at + m], bases_of(parts[b]), parity, width // 2, wd.at[b])
             )
             at += m
-        sibling_hl = pltpu.make_async_copy(hl_near.at[1], near, sems.at[n])
         cots = []
         for k in range(reach):
             for c in range(cap):
@@ -840,19 +816,17 @@
                         pltpu.make_async_copy(
                             og_refs[k].at[c, pl.ds(pl.multiple_of((mi ^ kk) * quarter, quarter), quarter)],
                             og_buf.at[pl.ds(r * full + kk * quarter, quarter)],
-                            sems.at[n + 1 + r * count + kk],
+                            sems.at[r * count + kk],
                         )
                     )
-        for copy in groups[0] + groups[1] + cots + [sibling_hl]:
+        for copy in cots:
             copy.start()
         b_down, gain_f, bias_f = (v[...].reshape(1, width) for v in vec_refs)
         half = tokens // 2
         for b in range(2):
-            for copy in groups[b]:
-                copy.wait()
             for m in range(2):
                 span = slice(m * half, (m + 1) * half)
-                part = mm(hl_far[b, span, :], wd[b])
+                part = mm(hl_far[b][span, :], blocks[b][...])
                 if b == 0:
                     acc_ref[span, :] = part + near_ref[span, :]
                 else:
@@ -889,11 +863,10 @@
             sums_out[0:1, :] += jnp.sum(dz, axis=0, keepdims=True)
             sums_out[1:2, :] += jnp.sum(cot * hat, axis=0, keepdims=True)
             sums_out[2:3, :] += jnp.sum(cot, axis=0, keepdims=True)
-        sibling_hl.wait()
         for b in range(2):
             for c in range(hidden // 256):
                 cols = slice(c * 256, (c + 1) * 256)
-                left = near[:, cols] if b == 0 else hl_far[1, :, cols]
+                left = (hl1, hl3)[b][:, cols]
                 down_out[b, cols, :] = mm_tn(left, low_out[...]).astype(bf16)
 
     wide = (tokens, width)
@@ -905,13 +878,12 @@
             shape_of((8, width), f32), shape_of((2, hidden, width)),
         ],
         [VM] * 7,
-        [SM, SM, VM, VM, VM, HB, VM] + [VM] * 3 + [HB] * reach + [VM] + [HB] * n,
+        [SM, SM] + [VM] * 9 + [HB] * reach + [VM] * (1 + n),
         [
             pltpu.VMEM((2, hidden, width), bf16),
             pltpu.VMEM(wide, bf16),
-            pltpu.VMEM(wide, bf16),
             pltpu.VMEM(wide, f32),
-            pltpu.SemaphoreType.DMA((n + 1 + here * count,)),
+            pltpu.SemaphoreType.DMA((here * count,)),
         ],
         us=9,
         name="ffn_down",
@@ -926,96 +898,71 @@
     flat = [ref for p in parts for ref, _ in p]
     n = len(flat)
 
-    def body(ids_ref, low_ref, gp_near, gp_far, *refs):
-        dn_refs = refs[:n]
-        du_out, bin_out, wd, gpb, du, sems, out_sems = refs[n:]
+    def body(ids_ref, low_ref, *refs):
+        gp_refs, dn_refs = refs[:count], refs[count : count + n]
+        du_outs = refs[count + n : 2 * count + n]
+        bin_out, wd = refs[2 * count + n :]
         parity = parity_of(ids_ref, 2)
-        copies = []
+        blocks = []
         at = 0
         for kk in range(count):
             m = len(parts[kk])
-            copies.append(
-                load_parts(
-                    dn_refs[at : at + m], bases_of(parts[kk]), parity, width // 2, wd.at[kk], sems, at
+            blocks.append(
+                whole_block(
+                    dn_refs[at : at + m], bases_of(parts[kk]), parity, width // 2, wd.at[kk % 2],
                 )
-                + [
-                    pltpu.make_async_copy(
-                        (gp_near, gp_far)[kk // 2].at[kk % 2], gpb.at[kk], sems.at[n + kk]
-                    )
-                ]
             )
             at += m
-        outs = []
-        turn = (1, 3, 2, 0)
-        for kk in turn:
-            for copy in copies[kk]:
-                copy.start()
         half = tokens // 2
-        for kk in turn:
-            for copy in copies[kk]:
-                copy.wait()
+        for kk in (1, 3, 2, 0):
             total = jnp.zeros((1, hidden), f32)
             for m in range(2):
                 span = slice(m * half, (m + 1) * half)
-                part = (mm_nt(low_ref[span, :], wd[kk]) * gpb[kk, span, :].astype(f32)).astype(bf16)
-                du[kk, span, :] = part
+                part = (
+                    mm_nt(low_ref[span, :], blocks[kk][...]) * gp_refs[kk][span, :].astype(f32)
+                ).astype(bf16)
+                du_outs[kk][span, :] = part
                 total = total + jnp.sum(part.astype(f32), axis=0, keepdims=True)
             bin_out[kk : kk + 1, :] = total
-            copy = pltpu.make_async_copy(du.at[kk], du_out.at[kk], out_sems.at[kk])
-            copy.start()
-            outs.append(copy)
-        for copy in outs:
-            copy.wait()
-
-    return call(
-        body,
-        [shape_of((count, tokens, hidden)), shape_of((count, hidden), f32)],
-        [HB, VM],
-        [SM, VM, HB, HB] + [HB] * n,
-        [
-            pltpu.VMEM((count, hidden, width), bf16),
-            pltpu.VMEM((count, tokens, hidden), bf16),
-            pltpu.VMEM((count, tokens, hidden), bf16),
-            pltpu.SemaphoreType.DMA((n + count,)),
-            pltpu.SemaphoreType.DMA((count,)),
-        ],
+
+    return call(
+        body,
+        [shape_of((tokens, hidden))] * count + [shape_of((count, hidden), f32)],
+        [VM] * (count + 1),
+        [SM, VM] + [VM] * (count + n),
+        [pltpu.VMEM((2, hidden, width), bf16)],
         us=5,
         name="ffn_back",
         room=22,
     )(ids, low, *gps, *flat)
 
 
-def norm_back_attn(ids, du, al, dz, hat, inv, gain, parts, dims, after=()):
+def norm_back_attn(ids, dus, al, dz, hat, inv, gain, parts, dims, after=()):
     devices, count, rows, quarter, full, width = dims
     tokens = al.shape[0]
     hidden = width
     flat = [ref for p in parts for ref, _ in p]
     n = len(flat)
 
-    def body(ids_ref, du_ref, al_ref, dz_ref, hat_ref, inv_ref, vec_ref, *refs):
+    def body(ids_ref, al_ref, dz_ref, hat_ref, inv_ref, vec_ref, *refs):
+        du_refs, refs = refs[:count], refs[count:]
         oi_refs = refs[:n]
-        dz1_out, low_out, sums_out, in_out, wi, dub, acc, sems = refs[n:]
-        copies = []
+        dz1_out, low_out, sums_out, in_out, wi, acc = refs[n:]
+        blocks = []
         at = 0
         for kk in range(count):
             m = len(parts[kk])
-            copies.append(
-                [pltpu.make_async_copy(du_ref.at[kk], dub.at[kk], sems.at[n + kk])]
-                + load_parts(
-                    oi_refs[at : at + m], bases_of(parts[kk]), ids_ref[2], width // 2, wi.at[kk], sems, at
+            blocks.append(
+                whole_block(
+                    oi_refs[at : at + m], bases_of(parts[kk]), ids_ref[2], width // 2, wi.at[kk % 2]
                 )
             )
             at += m
-        for group in copies:
-            for copy in group:
-                copy.start()
         half = tokens // 2
         for kk in range(count):
-            for copy in copies[kk]:
-                copy.wait()
             for m in range(2):
                 span = slice(m * half, (m + 1) * half)
-                part = mm_nt(dub[kk, span, :], wi[kk])
+                part = mm_nt(du_refs[kk][span, :], blocks[kk][...])
                 if kk == 0:
                     acc[span, :] = part + dz_ref[span, :]
                 else:
@@ -1041,7 +988,7 @@
         for b, kk in enumerate((1, 3)):
             for c in range(width // 256):
                 cols = slice(c * 256, (c + 1) * 256)
-                in_out[b, cols, :] = mm_tn(al_ref[:, cols], dub[kk]).astype(bf16)
+                in_out[b, cols, :] = mm_tn(al_ref[:, cols], du_refs[kk][...]).astype(bf16)
 
     wide = (tokens, width)
     return call(
@@ -1051,18 +998,16 @@
             shape_of((2, width, hidden)),
         ],
         [VM] * 4,
-        [SM, HB, VM, VM, VM, VM, VM] + [HB] * n,
+        [SM] + [VM] * (5 + count + n),
         [
-            pltpu.VMEM((count, width, hidden), bf16),
-            pltpu.VMEM((count, tokens, hidden), bf16),
+            pltpu.VMEM((2, width, hidden), bf16),
             pltpu.VMEM(wide, f32),
-            pltpu.SemaphoreType.DMA((n + count,)),
         ],
         us=8,
         name="norm_back",
         room=26,
         after=after,
-    )(ids, du, al, dz, hat, inv, gain, *flat)
+    )(ids, al, dz, hat, inv, gain, *dus, *flat)
 
 
 def attend_back(ids, low, x, blocks, extras, dims, after=()):
@@ -1079,20 +1024,18 @@
     def body(ids_ref, low_ref, x_ref, bin_ref, ffn_ref, norm_ref, *refs):
         data = refs[: 3 * nb]
         w_refs = refs[3 * nb : 3 * nb + n]
-        mix_out, grad_out, wo, sums, sems = refs[3 * nb + n :]
-        copies = []
+        mix_out, grad_out, wo, sums = refs[3 * nb + n :]
+        w_out = []
         at = 0
         for b in range(nb):
             m = len(blocks[b][5])
-            copies += load_parts(
-                w_refs[at : at + m], bases_of(blocks[b][5]), ids_ref[2], half_out, wo.at[b], sems, at,
-                inner // 2,
+            w_out.append(
+                whole_block(
+                    w_refs[at : at + m], bases_of(blocks[b][5]), ids_ref[2], half_out, wo.at[b],
+                    inner // 2,
+                )
             )
             at += m
-        for copy in copies:
-            copy.start()
-        for copy in copies:
-            copy.wait()
         masks = head_masks(head_width)
         sums[...] = jnp.zeros_like(sums)
         for b in range(nb):
@@ -1102,7 +1045,7 @@
             @pl.loop(0, here)
             def _(r):
                 span = pl.ds(pl.multiple_of(r * full, full), full)
-                dol = mm_nt(low_ref[span, :], wo[b]).astype(bf16)
+                dol = mm_nt(low_ref[span, :], w_out[b][...]).astype(bf16)
                 query, key, value = (qkv_ref[place, i, span, :] for i in range(3))
                 low_p = p_ref[place, r]
                 prob = low_p.astype(f32)
@@ -1133,11 +1076,10 @@
         body,
         [shape_of((nb, tokens, inner)), shape_of((nb, width + 16, width))],
         [VM] * 2,
-        [SM] + [VM] * (5 + 3 * nb) + [HB] * n,
+        [SM] + [VM] * (5 + 3 * nb + n),
         [
             pltpu.VMEM((nb, head_width, width), bf16),
             pltpu.VMEM((8, width), f32),
-            pltpu.SemaphoreType.DMA((n,)),
         ],
         us=13,
         name="attend_back",
@@ -1155,36 +1097,23 @@
     return lines[0:8].astype(f32) + lines[8:16].astype(f32)
 
 
-def peer_grad(lhs, rhs, got, at, after=()):
+def peer_grad(lhs, rhs, got, after=()):
     tokens, width = rhs.shape
-    hidden = lhs.shape[-1]
-
-    def body(lhs_ref, rhs_ref, got_ref, out, a_buf, g_buf, sems):
-        copies = [
-            pltpu.make_async_copy(lhs_ref.at[at], a_buf, sems.at[0]),
-            pltpu.make_async_copy(got_ref.at[1], g_buf, sems.at[1]),
-        ]
-        for copy in copies:
-            copy.start()
-        for copy in copies:
-            copy.wait()
-        for c in range(hidden // 256):
+    rows = lhs.shape[1]
+
+    def body(lhs_ref, rhs_ref, got_ref, out):
+        for c in range(rows // 256):
             cols = slice(c * 256, (c + 1) * 256)
-            out[cols, :] = (mm_tn(a_buf[:, cols], rhs_ref[...]) + g_buf[cols, :].astype(f32)).astype(
-                bf16
-            )
-
-    return call(
-        body,
-        shape_of((hidden, width)),
+            out[cols, :] = (
+                mm_tn(lhs_ref[:, cols], rhs_ref[...]) + got_ref[1, cols, :].astype(f32)
+            ).astype(bf16)
+
+    return call(
+        body,
+        shape_of((rows, width)),
         VM,
-        [HB, VM, HB],
-        [
-            pltpu.VMEM((tokens, hidden), bf16),
-            pltpu.VMEM((hidden, width), bf16),
-            pltpu.SemaphoreType.DMA((2,)),
-        ],
-        us=3,
+        [VM, VM, VM],
+        us=0.2,
         name="peer_grad",
         room=10,
         after=after,
@@ -1202,85 +1131,33 @@
             send[q * size : (q + 1) * size, :] = rows.astype(bf16)
 
 
-def own_grad(ids, lhs, rhs, got, crossed, devices, lhs_own, after=()):
-    tokens = rhs.shape[-2]
-    width = rhs.shape[-1]
-    hidden = lhs.shape[-1]
+def own_grad(ids, lhs, rhs, got, crossed, devices, after=()):
+    tokens, width = rhs.shape
+    rows = lhs.shape[1]
     bits = devices.bit_length() - 1
-    size = hidden // devices
-
-    def body(ids_ref, lhs_ref, rhs_ref, got_ref, cross_ref, send, keep, a_buf, b_buf, g_buf, acc, sems):
-        copies = [
-            pltpu.make_async_copy(lhs_ref.at[0] if lhs_own else lhs_ref, a_buf, sems.at[0]),
-            pltpu.make_async_copy(rhs_ref if lhs_own else rhs_ref.at[0], b_buf, sems.at[1]),
-            pltpu.make_async_copy(got_ref.at[0], g_buf, sems.at[2]),
-        ]
-        for copy in copies:
-            copy.start()
-        for copy in copies:
-            copy.wait()
-        for c in range(hidden // 256):
+    size = rows // devices
+
+    def body(ids_ref, lhs_ref, rhs_ref, got_ref, cross_ref, send, keep, acc):
+        for c in range(rows // 256):
             cols = slice(c * 256, (c + 1) * 256)
             acc[cols, :] = (
-                mm_tn(a_buf[:, cols], b_buf[...])
-                + g_buf[cols, :].astype(f32)
+                mm_tn(lhs_ref[:, cols], rhs_ref[...])
+                + got_ref[0, cols, :].astype(f32)
                 + cross_ref[cols, :].astype(f32)
             )
         shards(acc, ids_ref, devices, bits, size, send, keep)
 
     return call(
         body,
-        [shape_of((hidden // 2, width)), shape_of((hidden // 2, width), f32)],
+        [shape_of((rows // 2, width)), shape_of((rows // 2, width), f32)],
         [VM, VM],
-        [SM, HB, HB, HB, VM],
-        [
-            pltpu.VMEM((tokens, hidden), bf16),
-            pltpu.VMEM((tokens, width), bf16),
-            pltpu.VMEM((hidden, width), bf16),
-            pltpu.VMEM((hidden, width), f32),
-            pltpu.SemaphoreType.DMA((3,)),
-        ],
-        us=3,
+        [SM, VM, VM, VM, VM],
+        [pltpu.VMEM((rows, width), f32)],
+        us=0.2,
         name="own_grad",
         room=14,
         after=after,
     )(ids, lhs, rhs, got, crossed)
-
-
-def peer_grad_in(al, du, got, after=()):
-    tokens, width = al.shape
-    hidden = du.shape[-1]
-
-    def body(al_ref, du_ref, got_ref, out, b_buf, g_buf, sems):
-        copies = [
-            pltpu.make_async_copy(du_ref.at[2], b_buf, sems.at[0]),
-            pltpu.make_async_copy(got_ref.at[1], g_buf, sems.at[1]),
-        ]
-        for copy in copies:
-            copy.start()
-        for copy in copies:
-            copy.wait()
-        for c in range(width // 256):
-            cols = slice(c * 256, (c + 1) * 256)
-            out[cols, :] = (mm_tn(al_ref[:, cols], b_buf[...]) + g_buf[cols, :].astype(f32)).astype(
-                bf16
-            )
-
-    return call(
-        body,
-        shape_of((width, hidden)),
-        VM,
-        [VM, HB, HB],
-        [
-            pltpu.VMEM((tokens, hidden), bf16),
-            pltpu.VMEM((width, hidden), bf16),
-            pltpu.SemaphoreType.DMA((2,)),
-        ],
-        us=3,
-        name="peer_grad_in",
-        room=10,
-        after=after,
-    )(al, du, got)
 
 
 def peer_last(grads, got, at, after=()):
@@ -1295,7 +1172,7 @@
         )
 
     return call(
-        body, shape_of((high, width)), VM, [VM, VM], us=2, name="peer_last",
+        body, shape_of((high, width)), VM, [VM, VM], us=0.2, name="peer_last",
         room=12,
         after=after,
     )(grads, got)
@@ -1332,7 +1209,7 @@
         [VM] * 3,
         [SM, VM, VM, VM],
         [pltpu.VMEM((body_rows, width), f32)],
-        us=3,
+        us=0.2,
         name="own_last",
         room=16,
         after=after,
@@ -1368,7 +1245,7 @@
         outs.append(shape_of((8, width), f32))
         args.append(vec)
     return call(
-        body, outs, [VM] * len(outs), [VM] * len(args), us=1, name="cut", room=8, after=after
+        body, outs, [VM] * len(outs), [VM] * len(args), us=0.1, name="cut", room=8, after=after
     )(*args)
 
 
@@ -1396,7 +1273,7 @@
         outs.append(shape_of((8, width), f32))
         args.append(vec)
     return call(
-        body, outs, [VM] * len(outs), [VM] * len(args), us=1, name="gather_sum", room=8, after=after
+        body, outs, [VM] * len(outs), [VM] * len(args), us=0.1, name="gather_sum", room=8, after=after
     )(*args)
 
 
@@ -1409,7 +1286,7 @@
             refs[n][p * size : (p + 1) * size, :] = refs[p][...]
 
     return call(
-        body, shape_of((n * size, width)), VM, [VM] * n, us=1, name="join", room=4, after=after
+        body, shape_of((n * size, width)), VM, [VM] * n, us=0.1, name="join", room=4, after=after
     )(*pieces)
 
 
@@ -1451,7 +1328,7 @@
         [VM] * len(cuts),
         [SM] + [VM] * n,
         [pltpu.VMEM((size * devices, width), f32)] if len(cuts) > 1 else [],
-        us=2,
+        us=0.5,
         name="whole_grad",
         room=12,
         after=after,
@@ -1471,26 +1348,23 @@
     def body(ids_ref, dz_ref, m_a, m_b, pool_ref, *refs):
         w_refs = refs[:n]
         own, near, far = refs[n : n + 3]
-        wq, acc, sems = refs[n + 3 :]
-        copies = []
+        wq, acc = refs[n + 3 :]
+        blocks = []
         at = 0
         for kk in range(count):
             m = len(parts[kk])
-            copies.append(
-                load_parts(w_refs[at : at + m], bases_of(parts[kk]), ids_ref[2], inner // 2, wq.at[kk], sems, at)
+            blocks.append(
+                whole_block(
+                    w_refs[at : at + m], bases_of(parts[kk]), ids_ref[2], inner // 2, wq.at[kk % 2]
+                )
             )
             at += m
-        for kk in turn:
-            for copy in copies[kk]:
-                copy.start()
         half = tokens // 2
         for i, kk in enumerate(turn):
-            for copy in copies[kk]:
-                copy.wait()
             mix = (m_a, m_b)[i // 2]
             for m in range(2):
                 span = slice(m * half, (m + 1) * half)
-                part = mm(mix[i % 2, span, :], wq[kk])
+                part = mm(mix[i % 2, span, :], blocks[kk][...])
                 if i == 0:
                     acc[span, :] = part + dz_ref[span, :]
                 else:
@@ -1507,11 +1381,10 @@
         body,
         [shape_of((m * (tile + here * SEGS), width)) for m in (1, 1, 2)],
         [VM] * 3,
-        [SM] + [VM] * 4 + [HB] * n,
+        [SM] + [VM] * (4 + n),
         [
-            pltpu.VMEM((count, inner, width), bf16),
+            pltpu.VMEM((2, inner, width), bf16),
             pltpu.VMEM((tokens, width), f32),
-            pltpu.SemaphoreType.DMA((n,)),
         ],
         us=6,
         name="grad_input_rows",
@@ -1551,7 +1424,7 @@
         [HB, VM],
         [SM] + [VM] * count,
         [pltpu.SemaphoreType.DMA((rows,))],
-        us=2,
+        us=0.5,
         name="land_grad",
         room=8,
         after=after,
@@ -1588,7 +1461,7 @@
         [VM, VM],
         [HB] * reach,
         [pltpu.SemaphoreType.DMA((3 * reach,))],
-        us=2,
+        us=0.1,
         name="turn_output",
         room=8,
         after=after,
@@ -1625,7 +1498,7 @@
         HB,
         [SM] + [VM] * (reach + count - 1),
         [pltpu.SemaphoreType.DMA((rows,))],
-        us=2,
+        us=0.5,
         name="land_output",
         room=8,
         after=after,
@@ -1664,10 +1537,10 @@
     *sends, segr, sent, spots, ids = prep_rows(
         route, seg, tokens_in, b_qv, b_in, (wq, w_out), dims
     )
-    pieces = exchange(*sends)
-
-    def sibling(values):
-        return tuple(swap(v, "mp", 1) for v in values)
+    near_q, near_o, near_i, near_d = (swap(v, "mp", 1) for v in (wq, w_out, w_in, w_down))
+    og_sends = prep_cot(spots, out_grad, dims, (near_q,))
+    ogs = [hop(og_sends[k], k) for k in range(reach)]
+    pieces = exchange(*sends, before=(near_q, near_o, near_i, near_d, *ogs))
 
     def later(values, after):
         return lax.optimization_barrier((values, after))[0]
@@ -1683,42 +1556,38 @@
 
     below = sends[2].shape[0] - half_rows
     relay_q = swap(pieces[2][below:], "dp", 1)
-    near_q, near_o = sibling((wq, w_out))
-    near_i, near_d = sibling((w_in, w_down))
     half_in = prep_halves((w_in,), 1, (pieces[2],))
     x, ol_a, qkv_a, p_a = attend(
         ids, segr, pieces, [[(wq, 0)], [(near_q, 0)]], (0, 1), inner, dims, True,
-        (near_o, near_i, near_d, half_in),
+        (half_in,),
     )
     relay_q3 = swap(later(relay_q, x), "mp", 1)
     far_q = [(pieces[2], below), (relay_q, 0)]
     far_q3 = [(pieces[3], below), (relay_q3, 0)]
     half_dn = prep_halves((w_down,), 2, (x,))
-    og_sends = prep_cot(spots, out_grad, dims, (half_dn,))
-    ogs = [hop(og_sends[k], k) for k in range(reach)]
     ol_b, qkv_b, p_b = attend(
-        ids, segr, pieces, [far_q, far_q3], (2, 3), inner, dims, False, (og_sends[0],)
+        ids, segr, pieces, [far_q, far_q3], (2, 3), inner, dims, False, (half_dn,)
     )
     q_parts = [[(wq, 0)], [(near_q, 0)], far_q, far_q3]
     wo_parts = [[(w_out, 0)], [(near_o, 0)], far_q, far_q3]
-    al, hat, inv, acc, hl, gp = ffn_near(
+    al, hat, inv, acc, hl0, hl1, gp0, gp1 = ffn_near(
         ids, x, (ol_a, ol_b), pieces, (b_out, gain_attn, bias_attn), wo_parts, (w_in, near_i),
         (w_down, near_d), inner, dims,
     )
     in_parts = [[(w_in, 0)], [(near_i, 0)], *crossed(half_in, 1, x, ol_b)]
-    dn_parts = [[(w_down, 0)], [(near_d, 0)], *crossed(half_dn, 2, ol_b, al)]
-    hl_far, gp_far = ffn_far(ids, al, pieces, in_parts[2:], dims)
+    hl2, hl3, gp2, gp3 = ffn_far(ids, al, pieces, in_parts[2:], dims)
+    dn_parts = [[(w_down, 0)], [(near_d, 0)], *crossed(half_dn, 2, ol_b, hl2)]
     tk0, tk1, pooled, dz, low, ffn_sums, down_pair = ffn_down(
-        ids, sent, segr, al, acc, (hl, hl_far), (b_down, gain_ffn, bias_ffn), ogs, pool_grad,
+        ids, sent, segr, al, acc, (hl1, hl2, hl3), (b_down, gain_ffn, bias_ffn), ogs, pool_grad,
         dn_parts[2:], dims,
     )
     got_down = swap(down_pair, "mp", 1)
-    du, bin_sums = ffn_back(ids, low, (gp, gp_far), dn_parts, dims)
-    down_far = peer_grad(hl_far, low, got_down, 0, (bin_sums,))
+    *dus, bin_sums = ffn_back(ids, low, (gp0, gp1, gp2, gp3), dn_parts, dims)
+    down_far = peer_grad(hl2, low, got_down, (bin_sums,))
     hops = [hop(t, k) for k, t in enumerate(lax.optimization_barrier((tk0, tk1, down_far))[:2])]
     crossed_down = swap(down_far, "mp", 2)
     dz1, low1, norm_sums, in_pair = norm_back_attn(
-        ids, du, al, dz, hat, inv, gain_attn, in_parts, dims, (down_far,)
+        ids, dus, al, dz, hat, inv, gain_attn, in_parts, dims, (down_far,)
     )
     got_in = swap(in_pair, "mp", 1)
     extras = (bin_sums, ffn_sums, norm_sums)
@@ -1728,11 +1597,11 @@
         extras, dims,
     )
     got_last = swap(grads_a, "mp", 1)
-    in_far = peer_grad_in(al, du, got_in, (grads_a,))
+    in_far = peer_grad(al, dus[2], got_in, (grads_a,))
     crossed_in = swap(in_far, "mp", 2)
     turned = turn_output(hops, dims, (in_far,))
     send_down, keep_down = own_grad(
-        ids, hl, low, got_down, crossed_down, devices, True, (turned[0],)
+        ids, hl0, low, got_down, crossed_down, devices, (turned[0],)
     )
     mix_b, grads_b = attend_back(
         ids, low1, x,
@@ -1751,34 +1620,34 @@
     (shard_down,) = gather_sum(cut_down[3], down_places, None, (gx[0],))
     down_spread = [shard_down] + places_of([shard_down] * 3)
     send_in, keep_in = own_grad(
-        ids, al, du, got_in, crossed_in, devices, False, (shard_down,)
+        ids, al, dus[0], got_in, crossed_in, devices, (shard_down,)
     )
     in_half = swap(send_in, "dp", 1)
-    half_down = join(down_spread, (send_in,))
+    cut_in = cut(keep_in, in_half, None, (send_in,))
+    in_places = places_of(cut_in[:3])
+    half_down = join(down_spread, (cut_in[0],))
     down_spread.append(swap(half_down, "dp", 1))
-    cut_in = cut(keep_in, in_half, None, (half_down,))
-    in_places = places_of(cut_in[:3])
+    (shard_in,) = gather_sum(cut_in[3], in_places, None, (half_down,))
+    in_spread = [shard_in] + places_of([shard_in] * 3)
     send, keep, vec = own_last(
-        ids, grads_b, got_last, crossed_last, 1, devices, (cut_in[0],)
+        ids, grads_b, got_last, crossed_last, 1, devices, (shard_in,)
     )
     last_half = swap(send, "dp", 1)
-    (shard_in,) = gather_sum(cut_in[3], in_places, None, (send,))
-    in_spread = [shard_in] + places_of([shard_in] * 3)
-    cut_last = cut(keep, last_half, vec, (shard_in,))
-    last_places = places_of(cut_last[:3])
-    *gx, turned_near, turned_far, _ = lax.optimization_barrier((*gx, *turned, cut_last[0]))
+    *gx, turned_near, turned_far, _ = lax.optimization_barrier((*gx, *turned, send))
     landed = exchange(None, turned_near, turned_far)[1:]
     gx_landed = exchange(*gx)
-    half_in = join(in_spread, (cut_last[0],))
+    half_in = join(in_spread, (send,))
     in_spread.append(swap(half_in, "dp", 1))
-    shard_last, vec = gather_sum(cut_last[3], last_places, cut_last[4], (half_in,))
+    cut_last = cut(keep, last_half, vec, (half_in,))
+    last_places = places_of(cut_last[:3])
+    shard_last, vec = gather_sum(cut_last[3], last_places, cut_last[4])
     last_spread = [shard_last] + places_of([shard_last] * 3)
-    tokens_out = land_output(spots, hops, landed, dims, (shard_last,))
-    grad_input, pooled_out = land_grad(sent, gx_landed, dims, (shard_last,))
-    (g_down,) = whole_grad(ids, down_spread, devices, (width,), (shard_last,))
-    half_last = join(last_spread, (g_down,))
+    half_last = join(last_spread, (shard_last,))
     last_spread.append(swap(half_last, "dp", 1))
+    (g_down,) = whole_grad(ids, down_spread, devices, (width,), (half_last,))
     (g_in,) = whole_grad(ids, in_spread, devices, (width,), (half_last,))
+    tokens_out = land_output(spots, hops, landed, dims, (half_last,))
+    grad_input, pooled_out = land_grad(sent, gx_landed, dims, (half_last,))
     g_qkv, g_out = whole_grad(ids, last_spread, devices, (inner, head_width))
     g_qkv = g_qkv.reshape(3, head_width, width).transpose(2, 0, 1)
     g_bqv = jnp.stack([vec[0, :head_width], vec[0, 256 : 256 + head_width]])

time: 282 us -> 257 us (0.911)
  Pallas kernels: 104 us -> 95.1 us
  waiting for transfers between devices: 97.9 us -> 89.4 us
  starting transfers between devices: 61.8 us -> 57.4 us
    ppermute x53, waiting for transfers between devices: 97.9 us -> 87 us  [swap(): lax.ppermute(values, axis, [(i, i ^ bit) for i in range(lax.axis_size(axi...]
    pallas_call x35, Pallas kernels: 104 us -> 95.1 us  [run(): return made(*args)]
    ppermute x53, starting transfers between devices: 49.3 us -> 45.2 us  [swap(): lax.ppermute(values, axis, [(i, i ^ bit) for i in range(lax.axis_size(axi...]
  transfers between devices with their start and end apart: 57 -> 57, of which waited for: 26 -> 24; matrix products, arithmetic and copies ran while one was open for 0% -> 1% of each run, Pallas kernels for 31% -> 33%
where the time goes in v3:
time: 257 us; the launch traced here: 252 us
  Pallas kernels  95.1 us (37%)
  waiting for transfers between devices  89.4 us (35%)
  starting transfers between devices  57.4 us (22%)
  local copies, waits for them, and re-layouts  8 us (3%)
    pallas_call x35, Pallas kernels, run(): return made(*args)  95.1 us
    ppermute x53, waiting for transfers between devices, swap(): lax.ppermute(values, axis, [(i, i ^ bit) for i in range(lax.axis_size(axi...  87 us
    ppermute x53, starting transfers between devices, swap(): lax.ppermute(values, axis, [(i, i ^ bit) for i in range(lax.axis_size(axi...  45.2 us
    ppermute x4, starting transfers between devices, hop(): lax.ppermute(values, ('dp', 'mp'), [(s * count + f, (s ^ f + count * k) *...  12.1 us
    unnamed x102, local copies, waits for them, and re-layouts  7.31 us
  transfers between devices with their start and end apart: 57, of which 24 were waited for; matrix products, arithmetic and copies ran while one was open for 1% of the time, Pallas kernels for 33%

profile of v3, /device:TPU:4, one launch (start us, length us, event | category | flops | bytes accessed | tf_op | source)
XLA Modules:
  0.0 252.2 jit_solution(16442034590436150795)
XLA Ops:
  1.3 4.1 %prep_rows.1 = (bf16[144,768]{1,0:T(8,128)(2,1)}, bf16[144,768]{1,0:T(8,128)(2,1)}, bf16[672,768]{1,0:T(8,128)(2,1)}, s32[8,128]{1,0:T(8,128)}, s32[128]{0:T(128)}, /*index=5*/s32[128]{0:T(128)}, s32[3]{0:T(128)}) custom-call(s32[128]{0:T(128)} %route_ref.1, s32[128,128]{1,0:T(8,128)} %seg_ref.1, bf16[16,32,768]{2,1,0:T(8,128)(2,1)} %tok.1, ...), custom_call_target="tpu_custom_call" | custom-call | flops 4000000000 | tf_op jit(solution)/shard_map/prep_rows/pallas_call | solution.py:289
  8.4 4.0 %collective-permute-start.6 = (bf16[2,128,768]{2,1,0:T(8,128)(2,1)S(1)}, bf16[2,128,768]{2,1,0:T(8,128)(2,1)S(1)}, u32[]{:S(2)}, u32[]{:S(2)}) collective-permute-start(bf16[2,128,768]{2,1,0:T(8,128)(2,1)S(1)} %get-tuple-element.139), channel_id=1, source_target_pairs={{0,0},{1,5},{2,10},{3,15},{4,4},{5,1},{6,14},{7,11},{8,8},{9,13},{... | collective-permute-start | bytes 1179656 | tf_op jit(solution)/shard_map/ppermute | solution.py:1525
  12.5 2.5 %collective-permute-start.7 = (bf16[2,128,768]{2,1,0:T(8,128)(2,1)S(1)}, bf16[2,128,768]{2,1,0:T(8,128)(2,1)S(1)}, u32[]{:S(2)}, u32[]{:S(2)}) collective-permute-start(bf16[2,128,768]{2,1,0:T(8,128)(2,1)S(1)} %get-tuple-element.140), channel_id=1, source_target_pairs={{0,16},{1,21},{2,26},{3,31},{4,20},{5,17},{6,30},{7,27},{8,24},{9,... | collective-permute-start | bytes 1179656 | tf_op jit(solution)/shard_map/ppermute | solution.py:1525
  15.0 15.8 %collective-permute-done.refs_2_.refs_4_.refs_9_.refs_6_ = bf16[672,768]{1,0:T(8,128)(2,1)S(1)} collective-permute-done((bf16[672,768]{1,0:T(8,128)(2,1)}, bf16[672,768]{1,0:T(8,128)(2,1)S(1)}, u32[]{:S(2)}, u32[]{:S(2)}) %collective-permute-start) | collective-permute-done | bytes 1032224 | tf_op jit(solution)/shard_map/ppermute | solution.py:1509
  30.9 2.4 collective-permute-done.7.refs_4_
  36.0 9.0 %attend.2 = (bf16[512,768]{1,0:T(8,128)(2,1)S(1)}, bf16[2,512,192]{2,1,0:T(8,128)(2,1)S(1)}, bf16[2,3,512,192]{3,2,1,0:T(8,128)(2,1)S(1)}, bf16[2,4,384,128]{3,2,1,0:T(8,128)(2,1)S(1)}) custom-call(s32[3]{0:T(128)S(1)} %copy-done.3, s32[8,128]{1,0:T(8,128)S(1)} %copy-done.50, bf16[144,768]{1,0:T(8,128)(2,1)S(1)} %copy-done.19, ...), custom_call_target="tpu_custom_call" | custom-call | flops 20000000000 | tf_op jit(solution)/shard_map/attend/pallas_call | solution.py:289
  45.9 3.5 %collective-permute-done.9.refs_5_.refs_10_.refs_7_.refs_3_ = bf16[384,768]{1,0:T(8,128)(2,1)S(1)} collective-permute-done((bf16[384,768]{1,0:T(8,128)(2,1)S(1)}, bf16[384,768]{1,0:T(8,128)(2,1)S(1)}, u32[]{:S(2)}, u32[]{:S(2)}) %collective-permute-start.9) | collective-permute-done | bytes 589856 | tf_op jit(solution)/shard_map/ppermute | solution.py:1509
  52.5 9.6 %attend.3 = (bf16[2,512,192]{2,1,0:T(8,128)(2,1)S(1)}, bf16[2,3,512,192]{3,2,1,0:T(8,128)(2,1)S(1)}, bf16[2,4,384,128]{3,2,1,0:T(8,128)(2,1)S(1)}) custom-call(s32[3]{0:T(128)S(1)} %copy-done.3, s32[8,128]{1,0:T(8,128)S(1)} %copy-done.50, bf16[144,768]{1,0:T(8,128)(2,1)S(1)} %copy-done.19, bf16[144,768]{1,0:T(8,128)(2,1)S(1)} %collective-permute-done.1.refs_1_, ...), custom_call_target="tpu_custom_call" | custom-call | flops 20000000000 | tf_op jit(solution)/shard_map/attend/pallas_call | solution.py:289
  67.1 7.4 %ffn_near.1 = (bf16[512,768]{1,0:T(8,128)(2,1)S(1)}, f32[512,768]{1,0:T(8,128)S(1)}, f32[512,128]{1,0:T(8,128)S(1)}, f32[512,768]{1,0:T(8,128)S(1)}, bf16[512,76...) custom-call(s32[3]{0:T(128)S(1)} %copy-done.3, ...), custom_call_target="tpu_custom_call" | custom-call | flops 22000001024 | tf_op jit(solution)/shard_map/ffn_near/pallas_call | solution.py:289
  74.6 4.4 %ffn_far.1 = (bf16[512,768]{1,0:T(8,128)(2,1)S(1)}, bf16[512,768]{1,0:T(8,128)(2,1)S(1)}, bf16[512,768]{1,0:T(8,128)(2,1)S(1)}, bf16[512,768]{1,0:T(8,128)(2,1)S(1)}) custom-call(s32[3]{0:T(128)S(1)} %copy-done.3, bf16[512,768]{1,0:T(8,128)(2,1)S(1)} %get-tuple-element.187.al_ref.lhs_ref, bf16[144,768]{1,0:T(8,128)(2,1)S(1)} %copy-done.19, ...), custom_call_target="tpu_custom_call" | custom-call | flops 12000000000 | tf_op jit(solution)/shard_map/ffn_far/pallas_call | solution.py:289
  79.1 2.1 collective-permute-done.16.refs_7_
  81.1 2.0 collective-permute-done.18.refs_9_
  83.2 7.7 %ffn_down.1 = (bf16[4,64,768]{2,1,0:T(8,128)(2,1)}, bf16[4,64,768]{2,1,0:T(8,128)(2,1)}, f32[16,768]{1,0:T(8,128)S(1)}, f32[512,768]{1,0:T(8,128)S(1)}, bf16[512...) custom-call(s32[3]{0:T(128)S(1)} %copy-done.3, s32[128]{0:T(128)S(1)} %copy-done.49, ...), custom_call_target="tpu_custom_call" | custom-call | flops 17999998976 | tf_op jit(solution)/shard_map/ffn_down/pallas_call | solution.py:289
  91.1 4.4 %ffn_back.1 = (bf16[512,768]{1,0:T(8,128)(2,1)S(1)}, bf16[512,768]{1,0:T(8,128)(2,1)S(1)}, bf16[512,768]{1,0:T(8,128)(2,1)S(1)}, bf16[512,768]{1,0:T(8,128)(2,1)S(1)}, f32[4,768]{1,0:T(4,128)S(1)}) custom-call(s32[3]{0:T(128)S(1)} %copy-done.3, bf16[512,768]{1,0:T(8,128)(2,1)S(1)} %get-tuple-element.162.low_ref.rhs_ref, ...), custom_call_target="tpu_custom_call" | custom-call | flops 10000000000 | tf_op jit(solution)/shard_map/ffn_back/pallas_call | solution.py:289
  96.3 1.8 collective-permute-start.23
  98.0 2.2 collective-permute-start.20
  100.2 3.4 %collective-permute-start.22 = (bf16[4,64,768]{2,1,0:T(8,128)(2,1)}, bf16[4,64,768]{2,1,0:T(8,128)(2,1)S(1)}, u32[]{:S(2)}, u32[]{:S(2)}) collective-permute-start(bf16[4,64,768]{2,1,0:T(8,128)(2,1)} %get-tuple-element.190), channel_id=1, source_target_pairs={{0,16},{1,21},{2,26},{3,31},{4,20},{5,17},{6,30},{7,27},{8,24},{9,... | collective-permute-start | bytes 1179656 | tf_op jit(solution)/shard_map/ppermute | solution.py:1525
  103.7 6.9 %norm_back.1 = (f32[512,768]{1,0:T(8,128)S(1)}, bf16[512,768]{1,0:T(8,128)(2,1)S(1)}, f32[8,768]{1,0:T(8,128)S(1)}, bf16[2,768,768]{2,1,0:T(8,128)(2,1)S(1)}) custom-call(s32[3]{0:T(128)S(1)} %copy-done.3, bf16[512,768]{1,0:T(8,128)(2,1)S(1)} %get-tuple-element.187.al_ref.lhs_ref, f32[512,768]{1,0:T(8,128)S(1)} %get-tuple-element.172.dz_ref, ...), custom_call_target="tpu_custom_call" | custom-call | flops 16000000000 | tf_op jit(solution)/shard_map/norm_back/pallas_call | solution.py:289
  113.5 9.1 %attend_back.2 = (bf16[2,512,576]{2,1,0:T(8,128)(2,1)S(1)}, bf16[2,784,768]{2,1,0:T(8,128)(2,1)S(1)}) custom-call(s32[3]{0:T(128)S(1)} %copy-done.3, bf16[512,768]{1,0:T(8,128)(2,1)S(1)} %get-tuple-element.179.low_ref, bf16[512,768]{1,0:T(8,128)(2,1)S(1)} %copy-done.38, f32[4,768]{1,0:T(4,128)S(1)} %get-tuple-element.167.bin_ref, ...), custom_call_target="tpu_custom_call" | custom-call | flops 25999998976 | tf_op jit(solution)/shard_map/attend_back/pallas_call | solution.py:289
  129.0 9.4 %attend_back.3 = (bf16[2,512,576]{2,1,0:T(8,128)(2,1)S(1)}, bf16[2,784,768]{2,1,0:T(8,128)(2,1)S(1)}) custom-call(s32[3]{0:T(128)S(1)} %copy-done.3, bf16[512,768]{1,0:T(8,128)(2,1)S(1)} %copy-done.27, bf16[512,768]{1,0:T(8,128)(2,1)S(1)} %copy-done.39, f32[4,768]{1,0:T(4,128)S(1)} %get-tuple-element.167.bin_ref, f32[8,768]{1,0:T(8,128)S(1)} %get-tuple-element.180.ffn_ref, ...), custom_call_target="tpu_custom_call" | custom-call | flops 25999998976 | tf_op jit(solution)/shard_map/attend_back/pallas_call | solution.py:289
  138.7 2.1 collective-permute-start.37
  140.8 2.0 collective-permute-done.25.refs_1_
  144.4 3.0 %collective-permute-start.28 = (bf16[96,768]{1,0:T(8,128)(2,1)S(1)}, bf16[96,768]{1,0:T(8,128)(2,1)S(1)}, u32[]{:S(2)}, u32[]{:S(2)}) collective-permute-start(bf16[96,768]{1,0:T(8,128)(2,1)S(1)} %get-tuple-element.209), channel_id=1, source_target_pairs={{0,24},{4,28},{8,16},{12,20},{16,8},{20,12},{24,0},{28,4},{1,25},{... | collective-permute-start | bytes 442376 | tf_op jit(solution)/shard_map/ppermute | solution.py:1509
  147.4 3.2 %grad_input_rows.1 = (bf16[144,768]{1,0:T(8,128)(2,1)S(1)}, bf16[144,768]{1,0:T(8,128)(2,1)S(1)}, bf16[288,768]{1,0:T(8,128)(2,1)S(1)}) custom-call(s32[3]{0:T(128)S(1)} %copy-done.3, f32[512,768]{1,0:T(8,128)S(1)} %copy-done.21, bf16[2,512,576]{2,1,0:T(8,128)(2,1)S(1)} %copy-done.23, bf16[2,512,576]{2,1,0:T(8,128)(2,1)S(1)} %get-tuple-element.204.m_b, ...), custom_call_target="tpu_custom_call" | custom-call | flops 12000000000 | tf_op jit(solution)/shard_map/grad_input_rows/pallas_call | solution.py:289
  150.6 4.1 %collective-permute-done.27.refs_2_ = bf16[96,768]{1,0:T(8,128)(2,1)S(1)} collective-permute-done((bf16[96,768]{1,0:T(8,128)(2,1)S(1)}, bf16[96,768]{1,0:T(8,128)(2,1)S(1)}, u32[]{:S(2)}, u32[]{:S(2)}) %collective-permute-start.27) | collective-permute-done | bytes 147488 | tf_op jit(solution)/shard_map/ppermute | solution.py:1509
  154.7 3.0 %collective-permute-done.29.cross_ref = bf16[768,768]{1,0:T(8,128)(2,1)S(1)} collective-permute-done((bf16[768,768]{1,0:T(8,128)(2,1)S(1)}, bf16[768,768]{1,0:T(8,128)(2,1)S(1)}, u32[]{:S(2)}, u32[]{:S(2)}) %collective-permute-start.29) | collective-permute-done | bytes 1179680 | tf_op jit(solution)/shard_map/ppermute | solution.py:1509
  161.4 2.9 %collective-permute-start.31 = (bf16[96,768]{1,0:T(8,128)(2,1)S(1)}, bf16[96,768]{1,0:T(8,128)(2,1)S(1)}, u32[]{:S(2)}, u32[]{:S(2)}) collective-permute-start(bf16[96,768]{1,0:T(8,128)(2,1)S(1)} %gather_sum.3.refs_0_), channel_id=1, source_target_pairs={{0,16},{4,20},{8,24},{12,28},{16,0},{20,4},{24,8},{28,12},{1,17},{... | collective-permute-start | bytes 442376 | tf_op jit(solution)/shard_map/ppermute | solution.py:1509
  164.3 8.1 %collective-permute-done.30.refs_1_ = bf16[384,768]{1,0:T(8,128)(2,1)S(1)} collective-permute-done((bf16[384,768]{1,0:T(8,128)(2,1)S(1)}, bf16[384,768]{1,0:T(8,128)(2,1)S(1)}, u32[]{:S(2)}, u32[]{:S(2)}) %collective-permute-start.30) | collective-permute-done | bytes 589856 | tf_op jit(solution)/shard_map/ppermute | solution.py:1509
  172.5 2.1 collective-permute-start.35
  176.2 4.3 %collective-permute-done.35.refs_2_ = bf16[96,768]{1,0:T(8,128)(2,1)S(1)} collective-permute-done((bf16[96,768]{1,0:T(8,128)(2,1)S(1)}, bf16[96,768]{1,0:T(8,128)(2,1)S(1)}, u32[]{:S(2)}, u32[]{:S(2)}) %collective-permute-start.35) | collective-permute-done | bytes 147488 | tf_op jit(solution)/shard_map/ppermute | solution.py:1509
  180.5 2.6 %collective-permute-done.36.refs_3_ = bf16[96,768]{1,0:T(8,128)(2,1)S(1)} collective-permute-done((bf16[96,768]{1,0:T(8,128)(2,1)S(1)}, bf16[96,768]{1,0:T(8,128)(2,1)S(1)}, u32[]{:S(2)}, u32[]{:S(2)}) %collective-permute-start.36) | collective-permute-done | bytes 147488 | tf_op jit(solution)/shard_map/ppermute | solution.py:1509
  183.1 5.0 %collective-permute-done.34.refs_1_ = bf16[96,768]{1,0:T(8,128)(2,1)S(1)} collective-permute-done((bf16[96,768]{1,0:T(8,128)(2,1)S(1)}, bf16[96,768]{1,0:T(8,128)(2,1)S(1)}, u32[]{:S(2)}, u32[]{:S(2)}) %collective-permute-start.34) | collective-permute-done | bytes 147488 | tf_op jit(solution)/shard_map/ppermute | solution.py:1509
  192.6 2.9 %collective-permute-start.39 = (bf16[96,768]{1,0:T(8,128)(2,1)S(1)}, bf16[96,768]{1,0:T(8,128)(2,1)S(1)}, u32[]{:S(2)}, u32[]{:S(2)}) collective-permute-start(bf16[96,768]{1,0:T(8,128)(2,1)S(1)} %gather_sum.4.refs_0_), channel_id=1, source_target_pairs={{0,16},{4,20},{8,24},{12,28},{16,0},{20,4},{24,8},{28,12},{1,17},{... | collective-permute-start | bytes 442376 | tf_op jit(solution)/shard_map/ppermute | solution.py:1509
  195.4 4.1 %collective-permute-done.41.refs_3_ = bf16[96,768]{1,0:T(8,128)(2,1)S(1)} collective-permute-done((bf16[96,768]{1,0:T(8,128)(2,1)S(1)}, bf16[96,768]{1,0:T(8,128)(2,1)S(1)}, u32[]{:S(2)}, u32[]{:S(2)}) %collective-permute-start.41) | collective-permute-done | bytes 147488 | tf_op jit(solution)/shard_map/ppermute | solution.py:1509
  201.1 2.8 %collective-permute-done.39.refs_1_ = bf16[96,768]{1,0:T(8,128)(2,1)S(1)} collective-permute-done((bf16[96,768]{1,0:T(8,128)(2,1)S(1)}, bf16[96,768]{1,0:T(8,128)(2,1)S(1)}, u32[]{:S(2)}, u32[]{:S(2)}) %collective-permute-start.39) | collective-permute-done | bytes 147488 | tf_op jit(solution)/shard_map/ppermute | solution.py:1509
  205.0 2.2 collective-permute-start.43
  208.5 4.9 %collective-permute-done.42.refs_1_ = bf16[112,768]{1,0:T(8,128)(2,1)S(1)} collective-permute-done((bf16[112,768]{1,0:T(8,128)(2,1)S(1)}, bf16[112,768]{1,0:T(8,128)(2,1)S(1)}, u32[]{:S(2)}, u32[]{:S(2)}) %collective-permute-start.42) | collective-permute-done | bytes 172064 | tf_op jit(solution)/shard_map/ppermute | solution.py:1509
  213.4 2.0 collective-permute-start.44
  216.1 5.0 %collective-permute-done.44.refs_3_ = bf16[112,768]{1,0:T(8,128)(2,1)S(1)} collective-permute-done((bf16[112,768]{1,0:T(8,128)(2,1)S(1)}, bf16[112,768]{1,0:T(8,128)(2,1)S(1)}, u32[]{:S(2)}, u32[]{:S(2)}) %collective-permute-start.44) | collective-permute-done | bytes 172064 | tf_op jit(solution)/shard_map/ppermute | solution.py:1509
  223.7 1.9 collective-permute-start.45
  225.7 4.3 %collective-permute-done.47.refs_3_ = bf16[96,768]{1,0:T(8,128)(2,1)S(1)} collective-permute-done((bf16[96,768]{1,0:T(8,128)(2,1)S(1)}, bf16[96,768]{1,0:T(8,128)(2,1)S(1)}, u32[]{:S(2)}, u32[]{:S(2)}) %collective-permute-start.47) | collective-permute-done | bytes 147488 | tf_op jit(solution)/shard_map/ppermute | solution.py:1509
  230.5 4.8 %collective-permute-done.45.refs_1_ = bf16[96,768]{1,0:T(8,128)(2,1)S(1)} collective-permute-done((bf16[96,768]{1,0:T(8,128)(2,1)S(1)}, bf16[96,768]{1,0:T(8,128)(2,1)S(1)}, u32[]{:S(2)}, u32[]{:S(2)}) %collective-permute-start.45) | collective-permute-done | bytes 147488 | tf_op jit(solution)/shard_map/ppermute | solution.py:1509
  235.3 1.9 collective-permute-start.54
  238.9 2.1 whole_grad.5
  241.0 2.1 whole_grad.4
  244.7 2.2 land_grad.1
  247.0 2.8 %collective-permute-done.54.refs_4_ = bf16[384,768]{1,0:T(8,128)(2,1)S(1)} collective-permute-done((bf16[384,768]{1,0:T(8,128)(2,1)S(1)}, bf16[384,768]{1,0:T(8,128)(2,1)S(1)}, u32[]{:S(2)}, u32[]{:S(2)}) %collective-permute-start.54) | collective-permute-done | bytes 589856 | tf_op jit(solution)/shard_map/ppermute | solution.py:1509
  249.8 2.2 whole_grad.3
  (207 shorter events, 48.3 us)
Async XLA Ops:
  0.7 30.1 %collective-permute-start.4 = (bf16[768,768]{1,0:T(8,128)(2,1)}, bf16[768,768]{1,0:T(8,128)(2,1)}, u32[]{:S(2)}, u32[]{:S(2)}) collective-permute-start(bf16[768,768]{1,0:T(8,128)(2,1)} %refs_4_.5), channel_id=1, source_target_pairs={{0,1},{1,0},{2,3},{3,2},{4,5},{5,4},{6,7},{7,6},{8,9},{9,8},{10,11... | collective-permute-start | bytes 3538952 | tf_op jit(solution)/shard_map/ppermute | solution.py:1509
  1.2 29.7 %collective-permute-start.5 = (bf16[768,768]{1,0:T(8,128)(2,1)}, bf16[768,768]{1,0:T(8,128)(2,1)}, u32[]{:S(2)}, u32[]{:S(2)}) collective-permute-start(bf16[768,768]{1,0:T(8,128)(2,1)} %refs_4_.4), channel_id=1, source_target_pairs={{0,1},{1,0},{2,3},{3,2},{4,5},{5,4},{6,7},{7,6},{8,9},{9,8},{10,11... | collective-permute-start | bytes 3538952 | tf_op jit(solution)/shard_map/ppermute | solution.py:1509
  5.4 25.4 %collective-permute-start = (bf16[672,768]{1,0:T(8,128)(2,1)}, bf16[672,768]{1,0:T(8,128)(2,1)S(1)}, u32[]{:S(2)}, u32[]{:S(2)}) collective-permute-start(bf16[672,768]{1,0:T(8,128)(2,1)} %get-tuple-element.136), channel_id=1, source_target_pairs={{0,2},{1,3},{2,0},{3,1},{4,6},{5,7},{6,4},{7,5},{8,10},{9,11},{10,... | collective-permute-start | bytes 3096584 | tf_op jit(solution)/shard_map/ppermute | solution.py:1509
  8.4 22.4 %collective-permute-start.6 = (bf16[2,128,768]{2,1,0:T(8,128)(2,1)S(1)}, bf16[2,128,768]{2,1,0:T(8,128)(2,1)S(1)}, u32[]{:S(2)}, u32[]{:S(2)}) collective-permute-start(bf16[2,128,768]{2,1,0:T(8,128)(2,1)S(1)} %get-tuple-element.139), channel_id=1, source_target_pairs={{0,0},{1,5},{2,10},{3,15},{4,4},{5,1},{6,14},{7,11},{8,8},{9,13},{... | collective-permute-start | bytes 1179656 | tf_op jit(solution)/shard_map/ppermute | solution.py:1525
  12.5 20.8 %collective-permute-start.7 = (bf16[2,128,768]{2,1,0:T(8,128)(2,1)S(1)}, bf16[2,128,768]{2,1,0:T(8,128)(2,1)S(1)}, u32[]{:S(2)}, u32[]{:S(2)}) collective-permute-start(bf16[2,128,768]{2,1,0:T(8,128)(2,1)S(1)} %get-tuple-element.140), channel_id=1, source_target_pairs={{0,16},{1,21},{2,26},{3,31},{4,20},{5,17},{6,30},{7,27},{8,24},{9,... | collective-permute-start | bytes 1179656 | tf_op jit(solution)/shard_map/ppermute | solution.py:1525
  33.5 17.8 %collective-permute-start.11 = (bf16[384,768]{1,0:T(8,128)(2,1)S(1)}, bf16[384,768]{1,0:T(8,128)(2,1)S(1)}, u32[]{:S(2)}, u32[]{:S(2)}) collective-permute-start(bf16[384,768]{1,0:T(8,128)(2,1)S(1)} %prep_halves.2), channel_id=1, source_target_pairs={{0,2},{1,3},{2,0},{3,1},{4,6},{5,7},{6,4},{7,5},{8,10},{9,11},{10,... | collective-permute-start | bytes 1769480 | tf_op jit(solution)/shard_map/ppermute | solution.py:1509
  33.6 15.8 %collective-permute-start.9 = (bf16[384,768]{1,0:T(8,128)(2,1)S(1)}, bf16[384,768]{1,0:T(8,128)(2,1)S(1)}, u32[]{:S(2)}, u32[]{:S(2)}) collective-permute-start(bf16[384,768]{1,0:T(8,128)(2,1)S(1)} %slice.30), channel_id=1, source_target_pairs={{0,4},{4,0},{8,12},{12,8},{16,20},{20,16},{24,28},{28,24},{1,5},{5... | collective-permute-start | bytes 1769480 | tf_op jit(solution)/shard_map/ppermute | solution.py:1509
  49.6 15.8 %collective-permute-start.15 = (bf16[384,768]{1,0:T(8,128)(2,1)S(1)}, bf16[384,768]{1,0:T(8,128)(2,1)S(1)}, u32[]{:S(2)}, u32[]{:S(2)}) collective-permute-start(bf16[384,768]{1,0:T(8,128)(2,1)S(1)} %prep_halves.3), channel_id=1, source_target_pairs={{0,2},{1,3},{2,0},{3,1},{4,6},{5,7},{6,4},{7,5},{8,10},{9,11},{10,... | collective-permute-start | bytes 1769480 | tf_op jit(solution)/shard_map/ppermute | solution.py:1509
  51.3 23.2 %collective-permute-start.13 = (bf16[384,768]{1,0:T(8,128)(2,1)S(1)}, bf16[384,768]{1,0:T(8,128)(2,1)S(1)}, u32[]{:S(2)}, u32[]{:S(2)}) collective-permute-start(bf16[384,768]{1,0:T(8,128)(2,1)S(1)} %collective-permute-done.11.refs_4_.refs_6_), channel_id=1, source_target_pairs={{0,1},{1,0},{2,3},{3,2},{4,5},{5,4},{6,7},{7,6},{8,9},{9,8},{10,11... | collective-permute-start | bytes 1769480 | tf_op jit(solution)/shard_map/ppermute | solution.py:1509
  51.5 15.5 %collective-permute-start.12 = (bf16[384,768]{1,0:T(8,128)(2,1)S(1)}, bf16[384,768]{1,0:T(8,128)(2,1)S(1)}, u32[]{:S(2)}, u32[]{:S(2)}) collective-permute-start(bf16[384,768]{1,0:T(8,128)(2,1)S(1)} %collective-permute-done.11.refs_4_.refs_6_), channel_id=1, source_target_pairs={{0,4},{4,0},{8,12},{12,8},{16,20},{20,16},{24,28},{28,24},{1,5},{5... | collective-permute-start | bytes 1769480 | tf_op jit(solution)/shard_map/ppermute | solution.py:1509
  65.4 15.8 %collective-permute-start.17 = (bf16[384,768]{1,0:T(8,128)(2,1)S(1)}, bf16[384,768]{1,0:T(8,128)(2,1)S(1)}, u32[]{:S(2)}, u32[]{:S(2)}) collective-permute-start(bf16[384,768]{1,0:T(8,128)(2,1)S(1)} %collective-permute-done.15.refs_6_), channel_id=1, source_target_pairs={{0,1},{1,0},{2,3},{3,2},{4,5},{5,4},{6,7},{7,6},{8,9},{9,8},{10,11... | collective-permute-start | bytes 1769480 | tf_op jit(solution)/shard_map/ppermute | solution.py:1509
  65.4 15.7 %collective-permute-start.16 = (bf16[384,768]{1,0:T(8,128)(2,1)S(1)}, bf16[384,768]{1,0:T(8,128)(2,1)S(1)}, u32[]{:S(2)}, u32[]{:S(2)}) collective-permute-start(bf16[384,768]{1,0:T(8,128)(2,1)S(1)} %collective-permute-done.15.refs_6_), channel_id=1, source_target_pairs={{0,8},{4,12},{8,0},{12,4},{16,24},{20,28},{24,16},{28,20},{1,9},{5... | collective-permute-start | bytes 1769480 | tf_op jit(solution)/shard_map/ppermute | solution.py:1509
  67.1 7.5 %collective-permute-start.14 = (bf16[384,768]{1,0:T(8,128)(2,1)S(1)}, bf16[384,768]{1,0:T(8,128)(2,1)S(1)}, u32[]{:S(2)}, u32[]{:S(2)}) collective-permute-start(bf16[384,768]{1,0:T(8,128)(2,1)S(1)} %collective-permute-done.12.refs_5_.refs_7_), channel_id=1, source_target_pairs={{0,1},{1,0},{2,3},{3,2},{4,5},{5,4},{6,7},{7,6},{8,9},{9,8},{10,11... | collective-permute-start | bytes 1769480 | tf_op jit(solution)/shard_map/ppermute | solution.py:1509
  96.3 29.5 %collective-permute-start.23 = (bf16[768,768]{1,0:T(8,128)(2,1)S(1)}, bf16[768,768]{1,0:T(8,128)(2,1)S(1)}, u32[]{:S(2)}, u32[]{:S(2)}) collective-permute-start(bf16[768,768]{1,0:T(8,128)(2,1)S(1)} %peer_grad.2), channel_id=1, source_target_pairs={{0,2},{1,3},{2,0},{3,1},{4,6},{5,7},{6,4},{7,5},{8,10},{9,11},{10,... | collective-permute-start | bytes 3538952 | tf_op jit(solution)/shard_map/ppermute | solution.py:1509
  98.0 26.9 %collective-permute-start.20 = (bf16[4,64,768]{2,1,0:T(8,128)(2,1)}, bf16[4,64,768]{2,1,0:T(8,128)(2,1)S(1)}, u32[]{:S(2)}, u32[]{:S(2)}) collective-permute-start(bf16[4,64,768]{2,1,0:T(8,128)(2,1)} %get-tuple-element.170), channel_id=1, source_target_pairs={{0,0},{1,5},{2,10},{3,15},{4,4},{5,1},{6,14},{7,11},{8,8},{9,13},{... | collective-permute-start | bytes 1179656 | tf_op jit(solution)/shard_map/ppermute | solution.py:1525
  100.2 24.7 %collective-permute-start.22 = (bf16[4,64,768]{2,1,0:T(8,128)(2,1)}, bf16[4,64,768]{2,1,0:T(8,128)(2,1)S(1)}, u32[]{:S(2)}, u32[]{:S(2)}) collective-permute-start(bf16[4,64,768]{2,1,0:T(8,128)(2,1)} %get-tuple-element.190), channel_id=1, source_target_pairs={{0,16},{1,21},{2,26},{3,31},{4,20},{5,17},{6,30},{7,27},{8,24},{9,... | collective-permute-start | bytes 1179656 | tf_op jit(solution)/shard_map/ppermute | solution.py:1525
  110.6 13.6 %collective-permute-start.21 = (bf16[2,768,768]{2,1,0:T(8,128)(2,1)S(1)}, bf16[2,768,768]{2,1,0:T(8,128)(2,1)S(1)}, u32[]{:S(2)}, u32[]{:S(2)}) collective-permute-start(bf16[2,768,768]{2,1,0:T(8,128)(2,1)S(1)} %get-tuple-element.188), channel_id=1, source_target_pairs={{0,1},{1,0},{2,3},{3,2},{4,5},{5,4},{6,7},{7,6},{8,9},{9,8},{10,11... | collective-permute-start | bytes 7077896 | tf_op jit(solution)/shard_map/ppermute | solution.py:1509
  123.7 14.6 %collective-permute-start.24 = (bf16[2,784,768]{2,1,0:T(8,128)(2,1)S(1)}, bf16[2,784,768]{2,1,0:T(8,128)(2,1)S(1)}, u32[]{:S(2)}, u32[]{:S(2)}) collective-permute-start(bf16[2,784,768]{2,1,0:T(8,128)(2,1)S(1)} %get-tuple-element.186), channel_id=1, source_target_pairs={{0,1},{1,0},{2,3},{3,2},{4,5},{5,4},{6,7},{7,6},{8,9},{9,8},{10,11... | collective-permute-start | bytes 7225352 | tf_op jit(solution)/shard_map/ppermute | solution.py:1509
  127.4 15.4 %collective-permute-start.25 = (bf16[384,768]{1,0:T(8,128)(2,1)S(1)}, bf16[384,768]{1,0:T(8,128)(2,1)S(1)}, u32[]{:S(2)}, u32[]{:S(2)}) collective-permute-start(bf16[384,768]{1,0:T(8,128)(2,1)S(1)} %get-tuple-element.195), channel_id=1, source_target_pairs={{0,4},{4,0},{8,12},{12,8},{16,20},{20,16},{24,28},{28,24},{1,5},{5... | collective-permute-start | bytes 1769480 | tf_op jit(solution)/shard_map/ppermute | solution.py:1509
  128.9 28.9 %collective-permute-start.29 = (bf16[768,768]{1,0:T(8,128)(2,1)S(1)}, bf16[768,768]{1,0:T(8,128)(2,1)S(1)}, u32[]{:S(2)}, u32[]{:S(2)}) collective-permute-start(bf16[768,768]{1,0:T(8,128)(2,1)S(1)} %peer_grad.3), channel_id=1, source_target_pairs={{0,2},{1,3},{2,0},{3,1},{4,6},{5,7},{6,4},{7,5},{8,10},{9,11},{10,... | collective-permute-start | bytes 3538952 | tf_op jit(solution)/shard_map/ppermute | solution.py:1509
  138.7 49.5 %collective-permute-start.37 = (bf16[784,768]{1,0:T(8,128)(2,1)S(1)}, bf16[784,768]{1,0:T(8,128)(2,1)S(1)}, u32[]{:S(2)}, u32[]{:S(2)}) collective-permute-start(bf16[784,768]{1,0:T(8,128)(2,1)S(1)} %peer_last.1), channel_id=1, source_target_pairs={{0,2},{1,3},{2,0},{3,1},{4,6},{5,7},{6,4},{7,5},{8,10},{9,11},{10,... | collective-permute-start | bytes 3612680 | tf_op jit(solution)/shard_map/ppermute | solution.py:1509
  142.9 11.8 %collective-permute-start.26 = (bf16[96,768]{1,0:T(8,128)(2,1)S(1)}, bf16[96,768]{1,0:T(8,128)(2,1)S(1)}, u32[]{:S(2)}, u32[]{:S(2)}) collective-permute-start(bf16[96,768]{1,0:T(8,128)(2,1)S(1)} %get-tuple-element.200), channel_id=1, source_target_pairs={{0,16},{4,20},{8,24},{12,28},{16,0},{20,4},{24,8},{28,12},{1,17},{... | collective-permute-start | bytes 442376 | tf_op jit(solution)/shard_map/ppermute | solution.py:1509
  143.3 11.4 %collective-permute-start.27 = (bf16[96,768]{1,0:T(8,128)(2,1)S(1)}, bf16[96,768]{1,0:T(8,128)(2,1)S(1)}, u32[]{:S(2)}, u32[]{:S(2)}) collective-permute-start(bf16[96,768]{1,0:T(8,128)(2,1)S(1)} %get-tuple-element.208), channel_id=1, source_target_pairs={{0,8},{4,12},{8,0},{12,4},{16,24},{20,28},{24,16},{28,20},{1,9},{5... | collective-permute-start | bytes 442376 | tf_op jit(solution)/shard_map/ppermute | solution.py:1509
  144.4 10.3 %collective-permute-start.28 = (bf16[96,768]{1,0:T(8,128)(2,1)S(1)}, bf16[96,768]{1,0:T(8,128)(2,1)S(1)}, u32[]{:S(2)}, u32[]{:S(2)}) collective-permute-start(bf16[96,768]{1,0:T(8,128)(2,1)S(1)} %get-tuple-element.209), channel_id=1, source_target_pairs={{0,24},{4,28},{8,16},{12,20},{16,8},{20,12},{24,0},{28,4},{1,25},{... | collective-permute-start | bytes 442376 | tf_op jit(solution)/shard_map/ppermute | solution.py:1509
  159.3 13.1 %collective-permute-start.30 = (bf16[384,768]{1,0:T(8,128)(2,1)S(1)}, bf16[384,768]{1,0:T(8,128)(2,1)S(1)}, u32[]{:S(2)}, u32[]{:S(2)}) collective-permute-start(bf16[384,768]{1,0:T(8,128)(2,1)S(1)} %get-tuple-element.212), channel_id=1, source_target_pairs={{0,4},{4,0},{8,12},{12,8},{16,20},{20,16},{24,28},{28,24},{1,5},{5... | collective-permute-start | bytes 1769480 | tf_op jit(solution)/shard_map/ppermute | solution.py:1509
  159.9 14.7 %collective-permute-start.33 = (bf16[96,768]{1,0:T(8,128)(2,1)S(1)}, bf16[96,768]{1,0:T(8,128)(2,1)S(1)}, u32[]{:S(2)}, u32[]{:S(2)}) collective-permute-start(bf16[96,768]{1,0:T(8,128)(2,1)S(1)} %gather_sum.3.refs_0_), channel_id=1, source_target_pairs={{0,24},{4,28},{8,16},{12,20},{16,8},{20,12},{24,0},{28,4},{1,25},{... | collective-permute-start | bytes 442376 | tf_op jit(solution)/shard_map/ppermute | solution.py:1509
  161.4 13.9 %collective-permute-start.32 = (bf16[96,768]{1,0:T(8,128)(2,1)S(1)}, bf16[96,768]{1,0:T(8,128)(2,1)S(1)}, u32[]{:S(2)}, u32[]{:S(2)}) collective-permute-start(bf16[96,768]{1,0:T(8,128)(2,1)S(1)} %gather_sum.3.refs_0_), channel_id=1, source_target_pairs={{0,8},{4,12},{8,0},{12,4},{16,24},{20,28},{24,16},{28,20},{1,9},{5... | collective-permute-start | bytes 442376 | tf_op jit(solution)/shard_map/ppermute | solution.py:1509
  161.4 14.7 %collective-permute-start.31 = (bf16[96,768]{1,0:T(8,128)(2,1)S(1)}, bf16[96,768]{1,0:T(8,128)(2,1)S(1)}, u32[]{:S(2)}, u32[]{:S(2)}) collective-permute-start(bf16[96,768]{1,0:T(8,128)(2,1)S(1)} %gather_sum.3.refs_0_), channel_id=1, source_target_pairs={{0,16},{4,20},{8,24},{12,28},{16,0},{20,4},{24,8},{28,12},{1,17},{... | collective-permute-start | bytes 442376 | tf_op jit(solution)/shard_map/ppermute | solution.py:1509
  172.5 8.0 %collective-permute-start.35 = (bf16[96,768]{1,0:T(8,128)(2,1)S(1)}, bf16[96,768]{1,0:T(8,128)(2,1)S(1)}, u32[]{:S(2)}, u32[]{:S(2)}) collective-permute-start(bf16[96,768]{1,0:T(8,128)(2,1)S(1)} %get-tuple-element.218), channel_id=1, source_target_pairs={{0,8},{4,12},{8,0},{12,4},{16,24},{20,28},{24,16},{28,20},{1,9},{5... | collective-permute-start | bytes 442376 | tf_op jit(solution)/shard_map/ppermute | solution.py:1509
  174.6 8.5 %collective-permute-start.36 = (bf16[96,768]{1,0:T(8,128)(2,1)S(1)}, bf16[96,768]{1,0:T(8,128)(2,1)S(1)}, u32[]{:S(2)}, u32[]{:S(2)}) collective-permute-start(bf16[96,768]{1,0:T(8,128)(2,1)S(1)} %get-tuple-element.219), channel_id=1, source_target_pairs={{0,24},{4,28},{8,16},{12,20},{16,8},{20,12},{24,0},{28,4},{1,25},{... | collective-permute-start | bytes 442376 | tf_op jit(solution)/shard_map/ppermute | solution.py:1509
  175.3 12.9 %collective-permute-start.34 = (bf16[96,768]{1,0:T(8,128)(2,1)S(1)}, bf16[96,768]{1,0:T(8,128)(2,1)S(1)}, u32[]{:S(2)}, u32[]{:S(2)}) collective-permute-start(bf16[96,768]{1,0:T(8,128)(2,1)S(1)} %get-tuple-element.215), channel_id=1, source_target_pairs={{0,16},{4,20},{8,24},{12,28},{16,0},{20,4},{24,8},{28,12},{1,17},{... | collective-permute-start | bytes 442376 | tf_op jit(solution)/shard_map/ppermute | solution.py:1509
  189.6 14.3 %collective-permute-start.38 = (bf16[400,768]{1,0:T(8,128)(2,1)S(1)}, bf16[400,768]{1,0:T(8,128)(2,1)S(1)}, u32[]{:S(2)}, u32[]{:S(2)}) collective-permute-start(bf16[400,768]{1,0:T(8,128)(2,1)S(1)} %get-tuple-element.222), channel_id=1, source_target_pairs={{0,4},{4,0},{8,12},{12,8},{16,20},{20,16},{24,28},{28,24},{1,5},{5... | collective-permute-start | bytes 1843208 | tf_op jit(solution)/shard_map/ppermute | solution.py:1509
  191.0 8.4 %collective-permute-start.41 = (bf16[96,768]{1,0:T(8,128)(2,1)S(1)}, bf16[96,768]{1,0:T(8,128)(2,1)S(1)}, u32[]{:S(2)}, u32[]{:S(2)}) collective-permute-start(bf16[96,768]{1,0:T(8,128)(2,1)S(1)} %gather_sum.4.refs_0_), channel_id=1, source_target_pairs={{0,24},{4,28},{8,16},{12,20},{16,8},{20,12},{24,0},{28,4},{1,25},{... | collective-permute-start | bytes 442376 | tf_op jit(solution)/shard_map/ppermute | solution.py:1509
  192.6 8.5 %collective-permute-start.40 = (bf16[96,768]{1,0:T(8,128)(2,1)S(1)}, bf16[96,768]{1,0:T(8,128)(2,1)S(1)}, u32[]{:S(2)}, u32[]{:S(2)}) collective-permute-start(bf16[96,768]{1,0:T(8,128)(2,1)S(1)} %gather_sum.4.refs_0_), channel_id=1, source_target_pairs={{0,8},{4,12},{8,0},{12,4},{16,24},{20,28},{24,16},{28,20},{1,9},{5... | collective-permute-start | bytes 442376 | tf_op jit(solution)/shard_map/ppermute | solution.py:1509
  192.6 11.3 %collective-permute-start.39 = (bf16[96,768]{1,0:T(8,128)(2,1)S(1)}, bf16[96,768]{1,0:T(8,128)(2,1)S(1)}, u32[]{:S(2)}, u32[]{:S(2)}) collective-permute-start(bf16[96,768]{1,0:T(8,128)(2,1)S(1)} %gather_sum.4.refs_0_), channel_id=1, source_target_pairs={{0,16},{4,20},{8,24},{12,28},{16,0},{20,4},{24,8},{28,12},{1,17},{... | collective-permute-start | bytes 442376 | tf_op jit(solution)/shard_map/ppermute | solution.py:1509
  195.4 28.3 %collective-permute-start.52 = (bf16[288,768]{1,0:T(8,128)(2,1)S(1)}, bf16[288,768]{1,0:T(8,128)(2,1)S(1)}, u32[]{:S(2)}, u32[]{:S(2)}) collective-permute-start(bf16[288,768]{1,0:T(8,128)(2,1)S(1)} %get-tuple-element.242), channel_id=1, source_target_pairs={{0,2},{1,3},{2,0},{3,1},{4,6},{5,7},{6,4},{7,5},{8,10},{9,11},{10,... | collective-permute-start | bytes 1327112 | tf_op jit(solution)/shard_map/ppermute | solution.py:1509
  199.5 23.4 %collective-permute-start.49 = (bf16[256,768]{1,0:T(8,128)(2,1)S(1)}, bf16[256,768]{1,0:T(8,128)(2,1)S(1)}, u32[]{:S(2)}, u32[]{:S(2)}) collective-permute-start(bf16[256,768]{1,0:T(8,128)(2,1)S(1)} %get-tuple-element.238), channel_id=1, source_target_pairs={{0,2},{1,3},{2,0},{3,1},{4,6},{5,7},{6,4},{7,5},{8,10},{9,11},{10,... | collective-permute-start | bytes 1179656 | tf_op jit(solution)/shard_map/ppermute | solution.py:1509
  204.1 9.4 %collective-permute-start.42 = (bf16[112,768]{1,0:T(8,128)(2,1)S(1)}, bf16[112,768]{1,0:T(8,128)(2,1)S(1)}, u32[]{:S(2)}, u32[]{:S(2)}) collective-permute-start(bf16[112,768]{1,0:T(8,128)(2,1)S(1)} %get-tuple-element.227), channel_id=1, source_target_pairs={{0,16},{4,20},{8,24},{12,28},{16,0},{20,4},{24,8},{28,12},{1,17},{... | collective-permute-start | bytes 516104 | tf_op jit(solution)/shard_map/ppermute | solution.py:1509
  205.0 10.4 %collective-permute-start.43 = (bf16[112,768]{1,0:T(8,128)(2,1)S(1)}, bf16[112,768]{1,0:T(8,128)(2,1)S(1)}, u32[]{:S(2)}, u32[]{:S(2)}) collective-permute-start(bf16[112,768]{1,0:T(8,128)(2,1)S(1)} %get-tuple-element.228), channel_id=1, source_target_pairs={{0,8},{4,12},{8,0},{12,4},{16,24},{20,28},{24,16},{28,20},{1,9},{5... | collective-permute-start | bytes 516104 | tf_op jit(solution)/shard_map/ppermute | solution.py:1509
  207.2 30.7 %collective-permute-start.56 = (bf16[384,768]{1,0:T(8,128)(2,1)S(1)}, bf16[384,768]{1,0:T(8,128)(2,1)S(1)}, u32[]{:S(2)}, u32[]{:S(2)}) collective-permute-start(bf16[384,768]{1,0:T(8,128)(2,1)S(1)} %join.3), channel_id=1, source_target_pairs={{0,4},{4,0},{8,12},{12,8},{16,20},{20,16},{24,28},{28,24},{1,5},{5... | collective-permute-start | bytes 1769480 | tf_op jit(solution)/shard_map/ppermute | solution.py:1509
  213.4 7.7 %collective-permute-start.44 = (bf16[112,768]{1,0:T(8,128)(2,1)S(1)}, bf16[112,768]{1,0:T(8,128)(2,1)S(1)}, u32[]{:S(2)}, u32[]{:S(2)}) collective-permute-start(bf16[112,768]{1,0:T(8,128)(2,1)S(1)} %get-tuple-element.229), channel_id=1, source_target_pairs={{0,24},{4,28},{8,16},{12,20},{16,8},{20,12},{24,0},{28,4},{1,25},{... | collective-permute-start | bytes 516104 | tf_op jit(solution)/shard_map/ppermute | solution.py:1509
  215.4 23.0 %collective-permute-start.55 = (bf16[384,768]{1,0:T(8,128)(2,1)S(1)}, bf16[384,768]{1,0:T(8,128)(2,1)S(1)}, u32[]{:S(2)}, u32[]{:S(2)}) collective-permute-start(bf16[384,768]{1,0:T(8,128)(2,1)S(1)} %join.4), channel_id=1, source_target_pairs={{0,4},{4,0},{8,12},{12,8},{16,20},{20,16},{24,28},{28,24},{1,5},{5... | collective-permute-start | bytes 1769480 | tf_op jit(solution)/shard_map/ppermute | solution.py:1509
  221.2 8.8 %collective-permute-start.47 = (bf16[96,768]{1,0:T(8,128)(2,1)S(1)}, bf16[96,768]{1,0:T(8,128)(2,1)S(1)}, u32[]{:S(2)}, u32[]{:S(2)}) collective-permute-start(bf16[96,768]{1,0:T(8,128)(2,1)S(1)} %get-tuple-element.232.refs_0_), channel_id=1, source_target_pairs={{0,24},{4,28},{8,16},{12,20},{16,8},{20,12},{24,0},{28,4},{1,25},{... | collective-permute-start | bytes 442376 | tf_op jit(solution)/shard_map/ppermute | solution.py:1509
  222.9 7.5 %collective-permute-start.46 = (bf16[96,768]{1,0:T(8,128)(2,1)S(1)}, bf16[96,768]{1,0:T(8,128)(2,1)S(1)}, u32[]{:S(2)}, u32[]{:S(2)}) collective-permute-start(bf16[96,768]{1,0:T(8,128)(2,1)S(1)} %get-tuple-element.232.refs_0_), channel_id=1, source_target_pairs={{0,8},{4,12},{8,0},{12,4},{16,24},{20,28},{24,16},{28,20},{1,9},{5... | collective-permute-start | bytes 442376 | tf_op jit(solution)/shard_map/ppermute | solution.py:1509
  223.7 11.5 %collective-permute-start.45 = (bf16[96,768]{1,0:T(8,128)(2,1)S(1)}, bf16[96,768]{1,0:T(8,128)(2,1)S(1)}, u32[]{:S(2)}, u32[]{:S(2)}) collective-permute-start(bf16[96,768]{1,0:T(8,128)(2,1)S(1)} %get-tuple-element.232.refs_0_), channel_id=1, source_target_pairs={{0,16},{4,20},{8,24},{12,28},{16,0},{20,4},{24,8},{28,12},{1,17},{... | collective-permute-start | bytes 442376 | tf_op jit(solution)/shard_map/ppermute | solution.py:1509
  229.9 13.2 %collective-permute-start.50 = (bf16[256,768]{1,0:T(8,128)(2,1)S(1)}, bf16[256,768]{1,0:T(8,128)(2,1)S(1)}, u32[]{:S(2)}, u32[]{:S(2)}) collective-permute-start(bf16[256,768]{1,0:T(8,128)(2,1)S(1)} %collective-permute-done.49.refs_3_), channel_id=1, source_target_pairs={{0,1},{1,0},{2,3},{3,2},{4,5},{5,4},{6,7},{7,6},{8,9},{9,8},{10,11... | collective-permute-start | bytes 1179656 | tf_op jit(solution)/shard_map/ppermute | solution.py:1509
  230.4 14.3 %collective-permute-start.53 = (bf16[288,768]{1,0:T(8,128)(2,1)S(1)}, bf16[288,768]{1,0:T(8,128)(2,1)S(1)}, u32[]{:S(2)}, u32[]{:S(2)}) collective-permute-start(bf16[288,768]{1,0:T(8,128)(2,1)S(1)} %collective-permute-done.52.refs_2_), channel_id=1, source_target_pairs={{0,1},{1,0},{2,3},{3,2},{4,5},{5,4},{6,7},{7,6},{8,9},{9,8},{10,11... | collective-permute-start | bytes 1327112 | tf_op jit(solution)/shard_map/ppermute | solution.py:1509
  235.3 14.5 %collective-permute-start.54 = (bf16[384,768]{1,0:T(8,128)(2,1)S(1)}, bf16[384,768]{1,0:T(8,128)(2,1)S(1)}, u32[]{:S(2)}, u32[]{:S(2)}) collective-permute-start(bf16[384,768]{1,0:T(8,128)(2,1)S(1)} %join.5), channel_id=1, source_target_pairs={{0,4},{4,0},{8,12},{12,8},{16,20},{20,16},{24,28},{28,24},{1,5},{5... | collective-permute-start | bytes 1769480 | tf_op jit(solution)/shard_map/ppermute | solution.py:1509
  (60 other events, 572.7 us)

commit v4 on v3

--- a/solution.py
+++ b/solution.py
@@ -593,7 +593,7 @@
             bias = bias_rows(ref, base + tile, 0)
             bias_q, bias_v = bias[:, 0:head_width], bias[:, 256 : 256 + head_width]
 
-            @pl.loop(0, here)
+            @pl.loop(0, here, unroll=True)
             def _(r):
                 start = pl.multiple_of(r * full, full)
                 projected = mm_nt(x_ref[pl.ds(start, full), :], blocks[b][...])
@@ -1042,7 +1042,7 @@
             kk, place = blocks[b][:2]
             ol_ref, qkv_ref, p_ref = data[3 * b : 3 * b + 3]
 
-            @pl.loop(0, here)
+            @pl.loop(0, here, unroll=True)
             def _(r):
                 span = pl.ds(pl.multiple_of(r * full, full), full)
                 dol = mm_nt(low_ref[span, :], w_out[b][...]).astype(bf16)
@@ -1576,7 +1576,7 @@
     )
     in_parts = [[(w_in, 0)], [(near_i, 0)], *crossed(half_in, 1, x, ol_b)]
     hl2, hl3, gp2, gp3 = ffn_far(ids, al, pieces, in_parts[2:], dims)
-    dn_parts = [[(w_down, 0)], [(near_d, 0)], *crossed(half_dn, 2, ol_b, hl2)]
+    dn_parts = [[(w_down, 0)], [(near_d, 0)], *crossed(half_dn, 2, x, al)]
     tk0, tk1, pooled, dz, low, ffn_sums, down_pair = ffn_down(
         ids, sent, segr, al, acc, (hl1, hl2, hl3), (b_down, gain_ffn, bias_ffn), ogs, pool_grad,
         dn_parts[2:], dims,

time: 257 us -> 255 us (level)
  Pallas kernels: 95.1 us -> 87.6 us
  starting transfers between devices: 57.4 us -> 60.4 us
    pallas_call x35, Pallas kernels: 95.1 us -> 87.6 us  [run(): return made(*args)]
  transfers between devices with their start and end apart: 57 -> 57, of which waited for: 24 -> 23; matrix products, arithmetic and copies ran while one was open for 1% -> 1% of each run, Pallas kernels for 33% -> 30%
where the time goes in v4:
time: 255 us; the launch traced here: 250 us
  waiting for transfers between devices  91.7 us (36%)
  Pallas kernels  87.6 us (34%)
  starting transfers between devices  60.4 us (24%)
  local copies, waits for them, and re-layouts  8.05 us (3%)
    ppermute x53, waiting for transfers between devices, swap(): lax.ppermute(values, axis, [(i, i ^ bit) for i in range(lax.axis_size(axi...  89.3 us
    pallas_call x35, Pallas kernels, run(): return made(*args)  87.6 us
    ppermute x53, starting transfers between devices, swap(): lax.ppermute(values, axis, [(i, i ^ bit) for i in range(lax.axis_size(axi...  47.2 us
    ppermute x4, starting transfers between devices, hop(): lax.ppermute(values, ('dp', 'mp'), [(s * count + f, (s ^ f + count * k) *...  13.2 us
    unnamed x102, local copies, waits for them, and re-layouts  7.35 us
  transfers between devices with their start and end apart: 57, of which 23 were waited for; matrix products, arithmetic and copies ran while one was open for 1% of the time, Pallas kernels for 30%

profile of v4, /device:TPU:4, one launch (start us, length us, event | category | flops | bytes accessed | tf_op | source)
XLA Modules:
  0.0 250.3 jit_solution(5865548778120982728)
XLA Ops:
  1.3 4.1 %prep_rows.1 = (bf16[144,768]{1,0:T(8,128)(2,1)}, bf16[144,768]{1,0:T(8,128)(2,1)}, bf16[672,768]{1,0:T(8,128)(2,1)}, s32[8,128]{1,0:T(8,128)}, s32[128]{0:T(128)}, /*index=5*/s32[128]{0:T(128)}, s32[3]{0:T(128)}) custom-call(s32[128]{0:T(128)} %route_ref.1, s32[128,128]{1,0:T(8,128)} %seg_ref.1, bf16[16,32,768]{2,1,0:T(8,128)(2,1)} %tok.1, ...), custom_call_target="tpu_custom_call" | custom-call | flops 4000000000 | tf_op jit(solution)/shard_map/prep_rows/pallas_call | solution.py:289
  8.4 4.0 %collective-permute-start.6 = (bf16[2,128,768]{2,1,0:T(8,128)(2,1)S(1)}, bf16[2,128,768]{2,1,0:T(8,128)(2,1)S(1)}, u32[]{:S(2)}, u32[]{:S(2)}) collective-permute-start(bf16[2,128,768]{2,1,0:T(8,128)(2,1)S(1)} %get-tuple-element.139), channel_id=1, source_target_pairs={{0,0},{1,5},{2,10},{3,15},{4,4},{5,1},{6,14},{7,11},{8,8},{9,13},{... | collective-permute-start | bytes 1179656 | tf_op jit(solution)/shard_map/ppermute | solution.py:1525
  12.5 2.5 %collective-permute-start.7 = (bf16[2,128,768]{2,1,0:T(8,128)(2,1)S(1)}, bf16[2,128,768]{2,1,0:T(8,128)(2,1)S(1)}, u32[]{:S(2)}, u32[]{:S(2)}) collective-permute-start(bf16[2,128,768]{2,1,0:T(8,128)(2,1)S(1)} %get-tuple-element.140), channel_id=1, source_target_pairs={{0,16},{1,21},{2,26},{3,31},{4,20},{5,17},{6,30},{7,27},{8,24},{9,... | collective-permute-start | bytes 1179656 | tf_op jit(solution)/shard_map/ppermute | solution.py:1525
  15.0 15.8 %collective-permute-done.refs_2_.refs_4_.refs_9_.refs_6_ = bf16[672,768]{1,0:T(8,128)(2,1)S(1)} collective-permute-done((bf16[672,768]{1,0:T(8,128)(2,1)}, bf16[672,768]{1,0:T(8,128)(2,1)S(1)}, u32[]{:S(2)}, u32[]{:S(2)}) %collective-permute-start) | collective-permute-done | bytes 1032224 | tf_op jit(solution)/shard_map/ppermute | solution.py:1509
  30.9 2.4 collective-permute-done.7.refs_4_
  36.0 7.6 %attend.2 = (bf16[512,768]{1,0:T(8,128)(2,1)S(1)}, bf16[2,512,192]{2,1,0:T(8,128)(2,1)S(1)}, bf16[2,3,512,192]{3,2,1,0:T(8,128)(2,1)S(1)}, bf16[2,4,384,128]{3,2,1,0:T(8,128)(2,1)S(1)}) custom-call(s32[3]{0:T(128)S(1)} %copy-done.3, s32[8,128]{1,0:T(8,128)S(1)} %copy-done.50, bf16[144,768]{1,0:T(8,128)(2,1)S(1)} %copy-done.19, ...), custom_call_target="tpu_custom_call" | custom-call | flops 20000000000 | tf_op jit(solution)/shard_map/attend/pallas_call | solution.py:289
  46.2 3.2 %collective-permute-done.9.refs_5_.refs_10_.refs_7_.refs_3_ = bf16[384,768]{1,0:T(8,128)(2,1)S(1)} collective-permute-done((bf16[384,768]{1,0:T(8,128)(2,1)S(1)}, bf16[384,768]{1,0:T(8,128)(2,1)S(1)}, u32[]{:S(2)}, u32[]{:S(2)}) %collective-permute-start.9) | collective-permute-done | bytes 589856 | tf_op jit(solution)/shard_map/ppermute | solution.py:1509
  51.2 10.8 %collective-permute-done.15.refs_6_ = bf16[384,768]{1,0:T(8,128)(2,1)S(1)} collective-permute-done((bf16[384,768]{1,0:T(8,128)(2,1)S(1)}, bf16[384,768]{1,0:T(8,128)(2,1)S(1)}, u32[]{:S(2)}, u32[]{:S(2)}) %collective-permute-start.15) | collective-permute-done | bytes 589856 | tf_op jit(solution)/shard_map/ppermute | solution.py:1509
  62.1 7.7 %attend.3 = (bf16[2,512,192]{2,1,0:T(8,128)(2,1)S(1)}, bf16[2,3,512,192]{3,2,1,0:T(8,128)(2,1)S(1)}, bf16[2,4,384,128]{3,2,1,0:T(8,128)(2,1)S(1)}) custom-call(s32[3]{0:T(128)S(1)} %copy-done.3, s32[8,128]{1,0:T(8,128)S(1)} %copy-done.50, bf16[144,768]{1,0:T(8,128)(2,1)S(1)} %copy-done.19, bf16[144,768]{1,0:T(8,128)(2,1)S(1)} %collective-permute-done.1.refs_1_, ...), custom_call_target="tpu_custom_call" | custom-call | flops 20000000000 | tf_op jit(solution)/shard_map/attend/pallas_call | solution.py:289
  72.2 7.4 %ffn_near.1 = (bf16[512,768]{1,0:T(8,128)(2,1)S(1)}, f32[512,768]{1,0:T(8,128)S(1)}, f32[512,128]{1,0:T(8,128)S(1)}, f32[512,768]{1,0:T(8,128)S(1)}, bf16[512,76...) custom-call(s32[3]{0:T(128)S(1)} %copy-done.3, ...), custom_call_target="tpu_custom_call" | custom-call | flops 22000001024 | tf_op jit(solution)/shard_map/ffn_near/pallas_call | solution.py:289
  79.9 4.6 %ffn_far.1 = (bf16[512,768]{1,0:T(8,128)(2,1)S(1)}, bf16[512,768]{1,0:T(8,128)(2,1)S(1)}, bf16[512,768]{1,0:T(8,128)(2,1)S(1)}, bf16[512,768]{1,0:T(8,128)(2,1)S(1)}) custom-call(s32[3]{0:T(128)S(1)} %copy-done.3, bf16[512,768]{1,0:T(8,128)(2,1)S(1)} %get-tuple-element.187.al_ref.lhs_ref, bf16[144,768]{1,0:T(8,128)(2,1)S(1)} %copy-done.19, ...), custom_call_target="tpu_custom_call" | custom-call | flops 12000000000 | tf_op jit(solution)/shard_map/ffn_far/pallas_call | solution.py:289
  84.6 7.5 %ffn_down.1 = (bf16[4,64,768]{2,1,0:T(8,128)(2,1)}, bf16[4,64,768]{2,1,0:T(8,128)(2,1)}, f32[16,768]{1,0:T(8,128)S(1)}, f32[512,768]{1,0:T(8,128)S(1)}, bf16[512...) custom-call(s32[3]{0:T(128)S(1)} %copy-done.3, s32[128]{0:T(128)S(1)} %copy-done.49, ...), custom_call_target="tpu_custom_call" | custom-call | flops 17999998976 | tf_op jit(solution)/shard_map/ffn_down/pallas_call | solution.py:289
  92.5 4.4 %ffn_back.1 = (bf16[512,768]{1,0:T(8,128)(2,1)S(1)}, bf16[512,768]{1,0:T(8,128)(2,1)S(1)}, bf16[512,768]{1,0:T(8,128)(2,1)S(1)}, bf16[512,768]{1,0:T(8,128)(2,1)S(1)}, f32[4,768]{1,0:T(4,128)S(1)}) custom-call(s32[3]{0:T(128)S(1)} %copy-done.3, bf16[512,768]{1,0:T(8,128)(2,1)S(1)} %get-tuple-element.162.low_ref.rhs_ref, ...), custom_call_target="tpu_custom_call" | custom-call | flops 10000000000 | tf_op jit(solution)/shard_map/ffn_back/pallas_call | solution.py:289
  98.1 3.8 %collective-permute-start.20 = (bf16[4,64,768]{2,1,0:T(8,128)(2,1)}, bf16[4,64,768]{2,1,0:T(8,128)(2,1)S(1)}, u32[]{:S(2)}, u32[]{:S(2)}) collective-permute-start(bf16[4,64,768]{2,1,0:T(8,128)(2,1)} %get-tuple-element.170), channel_id=1, source_target_pairs={{0,0},{1,5},{2,10},{3,15},{4,4},{5,1},{6,14},{7,11},{8,8},{9,13},{... | collective-permute-start | bytes 1179656 | tf_op jit(solution)/shard_map/ppermute | solution.py:1525
  102.0 2.8 %collective-permute-start.22 = (bf16[4,64,768]{2,1,0:T(8,128)(2,1)}, bf16[4,64,768]{2,1,0:T(8,128)(2,1)S(1)}, u32[]{:S(2)}, u32[]{:S(2)}) collective-permute-start(bf16[4,64,768]{2,1,0:T(8,128)(2,1)} %get-tuple-element.190), channel_id=1, source_target_pairs={{0,16},{1,21},{2,26},{3,31},{4,20},{5,17},{6,30},{7,27},{8,24},{9,... | collective-permute-start | bytes 1179656 | tf_op jit(solution)/shard_map/ppermute | solution.py:1525
  104.8 6.7 %norm_back.1 = (f32[512,768]{1,0:T(8,128)S(1)}, bf16[512,768]{1,0:T(8,128)(2,1)S(1)}, f32[8,768]{1,0:T(8,128)S(1)}, bf16[2,768,768]{2,1,0:T(8,128)(2,1)S(1)}) custom-call(s32[3]{0:T(128)S(1)} %copy-done.3, bf16[512,768]{1,0:T(8,128)(2,1)S(1)} %get-tuple-element.187.al_ref.lhs_ref, f32[512,768]{1,0:T(8,128)S(1)} %get-tuple-element.172.dz_ref, ...), custom_call_target="tpu_custom_call" | custom-call | flops 16000000000 | tf_op jit(solution)/shard_map/norm_back/pallas_call | solution.py:289
  114.5 6.9 %attend_back.2 = (bf16[2,512,576]{2,1,0:T(8,128)(2,1)S(1)}, bf16[2,784,768]{2,1,0:T(8,128)(2,1)S(1)}) custom-call(s32[3]{0:T(128)S(1)} %copy-done.3, bf16[512,768]{1,0:T(8,128)(2,1)S(1)} %get-tuple-element.179.low_ref, bf16[512,768]{1,0:T(8,128)(2,1)S(1)} %copy-done.38, f32[4,768]{1,0:T(4,128)S(1)} %get-tuple-element.167.bin_ref, ...), custom_call_target="tpu_custom_call" | custom-call | flops 25999998976 | tf_op jit(solution)/shard_map/attend_back/pallas_call | solution.py:289
  129.3 7.0 %attend_back.3 = (bf16[2,512,576]{2,1,0:T(8,128)(2,1)S(1)}, bf16[2,784,768]{2,1,0:T(8,128)(2,1)S(1)}) custom-call(s32[3]{0:T(128)S(1)} %copy-done.3, bf16[512,768]{1,0:T(8,128)(2,1)S(1)} %copy-done.27, bf16[512,768]{1,0:T(8,128)(2,1)S(1)} %copy-done.39, f32[4,768]{1,0:T(4,128)S(1)} %get-tuple-element.167.bin_ref, f32[8,768]{1,0:T(8,128)S(1)} %get-tuple-element.180.ffn_ref, ...), custom_call_target="tpu_custom_call" | custom-call | flops 25999998976 | tf_op jit(solution)/shard_map/attend_back/pallas_call | solution.py:289
  138.4 3.6 %collective-permute-done.25.refs_1_ = bf16[384,768]{1,0:T(8,128)(2,1)S(1)} collective-permute-done((bf16[384,768]{1,0:T(8,128)(2,1)S(1)}, bf16[384,768]{1,0:T(8,128)(2,1)S(1)}, u32[]{:S(2)}, u32[]{:S(2)}) %collective-permute-start.25) | collective-permute-done | bytes 589856 | tf_op jit(solution)/shard_map/ppermute | solution.py:1509
  142.2 2.1 collective-permute-start.26
  144.3 2.1 collective-permute-start.27
  146.6 3.2 %grad_input_rows.1 = (bf16[144,768]{1,0:T(8,128)(2,1)S(1)}, bf16[144,768]{1,0:T(8,128)(2,1)S(1)}, bf16[288,768]{1,0:T(8,128)(2,1)S(1)}) custom-call(s32[3]{0:T(128)S(1)} %copy-done.3, f32[512,768]{1,0:T(8,128)S(1)} %copy-done.21, bf16[2,512,576]{2,1,0:T(8,128)(2,1)S(1)} %copy-done.23, bf16[2,512,576]{2,1,0:T(8,128)(2,1)S(1)} %get-tuple-element.204.m_b, ...), custom_call_target="tpu_custom_call" | custom-call | flops 12000000000 | tf_op jit(solution)/shard_map/grad_input_rows/pallas_call | solution.py:289
  151.1 4.3 %collective-permute-done.28.refs_3_ = bf16[96,768]{1,0:T(8,128)(2,1)S(1)} collective-permute-done((bf16[96,768]{1,0:T(8,128)(2,1)S(1)}, bf16[96,768]{1,0:T(8,128)(2,1)S(1)}, u32[]{:S(2)}, u32[]{:S(2)}) %collective-permute-start.28) | collective-permute-done | bytes 147488 | tf_op jit(solution)/shard_map/ppermute | solution.py:1509
  155.4 2.4 collective-permute-done.29.cross_ref
  160.0 3.4 %collective-permute-start.33 = (bf16[96,768]{1,0:T(8,128)(2,1)S(1)}, bf16[96,768]{1,0:T(8,128)(2,1)S(1)}, u32[]{:S(2)}, u32[]{:S(2)}) collective-permute-start(bf16[96,768]{1,0:T(8,128)(2,1)S(1)} %gather_sum.3.refs_0_), channel_id=1, source_target_pairs={{0,24},{4,28},{8,16},{12,20},{16,8},{20,12},{24,0},{28,4},{1,25},{... | collective-permute-start | bytes 442376 | tf_op jit(solution)/shard_map/ppermute | solution.py:1509
  164.4 6.8 %collective-permute-done.30.refs_1_ = bf16[384,768]{1,0:T(8,128)(2,1)S(1)} collective-permute-done((bf16[384,768]{1,0:T(8,128)(2,1)S(1)}, bf16[384,768]{1,0:T(8,128)(2,1)S(1)}, u32[]{:S(2)}, u32[]{:S(2)}) %collective-permute-start.30) | collective-permute-done | bytes 589856 | tf_op jit(solution)/shard_map/ppermute | solution.py:1509
  171.3 2.4 collective-permute-start.35
  173.7 2.4 collective-permute-start.36
  176.2 2.3 collective-permute-done.35.refs_2_
  178.5 3.0 %collective-permute-done.36.refs_3_ = bf16[96,768]{1,0:T(8,128)(2,1)S(1)} collective-permute-done((bf16[96,768]{1,0:T(8,128)(2,1)S(1)}, bf16[96,768]{1,0:T(8,128)(2,1)S(1)}, u32[]{:S(2)}, u32[]{:S(2)}) %collective-permute-start.36) | collective-permute-done | bytes 147488 | tf_op jit(solution)/shard_map/ppermute | solution.py:1509
  181.5 4.6 %collective-permute-done.34.refs_1_ = bf16[96,768]{1,0:T(8,128)(2,1)S(1)} collective-permute-done((bf16[96,768]{1,0:T(8,128)(2,1)S(1)}, bf16[96,768]{1,0:T(8,128)(2,1)S(1)}, u32[]{:S(2)}, u32[]{:S(2)}) %collective-permute-start.34) | collective-permute-done | bytes 147488 | tf_op jit(solution)/shard_map/ppermute | solution.py:1509
  187.6 2.4 collective-permute-start.38
  190.1 2.0 collective-permute-start.41
  192.1 2.4 collective-permute-start.39
  196.1 2.7 %collective-permute-done.41.refs_3_ = bf16[96,768]{1,0:T(8,128)(2,1)S(1)} collective-permute-done((bf16[96,768]{1,0:T(8,128)(2,1)S(1)}, bf16[96,768]{1,0:T(8,128)(2,1)S(1)}, u32[]{:S(2)}, u32[]{:S(2)}) %collective-permute-start.41) | collective-permute-done | bytes 147488 | tf_op jit(solution)/shard_map/ppermute | solution.py:1509
  200.4 2.9 %collective-permute-done.39.refs_1_ = bf16[96,768]{1,0:T(8,128)(2,1)S(1)} collective-permute-done((bf16[96,768]{1,0:T(8,128)(2,1)S(1)}, bf16[96,768]{1,0:T(8,128)(2,1)S(1)}, u32[]{:S(2)}, u32[]{:S(2)}) %collective-permute-start.39) | collective-permute-done | bytes 147488 | tf_op jit(solution)/shard_map/ppermute | solution.py:1509
  203.6 2.7 %collective-permute-start.43 = (bf16[112,768]{1,0:T(8,128)(2,1)S(1)}, bf16[112,768]{1,0:T(8,128)(2,1)S(1)}, u32[]{:S(2)}, u32[]{:S(2)}) collective-permute-start(bf16[112,768]{1,0:T(8,128)(2,1)S(1)} %get-tuple-element.228), channel_id=1, source_target_pairs={{0,8},{4,12},{8,0},{12,4},{16,24},{20,28},{24,16},{28,20},{1,9},{5... | collective-permute-start | bytes 516104 | tf_op jit(solution)/shard_map/ppermute | solution.py:1509
  206.7 6.5 %collective-permute-done.42.refs_1_ = bf16[112,768]{1,0:T(8,128)(2,1)S(1)} collective-permute-done((bf16[112,768]{1,0:T(8,128)(2,1)S(1)}, bf16[112,768]{1,0:T(8,128)(2,1)S(1)}, u32[]{:S(2)}, u32[]{:S(2)}) %collective-permute-start.42) | collective-permute-done | bytes 172064 | tf_op jit(solution)/shard_map/ppermute | solution.py:1509
  213.2 2.8 %collective-permute-start.44 = (bf16[112,768]{1,0:T(8,128)(2,1)S(1)}, bf16[112,768]{1,0:T(8,128)(2,1)S(1)}, u32[]{:S(2)}, u32[]{:S(2)}) collective-permute-start(bf16[112,768]{1,0:T(8,128)(2,1)S(1)} %get-tuple-element.229), channel_id=1, source_target_pairs={{0,24},{4,28},{8,16},{12,20},{16,8},{20,12},{24,0},{28,4},{1,25},{... | collective-permute-start | bytes 516104 | tf_op jit(solution)/shard_map/ppermute | solution.py:1509
  216.0 5.0 %collective-permute-done.44.refs_3_ = bf16[112,768]{1,0:T(8,128)(2,1)S(1)} collective-permute-done((bf16[112,768]{1,0:T(8,128)(2,1)S(1)}, bf16[112,768]{1,0:T(8,128)(2,1)S(1)}, u32[]{:S(2)}, u32[]{:S(2)}) %collective-permute-start.44) | collective-permute-done | bytes 172064 | tf_op jit(solution)/shard_map/ppermute | solution.py:1509
  221.2 4.1 %collective-permute-start.47 = (bf16[96,768]{1,0:T(8,128)(2,1)S(1)}, bf16[96,768]{1,0:T(8,128)(2,1)S(1)}, u32[]{:S(2)}, u32[]{:S(2)}) collective-permute-start(bf16[96,768]{1,0:T(8,128)(2,1)S(1)} %get-tuple-element.232.refs_0_), channel_id=1, source_target_pairs={{0,24},{4,28},{8,16},{12,20},{16,8},{20,12},{24,0},{28,4},{1,25},{... | collective-permute-start | bytes 442376 | tf_op jit(solution)/shard_map/ppermute | solution.py:1509
  225.9 2.6 %collective-permute-done.47.refs_3_ = bf16[96,768]{1,0:T(8,128)(2,1)S(1)} collective-permute-done((bf16[96,768]{1,0:T(8,128)(2,1)S(1)}, bf16[96,768]{1,0:T(8,128)(2,1)S(1)}, u32[]{:S(2)}, u32[]{:S(2)}) %collective-permute-start.47) | collective-permute-done | bytes 147488 | tf_op jit(solution)/shard_map/ppermute | solution.py:1509
  228.5 3.4 %collective-permute-done.46.refs_2_ = bf16[96,768]{1,0:T(8,128)(2,1)S(1)} collective-permute-done((bf16[96,768]{1,0:T(8,128)(2,1)S(1)}, bf16[96,768]{1,0:T(8,128)(2,1)S(1)}, u32[]{:S(2)}, u32[]{:S(2)}) %collective-permute-start.46) | collective-permute-done | bytes 147488 | tf_op jit(solution)/shard_map/ppermute | solution.py:1509
  234.9 2.1 whole_grad.5
  237.0 2.1 whole_grad.4
  240.7 2.2 land_grad.1
  243.0 4.7 %collective-permute-done.54.refs_4_ = bf16[384,768]{1,0:T(8,128)(2,1)S(1)} collective-permute-done((bf16[384,768]{1,0:T(8,128)(2,1)S(1)}, bf16[384,768]{1,0:T(8,128)(2,1)S(1)}, u32[]{:S(2)}, u32[]{:S(2)}) %collective-permute-start.54) | collective-permute-done | bytes 589856 | tf_op jit(solution)/shard_map/ppermute | solution.py:1509
  247.7 2.2 whole_grad.3
  (207 shorter events, 43.7 us)
Async XLA Ops:
  0.7 30.1 %collective-permute-start.4 = (bf16[768,768]{1,0:T(8,128)(2,1)}, bf16[768,768]{1,0:T(8,128)(2,1)}, u32[]{:S(2)}, u32[]{:S(2)}) collective-permute-start(bf16[768,768]{1,0:T(8,128)(2,1)} %refs_4_.5), channel_id=1, source_target_pairs={{0,1},{1,0},{2,3},{3,2},{4,5},{5,4},{6,7},{7,6},{8,9},{9,8},{10,11... | collective-permute-start | bytes 3538952 | tf_op jit(solution)/shard_map/ppermute | solution.py:1509
  1.2 29.7 %collective-permute-start.5 = (bf16[768,768]{1,0:T(8,128)(2,1)}, bf16[768,768]{1,0:T(8,128)(2,1)}, u32[]{:S(2)}, u32[]{:S(2)}) collective-permute-start(bf16[768,768]{1,0:T(8,128)(2,1)} %refs_4_.4), channel_id=1, source_target_pairs={{0,1},{1,0},{2,3},{3,2},{4,5},{5,4},{6,7},{7,6},{8,9},{9,8},{10,11... | collective-permute-start | bytes 3538952 | tf_op jit(solution)/shard_map/ppermute | solution.py:1509
  5.4 25.4 %collective-permute-start = (bf16[672,768]{1,0:T(8,128)(2,1)}, bf16[672,768]{1,0:T(8,128)(2,1)S(1)}, u32[]{:S(2)}, u32[]{:S(2)}) collective-permute-start(bf16[672,768]{1,0:T(8,128)(2,1)} %get-tuple-element.136), channel_id=1, source_target_pairs={{0,2},{1,3},{2,0},{3,1},{4,6},{5,7},{6,4},{7,5},{8,10},{9,11},{10,... | collective-permute-start | bytes 3096584 | tf_op jit(solution)/shard_map/ppermute | solution.py:1509
  5.5 7.0 %collective-permute-start.3 = (bf16[192,768]{1,0:T(8,128)(2,1)}, bf16[192,768]{1,0:T(8,128)(2,1)S(1)}, u32[]{:S(2)}, u32[]{:S(2)}) collective-permute-start(bf16[192,768]{1,0:T(8,128)(2,1)} %refs_8_.1), channel_id=1, source_target_pairs={{0,1},{1,0},{2,3},{3,2},{4,5},{5,4},{6,7},{7,6},{8,9},{9,8},{10,11... | collective-permute-start | bytes 884744 | tf_op jit(solution)/shard_map/ppermute | solution.py:1509
  8.4 22.4 %collective-permute-start.6 = (bf16[2,128,768]{2,1,0:T(8,128)(2,1)S(1)}, bf16[2,128,768]{2,1,0:T(8,128)(2,1)S(1)}, u32[]{:S(2)}, u32[]{:S(2)}) collective-permute-start(bf16[2,128,768]{2,1,0:T(8,128)(2,1)S(1)} %get-tuple-element.139), channel_id=1, source_target_pairs={{0,0},{1,5},{2,10},{3,15},{4,4},{5,1},{6,14},{7,11},{8,8},{9,13},{... | collective-permute-start | bytes 1179656 | tf_op jit(solution)/shard_map/ppermute | solution.py:1525
  12.5 20.8 %collective-permute-start.7 = (bf16[2,128,768]{2,1,0:T(8,128)(2,1)S(1)}, bf16[2,128,768]{2,1,0:T(8,128)(2,1)S(1)}, u32[]{:S(2)}, u32[]{:S(2)}) collective-permute-start(bf16[2,128,768]{2,1,0:T(8,128)(2,1)S(1)} %get-tuple-element.140), channel_id=1, source_target_pairs={{0,16},{1,21},{2,26},{3,31},{4,20},{5,17},{6,30},{7,27},{8,24},{9,... | collective-permute-start | bytes 1179656 | tf_op jit(solution)/shard_map/ppermute | solution.py:1525
  33.5 16.2 %collective-permute-start.11 = (bf16[384,768]{1,0:T(8,128)(2,1)S(1)}, bf16[384,768]{1,0:T(8,128)(2,1)S(1)}, u32[]{:S(2)}, u32[]{:S(2)}) collective-permute-start(bf16[384,768]{1,0:T(8,128)(2,1)S(1)} %prep_halves.2), channel_id=1, source_target_pairs={{0,2},{1,3},{2,0},{3,1},{4,6},{5,7},{6,4},{7,5},{8,10},{9,11},{10,... | collective-permute-start | bytes 1769480 | tf_op jit(solution)/shard_map/ppermute | solution.py:1509
  33.6 15.8 %collective-permute-start.9 = (bf16[384,768]{1,0:T(8,128)(2,1)S(1)}, bf16[384,768]{1,0:T(8,128)(2,1)S(1)}, u32[]{:S(2)}, u32[]{:S(2)}) collective-permute-start(bf16[384,768]{1,0:T(8,128)(2,1)S(1)} %slice.30), channel_id=1, source_target_pairs={{0,4},{4,0},{8,12},{12,8},{16,20},{20,16},{24,28},{28,24},{1,5},{5... | collective-permute-start | bytes 1769480 | tf_op jit(solution)/shard_map/ppermute | solution.py:1509
  45.1 16.9 %collective-permute-start.15 = (bf16[384,768]{1,0:T(8,128)(2,1)S(1)}, bf16[384,768]{1,0:T(8,128)(2,1)S(1)}, u32[]{:S(2)}, u32[]{:S(2)}) collective-permute-start(bf16[384,768]{1,0:T(8,128)(2,1)S(1)} %prep_halves.3), channel_id=1, source_target_pairs={{0,2},{1,3},{2,0},{3,1},{4,6},{5,7},{6,4},{7,5},{8,10},{9,11},{10,... | collective-permute-start | bytes 1769480 | tf_op jit(solution)/shard_map/ppermute | solution.py:1509
  49.4 12.7 %collective-permute-start.10 = (bf16[384,768]{1,0:T(8,128)(2,1)S(1)}, bf16[384,768]{1,0:T(8,128)(2,1)S(1)}, u32[]{:S(2)}, u32[]{:S(2)}) collective-permute-start(bf16[384,768]{1,0:T(8,128)(2,1)S(1)} %collective-permute-done.9.refs_5_.refs_10_.refs_7_.refs_3_), channel_id=1, source_target_pairs={{0,1},{1,0},{2,3},{3,2},{4,5},{5,4},{6,7},{7,6},{8,9},{9,8},{10,11... | collective-permute-start | bytes 1769480 | tf_op jit(solution)/shard_map/ppermute | solution.py:1509
  49.7 30.2 %collective-permute-start.13 = (bf16[384,768]{1,0:T(8,128)(2,1)S(1)}, bf16[384,768]{1,0:T(8,128)(2,1)S(1)}, u32[]{:S(2)}, u32[]{:S(2)}) collective-permute-start(bf16[384,768]{1,0:T(8,128)(2,1)S(1)} %collective-permute-done.11.refs_4_.refs_6_), channel_id=1, source_target_pairs={{0,1},{1,0},{2,3},{3,2},{4,5},{5,4},{6,7},{7,6},{8,9},{9,8},{10,11... | collective-permute-start | bytes 1769480 | tf_op jit(solution)/shard_map/ppermute | solution.py:1509
  49.9 21.9 %collective-permute-start.12 = (bf16[384,768]{1,0:T(8,128)(2,1)S(1)}, bf16[384,768]{1,0:T(8,128)(2,1)S(1)}, u32[]{:S(2)}, u32[]{:S(2)}) collective-permute-start(bf16[384,768]{1,0:T(8,128)(2,1)S(1)} %collective-permute-done.11.refs_4_.refs_6_), channel_id=1, source_target_pairs={{0,4},{4,0},{8,12},{12,8},{16,20},{20,16},{24,28},{28,24},{1,5},{5... | collective-permute-start | bytes 1769480 | tf_op jit(solution)/shard_map/ppermute | solution.py:1509
  62.0 22.6 %collective-permute-start.17 = (bf16[384,768]{1,0:T(8,128)(2,1)S(1)}, bf16[384,768]{1,0:T(8,128)(2,1)S(1)}, u32[]{:S(2)}, u32[]{:S(2)}) collective-permute-start(bf16[384,768]{1,0:T(8,128)(2,1)S(1)} %collective-permute-done.15.refs_6_), channel_id=1, source_target_pairs={{0,1},{1,0},{2,3},{3,2},{4,5},{5,4},{6,7},{7,6},{8,9},{9,8},{10,11... | collective-permute-start | bytes 1769480 | tf_op jit(solution)/shard_map/ppermute | solution.py:1509
  62.0 17.7 %collective-permute-start.16 = (bf16[384,768]{1,0:T(8,128)(2,1)S(1)}, bf16[384,768]{1,0:T(8,128)(2,1)S(1)}, u32[]{:S(2)}, u32[]{:S(2)}) collective-permute-start(bf16[384,768]{1,0:T(8,128)(2,1)S(1)} %collective-permute-done.15.refs_6_), channel_id=1, source_target_pairs={{0,8},{4,12},{8,0},{12,4},{16,24},{20,28},{24,16},{28,20},{1,9},{5... | collective-permute-start | bytes 1769480 | tf_op jit(solution)/shard_map/ppermute | solution.py:1509
  71.8 8.1 %collective-permute-start.14 = (bf16[384,768]{1,0:T(8,128)(2,1)S(1)}, bf16[384,768]{1,0:T(8,128)(2,1)S(1)}, u32[]{:S(2)}, u32[]{:S(2)}) collective-permute-start(bf16[384,768]{1,0:T(8,128)(2,1)S(1)} %collective-permute-done.12.refs_5_.refs_7_), channel_id=1, source_target_pairs={{0,1},{1,0},{2,3},{3,2},{4,5},{5,4},{6,7},{7,6},{8,9},{9,8},{10,11... | collective-permute-start | bytes 1769480 | tf_op jit(solution)/shard_map/ppermute | solution.py:1509
  97.8 28.1 %collective-permute-start.23 = (bf16[768,768]{1,0:T(8,128)(2,1)S(1)}, bf16[768,768]{1,0:T(8,128)(2,1)S(1)}, u32[]{:S(2)}, u32[]{:S(2)}) collective-permute-start(bf16[768,768]{1,0:T(8,128)(2,1)S(1)} %peer_grad.2), channel_id=1, source_target_pairs={{0,2},{1,3},{2,0},{3,1},{4,6},{5,7},{6,4},{7,5},{8,10},{9,11},{10,... | collective-permute-start | bytes 3538952 | tf_op jit(solution)/shard_map/ppermute | solution.py:1509
  98.1 25.6 %collective-permute-start.20 = (bf16[4,64,768]{2,1,0:T(8,128)(2,1)}, bf16[4,64,768]{2,1,0:T(8,128)(2,1)S(1)}, u32[]{:S(2)}, u32[]{:S(2)}) collective-permute-start(bf16[4,64,768]{2,1,0:T(8,128)(2,1)} %get-tuple-element.170), channel_id=1, source_target_pairs={{0,0},{1,5},{2,10},{3,15},{4,4},{5,1},{6,14},{7,11},{8,8},{9,13},{... | collective-permute-start | bytes 1179656 | tf_op jit(solution)/shard_map/ppermute | solution.py:1525
  102.0 21.8 %collective-permute-start.22 = (bf16[4,64,768]{2,1,0:T(8,128)(2,1)}, bf16[4,64,768]{2,1,0:T(8,128)(2,1)S(1)}, u32[]{:S(2)}, u32[]{:S(2)}) collective-permute-start(bf16[4,64,768]{2,1,0:T(8,128)(2,1)} %get-tuple-element.190), channel_id=1, source_target_pairs={{0,16},{1,21},{2,26},{3,31},{4,20},{5,17},{6,30},{7,27},{8,24},{9,... | collective-permute-start | bytes 1179656 | tf_op jit(solution)/shard_map/ppermute | solution.py:1525
  111.5 11.4 %collective-permute-start.21 = (bf16[2,768,768]{2,1,0:T(8,128)(2,1)S(1)}, bf16[2,768,768]{2,1,0:T(8,128)(2,1)S(1)}, u32[]{:S(2)}, u32[]{:S(2)}) collective-permute-start(bf16[2,768,768]{2,1,0:T(8,128)(2,1)S(1)} %get-tuple-element.188), channel_id=1, source_target_pairs={{0,1},{1,0},{2,3},{3,2},{4,5},{5,4},{6,7},{7,6},{8,9},{9,8},{10,11... | collective-permute-start | bytes 7077896 | tf_op jit(solution)/shard_map/ppermute | solution.py:1509
  122.5 13.8 %collective-permute-start.24 = (bf16[2,784,768]{2,1,0:T(8,128)(2,1)S(1)}, bf16[2,784,768]{2,1,0:T(8,128)(2,1)S(1)}, u32[]{:S(2)}, u32[]{:S(2)}) collective-permute-start(bf16[2,784,768]{2,1,0:T(8,128)(2,1)S(1)} %get-tuple-element.186), channel_id=1, source_target_pairs={{0,1},{1,0},{2,3},{3,2},{4,5},{5,4},{6,7},{7,6},{8,9},{9,8},{10,11... | collective-permute-start | bytes 7225352 | tf_op jit(solution)/shard_map/ppermute | solution.py:1509
  127.4 14.7 %collective-permute-start.25 = (bf16[384,768]{1,0:T(8,128)(2,1)S(1)}, bf16[384,768]{1,0:T(8,128)(2,1)S(1)}, u32[]{:S(2)}, u32[]{:S(2)}) collective-permute-start(bf16[384,768]{1,0:T(8,128)(2,1)S(1)} %get-tuple-element.195), channel_id=1, source_target_pairs={{0,4},{4,0},{8,12},{12,8},{16,20},{20,16},{24,28},{28,24},{1,5},{5... | collective-permute-start | bytes 1769480 | tf_op jit(solution)/shard_map/ppermute | solution.py:1509
  129.0 28.9 %collective-permute-start.29 = (bf16[768,768]{1,0:T(8,128)(2,1)S(1)}, bf16[768,768]{1,0:T(8,128)(2,1)S(1)}, u32[]{:S(2)}, u32[]{:S(2)}) collective-permute-start(bf16[768,768]{1,0:T(8,128)(2,1)S(1)} %peer_grad.3), channel_id=1, source_target_pairs={{0,2},{1,3},{2,0},{3,1},{4,6},{5,7},{6,4},{7,5},{8,10},{9,11},{10,... | collective-permute-start | bytes 3538952 | tf_op jit(solution)/shard_map/ppermute | solution.py:1509
  136.6 49.6 %collective-permute-start.37 = (bf16[784,768]{1,0:T(8,128)(2,1)S(1)}, bf16[784,768]{1,0:T(8,128)(2,1)S(1)}, u32[]{:S(2)}, u32[]{:S(2)}) collective-permute-start(bf16[784,768]{1,0:T(8,128)(2,1)S(1)} %peer_last.1), channel_id=1, source_target_pairs={{0,2},{1,3},{2,0},{3,1},{4,6},{5,7},{6,4},{7,5},{8,10},{9,11},{10,... | collective-permute-start | bytes 3612680 | tf_op jit(solution)/shard_map/ppermute | solution.py:1509
  142.2 13.2 %collective-permute-start.26 = (bf16[96,768]{1,0:T(8,128)(2,1)S(1)}, bf16[96,768]{1,0:T(8,128)(2,1)S(1)}, u32[]{:S(2)}, u32[]{:S(2)}) collective-permute-start(bf16[96,768]{1,0:T(8,128)(2,1)S(1)} %get-tuple-element.200), channel_id=1, source_target_pairs={{0,16},{4,20},{8,24},{12,28},{16,0},{20,4},{24,8},{28,12},{1,17},{... | collective-permute-start | bytes 442376 | tf_op jit(solution)/shard_map/ppermute | solution.py:1509
  146.3 9.0 %collective-permute-start.28 = (bf16[96,768]{1,0:T(8,128)(2,1)S(1)}, bf16[96,768]{1,0:T(8,128)(2,1)S(1)}, u32[]{:S(2)}, u32[]{:S(2)}) collective-permute-start(bf16[96,768]{1,0:T(8,128)(2,1)S(1)} %get-tuple-element.209), channel_id=1, source_target_pairs={{0,24},{4,28},{8,16},{12,20},{16,8},{20,12},{24,0},{28,4},{1,25},{... | collective-permute-start | bytes 442376 | tf_op jit(solution)/shard_map/ppermute | solution.py:1509
  159.4 11.8 %collective-permute-start.30 = (bf16[384,768]{1,0:T(8,128)(2,1)S(1)}, bf16[384,768]{1,0:T(8,128)(2,1)S(1)}, u32[]{:S(2)}, u32[]{:S(2)}) collective-permute-start(bf16[384,768]{1,0:T(8,128)(2,1)S(1)} %get-tuple-element.212), channel_id=1, source_target_pairs={{0,4},{4,0},{8,12},{12,8},{16,20},{20,16},{24,28},{28,24},{1,5},{5... | collective-permute-start | bytes 1769480 | tf_op jit(solution)/shard_map/ppermute | solution.py:1509
  160.0 13.7 %collective-permute-start.33 = (bf16[96,768]{1,0:T(8,128)(2,1)S(1)}, bf16[96,768]{1,0:T(8,128)(2,1)S(1)}, u32[]{:S(2)}, u32[]{:S(2)}) collective-permute-start(bf16[96,768]{1,0:T(8,128)(2,1)S(1)} %gather_sum.3.refs_0_), channel_id=1, source_target_pairs={{0,24},{4,28},{8,16},{12,20},{16,8},{20,12},{24,0},{28,4},{1,25},{... | collective-permute-start | bytes 442376 | tf_op jit(solution)/shard_map/ppermute | solution.py:1509
  163.4 12.7 %collective-permute-start.32 = (bf16[96,768]{1,0:T(8,128)(2,1)S(1)}, bf16[96,768]{1,0:T(8,128)(2,1)S(1)}, u32[]{:S(2)}, u32[]{:S(2)}) collective-permute-start(bf16[96,768]{1,0:T(8,128)(2,1)S(1)} %gather_sum.3.refs_0_), channel_id=1, source_target_pairs={{0,8},{4,12},{8,0},{12,4},{16,24},{20,28},{24,16},{28,20},{1,9},{5... | collective-permute-start | bytes 442376 | tf_op jit(solution)/shard_map/ppermute | solution.py:1509
  163.4 12.7 %collective-permute-start.31 = (bf16[96,768]{1,0:T(8,128)(2,1)S(1)}, bf16[96,768]{1,0:T(8,128)(2,1)S(1)}, u32[]{:S(2)}, u32[]{:S(2)}) collective-permute-start(bf16[96,768]{1,0:T(8,128)(2,1)S(1)} %gather_sum.3.refs_0_), channel_id=1, source_target_pairs={{0,16},{4,20},{8,24},{12,28},{16,0},{20,4},{24,8},{28,12},{1,17},{... | collective-permute-start | bytes 442376 | tf_op jit(solution)/shard_map/ppermute | solution.py:1509
  171.3 7.2 %collective-permute-start.35 = (bf16[96,768]{1,0:T(8,128)(2,1)S(1)}, bf16[96,768]{1,0:T(8,128)(2,1)S(1)}, u32[]{:S(2)}, u32[]{:S(2)}) collective-permute-start(bf16[96,768]{1,0:T(8,128)(2,1)S(1)} %get-tuple-element.218), channel_id=1, source_target_pairs={{0,8},{4,12},{8,0},{12,4},{16,24},{20,28},{24,16},{28,20},{1,9},{5... | collective-permute-start | bytes 442376 | tf_op jit(solution)/shard_map/ppermute | solution.py:1509
  173.7 7.8 %collective-permute-start.36 = (bf16[96,768]{1,0:T(8,128)(2,1)S(1)}, bf16[96,768]{1,0:T(8,128)(2,1)S(1)}, u32[]{:S(2)}, u32[]{:S(2)}) collective-permute-start(bf16[96,768]{1,0:T(8,128)(2,1)S(1)} %get-tuple-element.219), channel_id=1, source_target_pairs={{0,24},{4,28},{8,16},{12,20},{16,8},{20,12},{24,0},{28,4},{1,25},{... | collective-permute-start | bytes 442376 | tf_op jit(solution)/shard_map/ppermute | solution.py:1509
  176.1 10.0 %collective-permute-start.34 = (bf16[96,768]{1,0:T(8,128)(2,1)S(1)}, bf16[96,768]{1,0:T(8,128)(2,1)S(1)}, u32[]{:S(2)}, u32[]{:S(2)}) collective-permute-start(bf16[96,768]{1,0:T(8,128)(2,1)S(1)} %get-tuple-element.215), channel_id=1, source_target_pairs={{0,16},{4,20},{8,24},{12,28},{16,0},{20,4},{24,8},{28,12},{1,17},{... | collective-permute-start | bytes 442376 | tf_op jit(solution)/shard_map/ppermute | solution.py:1509
  187.6 15.7 %collective-permute-start.38 = (bf16[400,768]{1,0:T(8,128)(2,1)S(1)}, bf16[400,768]{1,0:T(8,128)(2,1)S(1)}, u32[]{:S(2)}, u32[]{:S(2)}) collective-permute-start(bf16[400,768]{1,0:T(8,128)(2,1)S(1)} %get-tuple-element.222), channel_id=1, source_target_pairs={{0,4},{4,0},{8,12},{12,8},{16,20},{20,16},{24,28},{28,24},{1,5},{5... | collective-permute-start | bytes 1843208 | tf_op jit(solution)/shard_map/ppermute | solution.py:1509
  190.1 8.7 %collective-permute-start.41 = (bf16[96,768]{1,0:T(8,128)(2,1)S(1)}, bf16[96,768]{1,0:T(8,128)(2,1)S(1)}, u32[]{:S(2)}, u32[]{:S(2)}) collective-permute-start(bf16[96,768]{1,0:T(8,128)(2,1)S(1)} %gather_sum.4.refs_0_), channel_id=1, source_target_pairs={{0,24},{4,28},{8,16},{12,20},{16,8},{20,12},{24,0},{28,4},{1,25},{... | collective-permute-start | bytes 442376 | tf_op jit(solution)/shard_map/ppermute | solution.py:1509
  192.0 8.4 %collective-permute-start.40 = (bf16[96,768]{1,0:T(8,128)(2,1)S(1)}, bf16[96,768]{1,0:T(8,128)(2,1)S(1)}, u32[]{:S(2)}, u32[]{:S(2)}) collective-permute-start(bf16[96,768]{1,0:T(8,128)(2,1)S(1)} %gather_sum.4.refs_0_), channel_id=1, source_target_pairs={{0,8},{4,12},{8,0},{12,4},{16,24},{20,28},{24,16},{28,20},{1,9},{5... | collective-permute-start | bytes 442376 | tf_op jit(solution)/shard_map/ppermute | solution.py:1509
  192.1 11.2 %collective-permute-start.39 = (bf16[96,768]{1,0:T(8,128)(2,1)S(1)}, bf16[96,768]{1,0:T(8,128)(2,1)S(1)}, u32[]{:S(2)}, u32[]{:S(2)}) collective-permute-start(bf16[96,768]{1,0:T(8,128)(2,1)S(1)} %gather_sum.4.refs_0_), channel_id=1, source_target_pairs={{0,16},{4,20},{8,24},{12,28},{16,0},{20,4},{24,8},{28,12},{1,17},{... | collective-permute-start | bytes 442376 | tf_op jit(solution)/shard_map/ppermute | solution.py:1509
  194.5 30.8 %collective-permute-start.52 = (bf16[288,768]{1,0:T(8,128)(2,1)S(1)}, bf16[288,768]{1,0:T(8,128)(2,1)S(1)}, u32[]{:S(2)}, u32[]{:S(2)}) collective-permute-start(bf16[288,768]{1,0:T(8,128)(2,1)S(1)} %get-tuple-element.242), channel_id=1, source_target_pairs={{0,2},{1,3},{2,0},{3,1},{4,6},{5,7},{6,4},{7,5},{8,10},{9,11},{10,... | collective-permute-start | bytes 1327112 | tf_op jit(solution)/shard_map/ppermute | solution.py:1509
  198.8 26.5 %collective-permute-start.49 = (bf16[256,768]{1,0:T(8,128)(2,1)S(1)}, bf16[256,768]{1,0:T(8,128)(2,1)S(1)}, u32[]{:S(2)}, u32[]{:S(2)}) collective-permute-start(bf16[256,768]{1,0:T(8,128)(2,1)S(1)} %get-tuple-element.238), channel_id=1, source_target_pairs={{0,2},{1,3},{2,0},{3,1},{4,6},{5,7},{6,4},{7,5},{8,10},{9,11},{10,... | collective-permute-start | bytes 1179656 | tf_op jit(solution)/shard_map/ppermute | solution.py:1509
  203.5 9.8 %collective-permute-start.42 = (bf16[112,768]{1,0:T(8,128)(2,1)S(1)}, bf16[112,768]{1,0:T(8,128)(2,1)S(1)}, u32[]{:S(2)}, u32[]{:S(2)}) collective-permute-start(bf16[112,768]{1,0:T(8,128)(2,1)S(1)} %get-tuple-element.227), channel_id=1, source_target_pairs={{0,16},{4,20},{8,24},{12,28},{16,0},{20,4},{24,8},{28,12},{1,17},{... | collective-permute-start | bytes 516104 | tf_op jit(solution)/shard_map/ppermute | solution.py:1509
  203.6 12.5 %collective-permute-start.43 = (bf16[112,768]{1,0:T(8,128)(2,1)S(1)}, bf16[112,768]{1,0:T(8,128)(2,1)S(1)}, u32[]{:S(2)}, u32[]{:S(2)}) collective-permute-start(bf16[112,768]{1,0:T(8,128)(2,1)S(1)} %get-tuple-element.228), channel_id=1, source_target_pairs={{0,8},{4,12},{8,0},{12,4},{16,24},{20,28},{24,16},{28,20},{1,9},{5... | collective-permute-start | bytes 516104 | tf_op jit(solution)/shard_map/ppermute | solution.py:1509
  206.3 27.6 %collective-permute-start.56 = (bf16[384,768]{1,0:T(8,128)(2,1)S(1)}, bf16[384,768]{1,0:T(8,128)(2,1)S(1)}, u32[]{:S(2)}, u32[]{:S(2)}) collective-permute-start(bf16[384,768]{1,0:T(8,128)(2,1)S(1)} %join.3), channel_id=1, source_target_pairs={{0,4},{4,0},{8,12},{12,8},{16,20},{20,16},{24,28},{28,24},{1,5},{5... | collective-permute-start | bytes 1769480 | tf_op jit(solution)/shard_map/ppermute | solution.py:1509
  213.2 7.8 %collective-permute-start.44 = (bf16[112,768]{1,0:T(8,128)(2,1)S(1)}, bf16[112,768]{1,0:T(8,128)(2,1)S(1)}, u32[]{:S(2)}, u32[]{:S(2)}) collective-permute-start(bf16[112,768]{1,0:T(8,128)(2,1)S(1)} %get-tuple-element.229), channel_id=1, source_target_pairs={{0,24},{4,28},{8,16},{12,20},{16,8},{20,12},{24,0},{28,4},{1,25},{... | collective-permute-start | bytes 516104 | tf_op jit(solution)/shard_map/ppermute | solution.py:1509
  216.0 18.4 %collective-permute-start.55 = (bf16[384,768]{1,0:T(8,128)(2,1)S(1)}, bf16[384,768]{1,0:T(8,128)(2,1)S(1)}, u32[]{:S(2)}, u32[]{:S(2)}) collective-permute-start(bf16[384,768]{1,0:T(8,128)(2,1)S(1)} %join.4), channel_id=1, source_target_pairs={{0,4},{4,0},{8,12},{12,8},{16,20},{20,16},{24,28},{28,24},{1,5},{5... | collective-permute-start | bytes 1769480 | tf_op jit(solution)/shard_map/ppermute | solution.py:1509
  221.2 7.3 %collective-permute-start.47 = (bf16[96,768]{1,0:T(8,128)(2,1)S(1)}, bf16[96,768]{1,0:T(8,128)(2,1)S(1)}, u32[]{:S(2)}, u32[]{:S(2)}) collective-permute-start(bf16[96,768]{1,0:T(8,128)(2,1)S(1)} %get-tuple-element.232.refs_0_), channel_id=1, source_target_pairs={{0,24},{4,28},{8,16},{12,20},{16,8},{20,12},{24,0},{28,4},{1,25},{... | collective-permute-start | bytes 442376 | tf_op jit(solution)/shard_map/ppermute | solution.py:1509
  225.2 7.7 %collective-permute-start.45 = (bf16[96,768]{1,0:T(8,128)(2,1)S(1)}, bf16[96,768]{1,0:T(8,128)(2,1)S(1)}, u32[]{:S(2)}, u32[]{:S(2)}) collective-permute-start(bf16[96,768]{1,0:T(8,128)(2,1)S(1)} %get-tuple-element.232.refs_0_), channel_id=1, source_target_pairs={{0,16},{4,20},{8,24},{12,28},{16,0},{20,4},{24,8},{28,12},{1,17},{... | collective-permute-start | bytes 442376 | tf_op jit(solution)/shard_map/ppermute | solution.py:1509
  228.4 10.7 %collective-permute-start.50 = (bf16[256,768]{1,0:T(8,128)(2,1)S(1)}, bf16[256,768]{1,0:T(8,128)(2,1)S(1)}, u32[]{:S(2)}, u32[]{:S(2)}) collective-permute-start(bf16[256,768]{1,0:T(8,128)(2,1)S(1)} %collective-permute-done.49.refs_3_), channel_id=1, source_target_pairs={{0,1},{1,0},{2,3},{3,2},{4,5},{5,4},{6,7},{7,6},{8,9},{9,8},{10,11... | collective-permute-start | bytes 1179656 | tf_op jit(solution)/shard_map/ppermute | solution.py:1509
  231.8 8.9 %collective-permute-start.53 = (bf16[288,768]{1,0:T(8,128)(2,1)S(1)}, bf16[288,768]{1,0:T(8,128)(2,1)S(1)}, u32[]{:S(2)}, u32[]{:S(2)}) collective-permute-start(bf16[288,768]{1,0:T(8,128)(2,1)S(1)} %collective-permute-done.52.refs_2_), channel_id=1, source_target_pairs={{0,1},{1,0},{2,3},{3,2},{4,5},{5,4},{6,7},{7,6},{8,9},{9,8},{10,11... | collective-permute-start | bytes 1327112 | tf_op jit(solution)/shard_map/ppermute | solution.py:1509
  233.0 14.7 %collective-permute-start.54 = (bf16[384,768]{1,0:T(8,128)(2,1)S(1)}, bf16[384,768]{1,0:T(8,128)(2,1)S(1)}, u32[]{:S(2)}, u32[]{:S(2)}) collective-permute-start(bf16[384,768]{1,0:T(8,128)(2,1)S(1)} %join.5), channel_id=1, source_target_pairs={{0,4},{4,0},{8,12},{12,8},{16,20},{20,16},{24,28},{28,24},{1,5},{5... | collective-permute-start | bytes 1769480 | tf_op jit(solution)/shard_map/ppermute | solution.py:1509
  (60 other events, 626.8 us)
